TPU v7x, 256 devices: a whole 4x4x8 slice. The times are simulated.
256 devices in a mesh: ctx: 32 (over y, z_lo, core), mp: 8 (over x, z_hi).
Axes of the slice: x: 4, y: 4, z: 8 (z_hi: 2, z_lo: 4; z = z_hi * 4 + z_lo), core: 2. Of those that a mesh axis runs over, the one named last changes fastest.
Arguments:
- query_mr: bfloat16 [8192, 4096], P('ctx', 'mp'), may hold values from -6 to 6
- key_mr: bfloat16 [8192, 4096], P('ctx', 'mp'), may hold values from -6 to 6
- value_mr: bfloat16 [8192, 4096], P('ctx', 'mp'), may hold values from -6 to 6
- featurizer_mr: float32 [3, 3, 4096], P(None, None, 'mp'), may hold values from -3 to 3
- mr_taps: float32 [128, 256], P(None, 'mp'), may hold values from -0.5 to 0.5
- out_mr: bfloat16 [4096, 4096], P('mp'), may hold values from -0.09375 to 0.09375
- residual: bfloat16 [8192, 4096], P('ctx', 'mp'), may hold values from -6 to 6
- in_weight: bfloat16 [3, 4096, 4096], P(None, 'mp', 'ctx'), may hold values from -0.09375 to 0.09375
- featurizer_li: float32 [3, 3, 4096], P(None, None, 'mp'), may hold values from -3 to 3
- li_rates: float32 [256, 16], P('mp'), may hold values from 0.0001 to 0.1
- li_residues: float32 [256, 16], P('mp'), may hold values from -0.06 to 0.06
- out_li: bfloat16 [4096, 4096], P('mp'), may hold values from -0.09375 to 0.09375
Outputs:
- block_output: bfloat16 [8192, 4096], P('ctx', 'mp')
All inputs are finite; a program needn't handle non-finite values.
Results may differ from a plain program's by a relative error of at most 0.03.
Values may be sent and summed in bfloat16 or wider, within the bound.
No kernel may reach another device: no remote copies, remote signals or barrier semaphores. Data moves between devices by JAX's collectives and lax.ppermute only.
A program may use at most 128 MiB of HBM per device.

v0:
```python
import functools
import jax
import jax.numpy as jnp
from jax import lax
from jax.experimental import pallas as pl
from jax.experimental.pallas import tpu as pltpu
from jax.sharding import PartitionSpec as P

F32 = jnp.float32
BF16 = jnp.bfloat16
GS = 16
LANES = 128
NG = LANES // GS
ROWS = 256
WIDTH = 512
HALO = 144
VMEM_BYTES = 48 * 1024 * 1024


def params():
    return pltpu.CompilerParams(vmem_limit_bytes=VMEM_BYTES)


def vspecs(n):
    return [pl.BlockSpec(memory_space=pltpu.VMEM)] * n


def hspecs(n):
    return [pl.BlockSpec(memory_space=pltpu.HBM)] * n


SMEM_SPEC = pl.BlockSpec(memory_space=pltpu.SMEM)


def own_lanes(group):
    lane = lax.broadcasted_iota(jnp.int32, (1, LANES), 1)
    return (lane // GS) == group


NY, NZ, NC, NX, NH = 4, 4, 2, 4, 2

def toeplitz_rows(near, far):
    row = lax.broadcasted_iota(jnp.int32, (LANES, LANES), 0)
    col = lax.broadcasted_iota(jnp.int32, (LANES, LANES), 1)
    near = pltpu.roll(jnp.broadcast_to(near, (LANES, LANES)), 0, 1, stride=1, stride_axis=0)
    upper = near
    if far is not None:
        far = pltpu.roll(jnp.broadcast_to(far, (LANES, LANES)), 0, 1, stride=1, stride_axis=0)
    else:
        far = 0.0
    upper = jnp.where(col > row, near, far).astype(BF16)
    lower = jnp.where(col <= row, near, 0.0).astype(BF16)
    return upper, lower


def toeplitz_kernel(near_ref, out_ref):
    def one(g, carry):
        upper, lower = toeplitz_rows(near_ref[pl.ds(g, 1), :], None)
        start = pl.multiple_of(g * LANES, LANES)
        out_ref[pl.ds(start, LANES), 0:LANES] = upper
        out_ref[pl.ds(start, LANES), LANES:] = lower
        return carry

    lax.fori_loop(0, near_ref.shape[0], one, 0)


def toeplitz(near):
    groups = near.shape[0]
    return pl.pallas_call(
        toeplitz_kernel,
        out_shape=jax.ShapeDtypeStruct((groups * LANES, 2 * LANES), BF16),
        in_specs=vspecs(1),
        out_specs=pl.BlockSpec(memory_space=pltpu.VMEM),
        compiler_params=params(),
        name="toeplitz",
    )(near)


def prep_kernel(rates_ref, res_ref, rate_row_ref, res_row_ref, toep_ref, leave_ref, enter_ref, lane_ref, near, far):
    groups = rates_ref.shape[0]
    back = lax.broadcasted_iota(jnp.int32, (groups, LANES), 1)
    back = jnp.where(back == 0, 0, LANES - back).astype(F32)
    near_sum = jnp.zeros((groups, LANES), F32)
    far_sum = jnp.zeros((groups, LANES), F32)
    for n in range(GS):
        rate = rates_ref[:, n : n + 1]
        weight = res_ref[:, n : n + 1]
        near_sum = near_sum + weight * jnp.exp(-rate * back)
        far_sum = far_sum + weight * jnp.exp(-rate * (back + LANES))
    near[...] = near_sum
    far[...] = far_sum

    def one(g, carry):
        upper, lower = toeplitz_rows(near[pl.ds(g, 1), :], far[pl.ds(g, 1), :])
        start = pl.multiple_of(g * LANES, LANES)
        toep_ref[pl.ds(start, LANES), 0:LANES] = upper
        toep_ref[pl.ds(start, LANES), LANES:] = lower
        return carry

    lax.fori_loop(0, groups, one, 0)
    step = lax.broadcasted_iota(jnp.int32, (ROWS, LANES), 0).astype(F32)
    for block in range(WIDTH // LANES):
        cols = slice(block * LANES, (block + 1) * LANES)
        rate = rate_row_ref[:, cols]
        leave_ref[:, cols] = res_row_ref[:, cols] * jnp.exp(-rate * step)
        enter_ref[:, cols] = jnp.exp(-rate * (ROWS - step))
    lane = lax.broadcasted_iota(jnp.int32, (groups, WIDTH), 1)
    member = lax.broadcasted_iota(jnp.int32, (groups, WIDTH), 0)
    pick = jnp.where(lane // GS == member, 1.0, 0.0)
    lane_ref[...] = lax.dot_general(
        rates_ref[...], pick, (((0,), (0,)), ((), ())),
        preferred_element_type=F32, precision=lax.Precision.HIGHEST,
    )


def prep(rates, residues):
    groups = rates.shape[0]
    return pl.pallas_call(
        prep_kernel,
        out_shape=[
            jax.ShapeDtypeStruct((groups * LANES, 2 * LANES), BF16),
            jax.ShapeDtypeStruct((ROWS, WIDTH), F32),
            jax.ShapeDtypeStruct((ROWS, WIDTH), F32),
            jax.ShapeDtypeStruct((GS, WIDTH), F32),
        ],
        in_specs=vspecs(4),
        out_specs=vspecs(4),
        scratch_shapes=[pltpu.VMEM((groups, LANES), F32)] * 2,
        compiler_params=params(),
        name="prep",
    )(rates, residues, rates.reshape(1, WIDTH), residues.reshape(1, WIDTH))


def feature(ext_ref, base, rows, taps):
    total = taps[0:1] * ext_ref[pl.ds(base, rows), :]
    for k in range(1, 3):
        total = total + taps[k : k + 1] * ext_ref[pl.ds(base - k, rows), :]
    return total


def filtered(toep_ref, block, early, middle, late):
    rhs = jnp.concatenate(
        [
            jnp.concatenate([early, middle], axis=0),
            jnp.concatenate([middle, late], axis=0),
        ],
        axis=1,
    )
    top = jnp.zeros((LANES, LANES), F32)
    low = jnp.zeros((LANES, LANES), F32)
    for g in range(NG):
        start = (block * NG + g) * LANES
        prod = jnp.dot(toep_ref[start : start + LANES, :], rhs, preferred_element_type=F32)
        mine = own_lanes(g)
        top = jnp.where(mine, prod[:, :LANES], top)
        low = jnp.where(mine, prod[:, LANES:], low)
    return top, low


def share_loads(where_ref, w_ref, wbuf, sems, flip):
    x = where_ref[0]
    zh = where_ref[1]
    half = zh if flip == 0 else 1 - zh
    copies = []
    for d in range(4):
        block = lax.rem(x + d, 4) * 2 + half
        copy = pltpu.make_async_copy(
            w_ref.at[:, pl.ds(pl.multiple_of(block * WIDTH, WIDTH), WIDTH)], wbuf.at[d], sems.at[d]
        )
        copy.start()
        copies.append(copy)
    return copies


def share_products(copies, y_ref, wbuf, outs):
    for d in (1, 3, 2, 0):
        copies[d].wait()
        outs[d][...] = jnp.dot(y_ref[...], wbuf[d], preferred_element_type=F32).astype(BF16)


SHARE_SCRATCH = [pltpu.VMEM((4, WIDTH, WIDTH), BF16), pltpu.SemaphoreType.DMA((4,))]
PIECE = jax.ShapeDtypeStruct((ROWS, WIDTH), BF16)


def share_kernel(flip, where_ref, y_ref, w_ref, o0, o1, o2, o3, wbuf, sems):
    copies = share_loads(where_ref, w_ref, wbuf, sems, flip)
    share_products(copies, y_ref, wbuf, (o0, o1, o2, o3))


def shares(where, y, weight, flip):
    return pl.pallas_call(
        functools.partial(share_kernel, flip),
        out_shape=[PIECE] * 4,
        in_specs=[SMEM_SPEC] + vspecs(1) + hspecs(1),
        out_specs=vspecs(4),
        scratch_shapes=SHARE_SCRATCH,
        compiler_params=params(),
        name="shares",
    )(where, y, weight)


def mr_kernel(
    where_ref, q_ref, k_ref, v_ref, halo_ref, feat_ref, toep_ref, w_ref,
    y_ref, o0, o1, o2, o3, kx, vx, qx, wbuf, sems,
):
    copies = share_loads(where_ref, w_ref, wbuf, sems, 1)
    for block in range(WIDTH // LANES):
        cols = slice(block * LANES, (block + 1) * LANES)
        kx[0:HALO, :] = halo_ref[0:HALO, cols].astype(F32)
        kx[HALO:, :] = k_ref[:, cols].astype(F32)
        vx[0:HALO, :] = halo_ref[HALO : 2 * HALO, cols].astype(F32)
        vx[HALO:, :] = v_ref[:, cols].astype(F32)
        qx[0:16, :] = halo_ref[2 * HALO : 2 * HALO + 16, cols].astype(F32)
        qx[16:, :] = q_ref[:, cols].astype(F32)
        zs = []
        for part in range(3):
            base = HALO - LANES + part * LANES
            kf = feature(kx, base, LANES, feat_ref[1, :, cols])
            vf = feature(vx, base, LANES, feat_ref[2, :, cols])
            zs.append((kf * vf).astype(BF16))
        top, low = filtered(toep_ref, block, *zs)
        for part, conv in ((0, top), (1, low)):
            qf = feature(qx, 16 + part * LANES, LANES, feat_ref[0, :, cols])
            y_ref[part * LANES : (part + 1) * LANES, cols] = (qf * conv).astype(BF16)
    share_products(copies, y_ref, wbuf, (o0, o1, o2, o3))


def mr_op(where, q, k, v, halo, feat, toep, weight):
    return pl.pallas_call(
        mr_kernel,
        out_shape=[PIECE] * 5,
        in_specs=[SMEM_SPEC] + vspecs(6) + hspecs(1),
        out_specs=vspecs(5),
        scratch_shapes=[
            pltpu.VMEM((HALO + ROWS, LANES), F32),
            pltpu.VMEM((HALO + ROWS, LANES), F32),
            pltpu.VMEM((16 + ROWS, LANES), F32),
        ] + SHARE_SCRATCH,
        compiler_params=params(),
        name="mr_op",
    )(where, q, k, v, halo, feat, toep, weight)


def project_kernel(flips, count, first, last, where_ref, *refs):
    n = len(flips) * 4
    hidden_refs = refs[:n]
    w_ref = refs[n]
    pos = n + 1
    acc_refs = ()
    if not first:
        acc_refs = refs[pos : pos + count]
        pos += count
    out_refs = refs[pos : pos + count]
    hbuf, wbuf, hsem, wsem = refs[pos + count :]
    x = where_ref[0]
    hcopies, wcopies = [], []
    for i in range(n):
        e, d = flips[i // 4], i % 4
        copy = pltpu.make_async_copy(hidden_refs[i], hbuf.at[i], hsem.at[i])
        copy.start()
        hcopies.append(copy)
        src_y = lax.rem(x + 4 - d, 4)
        for b in range(4):
            odd = 1 - b // 2
            high = odd if e == 1 else 1 - odd
            member = (src_y * 4 + high * 2 + odd) * 2 + b % 2
            copy = pltpu.make_async_copy(
                w_ref.at[member],
                wbuf.at[i, :, :, pl.ds(b * LANES, LANES)],
                wsem.at[i, b],
            )
            copy.start()
            wcopies.append(copy)
    sums = [None] * count
    for i in range(n):
        hcopies[i].wait()
        for b in range(4):
            wcopies[i * 4 + b].wait()
        for j in range(count):
            prod = jnp.dot(hbuf[i], wbuf[i, j], preferred_element_type=F32)
            if i == 0:
                sums[j] = prod if first else prod + acc_refs[j][...]
            else:
                sums[j] = sums[j] + prod
    for j in range(count):
        out_refs[j][...] = sums[j].astype(BF16) if last else sums[j]


def project(where, pieces, weights, flips, count, acc=(), last=True):
    n = len(pieces)
    return pl.pallas_call(
        functools.partial(project_kernel, flips, count, not acc, last),
        out_shape=[jax.ShapeDtypeStruct((ROWS, WIDTH), BF16 if last else F32)] * count,
        in_specs=[SMEM_SPEC] + hspecs(n + 1) + vspecs(len(acc)),
        out_specs=vspecs(count),
        scratch_shapes=[
            pltpu.VMEM((n, ROWS, WIDTH), BF16),
            pltpu.VMEM((n, count, WIDTH, WIDTH), BF16),
            pltpu.SemaphoreType.DMA((n,)),
            pltpu.SemaphoreType.DMA((n, 4)),
        ],
        compiler_params=params(),
        name="project",
    )(where, *pieces, weights, *acc)


def li_gate_kernel(k_ref, v_ref, halo_ref, feat_ref, enter_ref, z_ref, load_ref, kx, vx):
    over_rows = (((0,), (0,)), ((), ()))
    for block in range(WIDTH // LANES):
        cols = slice(block * LANES, (block + 1) * LANES)
        kx[0:16, :] = halo_ref[0:16, cols].astype(F32)
        kx[16:, :] = k_ref[:, cols].astype(F32)
        vx[0:16, :] = halo_ref[16:32, cols].astype(F32)
        vx[16:, :] = v_ref[:, cols].astype(F32)
        kf = feature(kx, 16, ROWS, feat_ref[1, :, cols])
        vf = feature(vx, 16, ROWS, feat_ref[2, :, cols])
        z = (kf * vf).astype(BF16)
        z_ref[:, cols] = z
        enter = enter_ref[:, cols]
        high = enter.astype(BF16)
        rest = (enter - high.astype(F32)).astype(BF16)
        prod = lax.dot_general(high, z, over_rows, preferred_element_type=F32)
        prod = prod + lax.dot_general(rest, z, over_rows, preferred_element_type=F32)
        load = jnp.zeros((GS, LANES), F32)
        for g in range(NG):
            load = jnp.where(own_lanes(g), prod[g * GS : (g + 1) * GS, :], load)
        load_ref[:, cols] = load


def li_gate(k, v, halo, feat, enter):
    return pl.pallas_call(
        li_gate_kernel,
        out_shape=[PIECE, STATE],
        in_specs=vspecs(5),
        out_specs=vspecs(2),
        scratch_shapes=[pltpu.VMEM((16 + ROWS, LANES), F32)] * 2,
        compiler_params=params(),
        name="li_gate",
    )(k, v, halo, feat, enter)


STATE = jax.ShapeDtypeStruct((GS, WIDTH), F32)


def chip_kernel(where_ref, load_ref, other_ref, rates_ref, chip_ref):
    k = where_ref[4]
    load, other = load_ref[...], other_ref[...]
    fade = jnp.exp(-rates_ref[...] * (1.0 * ROWS))
    chip_ref[...] = jnp.where(k == 0, load * fade + other, other * fade + load)


def chip_state(where, load, other, rates):
    return pl.pallas_call(
        chip_kernel,
        out_shape=STATE,
        in_specs=[SMEM_SPEC] + vspecs(3),
        out_specs=pl.BlockSpec(memory_space=pltpu.VMEM),
        compiler_params=params(),
        name="chip_state",
    )(where, load, other, rates)


def line_kernel(where_ref, c0, c1, c2, c3, rates_ref, total_ref, carry_ref):
    zl = where_ref[3]
    rates = rates_ref[...]
    total = jnp.zeros(rates.shape, F32)
    carry = jnp.zeros(rates.shape, F32)
    for s, ref in enumerate((c0, c1, c2, c3)):
        piece = ref[...]
        src = lax.rem(zl + NZ - s, NZ)
        gap = ((NZ - 1 - src) * (2 * ROWS)).astype(F32)
        total = total + jnp.exp(-rates * gap) * piece
        if s > 0:
            part = jnp.exp(-rates * (2.0 * ROWS * (s - 1))) * piece
            carry = carry + jnp.where(zl >= s, part, 0.0)
    total_ref[...] = total
    carry_ref[...] = carry


def line_state(where, pieces, rates):
    return pl.pallas_call(
        line_kernel,
        out_shape=[STATE] * 2,
        in_specs=[SMEM_SPEC] + vspecs(5),
        out_specs=vspecs(2),
        compiler_params=params(),
        name="line_state",
    )(where, *pieces, rates)


def li_inner_kernel(z_ref, toep_ref, conv_ref):
    for block in range(WIDTH // LANES):
        cols = slice(block * LANES, (block + 1) * LANES)
        first = z_ref[0:LANES, cols]
        second = z_ref[LANES:ROWS, cols]
        top, low = filtered(toep_ref, block, jnp.zeros_like(first), first, second)
        conv_ref[0:LANES, cols] = top
        conv_ref[LANES:ROWS, cols] = low


def li_inner(z, toep):
    return pl.pallas_call(
        li_inner_kernel,
        out_shape=jax.ShapeDtypeStruct((ROWS, WIDTH), F32),
        in_specs=vspecs(2),
        out_specs=pl.BlockSpec(memory_space=pltpu.VMEM),
        compiler_params=params(),
        name="li_inner",
    )(z, toep)


def li_outer_kernel(
    where_ref, conv_ref, q_ref, halo_ref, feat_ref, leave_ref, rates_ref,
    carry_ref, other_ref, y1_ref, y2_ref, y3_ref, w_ref,
    y_ref, o0, o1, o2, o3, qx, wbuf, sems,
):
    copies = share_loads(where_ref, w_ref, wbuf, sems, 1)
    zl, k = where_ref[3], where_ref[4]
    rates = rates_ref[...]
    above = y1_ref[...]
    above = above + jnp.exp(-rates * (2.0 * ROWS * NZ)) * y2_ref[...]
    above = above + jnp.exp(-rates * (4.0 * ROWS * NZ)) * y3_ref[...]
    chip = carry_ref[...] + jnp.exp(-rates * (zl * (2 * ROWS)).astype(F32)) * above
    full = jnp.where(k == 0, chip, jnp.exp(-rates * (1.0 * ROWS)) * chip + other_ref[...])
    for block in range(WIDTH // LANES):
        cols = slice(block * LANES, (block + 1) * LANES)
        qx[0:16, :] = halo_ref[:, cols].astype(F32)
        qx[16:, :] = q_ref[:, cols].astype(F32)
        qf = feature(qx, 16, ROWS, feat_ref[0, :, cols])
        state = full[:, cols]
        spread = jnp.concatenate(
            [jnp.where(own_lanes(g), state, 0.0) for g in range(NG)], axis=0
        )
        outer = jnp.dot(
            leave_ref[:, cols], spread, preferred_element_type=F32, precision=lax.Precision.HIGHEST
        )
        y_ref[:, cols] = (qf * (conv_ref[:, cols] + outer)).astype(BF16)
    share_products(copies, y_ref, wbuf, (o0, o1, o2, o3))


def li_outer(where, conv, q, halo, feat, leave, rates, carry, other, above, weight):
    return pl.pallas_call(
        li_outer_kernel,
        out_shape=[PIECE] * 5,
        in_specs=[SMEM_SPEC] + vspecs(11) + hspecs(1),
        out_specs=vspecs(5),
        scratch_shapes=[pltpu.VMEM((16 + ROWS, LANES), F32)] + SHARE_SCRATCH,
        compiler_params=params(),
        name="li_outer",
    )(where, conv, q, halo, feat, leave, rates, carry, other, *above, weight)


def ctx_of(y, zl, k):
    return (y * NZ + zl) * NC + k


def mp_of(x, zh):
    return x * NH + zh


def x_shift(by):
    return [(mp_of(x, h), mp_of((x + by) % NX, h)) for x in range(NX) for h in range(NH)]


H_SWAP = [(mp_of(x, h), mp_of(x, 1 - h)) for x in range(NX) for h in range(NH)]
CORE_SWAP = [(i, i ^ 1) for i in range(NY * NZ * NC)]


def z_shift(by):
    return [
        (ctx_of(y, z, k), ctx_of(y, (z + by) % NZ, k))
        for y in range(NY) for z in range(NZ) for k in range(NC)
    ]


def y_shift(by):
    return [
        (ctx_of(y, z, k), ctx_of((y + by) % NY, z, k))
        for y in range(NY) for z in range(NZ) for k in range(NC)
    ]


def weight_moves():
    moves = []
    for y in range(NY):
        for zl in range(NZ):
            for k in range(NC):
                for x in range(NX):
                    for h in range(NH):
                        x2, h2, y2 = y, zl // 2, x
                        l0 = zl % 2
                        odd = 1 - l0
                        outer = h ^ h2
                        high = odd if outer else 1 - odd
                        z2 = high * 2 + odd
                        src = ctx_of(y, zl, k) * (NX * NH) + mp_of(x, h)
                        dst = ctx_of(y2, z2, k) * (NX * NH) + mp_of(x2, h2)
                        moves.append((src, dst))
    return moves


def tied(*values):
    return lax.optimization_barrier(values)


def sum_shares(where, y, other, weight, own_extra, fillers):
    got = [lax.ppermute(other[d], "mp", x_shift(d)) for d in (1, 3, 2)]
    if fillers:
        held = tied(*got, *fillers)
        got, fillers = held[:3], held[3:]
    total_other = other[0].astype(F32)
    for piece in got:
        total_other = total_other + piece.astype(F32)
    total_other, *mine = tied(total_other.astype(BF16), *shares(where, y, weight, 0))
    crossed = lax.ppermute(total_other, "mp", H_SWAP)
    got_mine = [lax.ppermute(mine[d], "mp", x_shift(d)) for d in (1, 3, 2)]
    total = own_extra.astype(F32) + mine[0].astype(F32)
    for piece in got_mine:
        total = total + piece.astype(F32)
    return (total + crossed.astype(F32)).astype(BF16), fillers


def body(
    query_mr, key_mr, value_mr, featurizer_mr, mr_taps, out_mr,
    residual, in_weight, featurizer_li, li_rates, li_residues, out_li,
):
    ctx = lax.axis_index("ctx")
    mp = lax.axis_index("mp")
    x, zh = mp // NH, mp % NH
    y, zl, k = ctx // (NZ * NC), (ctx // NC) % NZ, ctx % NC
    where = jnp.stack([x, zh, y, zl, k]).astype(jnp.int32)

    forward = [(i, i + 1) for i in range(NY * NZ * NC - 1)]
    rim = jnp.concatenate(
        [key_mr[ROWS - HALO :], value_mr[ROWS - HALO :], query_mr[ROWS - 16 :]], axis=0
    )
    rim, in_weight = tied(rim, in_weight)
    halo = lax.ppermute(rim, "ctx", forward)
    moved_kv = lax.ppermute(in_weight[1:3], ("ctx", "mp"), weight_moves())
    moved_q = lax.ppermute(in_weight[0:1], ("ctx", "mp"), weight_moves())

    toep_mr = toeplitz(jnp.concatenate([mr_taps[:1], mr_taps[1:][::-1]], axis=0).T)

    halo, moved_kv, toep_mr = tied(halo, moved_kv, toep_mr)
    gated_one, *other_one = mr_op(
        where, query_mr, key_mr, value_mr, halo, featurizer_mr, toep_mr, out_mr
    )
    weights_kv = lax.all_gather(moved_kv, "ctx")
    filters = prep(li_rates, li_residues)
    hidden, filters = sum_shares(
        where, gated_one, other_one, out_mr, residual, tuple(filters) + (moved_q,)
    )
    toep_li, leave, enter, lane_rates, moved_q = filters

    hidden, moved_q = tied(hidden, moved_q)
    crossed = lax.ppermute(hidden, "mp", H_SWAP)
    own_pieces = [hidden] + [lax.ppermute(hidden, "mp", x_shift(d)) for d in (1, 2, 3)]
    weights_q = lax.all_gather(moved_q, "ctx")
    far_pieces = [crossed] + [lax.ppermute(crossed, "mp", x_shift(d)) for d in (1, 2, 3)]
    partial = project(where, own_pieces, weights_kv, (0,), 2, last=False)
    fresh_k, fresh_v = project(where, far_pieces, weights_kv, (1,), 2, acc=tuple(partial))
    halo_kv = lax.ppermute(
        jnp.concatenate([fresh_k[ROWS - 16 :], fresh_v[ROWS - 16 :]], axis=0), "ctx", forward
    )
    product, load = li_gate(fresh_k, fresh_v, halo_kv, featurizer_li, enter)
    other_load = lax.ppermute(load, "ctx", CORE_SWAP)
    chip = chip_state(where, load, other_load, lane_rates)
    before = [lax.ppermute(chip, "ctx", z_shift(s)) for s in (1, 2, 3)]
    line_total, line_carry = line_state(where, [chip] + before, lane_rates)
    above = []
    for s in (1, 2, 3):
        pairs = [
            (ctx_of(a, b, c), ctx_of(a + s, b, c))
            for a in range(NY - s) for b in range(NZ) for c in range(NC)
        ]
        above.append(lax.ppermute(line_total, "ctx", pairs))

    (fresh_q,) = project(where, own_pieces + far_pieces, weights_q, (0, 1), 1)
    halo_q = lax.ppermute(fresh_q[ROWS - 16 :], "ctx", forward)
    conv = li_inner(product, toep_li)

    gated_two, *other_two = li_outer(
        where, conv, fresh_q, halo_q, featurizer_li, leave, lane_rates,
        line_carry, other_load, above, out_li,
    )
    return sum_shares(where, gated_two, other_two, out_li, hidden, ())[0]


def solution(mesh):
    return jax.shard_map(
        body,
        mesh=mesh,
        in_specs=(
            P("ctx", "mp"),
            P("ctx", "mp"),
            P("ctx", "mp"),
            P(None, None, "mp"),
            P(None, "mp"),
            P("mp", None),
            P("ctx", "mp"),
            P(None, "mp", "ctx"),
            P(None, None, "mp"),
            P("mp", None),
            P("mp", None),
            P("mp", None),
        ),
        out_specs=P("ctx", "mp"),
        check_vma=False,
    )
```

profile of v0, /device:TPU:2, one launch (start us, length us, event | category | flops | bytes accessed | tf_op | source)
XLA Modules:
  0.0 253.4 jit_solution(4560027381411328439)
XLA Ops:
  12.7 3.1 %collective-permute-start.1 = (bf16[2,512,128]{2,1,0:T(8,128)(2,1)}, bf16[2,512,128]{2,1,0:T(8,128)(2,1)}, u32[]{:S(2)}, u32[]{:S(2)}) collective-permute-start(bf16[2,512,128]{2,1,0:T(8,128)(2,1)} %slice.33), channel_id=1, source_target_pairs={{0,16},{1,48},{2,80},{3,112},{4,144},{5,176},{6,208},{7,240},{8,24... | collective-permute-start | bytes 786440 | tf_op jit(solution)/shard_map/ppermute | solution.py:539
  17.4 2.7 %toeplitz.1.toep_ref = bf16[4096,256]{1,0:T(8,128)(2,1)S(1)} custom-call(f32[32,128]{1,0:T(8,128)S(1)} %maximum_bitcast_fusion.near_ref), custom_call_target="tpu_custom_call" | custom-call | tf_op jit(solution)/shard_map/toeplitz/pallas_call | solution.py:69
  20.2 9.4 %collective-permute-done.1 = bf16[2,512,128]{2,1,0:T(8,128)(2,1)} collective-permute-done((bf16[2,512,128]{2,1,0:T(8,128)(2,1)}, bf16[2,512,128]{2,1,0:T(8,128)(2,1)}, u32[]{:S(2)}, u32[]{:S(2)}) %collective-permute-start.1) | collective-permute-done | bytes 262176 | tf_op jit(solution)/shard_map/ppermute | solution.py:539
  29.8 4.7 %mr_op.1 = (bf16[256,512]{1,0:T(8,128)(2,1)S(1)}, bf16[256,512]{1,0:T(8,128)(2,1)S(1)}, bf16[256,512]{1,0:T(8,128)(2,1)}, bf16[256,512]{1,0:T(8,128)(2,1)}, bf16[256,512]{1,0:T(8,128)(2,1)}) custom-call(s32[5]{0:T(128)S(1)} %stack.23.where_ref, bf16[256,512]{1,0:T(8,128)(2,1)S(1)} %copy-done.8, bf16[256,512]{1,0:T(8,128)(2,1)S(1)} %copy-done.2, ...), custom_call_target="tpu_custom_call" | custom-call | tf_op jit(solution)/shard_map/mr_op/pallas_call | solution.py:229
  36.0 5.1 %collective-permute-start.2 = (bf16[256,512]{1,0:T(8,128)(2,1)}, bf16[256,512]{1,0:T(8,128)(2,1)}, u32[]{:S(2)}, u32[]{:S(2)}) collective-permute-start(bf16[256,512]{1,0:T(8,128)(2,1)} %get-tuple-element.65), channel_id=1, source_target_pairs={{0,2},{1,3},{2,4},{3,5},{4,6},{5,7},{6,0},{7,1},{8,10},{9,11},{10,... | collective-permute-start | bytes 786440 | tf_op jit(solution)/shard_map/ppermute | solution.py:507
  45.3 3.4 %prep.1 = (bf16[4096,256]{1,0:T(8,128)(2,1)S(1)}, f32[256,512]{1,0:T(8,128)S(1)}, f32[256,512]{1,0:T(8,128)S(1)}, f32[16,512]{1,0:T(8,128)S(1)}) custom-call(f32[32,16]{1,0:T(8,128)S(1)} %copy.23.rates_ref, f32[32,16]{1,0:T(8,128)S(1)} %copy.24.res_ref, f32[1,512]{1,0:T(1,128)S(1)} %reshape.6.rate_row_ref, f32[1,512]{1,0:T(1,128)S(1)} %reshape.7.res_row_ref), custom_call_target="tpu_custom_call" | custom-call | tf_op jit(solution)/shard_map/prep/pallas_call | solution.py:118
  55.7 3.3 %collective-permute-done.5 = bf16[1,512,128]{2,1,0:T(8,128)(2,1)} collective-permute-done((bf16[1,512,128]{2,1,0:T(8,128)(2,1)}, bf16[1,512,128]{2,1,0:T(8,128)(2,1)}, u32[]{:S(2)}, u32[]{:S(2)}) %collective-permute-start.5) | collective-permute-done | bytes 131104 | tf_op jit(solution)/shard_map/ppermute | solution.py:540
  64.1 9.2 %collective-permute-start.9 = (bf16[256,512]{1,0:T(8,128)(2,1)S(1)}, bf16[256,512]{1,0:T(8,128)(2,1)S(1)}, u32[]{:S(2)}, u32[]{:S(2)}) collective-permute-start(bf16[256,512]{1,0:T(8,128)(2,1)S(1)} %add_convert_fusion.3), channel_id=1, source_target_pairs={{0,1},{1,0},{2,3},{3,2},{4,5},{5,4},{6,7},{7,6},{8,9},{9,8},{10,11... | collective-permute-start | bytes 786440 | tf_op jit(solution)/shard_map/ppermute | solution.py:515
  73.3 3.3 %collective-permute-done.8 = bf16[256,512]{1,0:T(8,128)(2,1)S(1)} collective-permute-done((bf16[256,512]{1,0:T(8,128)(2,1)S(1)}, bf16[256,512]{1,0:T(8,128)(2,1)S(1)}, u32[]{:S(2)}, u32[]{:S(2)}) %collective-permute-start.8) | collective-permute-done | bytes 262176 | tf_op jit(solution)/shard_map/ppermute | solution.py:516
  76.6 14.1 %collective-permute-done.9 = bf16[256,512]{1,0:T(8,128)(2,1)S(1)} collective-permute-done((bf16[256,512]{1,0:T(8,128)(2,1)S(1)}, bf16[256,512]{1,0:T(8,128)(2,1)S(1)}, u32[]{:S(2)}, u32[]{:S(2)}) %collective-permute-start.9) | collective-permute-done | bytes 262176 | tf_op jit(solution)/shard_map/ppermute | solution.py:515
  91.9 5.7 %collective-permute-start.10 = (bf16[256,512]{1,0:T(8,128)(2,1)S(1)}, bf16[256,512]{1,0:T(8,128)(2,1)S(1)}, u32[]{:S(2)}, u32[]{:S(2)}) collective-permute-start(bf16[256,512]{1,0:T(8,128)(2,1)S(1)} %add_convert_fusion.2.refs_0_), channel_id=1, source_target_pairs={{0,1},{1,0},{2,3},{3,2},{4,5},{5,4},{6,7},{7,6},{8,9},{9,8},{10,11... | collective-permute-start | bytes 786440 | tf_op jit(solution)/shard_map/ppermute | solution.py:556
  102.2 12.2 %collective-permute-done.10.refs_0_.refs_4_ = bf16[256,512]{1,0:T(8,128)(2,1)S(1)} collective-permute-done((bf16[256,512]{1,0:T(8,128)(2,1)S(1)}, bf16[256,512]{1,0:T(8,128)(2,1)S(1)}, u32[]{:S(2)}, u32[]{:S(2)}) %collective-permute-start.10) | collective-permute-done | bytes 262176 | tf_op jit(solution)/shard_map/ppermute | solution.py:556
  118.3 8.4 %all-gather.5.cloned.1.call-done = bf16[64,512,128]{2,1,0:T(8,128)(2,1)} async-done(((bf16[2,512,128]{2,1,0:T(8,128)(2,1)}), bf16[64,512,128]{2,1,0:T(8,128)(2,1)}) %all-gather.5.cloned.1.call-update) | async-done | bytes 8388624 | tf_op jit(solution)/shard_map/all_gather | solution.py:548
  126.7 3.6 %project.3 = (f32[256,512]{1,0:T(8,128)S(1)}, f32[256,512]{1,0:T(8,128)S(1)}) custom-call(s32[5]{0:T(128)S(1)} %stack.23.where_ref, bf16[256,512]{1,0:T(8,128)(2,1)S(1)} %add_convert_fusion.2.refs_0_, bf16[256,512]{1,0:T(8,128)(2,1)S(1)} %collective-permute-done.14.refs_1_, bf16[256,512]{1,0:T(8,128)(2,1)S(1)} %collective-permute-done.15.refs_2_, ...), custom_call_target="tpu_custom_call" | custom-call | tf_op jit(solution)/shard_map/project/pallas_call | solution.py:291
  130.4 3.8 %project.4 = (bf16[256,512]{1,0:T(8,128)(2,1)S(1)}, bf16[256,512]{1,0:T(8,128)(2,1)S(1)}) custom-call(s32[5]{0:T(128)S(1)} %stack.23.where_ref, bf16[256,512]{1,0:T(8,128)(2,1)S(1)} %collective-permute-done.10.refs_0_.refs_4_, bf16[256,512]{1,0:T(8,128)(2,1)} %collective-permute-done.11.refs_1_.refs_5_, ...), custom_call_target="tpu_custom_call" | custom-call | tf_op jit(solution)/shard_map/project/pallas_call | solution.py:291
  151.3 5.6 %collective-permute-start.23 = (f32[16,512]{1,0:T(8,128)}, f32[16,512]{1,0:T(8,128)}, u32[]{:S(2)}, u32[]{:S(2)}) collective-permute-start(f32[16,512]{1,0:T(8,128)} %get-tuple-element.100), channel_id=1, source_target_pairs={{0,64},{8,72},{16,80},{24,88},{32,96},{40,104},{48,112},{56,120},{... | collective-permute-start | bytes 98312 | tf_op jit(solution)/shard_map/ppermute | solution.py:576
  156.9 4.4 %collective-permute-start.24 = (f32[16,512]{1,0:T(8,128)}, f32[16,512]{1,0:T(8,128)}, u32[]{:S(2)}, u32[]{:S(2)}) collective-permute-start(f32[16,512]{1,0:T(8,128)} %get-tuple-element.100), channel_id=1, source_target_pairs={{0,128},{8,136},{16,144},{24,152},{32,160},{40,168},{48,176},{56,1... | collective-permute-start | bytes 98312 | tf_op jit(solution)/shard_map/ppermute | solution.py:576
  163.2 33.5 %all-gather.7.cloned.1.call-done = bf16[32,512,128]{2,1,0:T(8,128)(2,1)} async-done(((bf16[1,512,128]{2,1,0:T(8,128)(2,1)}), bf16[32,512,128]{2,1,0:T(8,128)(2,1)}) %all-gather.7.cloned.1.call-update) | async-done | bytes 4194320 | tf_op jit(solution)/shard_map/all_gather | solution.py:558
  196.7 3.8 %project.5.q_ref = bf16[256,512]{1,0:T(8,128)(2,1)S(1)} custom-call(s32[5]{0:T(128)S(1)} %stack.23.where_ref, bf16[256,512]{1,0:T(8,128)(2,1)S(1)} %add_convert_fusion.2.refs_0_, bf16[256,512]{1,0:T(8,128)(2,1)S(1)} %collective-permute-done.14.refs_1_, bf16[256,512]{1,0:T(8,128)(2,1)S(1)} %collective-permute-done.15.refs_2_, ...), custom_call_target="tpu_custom_call" | custom-call | tf_op jit(solution)/shard_map/project/pallas_call | solution.py:291
  203.5 4.2 %li_outer.1 = (bf16[256,512]{1,0:T(8,128)(2,1)S(1)}, bf16[256,512]{1,0:T(8,128)(2,1)S(1)}, bf16[256,512]{1,0:T(8,128)(2,1)S(1)}, bf16[256,512]{1,0:T(8,128)(2,1)S(1)}, bf16[256,512]{1,0:T(8,128)(2,1)S(1)}) custom-call(s32[5]{0:T(128)S(1)} %stack.23.where_ref, f32[256,512]{1,0:T(8,128)S(1)} %li_inner.1.conv_ref, bf16[256,512]{1,0:T(8,128)(2,1)S(1)} %project.5.q_ref, ...), custom_call_target="tpu_custom_call" | custom-call | tf_op jit(solution)/shard_map/li_outer/pallas_call | solution.py:442
  218.2 6.3 %collective-permute-done.28 = bf16[256,512]{1,0:T(8,128)(2,1)S(1)} collective-permute-done((bf16[256,512]{1,0:T(8,128)(2,1)S(1)}, bf16[256,512]{1,0:T(8,128)(2,1)S(1)}, u32[]{:S(2)}, u32[]{:S(2)}) %collective-permute-start.28) | collective-permute-done | bytes 262176 | tf_op jit(solution)/shard_map/ppermute | solution.py:507
  228.6 5.0 %collective-permute-start.32 = (bf16[256,512]{1,0:T(8,128)(2,1)S(1)}, bf16[256,512]{1,0:T(8,128)(2,1)S(1)}, u32[]{:S(2)}, u32[]{:S(2)}) collective-permute-start(bf16[256,512]{1,0:T(8,128)(2,1)S(1)} %add_convert_fusion.1), channel_id=1, source_target_pairs={{0,1},{1,0},{2,3},{3,2},{4,5},{5,4},{6,7},{7,6},{8,9},{9,8},{10,11... | collective-permute-start | bytes 786440 | tf_op jit(solution)/shard_map/ppermute | solution.py:515
  233.9 6.4 %collective-permute-done.31 = bf16[256,512]{1,0:T(8,128)(2,1)S(1)} collective-permute-done((bf16[256,512]{1,0:T(8,128)(2,1)S(1)}, bf16[256,512]{1,0:T(8,128)(2,1)S(1)}, u32[]{:S(2)}, u32[]{:S(2)}) %collective-permute-start.31) | collective-permute-done | bytes 262176 | tf_op jit(solution)/shard_map/ppermute | solution.py:516
  240.3 5.4 %collective-permute-done.32 = bf16[256,512]{1,0:T(8,128)(2,1)S(1)} collective-permute-done((bf16[256,512]{1,0:T(8,128)(2,1)S(1)}, bf16[256,512]{1,0:T(8,128)(2,1)S(1)}, u32[]{:S(2)}, u32[]{:S(2)}) %collective-permute-start.32) | collective-permute-done | bytes 262176 | tf_op jit(solution)/shard_map/ppermute | solution.py:515
  (121 shorter events, 73.1 us)
Async XLA Ops:
  6.5 120.2 %all-gather.5.cloned.1.call-start = ((), (), s32[]{:S(2)}) async-start(), calls=%async_computation | async-start | bytes 8650752 | tf_op jit(solution)/shard_map/all_gather | solution.py:548
  9.2 20.3 %collective-permute-start = (bf16[304,512]{1,0:T(8,128)(2,1)S(1)}, bf16[304,512]{1,0:T(8,128)(2,1)S(1)}, u32[]{:S(2)}, u32[]{:S(2)}) collective-permute-start(bf16[304,512]{1,0:T(8,128)(2,1)S(1)} %pad_maximum_fusion), channel_id=1, source_target_pairs={{0,8},{8,16},{16,24},{24,32},{32,40},{40,48},{48,56},{56,64},{64,7... | collective-permute-start | bytes 933896 | tf_op jit(solution)/shard_map/ppermute | solution.py:538
  12.7 16.9 %collective-permute-start.1 = (bf16[2,512,128]{2,1,0:T(8,128)(2,1)}, bf16[2,512,128]{2,1,0:T(8,128)(2,1)}, u32[]{:S(2)}, u32[]{:S(2)}) collective-permute-start(bf16[2,512,128]{2,1,0:T(8,128)(2,1)} %slice.33), channel_id=1, source_target_pairs={{0,16},{1,48},{2,80},{3,112},{4,144},{5,176},{6,208},{7,240},{8,24... | collective-permute-start | bytes 786440 | tf_op jit(solution)/shard_map/ppermute | solution.py:539
  29.6 167.1 %all-gather.7.cloned.1.call-start = ((), (), s32[]{:S(2)}) async-start(), calls=%async_computation.1 | async-start | bytes 4325376 | tf_op jit(solution)/shard_map/all_gather | solution.py:558
  36.0 23.1 %collective-permute-start.2 = (bf16[256,512]{1,0:T(8,128)(2,1)}, bf16[256,512]{1,0:T(8,128)(2,1)}, u32[]{:S(2)}, u32[]{:S(2)}) collective-permute-start(bf16[256,512]{1,0:T(8,128)(2,1)} %get-tuple-element.65), channel_id=1, source_target_pairs={{0,2},{1,3},{2,4},{3,5},{4,6},{5,7},{6,0},{7,1},{8,10},{9,11},{10,... | collective-permute-start | bytes 786440 | tf_op jit(solution)/shard_map/ppermute | solution.py:507
  41.0 18.0 %collective-permute-start.3 = (bf16[256,512]{1,0:T(8,128)(2,1)}, bf16[256,512]{1,0:T(8,128)(2,1)}, u32[]{:S(2)}, u32[]{:S(2)}) collective-permute-start(bf16[256,512]{1,0:T(8,128)(2,1)} %get-tuple-element.66), channel_id=1, source_target_pairs={{0,6},{1,7},{2,0},{3,1},{4,2},{5,3},{6,4},{7,5},{8,14},{9,15},{10,... | collective-permute-start | bytes 786440 | tf_op jit(solution)/shard_map/ppermute | solution.py:507
  41.0 18.0 %collective-permute-start.4 = (bf16[256,512]{1,0:T(8,128)(2,1)}, bf16[256,512]{1,0:T(8,128)(2,1)}, u32[]{:S(2)}, u32[]{:S(2)}) collective-permute-start(bf16[256,512]{1,0:T(8,128)(2,1)} %get-tuple-element.67), channel_id=1, source_target_pairs={{0,4},{1,5},{2,6},{3,7},{4,0},{5,1},{6,2},{7,3},{8,12},{9,13},{10,... | collective-permute-start | bytes 786440 | tf_op jit(solution)/shard_map/ppermute | solution.py:507
  44.1 15.0 %collective-permute-start.5 = (bf16[1,512,128]{2,1,0:T(8,128)(2,1)}, bf16[1,512,128]{2,1,0:T(8,128)(2,1)}, u32[]{:S(2)}, u32[]{:S(2)}) collective-permute-start(bf16[1,512,128]{2,1,0:T(8,128)(2,1)} %slice.36), channel_id=1, source_target_pairs={{0,16},{1,48},{2,80},{3,112},{4,144},{5,176},{6,208},{7,240},{8,24... | collective-permute-start | bytes 393224 | tf_op jit(solution)/shard_map/ppermute | solution.py:540
  60.3 13.0 %collective-permute-start.6 = (bf16[256,512]{1,0:T(8,128)(2,1)S(1)}, bf16[256,512]{1,0:T(8,128)(2,1)S(1)}, u32[]{:S(2)}, u32[]{:S(2)}) collective-permute-start(bf16[256,512]{1,0:T(8,128)(2,1)S(1)} %get-tuple-element.81), channel_id=1, source_target_pairs={{0,2},{1,3},{2,4},{3,5},{4,6},{5,7},{6,0},{7,1},{8,10},{9,11},{10,... | collective-permute-start | bytes 786440 | tf_op jit(solution)/shard_map/ppermute | solution.py:516
  62.4 14.2 %collective-permute-start.8 = (bf16[256,512]{1,0:T(8,128)(2,1)S(1)}, bf16[256,512]{1,0:T(8,128)(2,1)S(1)}, u32[]{:S(2)}, u32[]{:S(2)}) collective-permute-start(bf16[256,512]{1,0:T(8,128)(2,1)S(1)} %get-tuple-element.83), channel_id=1, source_target_pairs={{0,4},{1,5},{2,6},{3,7},{4,0},{5,1},{6,2},{7,3},{8,12},{9,13},{10,... | collective-permute-start | bytes 786440 | tf_op jit(solution)/shard_map/ppermute | solution.py:516
  64.1 26.5 %collective-permute-start.9 = (bf16[256,512]{1,0:T(8,128)(2,1)S(1)}, bf16[256,512]{1,0:T(8,128)(2,1)S(1)}, u32[]{:S(2)}, u32[]{:S(2)}) collective-permute-start(bf16[256,512]{1,0:T(8,128)(2,1)S(1)} %add_convert_fusion.3), channel_id=1, source_target_pairs={{0,1},{1,0},{2,3},{3,2},{4,5},{5,4},{6,7},{7,6},{8,9},{9,8},{10,11... | collective-permute-start | bytes 786440 | tf_op jit(solution)/shard_map/ppermute | solution.py:515
  91.9 22.6 %collective-permute-start.10 = (bf16[256,512]{1,0:T(8,128)(2,1)S(1)}, bf16[256,512]{1,0:T(8,128)(2,1)S(1)}, u32[]{:S(2)}, u32[]{:S(2)}) collective-permute-start(bf16[256,512]{1,0:T(8,128)(2,1)S(1)} %add_convert_fusion.2.refs_0_), channel_id=1, source_target_pairs={{0,1},{1,0},{2,3},{3,2},{4,5},{5,4},{6,7},{7,6},{8,9},{9,8},{10,11... | collective-permute-start | bytes 786440 | tf_op jit(solution)/shard_map/ppermute | solution.py:556
  97.6 20.2 %collective-permute-start.14 = (bf16[256,512]{1,0:T(8,128)(2,1)S(1)}, bf16[256,512]{1,0:T(8,128)(2,1)S(1)}, u32[]{:S(2)}, u32[]{:S(2)}) collective-permute-start(bf16[256,512]{1,0:T(8,128)(2,1)S(1)} %add_convert_fusion.2.refs_0_), channel_id=1, source_target_pairs={{0,2},{1,3},{2,4},{3,5},{4,6},{5,7},{6,0},{7,1},{8,10},{9,11},{10,... | collective-permute-start | bytes 786440 | tf_op jit(solution)/shard_map/ppermute | solution.py:557
  100.1 18.2 %collective-permute-start.15 = (bf16[256,512]{1,0:T(8,128)(2,1)S(1)}, bf16[256,512]{1,0:T(8,128)(2,1)S(1)}, u32[]{:S(2)}, u32[]{:S(2)}) collective-permute-start(bf16[256,512]{1,0:T(8,128)(2,1)S(1)} %add_convert_fusion.2.refs_0_), channel_id=1, source_target_pairs={{0,4},{1,5},{2,6},{3,7},{4,0},{5,1},{6,2},{7,3},{8,12},{9,13},{10,... | collective-permute-start | bytes 786440 | tf_op jit(solution)/shard_map/ppermute | solution.py:557
  100.4 17.9 %collective-permute-start.16 = (bf16[256,512]{1,0:T(8,128)(2,1)S(1)}, bf16[256,512]{1,0:T(8,128)(2,1)S(1)}, u32[]{:S(2)}, u32[]{:S(2)}) collective-permute-start(bf16[256,512]{1,0:T(8,128)(2,1)S(1)} %add_convert_fusion.2.refs_0_), channel_id=1, source_target_pairs={{0,6},{1,7},{2,0},{3,1},{4,2},{5,3},{6,4},{7,5},{8,14},{9,15},{10,... | collective-permute-start | bytes 786440 | tf_op jit(solution)/shard_map/ppermute | solution.py:557
  114.4 15.9 %collective-permute-start.11 = (bf16[256,512]{1,0:T(8,128)(2,1)S(1)}, bf16[256,512]{1,0:T(8,128)(2,1)}, u32[]{:S(2)}, u32[]{:S(2)}) collective-permute-start(bf16[256,512]{1,0:T(8,128)(2,1)S(1)} %collective-permute-done.10.refs_0_.refs_4_), channel_id=1, source_target_pairs={{0,2},{1,3},{2,4},{3,5},{4,6},{5,7},{6,0},{7,1},{8,10},{9,11},{10,... | collective-permute-start | bytes 786440 | tf_op jit(solution)/shard_map/ppermute | solution.py:559
  116.3 14.1 %collective-permute-start.12 = (bf16[256,512]{1,0:T(8,128)(2,1)S(1)}, bf16[256,512]{1,0:T(8,128)(2,1)}, u32[]{:S(2)}, u32[]{:S(2)}) collective-permute-start(bf16[256,512]{1,0:T(8,128)(2,1)S(1)} %collective-permute-done.10.refs_0_.refs_4_), channel_id=1, source_target_pairs={{0,4},{1,5},{2,6},{3,7},{4,0},{5,1},{6,2},{7,3},{8,12},{9,13},{10,... | collective-permute-start | bytes 786440 | tf_op jit(solution)/shard_map/ppermute | solution.py:559
  117.8 12.6 %collective-permute-start.13 = (bf16[256,512]{1,0:T(8,128)(2,1)S(1)}, bf16[256,512]{1,0:T(8,128)(2,1)}, u32[]{:S(2)}, u32[]{:S(2)}) collective-permute-start(bf16[256,512]{1,0:T(8,128)(2,1)S(1)} %collective-permute-done.10.refs_0_.refs_4_), channel_id=1, source_target_pairs={{0,6},{1,7},{2,0},{3,1},{4,2},{5,3},{6,4},{7,5},{8,14},{9,15},{10,... | collective-permute-start | bytes 786440 | tf_op jit(solution)/shard_map/ppermute | solution.py:559
  151.3 52.2 %collective-permute-start.23 = (f32[16,512]{1,0:T(8,128)}, f32[16,512]{1,0:T(8,128)}, u32[]{:S(2)}, u32[]{:S(2)}) collective-permute-start(f32[16,512]{1,0:T(8,128)} %get-tuple-element.100), channel_id=1, source_target_pairs={{0,64},{8,72},{16,80},{24,88},{32,96},{40,104},{48,112},{56,120},{... | collective-permute-start | bytes 98312 | tf_op jit(solution)/shard_map/ppermute | solution.py:576
  156.9 46.6 %collective-permute-start.24 = (f32[16,512]{1,0:T(8,128)}, f32[16,512]{1,0:T(8,128)}, u32[]{:S(2)}, u32[]{:S(2)}) collective-permute-start(f32[16,512]{1,0:T(8,128)} %get-tuple-element.100), channel_id=1, source_target_pairs={{0,128},{8,136},{16,144},{24,152},{32,160},{40,168},{48,176},{56,1... | collective-permute-start | bytes 98312 | tf_op jit(solution)/shard_map/ppermute | solution.py:576
  161.3 42.2 %collective-permute-start.25 = (f32[16,512]{1,0:T(8,128)}, f32[16,512]{1,0:T(8,128)}, u32[]{:S(2)}, u32[]{:S(2)}) collective-permute-start(f32[16,512]{1,0:T(8,128)} %get-tuple-element.100), channel_id=1, source_target_pairs={{0,192},{8,200},{16,208},{24,216},{32,224},{40,232},{48,240},{56,2... | collective-permute-start | bytes 98312 | tf_op jit(solution)/shard_map/ppermute | solution.py:576
  210.0 14.6 %collective-permute-start.28 = (bf16[256,512]{1,0:T(8,128)(2,1)S(1)}, bf16[256,512]{1,0:T(8,128)(2,1)S(1)}, u32[]{:S(2)}, u32[]{:S(2)}) collective-permute-start(bf16[256,512]{1,0:T(8,128)(2,1)S(1)} %get-tuple-element.104), channel_id=1, source_target_pairs={{0,4},{1,5},{2,6},{3,7},{4,0},{5,1},{6,2},{7,3},{8,12},{9,13},{10,... | collective-permute-start | bytes 786440 | tf_op jit(solution)/shard_map/ppermute | solution.py:507
  226.8 13.5 %collective-permute-start.31 = (bf16[256,512]{1,0:T(8,128)(2,1)S(1)}, bf16[256,512]{1,0:T(8,128)(2,1)S(1)}, u32[]{:S(2)}, u32[]{:S(2)}) collective-permute-start(bf16[256,512]{1,0:T(8,128)(2,1)S(1)} %get-tuple-element.113), channel_id=1, source_target_pairs={{0,4},{1,5},{2,6},{3,7},{4,0},{5,1},{6,2},{7,3},{8,12},{9,13},{10,... | collective-permute-start | bytes 786440 | tf_op jit(solution)/shard_map/ppermute | solution.py:516
  228.6 17.0 %collective-permute-start.32 = (bf16[256,512]{1,0:T(8,128)(2,1)S(1)}, bf16[256,512]{1,0:T(8,128)(2,1)S(1)}, u32[]{:S(2)}, u32[]{:S(2)}) collective-permute-start(bf16[256,512]{1,0:T(8,128)(2,1)S(1)} %add_convert_fusion.1), channel_id=1, source_target_pairs={{0,1},{1,0},{2,3},{3,2},{4,5},{5,4},{6,7},{7,6},{8,9},{9,8},{10,11... | collective-permute-start | bytes 786440 | tf_op jit(solution)/shard_map/ppermute | solution.py:515
  (30 other events, 281.1 us)
Sparse Core Ops, SparseCore 0:
  29.7 96.9 all-gather.4
  128.6 68.0 all-gather.6
where the time goes:
time: 254 us; the launch traced here: 253 us
  waiting for transfers between devices  111 us (44%)
  starting transfers between devices  76.2 us (30%)
  Pallas kernels  33.6 us (13%)
  local copies, waits for them, and re-layouts  14.1 us (6%)
  between operations  13.8 us (5%)
  other arithmetic  4.26 us (2%)
    all_gather x1, waiting for transfers between devices, body(): weights_q = lax.all_gather(moved_q, 'ctx')  33.5 us
    ppermute x2, waiting for transfers between devices, sum_shares(): crossed = lax.ppermute(total_other, 'mp', H_SWAP)  19.4 us
    ppermute x2, starting transfers between devices, sum_shares(): crossed = lax.ppermute(total_other, 'mp', H_SWAP)  14.2 us
    ppermute x1, waiting for transfers between devices, body(): crossed = lax.ppermute(hidden, 'mp', H_SWAP)  12.2 us
    ppermute x3, starting transfers between devices, body(): above.append(lax.ppermute(line_total, 'ctx', pairs))  11.9 us
    pallas_call x3, Pallas kernels, project(): pl.pallas_call(functools.partial(project_kernel, flips, count, not acc, l...  11.3 us
    ppermute x6, starting transfers between devices, sum_shares(): got = [lax.ppermute(other[d], 'mp', x_shift(d)) for d in (1, 3, 2)]  10.7 us
    ppermute x6, waiting for transfers between devices, sum_shares(): got = [lax.ppermute(other[d], 'mp', x_shift(d)) for d in (1, 3, 2)]  10.5 us
  transfers between devices with their start and end apart: 35, of which 18 were waited for; matrix products, arithmetic and copies ran while one was open for 3% of the time, Pallas kernels for 12%

commit v1 on v0

--- a/solution.py
+++ b/solution.py
@@ -38,6 +38,38 @@
 
 
 NY, NZ, NC, NX, NH = 4, 4, 2, 4, 2
+
+def rim_kernel(q_ref, k_ref, v_ref, out_ref, sems):
+    parts = ((k_ref, HALO, 0), (v_ref, HALO, HALO), (q_ref, 16, 2 * HALO))
+    copies = []
+    for i, (ref, depth, at) in enumerate(parts):
+        copy = pltpu.make_async_copy(
+            ref.at[pl.ds(ROWS - depth, depth)], out_ref.at[pl.ds(at, depth)], sems.at[i]
+        )
+        copy.start()
+        copies.append(copy)
+    for copy in copies:
+        copy.wait()
+
+
+def rim_rows(q, k, v):
+    return pl.pallas_call(
+        rim_kernel,
+        out_shape=jax.ShapeDtypeStruct((2 * HALO + 16, WIDTH), BF16),
+        in_specs=hspecs(3),
+        out_specs=pl.BlockSpec(memory_space=pltpu.VMEM),
+        scratch_shapes=[pltpu.SemaphoreType.DMA((3,))],
+        compiler_params=params(),
+        name="rim_rows",
+    )(q, k, v)
+
+
+OVER_FIRST = (((0,), (0,)), ((), ()))
+
+
+def exact(a, b):
+    return lax.dot_general(a, b, OVER_FIRST, preferred_element_type=F32, precision=lax.Precision.HIGHEST)
+
 
 def toeplitz_rows(near, far):
     row = lax.broadcasted_iota(jnp.int32, (LANES, LANES), 0)
@@ -53,38 +85,48 @@
     return upper, lower
 
 
-def toeplitz_kernel(near_ref, out_ref):
+def toeplitz_kernel(taps_ref, out_ref, near):
+    tap = lax.broadcasted_iota(jnp.int32, (LANES, LANES), 0)
+    at = lax.broadcasted_iota(jnp.int32, (LANES, LANES), 1)
+    near[...] = exact(taps_ref[...], jnp.where(tap == lax.rem(LANES - at, LANES), 1.0, 0.0))
+
     def one(g, carry):
-        upper, lower = toeplitz_rows(near_ref[pl.ds(g, 1), :], None)
+        upper, lower = toeplitz_rows(near[pl.ds(g, 1), :], None)
         start = pl.multiple_of(g * LANES, LANES)
         out_ref[pl.ds(start, LANES), 0:LANES] = upper
         out_ref[pl.ds(start, LANES), LANES:] = lower
         return carry
 
-    lax.fori_loop(0, near_ref.shape[0], one, 0)
-
-
-def toeplitz(near):
-    groups = near.shape[0]
+    lax.fori_loop(0, near.shape[0], one, 0)
+
+
+def toeplitz(taps):
+    groups = taps.shape[1]
     return pl.pallas_call(
         toeplitz_kernel,
         out_shape=jax.ShapeDtypeStruct((groups * LANES, 2 * LANES), BF16),
         in_specs=vspecs(1),
         out_specs=pl.BlockSpec(memory_space=pltpu.VMEM),
+        scratch_shapes=[pltpu.VMEM((groups, LANES), F32)],
         compiler_params=params(),
         name="toeplitz",
-    )(near)
-
-
-def prep_kernel(rates_ref, res_ref, rate_row_ref, res_row_ref, toep_ref, leave_ref, enter_ref, lane_ref, near, far):
-    groups = rates_ref.shape[0]
+    )(taps)
+
+
+def prep_kernel(rates_ref, res_ref, toep_ref, leave_ref, enter_ref, lane_ref, near, far):
+    modes, groups = rates_ref.shape
+    mode_r = lax.broadcasted_iota(jnp.int32, (modes, modes), 0)
+    mode_c = lax.broadcasted_iota(jnp.int32, (modes, modes), 1)
+    same = jnp.where(mode_r == mode_c, 1.0, 0.0)
+    rates = exact(rates_ref[...], same)
+    weights = exact(res_ref[...], same)
     back = lax.broadcasted_iota(jnp.int32, (groups, LANES), 1)
     back = jnp.where(back == 0, 0, LANES - back).astype(F32)
     near_sum = jnp.zeros((groups, LANES), F32)
     far_sum = jnp.zeros((groups, LANES), F32)
     for n in range(GS):
-        rate = rates_ref[:, n : n + 1]
-        weight = res_ref[:, n : n + 1]
+        rate = rates[:, n : n + 1]
+        weight = weights[:, n : n + 1]
         near_sum = near_sum + weight * jnp.exp(-rate * back)
         far_sum = far_sum + weight * jnp.exp(-rate * (back + LANES))
     near[...] = near_sum
@@ -98,23 +140,26 @@
         return carry
 
     lax.fori_loop(0, groups, one, 0)
+    lane = lax.broadcasted_iota(jnp.int32, (groups, WIDTH), 1)
+    member = lax.broadcasted_iota(jnp.int32, (groups, WIDTH), 0)
+    pick = jnp.where(lane // GS == member, 1.0, 0.0)
+    lane_rates = exact(rates, pick)
+    lane_ref[...] = lane_rates
+    lane = lax.broadcasted_iota(jnp.int32, (modes, WIDTH), 1)
+    member = lax.broadcasted_iota(jnp.int32, (modes, WIDTH), 0)
+    ours = lax.rem(lane, GS) == member
+    rate_row = jnp.sum(jnp.where(ours, lane_rates, 0.0), axis=0, keepdims=True)
+    weight_row = jnp.sum(jnp.where(ours, exact(weights, pick), 0.0), axis=0, keepdims=True)
     step = lax.broadcasted_iota(jnp.int32, (ROWS, LANES), 0).astype(F32)
     for block in range(WIDTH // LANES):
         cols = slice(block * LANES, (block + 1) * LANES)
-        rate = rate_row_ref[:, cols]
-        leave_ref[:, cols] = res_row_ref[:, cols] * jnp.exp(-rate * step)
+        rate = rate_row[:, cols]
+        leave_ref[:, cols] = weight_row[:, cols] * jnp.exp(-rate * step)
         enter_ref[:, cols] = jnp.exp(-rate * (ROWS - step))
-    lane = lax.broadcasted_iota(jnp.int32, (groups, WIDTH), 1)
-    member = lax.broadcasted_iota(jnp.int32, (groups, WIDTH), 0)
-    pick = jnp.where(lane // GS == member, 1.0, 0.0)
-    lane_ref[...] = lax.dot_general(
-        rates_ref[...], pick, (((0,), (0,)), ((), ())),
-        preferred_element_type=F32, precision=lax.Precision.HIGHEST,
-    )
 
 
 def prep(rates, residues):
-    groups = rates.shape[0]
+    groups = rates.shape[1]
     return pl.pallas_call(
         prep_kernel,
         out_shape=[
@@ -123,12 +168,12 @@
             jax.ShapeDtypeStruct((ROWS, WIDTH), F32),
             jax.ShapeDtypeStruct((GS, WIDTH), F32),
         ],
-        in_specs=vspecs(4),
+        in_specs=vspecs(2),
         out_specs=vspecs(4),
         scratch_shapes=[pltpu.VMEM((groups, LANES), F32)] * 2,
         compiler_params=params(),
         name="prep",
-    )(rates, residues, rates.reshape(1, WIDTH), residues.reshape(1, WIDTH))
+    )(rates, residues)
 
 
 def feature(ext_ref, base, rows, taps):
@@ -241,8 +286,9 @@
     )(where, q, k, v, halo, feat, toep, weight)
 
 
-def project_kernel(flips, count, first, last, where_ref, *refs):
+def project_kernel(flips, slots, first, last, where_ref, *refs):
     n = len(flips) * 4
+    count = len(slots)
     hidden_refs = refs[:n]
     w_ref = refs[n]
     pos = n + 1
@@ -255,7 +301,7 @@
     x = where_ref[0]
     hcopies, wcopies = [], []
     for i in range(n):
-        e, d = flips[i // 4], i % 4
+        e, d = flips[i // 4], (0, 1, 3, 2)[i % 4]
         copy = pltpu.make_async_copy(hidden_refs[i], hbuf.at[i], hsem.at[i])
         copy.start()
         hcopies.append(copy)
@@ -265,7 +311,7 @@
             high = odd if e == 1 else 1 - odd
             member = (src_y * 4 + high * 2 + odd) * 2 + b % 2
             copy = pltpu.make_async_copy(
-                w_ref.at[member],
+                w_ref.at[member, pl.ds(slots[0], count)],
                 wbuf.at[i, :, :, pl.ds(b * LANES, LANES)],
                 wsem.at[i, b],
             )
@@ -286,10 +332,10 @@
         out_refs[j][...] = sums[j].astype(BF16) if last else sums[j]
 
 
-def project(where, pieces, weights, flips, count, acc=(), last=True):
-    n = len(pieces)
-    return pl.pallas_call(
-        functools.partial(project_kernel, flips, count, not acc, last),
+def project(where, pieces, weights, flips, slots, acc=(), last=True):
+    n, count = len(pieces), len(slots)
+    return pl.pallas_call(
+        functools.partial(project_kernel, flips, slots, not acc, last),
         out_shape=[jax.ShapeDtypeStruct((ROWS, WIDTH), BF16 if last else F32)] * count,
         in_specs=[SMEM_SPEC] + hspecs(n + 1) + vspecs(len(acc)),
         out_specs=vspecs(count),
@@ -305,7 +351,6 @@
 
 
 def li_gate_kernel(k_ref, v_ref, halo_ref, feat_ref, enter_ref, z_ref, load_ref, kx, vx):
-    over_rows = (((0,), (0,)), ((), ()))
     for block in range(WIDTH // LANES):
         cols = slice(block * LANES, (block + 1) * LANES)
         kx[0:16, :] = halo_ref[0:16, cols].astype(F32)
@@ -319,8 +364,8 @@
         enter = enter_ref[:, cols]
         high = enter.astype(BF16)
         rest = (enter - high.astype(F32)).astype(BF16)
-        prod = lax.dot_general(high, z, over_rows, preferred_element_type=F32)
-        prod = prod + lax.dot_general(rest, z, over_rows, preferred_element_type=F32)
+        prod = lax.dot_general(high, z, OVER_FIRST, preferred_element_type=F32)
+        prod = prod + lax.dot_general(rest, z, OVER_FIRST, preferred_element_type=F32)
         load = jnp.zeros((GS, LANES), F32)
         for g in range(NG):
             load = jnp.where(own_lanes(g), prod[g * GS : (g + 1) * GS, :], load)
@@ -531,34 +576,24 @@
     where = jnp.stack([x, zh, y, zl, k]).astype(jnp.int32)
 
     forward = [(i, i + 1) for i in range(NY * NZ * NC - 1)]
-    rim = jnp.concatenate(
-        [key_mr[ROWS - HALO :], value_mr[ROWS - HALO :], query_mr[ROWS - 16 :]], axis=0
-    )
-    rim, in_weight = tied(rim, in_weight)
-    halo = lax.ppermute(rim, "ctx", forward)
-    moved_kv = lax.ppermute(in_weight[1:3], ("ctx", "mp"), weight_moves())
-    moved_q = lax.ppermute(in_weight[0:1], ("ctx", "mp"), weight_moves())
-
-    toep_mr = toeplitz(jnp.concatenate([mr_taps[:1], mr_taps[1:][::-1]], axis=0).T)
-
-    halo, moved_kv, toep_mr = tied(halo, moved_kv, toep_mr)
+    moved = lax.ppermute(in_weight, ("ctx", "mp"), weight_moves())
+    halo = lax.ppermute(rim_rows(query_mr, key_mr, value_mr), "ctx", forward)
+    toep_mr = toeplitz(mr_taps)
     gated_one, *other_one = mr_op(
         where, query_mr, key_mr, value_mr, halo, featurizer_mr, toep_mr, out_mr
     )
-    weights_kv = lax.all_gather(moved_kv, "ctx")
-    filters = prep(li_rates, li_residues)
-    hidden, filters = sum_shares(
-        where, gated_one, other_one, out_mr, residual, tuple(filters) + (moved_q,)
-    )
-    toep_li, leave, enter, lane_rates, moved_q = filters
-
-    hidden, moved_q = tied(hidden, moved_q)
+    *other_one, moved = tied(*other_one, moved)
+    weights = lax.all_gather(moved, "ctx")
+    hidden, _ = sum_shares(where, gated_one, other_one, out_mr, residual, ())
+    filters = prep(li_rates.T, li_residues.T)
+
     crossed = lax.ppermute(hidden, "mp", H_SWAP)
-    own_pieces = [hidden] + [lax.ppermute(hidden, "mp", x_shift(d)) for d in (1, 2, 3)]
-    weights_q = lax.all_gather(moved_q, "ctx")
-    far_pieces = [crossed] + [lax.ppermute(crossed, "mp", x_shift(d)) for d in (1, 2, 3)]
-    partial = project(where, own_pieces, weights_kv, (0,), 2, last=False)
-    fresh_k, fresh_v = project(where, far_pieces, weights_kv, (1,), 2, acc=tuple(partial))
+    own_pieces = [hidden] + [lax.ppermute(hidden, "mp", x_shift(d)) for d in (1, 3, 2)]
+    crossed, *filters = tied(crossed, *filters)
+    toep_li, leave, enter, lane_rates = filters
+    far_pieces = [crossed] + [lax.ppermute(crossed, "mp", x_shift(d)) for d in (1, 3, 2)]
+    pieces = own_pieces + far_pieces
+    fresh_k, fresh_v = project(where, pieces, weights, (0, 1), (1, 2))
     halo_kv = lax.ppermute(
         jnp.concatenate([fresh_k[ROWS - 16 :], fresh_v[ROWS - 16 :]], axis=0), "ctx", forward
     )
@@ -575,7 +610,7 @@
         ]
         above.append(lax.ppermute(line_total, "ctx", pairs))
 
-    (fresh_q,) = project(where, own_pieces + far_pieces, weights_q, (0, 1), 1)
+    (fresh_q,) = project(where, pieces, weights, (0, 1), (0,))
     halo_q = lax.ppermute(fresh_q[ROWS - 16 :], "ctx", forward)
     conv = li_inner(product, toep_li)
 

time: 254 us -> 233 us (0.917)
  starting transfers between devices: 76.2 us -> 62.2 us
  waiting for transfers between devices: 111 us -> 107 us
  local copies, waits for them, and re-layouts: 14.1 us -> 17.5 us
  Pallas kernels: 33.6 us -> 30.4 us
  other arithmetic: 4.26 us -> 1.39 us
    all_gather x2 -> x1, waiting for transfers between devices: 41.9 us -> 28.6 us  [body(): weights = lax.all_gather(moved, 'ctx')]
    ppermute x3 -> x2, waiting for transfers between devices: 12.7 us -> 2.1 us  [the longest x1 2.1 us: body(): moved = lax.ppermute(in_weight, ('ctx', 'mp'), weight_moves())]
    unnamed x40 -> x53, local copies, waits for them, and re-layouts: 7.11 us -> 17.4 us
    ppermute x6, waiting for transfers between devices: 10.5 us -> 19.7 us  [sum_shares(): got = [lax.ppermute(other[d], 'mp', x_shift(d)) for d in (1, 3, 2)]]
    ppermute x3, waiting for transfers between devices: 0.01 us -> 8.08 us  [body(): lax.ppermute(crossed, 'mp', x_shift(d))]
    slice x6 -> x0, local copies, waits for them, and re-layouts: 6.66 us -> none  [the longest x1 1.67 us: body(): moved_kv = lax.ppermute(in_weight[1:3], ('ctx', 'mp'), weight_moves())]
    ppermute x2, starting transfers between devices: 14.2 us -> 7.85 us  [sum_shares(): crossed = lax.ppermute(total_other, 'mp', H_SWAP)]
    ppermute x6, waiting for transfers between devices: 9.92 us -> 15.4 us  [sum_shares(): got_mine = [lax.ppermute(mine[d], 'mp', x_shift(d)) for d in (1, 3, 2)]]
  transfers between devices with their start and end apart: 35 -> 33, of which waited for: 18 -> 22; matrix products, arithmetic and copies ran while one was open for 3% -> 1% of each run, Pallas kernels for 12% -> 9%
where the time goes in v1:
time: 233 us
  waiting for transfers between devices  107 us (46%)
  starting transfers between devices  62.2 us (27%)
  Pallas kernels  30.4 us (13%)
  local copies, waits for them, and re-layouts  17.5 us (8%)
  between operations  13.8 us (6%)
    all_gather x1, waiting for transfers between devices, body(): weights = lax.all_gather(moved, 'ctx')  28.6 us
    ppermute x6, waiting for transfers between devices, sum_shares(): got = [lax.ppermute(other[d], 'mp', x_shift(d)) for d in (1, 3, 2)]  19.7 us
    unnamed x53, local copies, waits for them, and re-layouts  17.4 us
    ppermute x2, waiting for transfers between devices, sum_shares(): crossed = lax.ppermute(total_other, 'mp', H_SWAP)  15.8 us
    ppermute x6, waiting for transfers between devices, sum_shares(): got_mine = [lax.ppermute(mine[d], 'mp', x_shift(d)) for d in (1, 3, 2)]  15.4 us
    ppermute x6, starting transfers between devices, sum_shares(): got = [lax.ppermute(other[d], 'mp', x_shift(d)) for d in (1, 3, 2)]  14.5 us
    ppermute x1, waiting for transfers between devices, body(): crossed = lax.ppermute(hidden, 'mp', H_SWAP)  10.9 us
    pallas_call x2, Pallas kernels, project(): pl.pallas_call(functools.partial(project_kernel, flips, slots, not acc, l...  8.91 us
  transfers between devices with their start and end apart: 33, of which 22 were waited for; matrix products, arithmetic and copies ran while one was open for 1% of the time, Pallas kernels for 9%

profile of v1, /device:TPU:2, one launch (start us, length us, event | category | flops | bytes accessed | tf_op | source)
XLA Modules:
  0.0 232.7 jit_solution(1936670953719464913)
XLA Ops:
  6.5 2.9 %collective-permute-start.1 = (bf16[3,512,128]{2,1,0:T(8,128)(2,1)}, bf16[3,512,128]{2,1,0:T(8,128)(2,1)}, u32[]{:S(2)}, u32[]{:S(2)}) collective-permute-start(bf16[3,512,128]{2,1,0:T(8,128)(2,1)} %param.19), channel_id=1, source_target_pairs={{0,16},{1,48},{2,80},{3,112},{4,144},{5,176},{6,208},{7,240},{8,24... | collective-permute-start | bytes 1179656 | tf_op jit(solution)/shard_map/ppermute | solution.py:579
  15.1 3.1 %toeplitz.1.toep_ref = bf16[4096,256]{1,0:T(8,128)(2,1)S(1)} custom-call(f32[128,32]{1,0:T(8,128)S(1)} %copy.14.taps_ref), custom_call_target="tpu_custom_call" | custom-call | tf_op jit(solution)/shard_map/toeplitz/pallas_call | solution.py:105
  21.8 4.0 %mr_op.1 = (bf16[256,512]{1,0:T(8,128)(2,1)S(1)}, bf16[256,512]{1,0:T(8,128)(2,1)S(1)}, bf16[256,512]{1,0:T(8,128)(2,1)S(1)}, bf16[256,512]{1,0:T(8,128)(2,1)S(1)}, bf16[256,512]{1,0:T(8,128)(2,1)S(1)}) custom-call(s32[5]{0:T(128)S(1)} %stack.23.where_ref, bf16[256,512]{1,0:T(8,128)(2,1)S(1)} %copy-done.10, bf16[256,512]{1,0:T(8,128)(2,1)S(1)} %copy-done.12, ...), custom_call_target="tpu_custom_call" | custom-call | tf_op jit(solution)/shard_map/mr_op/pallas_call | solution.py:274
  29.4 9.7 %collective-permute-start.2 = (bf16[256,512]{1,0:T(8,128)(2,1)}, bf16[256,512]{1,0:T(8,128)(2,1)S(1)}, u32[]{:S(2)}, u32[]{:S(2)}) collective-permute-start(bf16[256,512]{1,0:T(8,128)(2,1)} %copy-done.24), channel_id=1, source_target_pairs={{0,2},{1,3},{2,4},{3,5},{4,6},{5,7},{6,0},{7,1},{8,10},{9,11},{10,... | collective-permute-start | bytes 786440 | tf_op jit(solution)/shard_map/ppermute | solution.py:552
  44.9 4.8 %collective-permute-done.2 = bf16[256,512]{1,0:T(8,128)(2,1)S(1)} collective-permute-done((bf16[256,512]{1,0:T(8,128)(2,1)}, bf16[256,512]{1,0:T(8,128)(2,1)S(1)}, u32[]{:S(2)}, u32[]{:S(2)}) %collective-permute-start.2) | collective-permute-done | bytes 262176 | tf_op jit(solution)/shard_map/ppermute | solution.py:552
  49.7 4.2 %collective-permute-done.3 = bf16[256,512]{1,0:T(8,128)(2,1)S(1)} collective-permute-done((bf16[256,512]{1,0:T(8,128)(2,1)}, bf16[256,512]{1,0:T(8,128)(2,1)S(1)}, u32[]{:S(2)}, u32[]{:S(2)}) %collective-permute-start.3) | collective-permute-done | bytes 262176 | tf_op jit(solution)/shard_map/ppermute | solution.py:552
  56.1 3.8 %collective-permute-start.8 = (bf16[256,512]{1,0:T(8,128)(2,1)S(1)}, bf16[256,512]{1,0:T(8,128)(2,1)S(1)}, u32[]{:S(2)}, u32[]{:S(2)}) collective-permute-start(bf16[256,512]{1,0:T(8,128)(2,1)S(1)} %add_convert_fusion.3), channel_id=1, source_target_pairs={{0,1},{1,0},{2,3},{3,2},{4,5},{5,4},{6,7},{7,6},{8,9},{9,8},{10,11... | collective-permute-start | bytes 786440 | tf_op jit(solution)/shard_map/ppermute | solution.py:560
  59.9 3.4 %collective-permute-done.5 = bf16[256,512]{1,0:T(8,128)(2,1)S(1)} collective-permute-done((bf16[256,512]{1,0:T(8,128)(2,1)S(1)}, bf16[256,512]{1,0:T(8,128)(2,1)S(1)}, u32[]{:S(2)}, u32[]{:S(2)}) %collective-permute-start.5) | collective-permute-done | bytes 262176 | tf_op jit(solution)/shard_map/ppermute | solution.py:561
  63.3 4.7 %collective-permute-done.7 = bf16[256,512]{1,0:T(8,128)(2,1)S(1)} collective-permute-done((bf16[256,512]{1,0:T(8,128)(2,1)S(1)}, bf16[256,512]{1,0:T(8,128)(2,1)S(1)}, u32[]{:S(2)}, u32[]{:S(2)}) %collective-permute-start.7) | collective-permute-done | bytes 262176 | tf_op jit(solution)/shard_map/ppermute | solution.py:561
  68.1 10.4 %collective-permute-done.8 = bf16[256,512]{1,0:T(8,128)(2,1)S(1)} collective-permute-done((bf16[256,512]{1,0:T(8,128)(2,1)S(1)}, bf16[256,512]{1,0:T(8,128)(2,1)S(1)}, u32[]{:S(2)}, u32[]{:S(2)}) %collective-permute-start.8) | collective-permute-done | bytes 262176 | tf_op jit(solution)/shard_map/ppermute | solution.py:560
  82.1 3.8 %prep.1 = (bf16[4096,256]{1,0:T(8,128)(2,1)S(1)}, f32[256,512]{1,0:T(8,128)S(1)}, f32[256,512]{1,0:T(8,128)S(1)}, f32[16,512]{1,0:T(8,128)S(1)}) custom-call(f32[16,32]{1,0:T(8,128)S(1)} %bitcast.8, f32[16,32]{1,0:T(8,128)S(1)} %bitcast.9), custom_call_target="tpu_custom_call" | custom-call | tf_op jit(solution)/shard_map/prep/pallas_call | solution.py:163
  89.5 10.9 %collective-permute-done.12.refs_4_ = bf16[256,512]{1,0:T(8,128)(2,1)S(1)} collective-permute-done((bf16[256,512]{1,0:T(8,128)(2,1)S(1)}, bf16[256,512]{1,0:T(8,128)(2,1)S(1)}, u32[]{:S(2)}, u32[]{:S(2)}) %collective-permute-start.12) | collective-permute-done | bytes 262176 | tf_op jit(solution)/shard_map/ppermute | solution.py:590
  100.5 3.0 %collective-permute-start.15 = (bf16[256,512]{1,0:T(8,128)(2,1)S(1)}, bf16[256,512]{1,0:T(8,128)(2,1)S(1)}, u32[]{:S(2)}, u32[]{:S(2)}) collective-permute-start(bf16[256,512]{1,0:T(8,128)(2,1)S(1)} %collective-permute-done.12.refs_4_), channel_id=1, source_target_pairs={{0,4},{1,5},{2,6},{3,7},{4,0},{5,1},{6,2},{7,3},{8,12},{9,13},{10,... | collective-permute-start | bytes 786440 | tf_op jit(solution)/shard_map/ppermute | solution.py:594
  105.5 5.5 %collective-permute-done.15.refs_7_ = bf16[256,512]{1,0:T(8,128)(2,1)S(1)} collective-permute-done((bf16[256,512]{1,0:T(8,128)(2,1)S(1)}, bf16[256,512]{1,0:T(8,128)(2,1)S(1)}, u32[]{:S(2)}, u32[]{:S(2)}) %collective-permute-start.15) | collective-permute-done | bytes 262176 | tf_op jit(solution)/shard_map/ppermute | solution.py:594
  115.7 28.6 %all-gather.3.cloned.1.call-done = bf16[96,512,128]{2,1,0:T(8,128)(2,1)} async-done(((bf16[3,512,128]{2,1,0:T(8,128)(2,1)}), bf16[96,512,128]{2,1,0:T(8,128)(2,1)}) %all-gather.3.cloned.1.call-update) | async-done | bytes 12582928 | tf_op jit(solution)/shard_map/all_gather | solution.py:586
  147.1 5.1 %project.2 = (bf16[256,512]{1,0:T(8,128)(2,1)S(1)}, bf16[256,512]{1,0:T(8,128)(2,1)S(1)}) custom-call(s32[5]{0:T(128)S(1)} %stack.23.where_ref, bf16[256,512]{1,0:T(8,128)(2,1)S(1)} %add_convert_fusion.2.refs_0_, bf16[256,512]{1,0:T(8,128)(2,1)S(1)} %collective-permute-done.9.refs_1_, bf16[256,512]{1,0:T(8,128)(2,1)S(1)} %collective-permute-done.10.refs_2_, ...), custom_call_target="tpu_custom_call" | custom-call | tf_op jit(solution)/shard_map/project/pallas_call | solution.py:337
  169.5 4.0 %collective-permute-start.24 = (f32[16,512]{1,0:T(8,128)S(1)}, f32[16,512]{1,0:T(8,128)S(1)}, u32[]{:S(2)}, u32[]{:S(2)}) collective-permute-start(f32[16,512]{1,0:T(8,128)S(1)} %get-tuple-element.86), channel_id=1, source_target_pairs={{0,192},{8,200},{16,208},{24,216},{32,224},{40,232},{48,240},{56,2... | collective-permute-start | bytes 98312 | tf_op jit(solution)/shard_map/ppermute | solution.py:611
  177.6 3.8 %project.3.q_ref = bf16[256,512]{1,0:T(8,128)(2,1)S(1)} custom-call(s32[5]{0:T(128)S(1)} %stack.23.where_ref, bf16[256,512]{1,0:T(8,128)(2,1)S(1)} %add_convert_fusion.2.refs_0_, bf16[256,512]{1,0:T(8,128)(2,1)S(1)} %collective-permute-done.9.refs_1_, bf16[256,512]{1,0:T(8,128)(2,1)S(1)} %collective-permute-done.10.refs_2_, ...), custom_call_target="tpu_custom_call" | custom-call | tf_op jit(solution)/shard_map/project/pallas_call | solution.py:337
  183.6 3.5 %li_outer.1 = (bf16[256,512]{1,0:T(8,128)(2,1)S(1)}, bf16[256,512]{1,0:T(8,128)(2,1)S(1)}, bf16[256,512]{1,0:T(8,128)(2,1)S(1)}, bf16[256,512]{1,0:T(8,128)(2,1)S(1)}, bf16[256,512]{1,0:T(8,128)(2,1)S(1)}) custom-call(s32[5]{0:T(128)S(1)} %stack.23.where_ref, f32[256,512]{1,0:T(8,128)S(1)} %li_inner.1.conv_ref, bf16[256,512]{1,0:T(8,128)(2,1)S(1)} %project.3.q_ref, ...), custom_call_target="tpu_custom_call" | custom-call | tf_op jit(solution)/shard_map/li_outer/pallas_call | solution.py:487
  192.4 4.0 %collective-permute-done.25 = bf16[256,512]{1,0:T(8,128)(2,1)S(1)} collective-permute-done((bf16[256,512]{1,0:T(8,128)(2,1)S(1)}, bf16[256,512]{1,0:T(8,128)(2,1)S(1)}, u32[]{:S(2)}, u32[]{:S(2)}) %collective-permute-start.25) | collective-permute-done | bytes 262176 | tf_op jit(solution)/shard_map/ppermute | solution.py:552
  196.4 6.8 %collective-permute-done.26 = bf16[256,512]{1,0:T(8,128)(2,1)S(1)} collective-permute-done((bf16[256,512]{1,0:T(8,128)(2,1)S(1)}, bf16[256,512]{1,0:T(8,128)(2,1)S(1)}, u32[]{:S(2)}, u32[]{:S(2)}) %collective-permute-start.26) | collective-permute-done | bytes 262176 | tf_op jit(solution)/shard_map/ppermute | solution.py:552
  208.1 4.1 %collective-permute-start.31 = (bf16[256,512]{1,0:T(8,128)(2,1)S(1)}, bf16[256,512]{1,0:T(8,128)(2,1)S(1)}, u32[]{:S(2)}, u32[]{:S(2)}) collective-permute-start(bf16[256,512]{1,0:T(8,128)(2,1)S(1)} %add_convert_fusion.1), channel_id=1, source_target_pairs={{0,1},{1,0},{2,3},{3,2},{4,5},{5,4},{6,7},{7,6},{8,9},{9,8},{10,11... | collective-permute-start | bytes 786440 | tf_op jit(solution)/shard_map/ppermute | solution.py:560
  213.0 6.5 %collective-permute-done.30 = bf16[256,512]{1,0:T(8,128)(2,1)S(1)} collective-permute-done((bf16[256,512]{1,0:T(8,128)(2,1)S(1)}, bf16[256,512]{1,0:T(8,128)(2,1)S(1)}, u32[]{:S(2)}, u32[]{:S(2)}) %collective-permute-start.30) | collective-permute-done | bytes 262176 | tf_op jit(solution)/shard_map/ppermute | solution.py:561
  219.5 5.4 %collective-permute-done.31 = bf16[256,512]{1,0:T(8,128)(2,1)S(1)} collective-permute-done((bf16[256,512]{1,0:T(8,128)(2,1)S(1)}, bf16[256,512]{1,0:T(8,128)(2,1)S(1)}, u32[]{:S(2)}, u32[]{:S(2)}) %collective-permute-start.31) | collective-permute-done | bytes 262176 | tf_op jit(solution)/shard_map/ppermute | solution.py:560
  (118 shorter events, 72.9 us)
Async XLA Ops:
  6.5 137.7 %all-gather.3.cloned.1.call-start = ((), (), s32[]{:S(2)}) async-start(), calls=%async_computation | async-start | bytes 12976128 | tf_op jit(solution)/shard_map/all_gather | solution.py:586
  6.5 22.8 %collective-permute-start.1 = (bf16[3,512,128]{2,1,0:T(8,128)(2,1)}, bf16[3,512,128]{2,1,0:T(8,128)(2,1)}, u32[]{:S(2)}, u32[]{:S(2)}) collective-permute-start(bf16[3,512,128]{2,1,0:T(8,128)(2,1)} %param.19), channel_id=1, source_target_pairs={{0,16},{1,48},{2,80},{3,112},{4,144},{5,176},{6,208},{7,240},{8,24... | collective-permute-start | bytes 1179656 | tf_op jit(solution)/shard_map/ppermute | solution.py:579
  29.4 20.3 %collective-permute-start.2 = (bf16[256,512]{1,0:T(8,128)(2,1)}, bf16[256,512]{1,0:T(8,128)(2,1)S(1)}, u32[]{:S(2)}, u32[]{:S(2)}) collective-permute-start(bf16[256,512]{1,0:T(8,128)(2,1)} %copy-done.24), channel_id=1, source_target_pairs={{0,2},{1,3},{2,4},{3,5},{4,6},{5,7},{6,0},{7,1},{8,10},{9,11},{10,... | collective-permute-start | bytes 786440 | tf_op jit(solution)/shard_map/ppermute | solution.py:552
  39.1 14.8 %collective-permute-start.3 = (bf16[256,512]{1,0:T(8,128)(2,1)}, bf16[256,512]{1,0:T(8,128)(2,1)S(1)}, u32[]{:S(2)}, u32[]{:S(2)}) collective-permute-start(bf16[256,512]{1,0:T(8,128)(2,1)} %copy-done.23), channel_id=1, source_target_pairs={{0,6},{1,7},{2,0},{3,1},{4,2},{5,3},{6,4},{7,5},{8,14},{9,15},{10,... | collective-permute-start | bytes 786440 | tf_op jit(solution)/shard_map/ppermute | solution.py:552
  39.1 14.8 %collective-permute-start.4 = (bf16[256,512]{1,0:T(8,128)(2,1)S(1)}, bf16[256,512]{1,0:T(8,128)(2,1)S(1)}, u32[]{:S(2)}, u32[]{:S(2)}) collective-permute-start(bf16[256,512]{1,0:T(8,128)(2,1)S(1)} %get-tuple-element.60), channel_id=1, source_target_pairs={{0,4},{1,5},{2,6},{3,7},{4,0},{5,1},{6,2},{7,3},{8,12},{9,13},{10,... | collective-permute-start | bytes 786440 | tf_op jit(solution)/shard_map/ppermute | solution.py:552
  54.0 9.3 %collective-permute-start.5 = (bf16[256,512]{1,0:T(8,128)(2,1)S(1)}, bf16[256,512]{1,0:T(8,128)(2,1)S(1)}, u32[]{:S(2)}, u32[]{:S(2)}) collective-permute-start(bf16[256,512]{1,0:T(8,128)(2,1)S(1)} %get-tuple-element.67), channel_id=1, source_target_pairs={{0,2},{1,3},{2,4},{3,5},{4,6},{5,7},{6,0},{7,1},{8,10},{9,11},{10,... | collective-permute-start | bytes 786440 | tf_op jit(solution)/shard_map/ppermute | solution.py:561
  56.1 11.9 %collective-permute-start.7 = (bf16[256,512]{1,0:T(8,128)(2,1)S(1)}, bf16[256,512]{1,0:T(8,128)(2,1)S(1)}, u32[]{:S(2)}, u32[]{:S(2)}) collective-permute-start(bf16[256,512]{1,0:T(8,128)(2,1)S(1)} %get-tuple-element.69), channel_id=1, source_target_pairs={{0,4},{1,5},{2,6},{3,7},{4,0},{5,1},{6,2},{7,3},{8,12},{9,13},{10,... | collective-permute-start | bytes 786440 | tf_op jit(solution)/shard_map/ppermute | solution.py:561
  56.1 22.3 %collective-permute-start.8 = (bf16[256,512]{1,0:T(8,128)(2,1)S(1)}, bf16[256,512]{1,0:T(8,128)(2,1)S(1)}, u32[]{:S(2)}, u32[]{:S(2)}) collective-permute-start(bf16[256,512]{1,0:T(8,128)(2,1)S(1)} %add_convert_fusion.3), channel_id=1, source_target_pairs={{0,1},{1,0},{2,3},{3,2},{4,5},{5,4},{6,7},{7,6},{8,9},{9,8},{10,11... | collective-permute-start | bytes 786440 | tf_op jit(solution)/shard_map/ppermute | solution.py:560
  78.7 21.8 %collective-permute-start.12 = (bf16[256,512]{1,0:T(8,128)(2,1)S(1)}, bf16[256,512]{1,0:T(8,128)(2,1)S(1)}, u32[]{:S(2)}, u32[]{:S(2)}) collective-permute-start(bf16[256,512]{1,0:T(8,128)(2,1)S(1)} %add_convert_fusion.2.refs_0_), channel_id=1, source_target_pairs={{0,1},{1,0},{2,3},{3,2},{4,5},{5,4},{6,7},{7,6},{8,9},{9,8},{10,11... | collective-permute-start | bytes 786440 | tf_op jit(solution)/shard_map/ppermute | solution.py:590
  79.6 24.7 %collective-permute-start.11 = (bf16[256,512]{1,0:T(8,128)(2,1)S(1)}, bf16[256,512]{1,0:T(8,128)(2,1)S(1)}, u32[]{:S(2)}, u32[]{:S(2)}) collective-permute-start(bf16[256,512]{1,0:T(8,128)(2,1)S(1)} %add_convert_fusion.2.refs_0_), channel_id=1, source_target_pairs={{0,4},{1,5},{2,6},{3,7},{4,0},{5,1},{6,2},{7,3},{8,12},{9,13},{10,... | collective-permute-start | bytes 786440 | tf_op jit(solution)/shard_map/ppermute | solution.py:591
  87.5 18.0 %collective-permute-start.10 = (bf16[256,512]{1,0:T(8,128)(2,1)S(1)}, bf16[256,512]{1,0:T(8,128)(2,1)S(1)}, u32[]{:S(2)}, u32[]{:S(2)}) collective-permute-start(bf16[256,512]{1,0:T(8,128)(2,1)S(1)} %add_convert_fusion.2.refs_0_), channel_id=1, source_target_pairs={{0,6},{1,7},{2,0},{3,1},{4,2},{5,3},{6,4},{7,5},{8,14},{9,15},{10,... | collective-permute-start | bytes 786440 | tf_op jit(solution)/shard_map/ppermute | solution.py:591
  88.4 17.1 %collective-permute-start.9 = (bf16[256,512]{1,0:T(8,128)(2,1)S(1)}, bf16[256,512]{1,0:T(8,128)(2,1)S(1)}, u32[]{:S(2)}, u32[]{:S(2)}) collective-permute-start(bf16[256,512]{1,0:T(8,128)(2,1)S(1)} %add_convert_fusion.2.refs_0_), channel_id=1, source_target_pairs={{0,2},{1,3},{2,4},{3,5},{4,6},{5,7},{6,0},{7,1},{8,10},{9,11},{10,... | collective-permute-start | bytes 786440 | tf_op jit(solution)/shard_map/ppermute | solution.py:591
  100.5 10.5 %collective-permute-start.15 = (bf16[256,512]{1,0:T(8,128)(2,1)S(1)}, bf16[256,512]{1,0:T(8,128)(2,1)S(1)}, u32[]{:S(2)}, u32[]{:S(2)}) collective-permute-start(bf16[256,512]{1,0:T(8,128)(2,1)S(1)} %collective-permute-done.12.refs_4_), channel_id=1, source_target_pairs={{0,4},{1,5},{2,6},{3,7},{4,0},{5,1},{6,2},{7,3},{8,12},{9,13},{10,... | collective-permute-start | bytes 786440 | tf_op jit(solution)/shard_map/ppermute | solution.py:594
  103.4 10.3 %collective-permute-start.14 = (bf16[256,512]{1,0:T(8,128)(2,1)S(1)}, bf16[256,512]{1,0:T(8,128)(2,1)S(1)}, u32[]{:S(2)}, u32[]{:S(2)}) collective-permute-start(bf16[256,512]{1,0:T(8,128)(2,1)S(1)} %collective-permute-done.12.refs_4_), channel_id=1, source_target_pairs={{0,6},{1,7},{2,0},{3,1},{4,2},{5,3},{6,4},{7,5},{8,14},{9,15},{10,... | collective-permute-start | bytes 786440 | tf_op jit(solution)/shard_map/ppermute | solution.py:594
  104.3 10.7 %collective-permute-start.13 = (bf16[256,512]{1,0:T(8,128)(2,1)S(1)}, bf16[256,512]{1,0:T(8,128)(2,1)S(1)}, u32[]{:S(2)}, u32[]{:S(2)}) collective-permute-start(bf16[256,512]{1,0:T(8,128)(2,1)S(1)} %collective-permute-done.12.refs_4_), channel_id=1, source_target_pairs={{0,2},{1,3},{2,4},{3,5},{4,6},{5,7},{6,0},{7,1},{8,10},{9,11},{10,... | collective-permute-start | bytes 786440 | tf_op jit(solution)/shard_map/ppermute | solution.py:594
  169.5 14.1 %collective-permute-start.24 = (f32[16,512]{1,0:T(8,128)S(1)}, f32[16,512]{1,0:T(8,128)S(1)}, u32[]{:S(2)}, u32[]{:S(2)}) collective-permute-start(f32[16,512]{1,0:T(8,128)S(1)} %get-tuple-element.86), channel_id=1, source_target_pairs={{0,192},{8,200},{16,208},{24,216},{32,224},{40,232},{48,240},{56,2... | collective-permute-start | bytes 98312 | tf_op jit(solution)/shard_map/ppermute | solution.py:611
  173.5 10.0 %collective-permute-start.23 = (f32[16,512]{1,0:T(8,128)S(1)}, f32[16,512]{1,0:T(8,128)S(1)}, u32[]{:S(2)}, u32[]{:S(2)}) collective-permute-start(f32[16,512]{1,0:T(8,128)S(1)} %get-tuple-element.86), channel_id=1, source_target_pairs={{0,128},{8,136},{16,144},{24,152},{32,160},{40,168},{48,176},{56,1... | collective-permute-start | bytes 98312 | tf_op jit(solution)/shard_map/ppermute | solution.py:611
  187.1 9.3 %collective-permute-start.25 = (bf16[256,512]{1,0:T(8,128)(2,1)S(1)}, bf16[256,512]{1,0:T(8,128)(2,1)S(1)}, u32[]{:S(2)}, u32[]{:S(2)}) collective-permute-start(bf16[256,512]{1,0:T(8,128)(2,1)S(1)} %get-tuple-element.88), channel_id=1, source_target_pairs={{0,2},{1,3},{2,4},{3,5},{4,6},{5,7},{6,0},{7,1},{8,10},{9,11},{10,... | collective-permute-start | bytes 786440 | tf_op jit(solution)/shard_map/ppermute | solution.py:552
  188.6 14.5 %collective-permute-start.26 = (bf16[256,512]{1,0:T(8,128)(2,1)S(1)}, bf16[256,512]{1,0:T(8,128)(2,1)S(1)}, u32[]{:S(2)}, u32[]{:S(2)}) collective-permute-start(bf16[256,512]{1,0:T(8,128)(2,1)S(1)} %get-tuple-element.89), channel_id=1, source_target_pairs={{0,6},{1,7},{2,0},{3,1},{4,2},{5,3},{6,4},{7,5},{8,14},{9,15},{10,... | collective-permute-start | bytes 786440 | tf_op jit(solution)/shard_map/ppermute | solution.py:552
  189.2 13.9 %collective-permute-start.27 = (bf16[256,512]{1,0:T(8,128)(2,1)S(1)}, bf16[256,512]{1,0:T(8,128)(2,1)S(1)}, u32[]{:S(2)}, u32[]{:S(2)}) collective-permute-start(bf16[256,512]{1,0:T(8,128)(2,1)S(1)} %get-tuple-element.90), channel_id=1, source_target_pairs={{0,4},{1,5},{2,6},{3,7},{4,0},{5,1},{6,2},{7,3},{8,12},{9,13},{10,... | collective-permute-start | bytes 786440 | tf_op jit(solution)/shard_map/ppermute | solution.py:552
  203.3 9.3 %collective-permute-start.28 = (bf16[256,512]{1,0:T(8,128)(2,1)S(1)}, bf16[256,512]{1,0:T(8,128)(2,1)S(1)}, u32[]{:S(2)}, u32[]{:S(2)}) collective-permute-start(bf16[256,512]{1,0:T(8,128)(2,1)S(1)} %get-tuple-element.97), channel_id=1, source_target_pairs={{0,2},{1,3},{2,4},{3,5},{4,6},{5,7},{6,0},{7,1},{8,10},{9,11},{10,... | collective-permute-start | bytes 786440 | tf_op jit(solution)/shard_map/ppermute | solution.py:561
  203.7 9.3 %collective-permute-start.29 = (bf16[256,512]{1,0:T(8,128)(2,1)S(1)}, bf16[256,512]{1,0:T(8,128)(2,1)S(1)}, u32[]{:S(2)}, u32[]{:S(2)}) collective-permute-start(bf16[256,512]{1,0:T(8,128)(2,1)S(1)} %get-tuple-element.98), channel_id=1, source_target_pairs={{0,6},{1,7},{2,0},{3,1},{4,2},{5,3},{6,4},{7,5},{8,14},{9,15},{10,... | collective-permute-start | bytes 786440 | tf_op jit(solution)/shard_map/ppermute | solution.py:561
  205.4 14.1 %collective-permute-start.30 = (bf16[256,512]{1,0:T(8,128)(2,1)S(1)}, bf16[256,512]{1,0:T(8,128)(2,1)S(1)}, u32[]{:S(2)}, u32[]{:S(2)}) collective-permute-start(bf16[256,512]{1,0:T(8,128)(2,1)S(1)} %get-tuple-element.99), channel_id=1, source_target_pairs={{0,4},{1,5},{2,6},{3,7},{4,0},{5,1},{6,2},{7,3},{8,12},{9,13},{10,... | collective-permute-start | bytes 786440 | tf_op jit(solution)/shard_map/ppermute | solution.py:561
  208.1 16.8 %collective-permute-start.31 = (bf16[256,512]{1,0:T(8,128)(2,1)S(1)}, bf16[256,512]{1,0:T(8,128)(2,1)S(1)}, u32[]{:S(2)}, u32[]{:S(2)}) collective-permute-start(bf16[256,512]{1,0:T(8,128)(2,1)S(1)} %add_convert_fusion.1), channel_id=1, source_target_pairs={{0,1},{1,0},{2,3},{3,2},{4,5},{5,4},{6,7},{7,6},{8,9},{9,8},{10,11... | collective-permute-start | bytes 786440 | tf_op jit(solution)/shard_map/ppermute | solution.py:560
  (35 other events, 292.5 us)
Sparse Core Ops, SparseCore 0:
  29.5 114.6 all-gather.2

commit v2 on v1

--- a/solution.py
+++ b/solution.py
@@ -14,11 +14,10 @@
 ROWS = 256
 WIDTH = 512
 HALO = 144
-VMEM_BYTES = 48 * 1024 * 1024
-
-
-def params():
-    return pltpu.CompilerParams(vmem_limit_bytes=VMEM_BYTES)
+
+
+def params(mib=24):
+    return pltpu.CompilerParams(vmem_limit_bytes=mib * 1024 * 1024)
 
 
 def vspecs(n):
@@ -39,7 +38,7 @@
 
 NY, NZ, NC, NX, NH = 4, 4, 2, 4, 2
 
-def rim_kernel(q_ref, k_ref, v_ref, out_ref, sems):
+def rim_kernel(q_ref, k_ref, v_ref, out_ref, q_out, k_out, v_out, sems):
     parts = ((k_ref, HALO, 0), (v_ref, HALO, HALO), (q_ref, 16, 2 * HALO))
     copies = []
     for i, (ref, depth, at) in enumerate(parts):
@@ -48,6 +47,10 @@
         )
         copy.start()
         copies.append(copy)
+    for i, (ref, out) in enumerate(((q_ref, q_out), (k_ref, k_out), (v_ref, v_out))):
+        copy = pltpu.make_async_copy(ref, out, sems.at[3 + i])
+        copy.start()
+        copies.append(copy)
     for copy in copies:
         copy.wait()
 
@@ -55,10 +58,10 @@
 def rim_rows(q, k, v):
     return pl.pallas_call(
         rim_kernel,
-        out_shape=jax.ShapeDtypeStruct((2 * HALO + 16, WIDTH), BF16),
+        out_shape=[jax.ShapeDtypeStruct((2 * HALO + 16, WIDTH), BF16)] + [PIECE] * 3,
         in_specs=hspecs(3),
-        out_specs=pl.BlockSpec(memory_space=pltpu.VMEM),
-        scratch_shapes=[pltpu.SemaphoreType.DMA((3,))],
+        out_specs=vspecs(4),
+        scratch_shapes=[pltpu.SemaphoreType.DMA((6,))],
         compiler_params=params(),
         name="rim_rows",
     )(q, k, v)
@@ -239,7 +242,7 @@
         in_specs=[SMEM_SPEC] + vspecs(1) + hspecs(1),
         out_specs=vspecs(4),
         scratch_shapes=SHARE_SCRATCH,
-        compiler_params=params(),
+        compiler_params=params(48),
         name="shares",
     )(where, y, weight)
 
@@ -281,7 +284,7 @@
             pltpu.VMEM((HALO + ROWS, LANES), F32),
             pltpu.VMEM((16 + ROWS, LANES), F32),
         ] + SHARE_SCRATCH,
-        compiler_params=params(),
+        compiler_params=params(48),
         name="mr_op",
     )(where, q, k, v, halo, feat, toep, weight)
 
@@ -297,19 +300,16 @@
         acc_refs = refs[pos : pos + count]
         pos += count
     out_refs = refs[pos : pos + count]
-    hbuf, wbuf, hsem, wsem = refs[pos + count :]
+    wbuf, wsem = refs[pos + count :]
     x = where_ref[0]
-    hcopies, wcopies = [], []
+    wcopies = []
     for i in range(n):
         e, d = flips[i // 4], (0, 1, 3, 2)[i % 4]
-        copy = pltpu.make_async_copy(hidden_refs[i], hbuf.at[i], hsem.at[i])
-        copy.start()
-        hcopies.append(copy)
         src_y = lax.rem(x + 4 - d, 4)
         for b in range(4):
             odd = 1 - b // 2
             high = odd if e == 1 else 1 - odd
-            member = (src_y * 4 + high * 2 + odd) * 2 + b % 2
+            member = gathered_at(src_y, high * 2 + odd, b % 2)
             copy = pltpu.make_async_copy(
                 w_ref.at[member, pl.ds(slots[0], count)],
                 wbuf.at[i, :, :, pl.ds(b * LANES, LANES)],
@@ -319,11 +319,10 @@
             wcopies.append(copy)
     sums = [None] * count
     for i in range(n):
-        hcopies[i].wait()
         for b in range(4):
             wcopies[i * 4 + b].wait()
         for j in range(count):
-            prod = jnp.dot(hbuf[i], wbuf[i, j], preferred_element_type=F32)
+            prod = jnp.dot(hidden_refs[i][...], wbuf[i, j], preferred_element_type=F32)
             if i == 0:
                 sums[j] = prod if first else prod + acc_refs[j][...]
             else:
@@ -337,15 +336,13 @@
     return pl.pallas_call(
         functools.partial(project_kernel, flips, slots, not acc, last),
         out_shape=[jax.ShapeDtypeStruct((ROWS, WIDTH), BF16 if last else F32)] * count,
-        in_specs=[SMEM_SPEC] + hspecs(n + 1) + vspecs(len(acc)),
+        in_specs=[SMEM_SPEC] + vspecs(n) + hspecs(1) + vspecs(len(acc)),
         out_specs=vspecs(count),
         scratch_shapes=[
-            pltpu.VMEM((n, ROWS, WIDTH), BF16),
             pltpu.VMEM((n, count, WIDTH, WIDTH), BF16),
-            pltpu.SemaphoreType.DMA((n,)),
             pltpu.SemaphoreType.DMA((n, 4)),
         ],
-        compiler_params=params(),
+        compiler_params=params(48),
         name="project",
     )(where, *pieces, weights, *acc)
 
@@ -490,7 +487,7 @@
         in_specs=[SMEM_SPEC] + vspecs(11) + hspecs(1),
         out_specs=vspecs(5),
         scratch_shapes=[pltpu.VMEM((16 + ROWS, LANES), F32)] + SHARE_SCRATCH,
-        compiler_params=params(),
+        compiler_params=params(48),
         name="li_outer",
     )(where, conv, q, halo, feat, leave, rates, carry, other, *above, weight)
 
@@ -523,6 +520,18 @@
         (ctx_of(y, z, k), ctx_of((y + by) % NY, z, k))
         for y in range(NY) for z in range(NZ) for k in range(NC)
     ]
+
+
+GATHER_ORDER = [
+    ctx_of(y if z % 2 == 0 else NY - 1 - y, z, k)
+    for z in range(NZ) for y in range(NY) for k in range(NC)
+]
+
+
+def gathered_at(y, z, k):
+    if z % 2 == 1:
+        y = NY - 1 - y
+    return (z * NY + y) * NC + k
 
 
 def weight_moves():
@@ -548,21 +557,18 @@
     return lax.optimization_barrier(values)
 
 
-def sum_shares(where, y, other, weight, own_extra, fillers):
+def sum_shares(where, y, other, weight, own_extra):
     got = [lax.ppermute(other[d], "mp", x_shift(d)) for d in (1, 3, 2)]
-    if fillers:
-        held = tied(*got, *fillers)
-        got, fillers = held[:3], held[3:]
     total_other = other[0].astype(F32)
     for piece in got:
         total_other = total_other + piece.astype(F32)
     total_other, *mine = tied(total_other.astype(BF16), *shares(where, y, weight, 0))
     crossed = lax.ppermute(total_other, "mp", H_SWAP)
     got_mine = [lax.ppermute(mine[d], "mp", x_shift(d)) for d in (1, 3, 2)]
-    total = own_extra.astype(F32) + mine[0].astype(F32)
+    (total,) = tied(own_extra.astype(F32) + mine[0].astype(F32) + crossed.astype(F32))
     for piece in got_mine:
         total = total + piece.astype(F32)
-    return (total + crossed.astype(F32)).astype(BF16), fillers
+    return total.astype(BF16)
 
 
 def body(
@@ -577,14 +583,15 @@
 
     forward = [(i, i + 1) for i in range(NY * NZ * NC - 1)]
     moved = lax.ppermute(in_weight, ("ctx", "mp"), weight_moves())
-    halo = lax.ppermute(rim_rows(query_mr, key_mr, value_mr), "ctx", forward)
+    rim, query_mr, key_mr, value_mr = rim_rows(query_mr, key_mr, value_mr)
+    halo = lax.ppermute(rim, "ctx", forward)
     toep_mr = toeplitz(mr_taps)
+    halo, moved, toep_mr = tied(halo, moved, toep_mr)
+    weights = lax.all_gather(moved, "ctx", axis_index_groups=[GATHER_ORDER])
     gated_one, *other_one = mr_op(
         where, query_mr, key_mr, value_mr, halo, featurizer_mr, toep_mr, out_mr
     )
-    *other_one, moved = tied(*other_one, moved)
-    weights = lax.all_gather(moved, "ctx")
-    hidden, _ = sum_shares(where, gated_one, other_one, out_mr, residual, ())
+    hidden = sum_shares(where, gated_one, other_one, out_mr, residual)
     filters = prep(li_rates.T, li_residues.T)
 
     crossed = lax.ppermute(hidden, "mp", H_SWAP)
@@ -601,6 +608,10 @@
     other_load = lax.ppermute(load, "ctx", CORE_SWAP)
     chip = chip_state(where, load, other_load, lane_rates)
     before = [lax.ppermute(chip, "ctx", z_shift(s)) for s in (1, 2, 3)]
+    (fresh_q,) = project(where, pieces, weights, (0, 1), (0,))
+    conv = li_inner(product, toep_li)
+    *before, fresh_q, conv = tied(*before, fresh_q, conv)
+    halo_q = lax.ppermute(fresh_q[ROWS - 16 :], "ctx", forward)
     line_total, line_carry = line_state(where, [chip] + before, lane_rates)
     above = []
     for s in (1, 2, 3):
@@ -610,15 +621,11 @@
         ]
         above.append(lax.ppermute(line_total, "ctx", pairs))
 
-    (fresh_q,) = project(where, pieces, weights, (0, 1), (0,))
-    halo_q = lax.ppermute(fresh_q[ROWS - 16 :], "ctx", forward)
-    conv = li_inner(product, toep_li)
-
     gated_two, *other_two = li_outer(
         where, conv, fresh_q, halo_q, featurizer_li, leave, lane_rates,
         line_carry, other_load, above, out_li,
     )
-    return sum_shares(where, gated_two, other_two, out_li, hidden, ())[0]
+    return sum_shares(where, gated_two, other_two, out_li, hidden)
 
 
 def solution(mesh):

time: 233 us -> 222 us (0.953)
  waiting for transfers between devices: 107 us -> 93.2 us
  starting transfers between devices: 62.2 us -> 70.2 us
  local copies, waits for them, and re-layouts: 17.5 us -> 11.2 us
    ppermute x6, waiting for transfers between devices: 15.4 us -> 1.83 us  [sum_shares(): got_mine = [lax.ppermute(mine[d], 'mp', x_shift(d)) for d in (1, 3, 2)]]
    ppermute x1, waiting for transfers between devices: 2.1 us -> 10.4 us  [body(): moved = lax.ppermute(in_weight, ('ctx', 'mp'), weight_moves())]
    ppermute x2, waiting for transfers between devices: 15.8 us -> 22.6 us  [sum_shares(): crossed = lax.ppermute(total_other, 'mp', H_SWAP)]
    unnamed x53 -> x41, local copies, waits for them, and re-layouts: 17.4 us -> 11.1 us
    ppermute x3, waiting for transfers between devices: 4.99 us -> 0.01 us  [body(): before = [lax.ppermute(chip, 'ctx', z_shift(s)) for s in (1, 2, 3)]]
    ppermute x1, waiting for transfers between devices: 10.9 us -> 6.18 us  [body(): crossed = lax.ppermute(hidden, 'mp', H_SWAP)]
    all_gather x1, waiting for transfers between devices: 28.6 us -> 24.1 us  [body(): weights = lax.all_gather(moved, 'ctx', axis_index_groups=[GATHER_ORDER])]
    ppermute x1, starting transfers between devices: 0.9 us -> 4.8 us  [body(): crossed = lax.ppermute(hidden, 'mp', H_SWAP)]
  transfers between devices with their start and end apart: 33 -> 33, of which waited for: 22 -> 16; matrix products, arithmetic and copies ran while one was open for 1% -> 1% of each run, Pallas kernels for 9% -> 9%
where the time goes in v2:
time: 222 us; the launch traced here: 221 us
  waiting for transfers between devices  93.2 us (42%)
  starting transfers between devices  70.2 us (32%)
  Pallas kernels  31 us (14%)
  between operations  13.8 us (6%)
  local copies, waits for them, and re-layouts  11.2 us (5%)
    all_gather x1, waiting for transfers between devices, body(): weights = lax.all_gather(moved, 'ctx', axis_index_groups=[GATHER_ORDER])  24.1 us
    ppermute x2, waiting for transfers between devices, sum_shares(): crossed = lax.ppermute(total_other, 'mp', H_SWAP)  22.6 us
    ppermute x6, waiting for transfers between devices, sum_shares(): got = [lax.ppermute(other[d], 'mp', x_shift(d)) for d in (1, 3, 2)]  16.9 us
    ppermute x6, starting transfers between devices, sum_shares(): got = [lax.ppermute(other[d], 'mp', x_shift(d)) for d in (1, 3, 2)]  15.5 us
    unnamed x41, local copies, waits for them, and re-layouts  11.1 us
    ppermute x2, starting transfers between devices, sum_shares(): crossed = lax.ppermute(total_other, 'mp', H_SWAP)  10.9 us
    ppermute x1, waiting for transfers between devices, body(): moved = lax.ppermute(in_weight, ('ctx', 'mp'), weight_moves())  10.4 us
    ppermute x3, starting transfers between devices, body(): above.append(lax.ppermute(line_total, 'ctx', pairs))  8.92 us
  transfers between devices with their start and end apart: 33, of which 16 were waited for; matrix products, arithmetic and copies ran while one was open for 1% of the time, Pallas kernels for 9%

profile of v2, /device:TPU:2, one launch (start us, length us, event | category | flops | bytes accessed | tf_op | source)
XLA Modules:
  0.0 220.9 jit_solution(2245218641127046191)
XLA Ops:
  6.5 2.9 %collective-permute-start.1 = (bf16[3,512,128]{2,1,0:T(8,128)(2,1)}, bf16[3,512,128]{2,1,0:T(8,128)(2,1)}, u32[]{:S(2)}, u32[]{:S(2)}) collective-permute-start(bf16[3,512,128]{2,1,0:T(8,128)(2,1)} %param.19), channel_id=1, source_target_pairs={{0,16},{1,48},{2,80},{3,112},{4,144},{5,176},{6,208},{7,240},{8,24... | collective-permute-start | bytes 1179656 | tf_op jit(solution)/shard_map/ppermute | solution.py:585
  15.8 3.1 %toeplitz.1.toep_ref = bf16[4096,256]{1,0:T(8,128)(2,1)S(1)} custom-call(f32[128,32]{1,0:T(8,128)S(1)} %copy.14.taps_ref), custom_call_target="tpu_custom_call" | custom-call | tf_op jit(solution)/shard_map/toeplitz/pallas_call | solution.py:108
  18.9 10.4 %collective-permute-done.1 = bf16[3,512,128]{2,1,0:T(8,128)(2,1)} collective-permute-done((bf16[3,512,128]{2,1,0:T(8,128)(2,1)}, bf16[3,512,128]{2,1,0:T(8,128)(2,1)}, u32[]{:S(2)}, u32[]{:S(2)}) %collective-permute-start.1) | collective-permute-done | bytes 393248 | tf_op jit(solution)/shard_map/ppermute | solution.py:585
  30.4 4.0 %mr_op.1 = (bf16[256,512]{1,0:T(8,128)(2,1)S(1)}, bf16[256,512]{1,0:T(8,128)(2,1)S(1)}, bf16[256,512]{1,0:T(8,128)(2,1)S(1)}, bf16[256,512]{1,0:T(8,128)(2,1)S(1)}, bf16[256,512]{1,0:T(8,128)(2,1)S(1)}) custom-call(s32[5]{0:T(128)S(1)} %stack.23.where_ref, bf16[256,512]{1,0:T(8,128)(2,1)S(1)} %get-tuple-element.60.q_ref, ...), custom_call_target="tpu_custom_call" | custom-call | tf_op jit(solution)/shard_map/mr_op/pallas_call | solution.py:277
  34.4 9.8 %collective-permute-start.2 = (bf16[256,512]{1,0:T(8,128)(2,1)S(1)}, bf16[256,512]{1,0:T(8,128)(2,1)S(1)}, u32[]{:S(2)}, u32[]{:S(2)}) collective-permute-start(bf16[256,512]{1,0:T(8,128)(2,1)S(1)} %get-tuple-element.67), channel_id=1, source_target_pairs={{0,2},{1,3},{2,4},{3,5},{4,6},{5,7},{6,0},{7,1},{8,10},{9,11},{10,... | collective-permute-start | bytes 786440 | tf_op jit(solution)/shard_map/ppermute | solution.py:561
  47.8 5.1 %collective-permute-done.2 = bf16[256,512]{1,0:T(8,128)(2,1)S(1)} collective-permute-done((bf16[256,512]{1,0:T(8,128)(2,1)S(1)}, bf16[256,512]{1,0:T(8,128)(2,1)S(1)}, u32[]{:S(2)}, u32[]{:S(2)}) %collective-permute-start.2) | collective-permute-done | bytes 262176 | tf_op jit(solution)/shard_map/ppermute | solution.py:561
  55.1 5.9 %collective-permute-start.5 = (bf16[256,512]{1,0:T(8,128)(2,1)S(1)}, bf16[256,512]{1,0:T(8,128)(2,1)S(1)}, u32[]{:S(2)}, u32[]{:S(2)}) collective-permute-start(bf16[256,512]{1,0:T(8,128)(2,1)S(1)} %add_convert_fusion.3), channel_id=1, source_target_pairs={{0,1},{1,0},{2,3},{3,2},{4,5},{5,4},{6,7},{7,6},{8,9},{9,8},{10,11... | collective-permute-start | bytes 786440 | tf_op jit(solution)/shard_map/ppermute | solution.py:566
  64.9 12.5 %collective-permute-done.5 = bf16[256,512]{1,0:T(8,128)(2,1)S(1)} collective-permute-done((bf16[256,512]{1,0:T(8,128)(2,1)S(1)}, bf16[256,512]{1,0:T(8,128)(2,1)S(1)}, u32[]{:S(2)}, u32[]{:S(2)}) %collective-permute-start.5) | collective-permute-done | bytes 262176 | tf_op jit(solution)/shard_map/ppermute | solution.py:566
  77.7 4.8 %collective-permute-start.12 = (bf16[256,512]{1,0:T(8,128)(2,1)S(1)}, bf16[256,512]{1,0:T(8,128)(2,1)S(1)}, u32[]{:S(2)}, u32[]{:S(2)}) collective-permute-start(bf16[256,512]{1,0:T(8,128)(2,1)S(1)} %add_convert_fusion.2.refs_0_), channel_id=1, source_target_pairs={{0,1},{1,0},{2,3},{3,2},{4,5},{5,4},{6,7},{7,6},{8,9},{9,8},{10,11... | collective-permute-start | bytes 786440 | tf_op jit(solution)/shard_map/ppermute | solution.py:597
  82.5 2.1 collective-permute-start.11
  84.6 3.8 %prep.1 = (bf16[4096,256]{1,0:T(8,128)(2,1)S(1)}, f32[256,512]{1,0:T(8,128)S(1)}, f32[256,512]{1,0:T(8,128)S(1)}, f32[16,512]{1,0:T(8,128)S(1)}) custom-call(f32[16,32]{1,0:T(8,128)S(1)} %bitcast.8, f32[16,32]{1,0:T(8,128)S(1)} %bitcast.9), custom_call_target="tpu_custom_call" | custom-call | tf_op jit(solution)/shard_map/prep/pallas_call | solution.py:166
  92.1 6.2 %collective-permute-done.12.refs_4_ = bf16[256,512]{1,0:T(8,128)(2,1)S(1)} collective-permute-done((bf16[256,512]{1,0:T(8,128)(2,1)S(1)}, bf16[256,512]{1,0:T(8,128)(2,1)S(1)}, u32[]{:S(2)}, u32[]{:S(2)}) %collective-permute-start.12) | collective-permute-done | bytes 262176 | tf_op jit(solution)/shard_map/ppermute | solution.py:597
  102.3 6.6 %collective-permute-done.15.refs_7_ = bf16[256,512]{1,0:T(8,128)(2,1)S(1)} collective-permute-done((bf16[256,512]{1,0:T(8,128)(2,1)S(1)}, bf16[256,512]{1,0:T(8,128)(2,1)S(1)}, u32[]{:S(2)}, u32[]{:S(2)}) %collective-permute-start.15) | collective-permute-done | bytes 262176 | tf_op jit(solution)/shard_map/ppermute | solution.py:601
  113.0 24.1 %all-gather.3.cloned.1.call-done = bf16[96,512,128]{2,1,0:T(8,128)(2,1)} async-done(((bf16[3,512,128]{2,1,0:T(8,128)(2,1)}), bf16[96,512,128]{2,1,0:T(8,128)(2,1)}) %all-gather.3.cloned.1.call-update) | async-done | bytes 12582928 | tf_op jit(solution)/shard_map/all_gather | solution.py:590
  140.0 5.0 %project.2 = (bf16[256,512]{1,0:T(8,128)(2,1)S(1)}, bf16[256,512]{1,0:T(8,128)(2,1)S(1)}) custom-call(s32[5]{0:T(128)S(1)} %stack.23.where_ref, bf16[256,512]{1,0:T(8,128)(2,1)S(1)} %add_convert_fusion.2.refs_0_, bf16[256,512]{1,0:T(8,128)(2,1)S(1)} %collective-permute-done.9.refs_1_, bf16[256,512]{1,0:T(8,128)(2,1)S(1)} %collective-permute-done.10.refs_2_, ...), custom_call_target="tpu_custom_call" | custom-call | tf_op jit(solution)/shard_map/project/pallas_call | solution.py:336
  145.0 2.2 collective-permute-start.16
  151.4 3.5 %collective-permute-start.20 = (f32[16,512]{1,0:T(8,128)S(1)}, f32[16,512]{1,0:T(8,128)S(1)}, u32[]{:S(2)}, u32[]{:S(2)}) collective-permute-start(f32[16,512]{1,0:T(8,128)S(1)} %chip_state.1.c0), channel_id=1, source_target_pairs={{0,48},{8,56},{16,0},{24,8},{32,16},{40,24},{48,32},{56,40},{64,11... | collective-permute-start | bytes 98312 | tf_op jit(solution)/shard_map/ppermute | solution.py:610
  156.8 3.7 %project.3.q_ref = bf16[256,512]{1,0:T(8,128)(2,1)S(1)} custom-call(s32[5]{0:T(128)S(1)} %stack.23.where_ref, bf16[256,512]{1,0:T(8,128)(2,1)S(1)} %add_convert_fusion.2.refs_0_, bf16[256,512]{1,0:T(8,128)(2,1)S(1)} %collective-permute-done.9.refs_1_, bf16[256,512]{1,0:T(8,128)(2,1)S(1)} %collective-permute-done.10.refs_2_, ...), custom_call_target="tpu_custom_call" | custom-call | tf_op jit(solution)/shard_map/project/pallas_call | solution.py:336
  161.9 4.9 %collective-permute-start.24 = (f32[16,512]{1,0:T(8,128)S(1)}, f32[16,512]{1,0:T(8,128)S(1)}, u32[]{:S(2)}, u32[]{:S(2)}) collective-permute-start(f32[16,512]{1,0:T(8,128)S(1)} %get-tuple-element.100), channel_id=1, source_target_pairs={{0,192},{8,200},{16,208},{24,216},{32,224},{40,232},{48,240},{56,2... | collective-permute-start | bytes 98312 | tf_op jit(solution)/shard_map/ppermute | solution.py:622
  168.1 2.8 %collective-permute-start.22 = (f32[16,512]{1,0:T(8,128)S(1)}, f32[16,512]{1,0:T(8,128)S(1)}, u32[]{:S(2)}, u32[]{:S(2)}) collective-permute-start(f32[16,512]{1,0:T(8,128)S(1)} %get-tuple-element.100), channel_id=1, source_target_pairs={{0,64},{8,72},{16,80},{24,88},{32,96},{40,104},{48,112},{56,120},{... | collective-permute-start | bytes 98312 | tf_op jit(solution)/shard_map/ppermute | solution.py:622
  173.0 3.5 %li_outer.1 = (bf16[256,512]{1,0:T(8,128)(2,1)S(1)}, bf16[256,512]{1,0:T(8,128)(2,1)S(1)}, bf16[256,512]{1,0:T(8,128)(2,1)S(1)}, bf16[256,512]{1,0:T(8,128)(2,1)S(1)}, bf16[256,512]{1,0:T(8,128)(2,1)S(1)}) custom-call(s32[5]{0:T(128)S(1)} %stack.23.where_ref, f32[256,512]{1,0:T(8,128)S(1)} %li_inner.1.conv_ref, bf16[256,512]{1,0:T(8,128)(2,1)S(1)} %project.3.q_ref, ...), custom_call_target="tpu_custom_call" | custom-call | tf_op jit(solution)/shard_map/li_outer/pallas_call | solution.py:484
  186.4 6.2 %collective-permute-done.27 = bf16[256,512]{1,0:T(8,128)(2,1)S(1)} collective-permute-done((bf16[256,512]{1,0:T(8,128)(2,1)S(1)}, bf16[256,512]{1,0:T(8,128)(2,1)S(1)}, u32[]{:S(2)}, u32[]{:S(2)}) %collective-permute-start.27) | collective-permute-done | bytes 262176 | tf_op jit(solution)/shard_map/ppermute | solution.py:561
  192.7 4.9 %collective-permute-start.28 = (bf16[256,512]{1,0:T(8,128)(2,1)S(1)}, bf16[256,512]{1,0:T(8,128)(2,1)S(1)}, u32[]{:S(2)}, u32[]{:S(2)}) collective-permute-start(bf16[256,512]{1,0:T(8,128)(2,1)S(1)} %add_convert_fusion.1), channel_id=1, source_target_pairs={{0,1},{1,0},{2,3},{3,2},{4,5},{5,4},{6,7},{7,6},{8,9},{9,8},{10,11... | collective-permute-start | bytes 786440 | tf_op jit(solution)/shard_map/ppermute | solution.py:566
  201.2 10.1 %collective-permute-done.28 = bf16[256,512]{1,0:T(8,128)(2,1)S(1)} collective-permute-done((bf16[256,512]{1,0:T(8,128)(2,1)S(1)}, bf16[256,512]{1,0:T(8,128)(2,1)S(1)}, u32[]{:S(2)}, u32[]{:S(2)}) %collective-permute-start.28) | collective-permute-done | bytes 262176 | tf_op jit(solution)/shard_map/ppermute | solution.py:566
  (108 shorter events, 59.0 us)
Async XLA Ops:
  6.5 130.6 %all-gather.3.cloned.1.call-start = ((), (), s32[]{:S(2)}) async-start(), calls=%async_computation | async-start | bytes 12976128 | tf_op jit(solution)/shard_map/all_gather | solution.py:590
  6.5 22.8 %collective-permute-start.1 = (bf16[3,512,128]{2,1,0:T(8,128)(2,1)}, bf16[3,512,128]{2,1,0:T(8,128)(2,1)}, u32[]{:S(2)}, u32[]{:S(2)}) collective-permute-start(bf16[3,512,128]{2,1,0:T(8,128)(2,1)} %param.19), channel_id=1, source_target_pairs={{0,16},{1,48},{2,80},{3,112},{4,144},{5,176},{6,208},{7,240},{8,24... | collective-permute-start | bytes 1179656 | tf_op jit(solution)/shard_map/ppermute | solution.py:585
  34.4 18.5 %collective-permute-start.2 = (bf16[256,512]{1,0:T(8,128)(2,1)S(1)}, bf16[256,512]{1,0:T(8,128)(2,1)S(1)}, u32[]{:S(2)}, u32[]{:S(2)}) collective-permute-start(bf16[256,512]{1,0:T(8,128)(2,1)S(1)} %get-tuple-element.67), channel_id=1, source_target_pairs={{0,2},{1,3},{2,4},{3,5},{4,6},{5,7},{6,0},{7,1},{8,10},{9,11},{10,... | collective-permute-start | bytes 786440 | tf_op jit(solution)/shard_map/ppermute | solution.py:561
  44.2 10.8 %collective-permute-start.3 = (bf16[256,512]{1,0:T(8,128)(2,1)S(1)}, bf16[256,512]{1,0:T(8,128)(2,1)S(1)}, u32[]{:S(2)}, u32[]{:S(2)}) collective-permute-start(bf16[256,512]{1,0:T(8,128)(2,1)S(1)} %get-tuple-element.68), channel_id=1, source_target_pairs={{0,6},{1,7},{2,0},{3,1},{4,2},{5,3},{6,4},{7,5},{8,14},{9,15},{10,... | collective-permute-start | bytes 786440 | tf_op jit(solution)/shard_map/ppermute | solution.py:561
  44.2 10.8 %collective-permute-start.4 = (bf16[256,512]{1,0:T(8,128)(2,1)S(1)}, bf16[256,512]{1,0:T(8,128)(2,1)S(1)}, u32[]{:S(2)}, u32[]{:S(2)}) collective-permute-start(bf16[256,512]{1,0:T(8,128)(2,1)S(1)} %get-tuple-element.69), channel_id=1, source_target_pairs={{0,4},{1,5},{2,6},{3,7},{4,0},{5,1},{6,2},{7,3},{8,12},{9,13},{10,... | collective-permute-start | bytes 786440 | tf_op jit(solution)/shard_map/ppermute | solution.py:561
  55.1 22.3 %collective-permute-start.5 = (bf16[256,512]{1,0:T(8,128)(2,1)S(1)}, bf16[256,512]{1,0:T(8,128)(2,1)S(1)}, u32[]{:S(2)}, u32[]{:S(2)}) collective-permute-start(bf16[256,512]{1,0:T(8,128)(2,1)S(1)} %add_convert_fusion.3), channel_id=1, source_target_pairs={{0,1},{1,0},{2,3},{3,2},{4,5},{5,4},{6,7},{7,6},{8,9},{9,8},{10,11... | collective-permute-start | bytes 786440 | tf_op jit(solution)/shard_map/ppermute | solution.py:566
  61.1 16.4 %collective-permute-start.6 = (bf16[256,512]{1,0:T(8,128)(2,1)S(1)}, bf16[256,512]{1,0:T(8,128)(2,1)S(1)}, u32[]{:S(2)}, u32[]{:S(2)}) collective-permute-start(bf16[256,512]{1,0:T(8,128)(2,1)S(1)} %get-tuple-element.77), channel_id=1, source_target_pairs={{0,2},{1,3},{2,4},{3,5},{4,6},{5,7},{6,0},{7,1},{8,10},{9,11},{10,... | collective-permute-start | bytes 786440 | tf_op jit(solution)/shard_map/ppermute | solution.py:567
  61.4 16.2 %collective-permute-start.7 = (bf16[256,512]{1,0:T(8,128)(2,1)S(1)}, bf16[256,512]{1,0:T(8,128)(2,1)S(1)}, u32[]{:S(2)}, u32[]{:S(2)}) collective-permute-start(bf16[256,512]{1,0:T(8,128)(2,1)S(1)} %get-tuple-element.78), channel_id=1, source_target_pairs={{0,6},{1,7},{2,0},{3,1},{4,2},{5,3},{6,4},{7,5},{8,14},{9,15},{10,... | collective-permute-start | bytes 786440 | tf_op jit(solution)/shard_map/ppermute | solution.py:567
  63.1 14.4 %collective-permute-start.8 = (bf16[256,512]{1,0:T(8,128)(2,1)S(1)}, bf16[256,512]{1,0:T(8,128)(2,1)S(1)}, u32[]{:S(2)}, u32[]{:S(2)}) collective-permute-start(bf16[256,512]{1,0:T(8,128)(2,1)S(1)} %get-tuple-element.79), channel_id=1, source_target_pairs={{0,4},{1,5},{2,6},{3,7},{4,0},{5,1},{6,2},{7,3},{8,12},{9,13},{10,... | collective-permute-start | bytes 786440 | tf_op jit(solution)/shard_map/ppermute | solution.py:567
  77.7 20.5 %collective-permute-start.12 = (bf16[256,512]{1,0:T(8,128)(2,1)S(1)}, bf16[256,512]{1,0:T(8,128)(2,1)S(1)}, u32[]{:S(2)}, u32[]{:S(2)}) collective-permute-start(bf16[256,512]{1,0:T(8,128)(2,1)S(1)} %add_convert_fusion.2.refs_0_), channel_id=1, source_target_pairs={{0,1},{1,0},{2,3},{3,2},{4,5},{5,4},{6,7},{7,6},{8,9},{9,8},{10,11... | collective-permute-start | bytes 786440 | tf_op jit(solution)/shard_map/ppermute | solution.py:597
  82.5 17.7 %collective-permute-start.11 = (bf16[256,512]{1,0:T(8,128)(2,1)S(1)}, bf16[256,512]{1,0:T(8,128)(2,1)S(1)}, u32[]{:S(2)}, u32[]{:S(2)}) collective-permute-start(bf16[256,512]{1,0:T(8,128)(2,1)S(1)} %add_convert_fusion.2.refs_0_), channel_id=1, source_target_pairs={{0,4},{1,5},{2,6},{3,7},{4,0},{5,1},{6,2},{7,3},{8,12},{9,13},{10,... | collective-permute-start | bytes 786440 | tf_op jit(solution)/shard_map/ppermute | solution.py:598
  90.0 12.3 %collective-permute-start.10 = (bf16[256,512]{1,0:T(8,128)(2,1)S(1)}, bf16[256,512]{1,0:T(8,128)(2,1)S(1)}, u32[]{:S(2)}, u32[]{:S(2)}) collective-permute-start(bf16[256,512]{1,0:T(8,128)(2,1)S(1)} %add_convert_fusion.2.refs_0_), channel_id=1, source_target_pairs={{0,6},{1,7},{2,0},{3,1},{4,2},{5,3},{6,4},{7,5},{8,14},{9,15},{10,... | collective-permute-start | bytes 786440 | tf_op jit(solution)/shard_map/ppermute | solution.py:598
  90.0 12.3 %collective-permute-start.9 = (bf16[256,512]{1,0:T(8,128)(2,1)S(1)}, bf16[256,512]{1,0:T(8,128)(2,1)S(1)}, u32[]{:S(2)}, u32[]{:S(2)}) collective-permute-start(bf16[256,512]{1,0:T(8,128)(2,1)S(1)} %add_convert_fusion.2.refs_0_), channel_id=1, source_target_pairs={{0,2},{1,3},{2,4},{3,5},{4,6},{5,7},{6,0},{7,1},{8,10},{9,11},{10,... | collective-permute-start | bytes 786440 | tf_op jit(solution)/shard_map/ppermute | solution.py:598
  98.2 10.7 %collective-permute-start.15 = (bf16[256,512]{1,0:T(8,128)(2,1)S(1)}, bf16[256,512]{1,0:T(8,128)(2,1)S(1)}, u32[]{:S(2)}, u32[]{:S(2)}) collective-permute-start(bf16[256,512]{1,0:T(8,128)(2,1)S(1)} %collective-permute-done.12.refs_4_), channel_id=1, source_target_pairs={{0,4},{1,5},{2,6},{3,7},{4,0},{5,1},{6,2},{7,3},{8,12},{9,13},{10,... | collective-permute-start | bytes 786440 | tf_op jit(solution)/shard_map/ppermute | solution.py:601
  100.2 11.4 %collective-permute-start.14 = (bf16[256,512]{1,0:T(8,128)(2,1)S(1)}, bf16[256,512]{1,0:T(8,128)(2,1)S(1)}, u32[]{:S(2)}, u32[]{:S(2)}) collective-permute-start(bf16[256,512]{1,0:T(8,128)(2,1)S(1)} %collective-permute-done.12.refs_4_), channel_id=1, source_target_pairs={{0,6},{1,7},{2,0},{3,1},{4,2},{5,3},{6,4},{7,5},{8,14},{9,15},{10,... | collective-permute-start | bytes 786440 | tf_op jit(solution)/shard_map/ppermute | solution.py:601
  100.3 12.1 %collective-permute-start.13 = (bf16[256,512]{1,0:T(8,128)(2,1)S(1)}, bf16[256,512]{1,0:T(8,128)(2,1)S(1)}, u32[]{:S(2)}, u32[]{:S(2)}) collective-permute-start(bf16[256,512]{1,0:T(8,128)(2,1)S(1)} %collective-permute-done.12.refs_4_), channel_id=1, source_target_pairs={{0,2},{1,3},{2,4},{3,5},{4,6},{5,7},{6,0},{7,1},{8,10},{9,11},{10,... | collective-permute-start | bytes 786440 | tf_op jit(solution)/shard_map/ppermute | solution.py:601
  151.4 9.9 %collective-permute-start.20 = (f32[16,512]{1,0:T(8,128)S(1)}, f32[16,512]{1,0:T(8,128)S(1)}, u32[]{:S(2)}, u32[]{:S(2)}) collective-permute-start(f32[16,512]{1,0:T(8,128)S(1)} %chip_state.1.c0), channel_id=1, source_target_pairs={{0,48},{8,56},{16,0},{24,8},{32,16},{40,24},{48,32},{56,40},{64,11... | collective-permute-start | bytes 98312 | tf_op jit(solution)/shard_map/ppermute | solution.py:610
  161.9 11.1 %collective-permute-start.24 = (f32[16,512]{1,0:T(8,128)S(1)}, f32[16,512]{1,0:T(8,128)S(1)}, u32[]{:S(2)}, u32[]{:S(2)}) collective-permute-start(f32[16,512]{1,0:T(8,128)S(1)} %get-tuple-element.100), channel_id=1, source_target_pairs={{0,192},{8,200},{16,208},{24,216},{32,224},{40,232},{48,240},{56,2... | collective-permute-start | bytes 98312 | tf_op jit(solution)/shard_map/ppermute | solution.py:622
  178.1 8.2 %collective-permute-start.26 = (bf16[256,512]{1,0:T(8,128)(2,1)S(1)}, bf16[256,512]{1,0:T(8,128)(2,1)S(1)}, u32[]{:S(2)}, u32[]{:S(2)}) collective-permute-start(bf16[256,512]{1,0:T(8,128)(2,1)S(1)} %get-tuple-element.103), channel_id=1, source_target_pairs={{0,6},{1,7},{2,0},{3,1},{4,2},{5,3},{6,4},{7,5},{8,14},{9,15},{10,... | collective-permute-start | bytes 786440 | tf_op jit(solution)/shard_map/ppermute | solution.py:561
  178.6 13.9 %collective-permute-start.27 = (bf16[256,512]{1,0:T(8,128)(2,1)S(1)}, bf16[256,512]{1,0:T(8,128)(2,1)S(1)}, u32[]{:S(2)}, u32[]{:S(2)}) collective-permute-start(bf16[256,512]{1,0:T(8,128)(2,1)S(1)} %get-tuple-element.104), channel_id=1, source_target_pairs={{0,4},{1,5},{2,6},{3,7},{4,0},{5,1},{6,2},{7,3},{8,12},{9,13},{10,... | collective-permute-start | bytes 786440 | tf_op jit(solution)/shard_map/ppermute | solution.py:561
  192.7 18.6 %collective-permute-start.28 = (bf16[256,512]{1,0:T(8,128)(2,1)S(1)}, bf16[256,512]{1,0:T(8,128)(2,1)S(1)}, u32[]{:S(2)}, u32[]{:S(2)}) collective-permute-start(bf16[256,512]{1,0:T(8,128)(2,1)S(1)} %add_convert_fusion.1), channel_id=1, source_target_pairs={{0,1},{1,0},{2,3},{3,2},{4,5},{5,4},{6,7},{7,6},{8,9},{9,8},{10,11... | collective-permute-start | bytes 786440 | tf_op jit(solution)/shard_map/ppermute | solution.py:566
  197.6 13.8 %collective-permute-start.29 = (bf16[256,512]{1,0:T(8,128)(2,1)S(1)}, bf16[256,512]{1,0:T(8,128)(2,1)S(1)}, u32[]{:S(2)}, u32[]{:S(2)}) collective-permute-start(bf16[256,512]{1,0:T(8,128)(2,1)S(1)} %get-tuple-element.112), channel_id=1, source_target_pairs={{0,2},{1,3},{2,4},{3,5},{4,6},{5,7},{6,0},{7,1},{8,10},{9,11},{10,... | collective-permute-start | bytes 786440 | tf_op jit(solution)/shard_map/ppermute | solution.py:567
  197.6 13.8 %collective-permute-start.30 = (bf16[256,512]{1,0:T(8,128)(2,1)S(1)}, bf16[256,512]{1,0:T(8,128)(2,1)S(1)}, u32[]{:S(2)}, u32[]{:S(2)}) collective-permute-start(bf16[256,512]{1,0:T(8,128)(2,1)S(1)} %get-tuple-element.113), channel_id=1, source_target_pairs={{0,6},{1,7},{2,0},{3,1},{4,2},{5,3},{6,4},{7,5},{8,14},{9,15},{10,... | collective-permute-start | bytes 786440 | tf_op jit(solution)/shard_map/ppermute | solution.py:567
  199.6 13.6 %collective-permute-start.31 = (bf16[256,512]{1,0:T(8,128)(2,1)S(1)}, bf16[256,512]{1,0:T(8,128)(2,1)S(1)}, u32[]{:S(2)}, u32[]{:S(2)}) collective-permute-start(bf16[256,512]{1,0:T(8,128)(2,1)S(1)} %get-tuple-element.114), channel_id=1, source_target_pairs={{0,4},{1,5},{2,6},{3,7},{4,0},{5,1},{6,2},{7,3},{8,12},{9,13},{10,... | collective-permute-start | bytes 786440 | tf_op jit(solution)/shard_map/ppermute | solution.py:567
  (29 other events, 249.3 us)
Sparse Core Ops, SparseCore 0:
  29.5 107.6 all-gather.2

commit v3 on v2

--- a/solution.py
+++ b/solution.py
@@ -16,7 +16,7 @@
 HALO = 144
 
 
-def params(mib=24):
+def params(mib=16):
     return pltpu.CompilerParams(vmem_limit_bytes=mib * 1024 * 1024)
 
 
@@ -242,7 +242,7 @@
         in_specs=[SMEM_SPEC] + vspecs(1) + hspecs(1),
         out_specs=vspecs(4),
         scratch_shapes=SHARE_SCRATCH,
-        compiler_params=params(48),
+        compiler_params=params(52),
         name="shares",
     )(where, y, weight)
 
@@ -284,67 +284,83 @@
             pltpu.VMEM((HALO + ROWS, LANES), F32),
             pltpu.VMEM((16 + ROWS, LANES), F32),
         ] + SHARE_SCRATCH,
-        compiler_params=params(48),
+        compiler_params=params(52),
         name="mr_op",
     )(where, q, k, v, halo, feat, toep, weight)
 
 
-def project_kernel(flips, slots, first, last, where_ref, *refs):
-    n = len(flips) * 4
-    count = len(slots)
-    hidden_refs = refs[:n]
-    w_ref = refs[n]
-    pos = n + 1
-    acc_refs = ()
-    if not first:
-        acc_refs = refs[pos : pos + count]
-        pos += count
-    out_refs = refs[pos : pos + count]
-    wbuf, wsem = refs[pos + count :]
-    x = where_ref[0]
-    wcopies = []
-    for i in range(n):
-        e, d = flips[i // 4], (0, 1, 3, 2)[i % 4]
-        src_y = lax.rem(x + 4 - d, 4)
+def pack_kernel(*refs):
+    for i in range(8):
+        refs[8][i] = refs[i][...]
+
+
+def packed(pieces):
+    return pl.pallas_call(
+        pack_kernel,
+        out_shape=jax.ShapeDtypeStruct((8, ROWS, WIDTH), BF16),
+        in_specs=vspecs(8),
+        out_specs=pl.BlockSpec(memory_space=pltpu.VMEM),
+        compiler_params=params(),
+        name="packed",
+    )(*pieces)
+
+
+def project_kernel(count, sources, where_ref, *refs):
+    hidden_ref = refs[0]
+    n = len(sources)
+    weight_refs = refs[1 : 1 + n]
+    out_refs = refs[1 + n : 1 + n + count]
+    wbuf, wsem = refs[1 + n + count :]
+    x, zh, y, zl, k = [where_ref[i] for i in range(5)]
+    for ref, members in zip(weight_refs, sources):
+        for at, (sy, sz, sk) in members:
+            if at is None:
+                src_y, src_z, src_k = sy, sz, sk
+                at = (src_z * NY + (NY - 1 - src_y if src_z % 2 else src_y)) * NC + src_k
+            else:
+                src_y = lax.rem(y + NY - sy, NY)
+                src_z = lax.bitwise_xor(zl, jnp.int32(sz))
+                src_k = lax.bitwise_xor(k, jnp.int32(sk))
+            odd = lax.rem(jnp.int32(src_z), 2)
+            high = lax.div(jnp.int32(src_z), 2)
+            outer = jnp.where(odd == high, 1, 0)
+            piece = outer * 4 + lax.rem(x + 4 - src_y, 4)
+            block = (1 - odd) * 2 + src_k
+            pltpu.make_async_copy(
+                ref.at[at],
+                wbuf.at[piece, :, :, pl.ds(pl.multiple_of(block * LANES, LANES), LANES)],
+                wsem.at[piece, block],
+            ).start()
+    sums = [None] * count
+    for i in range(8):
         for b in range(4):
-            odd = 1 - b // 2
-            high = odd if e == 1 else 1 - odd
-            member = gathered_at(src_y, high * 2 + odd, b % 2)
-            copy = pltpu.make_async_copy(
-                w_ref.at[member, pl.ds(slots[0], count)],
-                wbuf.at[i, :, :, pl.ds(b * LANES, LANES)],
-                wsem.at[i, b],
-            )
-            copy.start()
-            wcopies.append(copy)
-    sums = [None] * count
-    for i in range(n):
-        for b in range(4):
-            wcopies[i * 4 + b].wait()
+            pltpu.make_async_copy(
+                weight_refs[0].at[0], wbuf.at[i, :, :, pl.ds(b * LANES, LANES)], wsem.at[i, b]
+            ).wait()
         for j in range(count):
-            prod = jnp.dot(hidden_refs[i][...], wbuf[i, j], preferred_element_type=F32)
-            if i == 0:
-                sums[j] = prod if first else prod + acc_refs[j][...]
-            else:
-                sums[j] = sums[j] + prod
+            prod = jnp.dot(hidden_ref[i], wbuf[i, j], preferred_element_type=F32)
+            sums[j] = prod if i == 0 else sums[j] + prod
     for j in range(count):
-        out_refs[j][...] = sums[j].astype(BF16) if last else sums[j]
-
-
-def project(where, pieces, weights, flips, slots, acc=(), last=True):
-    n, count = len(pieces), len(slots)
-    return pl.pallas_call(
-        functools.partial(project_kernel, flips, slots, not acc, last),
-        out_shape=[jax.ShapeDtypeStruct((ROWS, WIDTH), BF16 if last else F32)] * count,
-        in_specs=[SMEM_SPEC] + vspecs(n) + hspecs(1) + vspecs(len(acc)),
+        out_refs[j][...] = sums[j].astype(BF16)
+
+
+PERMUTED = [[(sz, (sy, sz, sk)) for sz in range(4)] for sk in range(2) for sy in range(4)]
+GATHERED = [[(None, (sy, sz, sk)) for sy in range(4) for sz in range(4) for sk in range(2)]]
+
+
+def project(where, pieces, weights, sources, count):
+    return pl.pallas_call(
+        functools.partial(project_kernel, count, sources),
+        out_shape=[PIECE] * count,
+        in_specs=[SMEM_SPEC] + vspecs(1) + hspecs(len(weights)),
         out_specs=vspecs(count),
         scratch_shapes=[
-            pltpu.VMEM((n, count, WIDTH, WIDTH), BF16),
-            pltpu.SemaphoreType.DMA((n, 4)),
+            pltpu.VMEM((8, count, WIDTH, WIDTH), BF16),
+            pltpu.SemaphoreType.DMA((8, 4)),
         ],
         compiler_params=params(48),
         name="project",
-    )(where, *pieces, weights, *acc)
+    )(where, pieces, *weights)
 
 
 def li_gate_kernel(k_ref, v_ref, halo_ref, feat_ref, enter_ref, z_ref, load_ref, kx, vx):
@@ -487,7 +503,7 @@
         in_specs=[SMEM_SPEC] + vspecs(11) + hspecs(1),
         out_specs=vspecs(5),
         scratch_shapes=[pltpu.VMEM((16 + ROWS, LANES), F32)] + SHARE_SCRATCH,
-        compiler_params=params(48),
+        compiler_params=params(52),
         name="li_outer",
     )(where, conv, q, halo, feat, leave, rates, carry, other, *above, weight)
 
@@ -528,10 +544,11 @@
 ]
 
 
-def gathered_at(y, z, k):
-    if z % 2 == 1:
-        y = NY - 1 - y
-    return (z * NY + y) * NC + k
+def z_swap(by):
+    return [
+        (ctx_of(y, z, k), ctx_of(y, z ^ by, k))
+        for y in range(NY) for z in range(NZ) for k in range(NC)
+    ]
 
 
 def weight_moves():
@@ -557,18 +574,23 @@
     return lax.optimization_barrier(values)
 
 
-def sum_shares(where, y, other, weight, own_extra):
+def sum_shares(where, y, other, weight, own_extra, rider=None):
     got = [lax.ppermute(other[d], "mp", x_shift(d)) for d in (1, 3, 2)]
     total_other = other[0].astype(F32)
     for piece in got:
         total_other = total_other + piece.astype(F32)
-    total_other, *mine = tied(total_other.astype(BF16), *shares(where, y, weight, 0))
+    total_other = total_other.astype(BF16)
+    mine = shares(where, y, weight, 0)
+    if rider is None:
+        total_other, *mine = tied(total_other, *mine)
+    else:
+        total_other, rider, *mine = tied(total_other, rider, *mine)
     crossed = lax.ppermute(total_other, "mp", H_SWAP)
     got_mine = [lax.ppermute(mine[d], "mp", x_shift(d)) for d in (1, 3, 2)]
     (total,) = tied(own_extra.astype(F32) + mine[0].astype(F32) + crossed.astype(F32))
     for piece in got_mine:
         total = total + piece.astype(F32)
-    return total.astype(BF16)
+    return total.astype(BF16), rider
 
 
 def body(
@@ -582,33 +604,50 @@
     where = jnp.stack([x, zh, y, zl, k]).astype(jnp.int32)
 
     forward = [(i, i + 1) for i in range(NY * NZ * NC - 1)]
-    moved = lax.ppermute(in_weight, ("ctx", "mp"), weight_moves())
+    moved_kv = lax.ppermute(in_weight[1:3], ("ctx", "mp"), weight_moves())
     rim, query_mr, key_mr, value_mr = rim_rows(query_mr, key_mr, value_mr)
     halo = lax.ppermute(rim, "ctx", forward)
     toep_mr = toeplitz(mr_taps)
-    halo, moved, toep_mr = tied(halo, moved, toep_mr)
-    weights = lax.all_gather(moved, "ctx", axis_index_groups=[GATHER_ORDER])
+    halo, raw_q, toep_mr = tied(halo, in_weight[0:1], toep_mr)
     gated_one, *other_one = mr_op(
         where, query_mr, key_mr, value_mr, halo, featurizer_mr, toep_mr, out_mr
     )
-    hidden = sum_shares(where, gated_one, other_one, out_mr, residual)
+    *other_one, moved_kv = tied(*other_one, moved_kv)
+    weights_kv = lax.all_gather(moved_kv, "ctx", axis_index_groups=[GATHER_ORDER])
+    moved_q = lax.ppermute(raw_q, ("ctx", "mp"), weight_moves())
+    hidden, moved_q = sum_shares(where, gated_one, other_one, out_mr, residual, moved_q)
+    near_q = lax.ppermute(moved_q, "ctx", z_swap(1))
     filters = prep(li_rates.T, li_residues.T)
 
+    hidden, near_q = tied(hidden, near_q)
     crossed = lax.ppermute(hidden, "mp", H_SWAP)
-    own_pieces = [hidden] + [lax.ppermute(hidden, "mp", x_shift(d)) for d in (1, 3, 2)]
-    crossed, *filters = tied(crossed, *filters)
-    toep_li, leave, enter, lane_rates = filters
-    far_pieces = [crossed] + [lax.ppermute(crossed, "mp", x_shift(d)) for d in (1, 3, 2)]
-    pieces = own_pieces + far_pieces
-    fresh_k, fresh_v = project(where, pieces, weights, (0, 1), (1, 2))
+    own_pieces = [lax.ppermute(hidden, "mp", x_shift(d)) for d in (1, 2, 3)]
+    pair_q = jnp.stack([moved_q, near_q])
+    far_q = lax.ppermute(pair_q, "ctx", z_swap(2))
+    crossed, far_q, *held = tied(crossed, far_q, *own_pieces, *filters)
+    own_pieces = [hidden] + held[:3]
+    toep_li, leave, enter, lane_rates = held[3:]
+    far_pieces = [lax.ppermute(crossed, "mp", x_shift(d)) for d in (1, 2, 3)]
+    line_q = jnp.concatenate([pair_q, far_q], axis=0)
+    up_q = lax.ppermute(line_q, "ctx", y_shift(1))
+    down_q = lax.ppermute(line_q, "ctx", y_shift(3))
+    up_q, down_q, line_q, *far_pieces = tied(up_q, down_q, line_q, *far_pieces)
+    over_q = lax.ppermute(line_q, "ctx", y_shift(2))
+    swapped_q = [lax.ppermute(piece, "ctx", CORE_SWAP) for piece in (line_q, up_q, down_q)]
+    pieces = packed(own_pieces + [crossed] + far_pieces)
+    pieces, line_x, up_x, down_x = tied(pieces, *swapped_q)
+    fresh_k, fresh_v = project(where, pieces, [weights_kv], GATHERED, 2)
     halo_kv = lax.ppermute(
         jnp.concatenate([fresh_k[ROWS - 16 :], fresh_v[ROWS - 16 :]], axis=0), "ctx", forward
     )
     product, load = li_gate(fresh_k, fresh_v, halo_kv, featurizer_li, enter)
+    load, over_q = tied(load, over_q)
     other_load = lax.ppermute(load, "ctx", CORE_SWAP)
+    over_x = lax.ppermute(over_q, "ctx", CORE_SWAP)
     chip = chip_state(where, load, other_load, lane_rates)
     before = [lax.ppermute(chip, "ctx", z_shift(s)) for s in (1, 2, 3)]
-    (fresh_q,) = project(where, pieces, weights, (0, 1), (0,))
+    weights_q = [line_q, up_q, over_q, down_q, line_x, up_x, over_x, down_x]
+    (fresh_q,) = project(where, pieces, weights_q, PERMUTED, 1)
     conv = li_inner(product, toep_li)
     *before, fresh_q, conv = tied(*before, fresh_q, conv)
     halo_q = lax.ppermute(fresh_q[ROWS - 16 :], "ctx", forward)
@@ -625,7 +664,7 @@
         where, conv, fresh_q, halo_q, featurizer_li, leave, lane_rates,
         line_carry, other_load, above, out_li,
     )
-    return sum_shares(where, gated_two, other_two, out_li, hidden)
+    return sum_shares(where, gated_two, other_two, out_li, hidden)[0]
 
 
 def solution(mesh):

time: 222 us -> 246 us (1.11)
  starting transfers between devices: 70.2 us -> 101 us
  waiting for transfers between devices: 93.2 us -> 78.3 us
  Pallas kernels: 31 us -> 35.9 us
  local copies, waits for them, and re-layouts: 11.2 us -> 14.6 us
    ppermute x7 -> x17, starting transfers between devices: 11.1 us -> 34.8 us  [the longest x3 9.04 us: body(): own_pieces = [lax.ppermute(hidden, 'mp', x_shift(d)) for d in (1, 2, 3)]]
    all_gather x1, waiting for transfers between devices: 24.1 us -> 4.42 us  [body(): lax.all_gather(moved_kv, 'ctx', axis_index_groups=[GATHER_ORDER])]
    ppermute x7 -> x17, waiting for transfers between devices: 19.1 us -> 35.6 us  [the longest x1 15.4 us: body(): far_q = lax.ppermute(pair_q, 'ctx', z_swap(2))]
    ppermute x1, waiting for transfers between devices: 6.18 us -> 0.01 us  [body(): crossed = lax.ppermute(hidden, 'mp', H_SWAP)]
    ppermute x3, starting transfers between devices: 8.92 us -> 14.8 us  [body(): above.append(lax.ppermute(line_total, 'ctx', pairs))]
    ppermute x3, starting transfers between devices: 5.47 us -> 10.4 us  [body(): before = [lax.ppermute(chip, 'ctx', z_shift(s)) for s in (1, 2, 3)]]
    ppermute x6, starting transfers between devices: 15.5 us -> 11 us  [sum_shares(): got = [lax.ppermute(other[d], 'mp', x_shift(d)) for d in (1, 3, 2)]]
    ppermute x6, waiting for transfers between devices: 16.9 us -> 12.9 us  [sum_shares(): got = [lax.ppermute(other[d], 'mp', x_shift(d)) for d in (1, 3, 2)]]
  transfers between devices with their start and end apart: 33 -> 43, of which waited for: 16 -> 19; matrix products, arithmetic and copies ran while one was open for 1% -> 1% of each run, Pallas kernels for 9% -> 12%
where the time goes in v3:
time: 246 us; the launch traced here: 245 us
  starting transfers between devices  101 us (41%)
  waiting for transfers between devices  78.3 us (32%)
  Pallas kernels  35.9 us (15%)
  local copies, waits for them, and re-layouts  14.6 us (6%)
  between operations  14 us (6%)
    ppermute x2, waiting for transfers between devices, sum_shares(): crossed = lax.ppermute(total_other, 'mp', H_SWAP)  19.8 us
    ppermute x1, waiting for transfers between devices, body(): far_q = lax.ppermute(pair_q, 'ctx', z_swap(2))  15.4 us
    ppermute x3, starting transfers between devices, body(): above.append(lax.ppermute(line_total, 'ctx', pairs))  14.8 us
    ppermute x6, waiting for transfers between devices, sum_shares(): got = [lax.ppermute(other[d], 'mp', x_shift(d)) for d in (1, 3, 2)]  12.9 us
    unnamed x55, local copies, waits for them, and re-layouts  12.6 us
    ppermute x2, starting transfers between devices, sum_shares(): crossed = lax.ppermute(total_other, 'mp', H_SWAP)  12.5 us
    ppermute x6, starting transfers between devices, sum_shares(): got = [lax.ppermute(other[d], 'mp', x_shift(d)) for d in (1, 3, 2)]  11 us
    ppermute x6, starting transfers between devices, sum_shares(): got_mine = [lax.ppermute(mine[d], 'mp', x_shift(d)) for d in (1, 3, 2)]  10.8 us
  transfers between devices with their start and end apart: 43, of which 19 were waited for; matrix products, arithmetic and copies ran while one was open for 1% of the time, Pallas kernels for 12%

profile of v3, /device:TPU:2, one launch (start us, length us, event | category | flops | bytes accessed | tf_op | source)
XLA Modules:
  0.0 244.9 jit_solution(1623748982049660645)
XLA Ops:
  24.2 5.2 %mr_op.1 = (bf16[256,512]{1,0:T(8,128)(2,1)S(1)}, bf16[256,512]{1,0:T(8,128)(2,1)S(1)}, bf16[256,512]{1,0:T(8,128)(2,1)S(1)}, bf16[256,512]{1,0:T(8,128)(2,1)S(1)}, bf16[256,512]{1,0:T(8,128)(2,1)S(1)}) custom-call(s32[5]{0:T(128)S(1)} %stack.32.where_ref, bf16[256,512]{1,0:T(8,128)(2,1)S(1)} %get-tuple-element.84.q_ref, ...), custom_call_target="tpu_custom_call" | custom-call | tf_op jit(solution)/shard_map/mr_op/pallas_call | solution.py:277
  30.2 3.4 %collective-permute-start.2 = (bf16[256,512]{1,0:T(8,128)(2,1)S(1)}, bf16[256,512]{1,0:T(8,128)(2,1)S(1)}, u32[]{:S(2)}, u32[]{:S(2)}) collective-permute-start(bf16[256,512]{1,0:T(8,128)(2,1)S(1)} %get-tuple-element.95), channel_id=1, source_target_pairs={{0,2},{1,3},{2,4},{3,5},{4,6},{5,7},{6,0},{7,1},{8,10},{9,11},{10,... | collective-permute-start | bytes 786440 | tf_op jit(solution)/shard_map/ppermute | solution.py:578
  45.4 6.6 %collective-permute-done.5 = bf16[1,512,128]{2,1,0:T(8,128)(2,1)S(1)} collective-permute-done((bf16[1,512,128]{2,1,0:T(8,128)(2,1)S(1)}, bf16[1,512,128]{2,1,0:T(8,128)(2,1)S(1)}, u32[]{:S(2)}, u32[]{:S(2)}) %collective-permute-start.5) | collective-permute-done | bytes 131104 | tf_op jit(solution)/shard_map/ppermute | solution.py:617
  52.1 7.8 %collective-permute-start.6 = (bf16[256,512]{1,0:T(8,128)(2,1)S(1)}, bf16[256,512]{1,0:T(8,128)(2,1)S(1)}, u32[]{:S(2)}, u32[]{:S(2)}) collective-permute-start(bf16[256,512]{1,0:T(8,128)(2,1)S(1)} %add_convert_fusion.3), channel_id=1, source_target_pairs={{0,1},{1,0},{2,3},{3,2},{4,5},{5,4},{6,7},{7,6},{8,9},{9,8},{10,11... | collective-permute-start | bytes 786440 | tf_op jit(solution)/shard_map/ppermute | solution.py:588
  59.8 3.6 %collective-permute-start.7 = (bf16[256,512]{1,0:T(8,128)(2,1)S(1)}, bf16[256,512]{1,0:T(8,128)(2,1)S(1)}, u32[]{:S(2)}, u32[]{:S(2)}) collective-permute-start(bf16[256,512]{1,0:T(8,128)(2,1)S(1)} %get-tuple-element.106), channel_id=1, source_target_pairs={{0,2},{1,3},{2,4},{3,5},{4,6},{5,7},{6,0},{7,1},{8,10},{9,11},{10,... | collective-permute-start | bytes 786440 | tf_op jit(solution)/shard_map/ppermute | solution.py:589
  67.5 9.7 %collective-permute-done.6 = bf16[256,512]{1,0:T(8,128)(2,1)S(1)} collective-permute-done((bf16[256,512]{1,0:T(8,128)(2,1)S(1)}, bf16[256,512]{1,0:T(8,128)(2,1)S(1)}, u32[]{:S(2)}, u32[]{:S(2)}) %collective-permute-start.6) | collective-permute-done | bytes 262176 | tf_op jit(solution)/shard_map/ppermute | solution.py:588
  78.8 3.3 %collective-permute-done.10 = bf16[1,512,128]{2,1,0:T(8,128)(2,1)S(1)} collective-permute-done((bf16[1,512,128]{2,1,0:T(8,128)(2,1)S(1)}, bf16[1,512,128]{2,1,0:T(8,128)(2,1)S(1)}, u32[]{:S(2)}, u32[]{:S(2)}) %collective-permute-start.10) | collective-permute-done | bytes 131104 | tf_op jit(solution)/shard_map/ppermute | solution.py:619
  84.0 5.5 %collective-permute-start.13 = (bf16[256,512]{1,0:T(8,128)(2,1)S(1)}, bf16[256,512]{1,0:T(8,128)(2,1)S(1)}, u32[]{:S(2)}, u32[]{:S(2)}) collective-permute-start(bf16[256,512]{1,0:T(8,128)(2,1)S(1)} %add_convert_fusion.2.refs_0_), channel_id=1, source_target_pairs={{0,2},{1,3},{2,4},{3,5},{4,6},{5,7},{6,0},{7,1},{8,10},{9,11},{10,... | collective-permute-start | bytes 786440 | tf_op jit(solution)/shard_map/ppermute | solution.py:624
  93.0 3.8 %prep.1 = (bf16[4096,256]{1,0:T(8,128)(2,1)S(1)}, f32[256,512]{1,0:T(8,128)S(1)}, f32[256,512]{1,0:T(8,128)S(1)}, f32[16,512]{1,0:T(8,128)S(1)}) custom-call(f32[16,32]{1,0:T(8,128)S(1)} %bitcast.10, f32[16,32]{1,0:T(8,128)S(1)} %bitcast.11), custom_call_target="tpu_custom_call" | custom-call | tf_op jit(solution)/shard_map/prep/pallas_call | solution.py:166
  98.3 15.4 %collective-permute-done.12 = bf16[2,1,512,128]{3,2,1,0:T(8,128)(2,1)S(1)} collective-permute-done((bf16[2,1,512,128]{3,2,1,0:T(8,128)(2,1)S(1)}, bf16[2,1,512,128]{3,2,1,0:T(8,128)(2,1)S(1)}, u32[]{:S(2)}, u32[]{:S(2)}) %collective-permute-start.12) | collective-permute-done | bytes 262176 | tf_op jit(solution)/shard_map/ppermute | solution.py:626
  117.1 3.4 %collective-permute-start.18 = (bf16[256,512]{1,0:T(8,128)(2,1)S(1)}, bf16[256,512]{1,0:T(8,128)(2,1)S(1)}, u32[]{:S(2)}, u32[]{:S(2)}) collective-permute-start(bf16[256,512]{1,0:T(8,128)(2,1)S(1)} %collective-permute-done.11.refs_4_), channel_id=1, source_target_pairs={{0,2},{1,3},{2,4},{3,5},{4,6},{5,7},{6,0},{7,1},{8,10},{9,11},{10,... | collective-permute-start | bytes 786440 | tf_op jit(solution)/shard_map/ppermute | solution.py:630
  120.5 4.3 %collective-permute-start.19 = (bf16[256,512]{1,0:T(8,128)(2,1)S(1)}, bf16[256,512]{1,0:T(8,128)(2,1)S(1)}, u32[]{:S(2)}, u32[]{:S(2)}) collective-permute-start(bf16[256,512]{1,0:T(8,128)(2,1)S(1)} %collective-permute-done.11.refs_4_), channel_id=1, source_target_pairs={{0,4},{1,5},{2,6},{3,7},{4,0},{5,1},{6,2},{7,3},{8,12},{9,13},{10,... | collective-permute-start | bytes 786440 | tf_op jit(solution)/shard_map/ppermute | solution.py:630
  124.8 5.0 %collective-permute-done.18.refs_5_ = bf16[256,512]{1,0:T(8,128)(2,1)S(1)} collective-permute-done((bf16[256,512]{1,0:T(8,128)(2,1)S(1)}, bf16[256,512]{1,0:T(8,128)(2,1)S(1)}, u32[]{:S(2)}, u32[]{:S(2)}) %collective-permute-start.18) | collective-permute-done | bytes 262176 | tf_op jit(solution)/shard_map/ppermute | solution.py:630
  135.6 6.3 %collective-permute-start.25 = (bf16[4,1,512,128]{3,2,1,0:T(8,128)(2,1)S(1)}, bf16[4,1,512,128]{3,2,1,0:T(8,128)(2,1)}, u32[]{:S(2)}, u32[]{:S(2)}) collective-permute-start(bf16[4,1,512,128]{3,2,1,0:T(8,128)(2,1)S(1)} %pad_maximum_fusion.refs_1_), channel_id=1, source_target_pairs={{0,128},{8,136},{16,144},{24,152},{32,160},{40,168},{48,176},{56,1... | collective-permute-start | bytes 1572872 | tf_op jit(solution)/shard_map/ppermute | solution.py:635
  144.6 4.4 %all-gather.3.cloned.1.call-done = bf16[64,512,128]{2,1,0:T(8,128)(2,1)} async-done(((bf16[2,512,128]{2,1,0:T(8,128)(2,1)}), bf16[64,512,128]{2,1,0:T(8,128)(2,1)}) %all-gather.3.cloned.1.call-update) | async-done | bytes 8388624 | tf_op jit(solution)/shard_map/all_gather | solution.py:616
  149.1 6.2 %project.2 = (bf16[256,512]{1,0:T(8,128)(2,1)S(1)}, bf16[256,512]{1,0:T(8,128)(2,1)S(1)}) custom-call(s32[5]{0:T(128)S(1)} %stack.32.where_ref, bf16[8,256,512]{2,1,0:T(8,128)(2,1)S(1)} %packed.1.refs_0_, bf16[32,2,512,128]{3,2,1,0:T(8,128)(2,1)} %bitcast.12), custom_call_target="tpu_custom_call" | custom-call | tf_op jit(solution)/shard_map/project/pallas_call | solution.py:352
  164.1 7.9 %collective-permute-start.28 = (f32[16,512]{1,0:T(8,128)S(1)}, f32[16,512]{1,0:T(8,128)S(1)}, u32[]{:S(2)}, u32[]{:S(2)}) collective-permute-start(f32[16,512]{1,0:T(8,128)S(1)} %chip_state.1.c0), channel_id=1, source_target_pairs={{0,32},{8,40},{16,48},{24,56},{32,0},{40,8},{48,16},{56,24},{64,96... | collective-permute-start | bytes 98312 | tf_op jit(solution)/shard_map/ppermute | solution.py:648
  173.7 4.3 %project.3.q_ref = bf16[256,512]{1,0:T(8,128)(2,1)S(1)} custom-call(s32[5]{0:T(128)S(1)} %stack.32.where_ref, bf16[8,256,512]{2,1,0:T(8,128)(2,1)} %copy-done, bf16[4,1,512,128]{3,2,1,0:T(8,128)(2,1)S(1)} %pad_maximum_fusion.refs_1_, bf16[4,1,512,128]{3,2,1,0:T(8,128)(2,1)S(1)} %copy-done.7, bf16[4,1,512,128]{3,2,1,0:T(8,128)(2,1)} %collective-permute-done.25.refs_3_, ...), custom_call_target="tpu_custom_call" | custom-call | tf_op jit(solution)/shard_map/project/pallas_call | solution.py:352
  178.6 7.4 %collective-permute-start.32 = (f32[16,512]{1,0:T(8,128)S(1)}, f32[16,512]{1,0:T(8,128)S(1)}, u32[]{:S(2)}, u32[]{:S(2)}) collective-permute-start(f32[16,512]{1,0:T(8,128)S(1)} %get-tuple-element.148), channel_id=1, source_target_pairs={{0,64},{8,72},{16,80},{24,88},{32,96},{40,104},{48,112},{56,120},{... | collective-permute-start | bytes 98312 | tf_op jit(solution)/shard_map/ppermute | solution.py:661
  186.0 6.1 %collective-permute-start.33 = (f32[16,512]{1,0:T(8,128)S(1)}, f32[16,512]{1,0:T(8,128)S(1)}, u32[]{:S(2)}, u32[]{:S(2)}) collective-permute-start(f32[16,512]{1,0:T(8,128)S(1)} %get-tuple-element.148), channel_id=1, source_target_pairs={{0,128},{8,136},{16,144},{24,152},{32,160},{40,168},{48,176},{56,1... | collective-permute-start | bytes 98312 | tf_op jit(solution)/shard_map/ppermute | solution.py:661
  195.6 4.2 %li_outer.1 = (bf16[256,512]{1,0:T(8,128)(2,1)S(1)}, bf16[256,512]{1,0:T(8,128)(2,1)S(1)}, bf16[256,512]{1,0:T(8,128)(2,1)S(1)}, bf16[256,512]{1,0:T(8,128)(2,1)S(1)}, bf16[256,512]{1,0:T(8,128)(2,1)S(1)}) custom-call(s32[5]{0:T(128)S(1)} %stack.32.where_ref, f32[256,512]{1,0:T(8,128)} %copy-done.4, bf16[256,512]{1,0:T(8,128)(2,1)S(1)} %project.3.q_ref, ...), custom_call_target="tpu_custom_call" | custom-call | tf_op jit(solution)/shard_map/li_outer/pallas_call | solution.py:500
  210.7 7.1 %collective-permute-done.37 = bf16[256,512]{1,0:T(8,128)(2,1)S(1)} collective-permute-done((bf16[256,512]{1,0:T(8,128)(2,1)S(1)}, bf16[256,512]{1,0:T(8,128)(2,1)S(1)}, u32[]{:S(2)}, u32[]{:S(2)}) %collective-permute-start.37) | collective-permute-done | bytes 262176 | tf_op jit(solution)/shard_map/ppermute | solution.py:578
  217.9 4.7 %collective-permute-start.38 = (bf16[256,512]{1,0:T(8,128)(2,1)S(1)}, bf16[256,512]{1,0:T(8,128)(2,1)S(1)}, u32[]{:S(2)}, u32[]{:S(2)}) collective-permute-start(bf16[256,512]{1,0:T(8,128)(2,1)S(1)} %add_convert_fusion.1), channel_id=1, source_target_pairs={{0,1},{1,0},{2,3},{3,2},{4,5},{5,4},{6,7},{7,6},{8,9},{9,8},{10,11... | collective-permute-start | bytes 786440 | tf_op jit(solution)/shard_map/ppermute | solution.py:588
  225.8 10.1 %collective-permute-done.38 = bf16[256,512]{1,0:T(8,128)(2,1)S(1)} collective-permute-done((bf16[256,512]{1,0:T(8,128)(2,1)S(1)}, bf16[256,512]{1,0:T(8,128)(2,1)S(1)}, u32[]{:S(2)}, u32[]{:S(2)}) %collective-permute-start.38) | collective-permute-done | bytes 262176 | tf_op jit(solution)/shard_map/ppermute | solution.py:588
  (147 shorter events, 85.0 us)
Async XLA Ops:
  6.5 142.5 %all-gather.3.cloned.1.call-start = ((), (), s32[]{:S(2)}) async-start(), calls=%async_computation | async-start | bytes 8650752 | tf_op jit(solution)/shard_map/all_gather | solution.py:616
  13.3 16.1 %collective-permute-start.1 = (bf16[2,512,128]{2,1,0:T(8,128)(2,1)S(1)}, bf16[2,512,128]{2,1,0:T(8,128)(2,1)S(1)}, u32[]{:S(2)}, u32[]{:S(2)}) collective-permute-start(bf16[2,512,128]{2,1,0:T(8,128)(2,1)S(1)} %slice.16), channel_id=1, source_target_pairs={{0,16},{1,48},{2,80},{3,112},{4,144},{5,176},{6,208},{7,240},{8,24... | collective-permute-start | bytes 786440 | tf_op jit(solution)/shard_map/ppermute | solution.py:607
  38.8 13.3 %collective-permute-start.5 = (bf16[1,512,128]{2,1,0:T(8,128)(2,1)S(1)}, bf16[1,512,128]{2,1,0:T(8,128)(2,1)S(1)}, u32[]{:S(2)}, u32[]{:S(2)}) collective-permute-start(bf16[1,512,128]{2,1,0:T(8,128)(2,1)S(1)} %slice.15), channel_id=1, source_target_pairs={{0,16},{1,48},{2,80},{3,112},{4,144},{5,176},{6,208},{7,240},{8,24... | collective-permute-start | bytes 393224 | tf_op jit(solution)/shard_map/ppermute | solution.py:617
  52.1 25.1 %collective-permute-start.6 = (bf16[256,512]{1,0:T(8,128)(2,1)S(1)}, bf16[256,512]{1,0:T(8,128)(2,1)S(1)}, u32[]{:S(2)}, u32[]{:S(2)}) collective-permute-start(bf16[256,512]{1,0:T(8,128)(2,1)S(1)} %add_convert_fusion.3), channel_id=1, source_target_pairs={{0,1},{1,0},{2,3},{3,2},{4,5},{5,4},{6,7},{7,6},{8,9},{9,8},{10,11... | collective-permute-start | bytes 786440 | tf_op jit(solution)/shard_map/ppermute | solution.py:588
  59.8 17.4 %collective-permute-start.7 = (bf16[256,512]{1,0:T(8,128)(2,1)S(1)}, bf16[256,512]{1,0:T(8,128)(2,1)S(1)}, u32[]{:S(2)}, u32[]{:S(2)}) collective-permute-start(bf16[256,512]{1,0:T(8,128)(2,1)S(1)} %get-tuple-element.106), channel_id=1, source_target_pairs={{0,2},{1,3},{2,4},{3,5},{4,6},{5,7},{6,0},{7,1},{8,10},{9,11},{10,... | collective-permute-start | bytes 786440 | tf_op jit(solution)/shard_map/ppermute | solution.py:589
  63.4 13.9 %collective-permute-start.8 = (bf16[256,512]{1,0:T(8,128)(2,1)S(1)}, bf16[256,512]{1,0:T(8,128)(2,1)S(1)}, u32[]{:S(2)}, u32[]{:S(2)}) collective-permute-start(bf16[256,512]{1,0:T(8,128)(2,1)S(1)} %get-tuple-element.107), channel_id=1, source_target_pairs={{0,6},{1,7},{2,0},{3,1},{4,2},{5,3},{6,4},{7,5},{8,14},{9,15},{10,... | collective-permute-start | bytes 786440 | tf_op jit(solution)/shard_map/ppermute | solution.py:589
  65.5 13.2 %collective-permute-start.9 = (bf16[256,512]{1,0:T(8,128)(2,1)S(1)}, bf16[256,512]{1,0:T(8,128)(2,1)S(1)}, u32[]{:S(2)}, u32[]{:S(2)}) collective-permute-start(bf16[256,512]{1,0:T(8,128)(2,1)S(1)} %get-tuple-element.108), channel_id=1, source_target_pairs={{0,4},{1,5},{2,6},{3,7},{4,0},{5,1},{6,2},{7,3},{8,12},{9,13},{10,... | collective-permute-start | bytes 786440 | tf_op jit(solution)/shard_map/ppermute | solution.py:589
  67.5 14.6 %collective-permute-start.10 = (bf16[1,512,128]{2,1,0:T(8,128)(2,1)S(1)}, bf16[1,512,128]{2,1,0:T(8,128)(2,1)S(1)}, u32[]{:S(2)}, u32[]{:S(2)}) collective-permute-start(bf16[1,512,128]{2,1,0:T(8,128)(2,1)S(1)} %collective-permute-done.5), channel_id=1, source_target_pairs={{0,16},{8,24},{16,0},{24,8},{32,48},{40,56},{48,32},{56,40},{64,80... | collective-permute-start | bytes 393224 | tf_op jit(solution)/shard_map/ppermute | solution.py:619
  82.2 31.6 %collective-permute-start.12 = (bf16[2,1,512,128]{3,2,1,0:T(8,128)(2,1)S(1)}, bf16[2,1,512,128]{3,2,1,0:T(8,128)(2,1)S(1)}, u32[]{:S(2)}, u32[]{:S(2)}) collective-permute-start(bf16[2,1,512,128]{3,2,1,0:T(8,128)(2,1)S(1)} %pad_maximum_fusion.1), channel_id=1, source_target_pairs={{0,32},{8,40},{16,48},{24,56},{32,0},{40,8},{48,16},{56,24},{64,96... | collective-permute-start | bytes 786440 | tf_op jit(solution)/shard_map/ppermute | solution.py:626
  83.2 30.6 %collective-permute-start.11 = (bf16[256,512]{1,0:T(8,128)(2,1)S(1)}, bf16[256,512]{1,0:T(8,128)(2,1)S(1)}, u32[]{:S(2)}, u32[]{:S(2)}) collective-permute-start(bf16[256,512]{1,0:T(8,128)(2,1)S(1)} %add_convert_fusion.2.refs_0_), channel_id=1, source_target_pairs={{0,1},{1,0},{2,3},{3,2},{4,5},{5,4},{6,7},{7,6},{8,9},{9,8},{10,11... | collective-permute-start | bytes 786440 | tf_op jit(solution)/shard_map/ppermute | solution.py:623
  84.0 29.8 %collective-permute-start.13 = (bf16[256,512]{1,0:T(8,128)(2,1)S(1)}, bf16[256,512]{1,0:T(8,128)(2,1)S(1)}, u32[]{:S(2)}, u32[]{:S(2)}) collective-permute-start(bf16[256,512]{1,0:T(8,128)(2,1)S(1)} %add_convert_fusion.2.refs_0_), channel_id=1, source_target_pairs={{0,2},{1,3},{2,4},{3,5},{4,6},{5,7},{6,0},{7,1},{8,10},{9,11},{10,... | collective-permute-start | bytes 786440 | tf_op jit(solution)/shard_map/ppermute | solution.py:624
  89.5 24.2 %collective-permute-start.14 = (bf16[256,512]{1,0:T(8,128)(2,1)S(1)}, bf16[256,512]{1,0:T(8,128)(2,1)S(1)}, u32[]{:S(2)}, u32[]{:S(2)}) collective-permute-start(bf16[256,512]{1,0:T(8,128)(2,1)S(1)} %add_convert_fusion.2.refs_0_), channel_id=1, source_target_pairs={{0,4},{1,5},{2,6},{3,7},{4,0},{5,1},{6,2},{7,3},{8,12},{9,13},{10,... | collective-permute-start | bytes 786440 | tf_op jit(solution)/shard_map/ppermute | solution.py:624
  91.3 22.4 %collective-permute-start.15 = (bf16[256,512]{1,0:T(8,128)(2,1)S(1)}, bf16[256,512]{1,0:T(8,128)(2,1)S(1)}, u32[]{:S(2)}, u32[]{:S(2)}) collective-permute-start(bf16[256,512]{1,0:T(8,128)(2,1)S(1)} %add_convert_fusion.2.refs_0_), channel_id=1, source_target_pairs={{0,6},{1,7},{2,0},{3,1},{4,2},{5,3},{6,4},{7,5},{8,14},{9,15},{10,... | collective-permute-start | bytes 786440 | tf_op jit(solution)/shard_map/ppermute | solution.py:624
  113.8 21.2 %collective-permute-start.16 = (bf16[4,1,512,128]{3,2,1,0:T(8,128)(2,1)S(1)}, bf16[4,1,512,128]{3,2,1,0:T(8,128)(2,1)S(1)}, u32[]{:S(2)}, u32[]{:S(2)}) collective-permute-start(bf16[4,1,512,128]{3,2,1,0:T(8,128)(2,1)S(1)} %pad_maximum_fusion.refs_1_), channel_id=1, source_target_pairs={{0,64},{8,72},{16,80},{24,88},{32,96},{40,104},{48,112},{56,120},{... | collective-permute-start | bytes 1572872 | tf_op jit(solution)/shard_map/ppermute | solution.py:632
  113.9 21.1 %collective-permute-start.17 = (bf16[4,1,512,128]{3,2,1,0:T(8,128)(2,1)S(1)}, bf16[4,1,512,128]{3,2,1,0:T(8,128)(2,1)S(1)}, u32[]{:S(2)}, u32[]{:S(2)}) collective-permute-start(bf16[4,1,512,128]{3,2,1,0:T(8,128)(2,1)S(1)} %pad_maximum_fusion.refs_1_), channel_id=1, source_target_pairs={{0,192},{8,200},{16,208},{24,216},{32,224},{40,232},{48,240},{56,2... | collective-permute-start | bytes 1572872 | tf_op jit(solution)/shard_map/ppermute | solution.py:633
  135.6 23.4 %collective-permute-start.25 = (bf16[4,1,512,128]{3,2,1,0:T(8,128)(2,1)S(1)}, bf16[4,1,512,128]{3,2,1,0:T(8,128)(2,1)}, u32[]{:S(2)}, u32[]{:S(2)}) collective-permute-start(bf16[4,1,512,128]{3,2,1,0:T(8,128)(2,1)S(1)} %pad_maximum_fusion.refs_1_), channel_id=1, source_target_pairs={{0,128},{8,136},{16,144},{24,152},{32,160},{40,168},{48,176},{56,1... | collective-permute-start | bytes 1572872 | tf_op jit(solution)/shard_map/ppermute | solution.py:635
  159.1 14.6 %collective-permute-start.30 = (bf16[4,1,512,128]{3,2,1,0:T(8,128)(2,1)}, bf16[4,1,512,128]{3,2,1,0:T(8,128)(2,1)S(1)}, u32[]{:S(2)}, u32[]{:S(2)}) collective-permute-start(bf16[4,1,512,128]{3,2,1,0:T(8,128)(2,1)} %collective-permute-done.25.refs_3_), channel_id=1, source_target_pairs={{0,8},{8,0},{16,24},{24,16},{32,40},{40,32},{48,56},{56,48},{64,72... | collective-permute-start | bytes 1572872 | tf_op jit(solution)/shard_map/ppermute | solution.py:646
  161.7 16.3 %collective-permute-start.27 = (f32[16,512]{1,0:T(8,128)S(1)}, f32[16,512]{1,0:T(8,128)S(1)}, u32[]{:S(2)}, u32[]{:S(2)}) collective-permute-start(f32[16,512]{1,0:T(8,128)S(1)} %chip_state.1.c0), channel_id=1, source_target_pairs={{0,16},{8,24},{16,32},{24,40},{32,48},{40,56},{48,0},{56,8},{64,80... | collective-permute-start | bytes 98312 | tf_op jit(solution)/shard_map/ppermute | solution.py:648
  164.1 13.8 %collective-permute-start.28 = (f32[16,512]{1,0:T(8,128)S(1)}, f32[16,512]{1,0:T(8,128)S(1)}, u32[]{:S(2)}, u32[]{:S(2)}) collective-permute-start(f32[16,512]{1,0:T(8,128)S(1)} %chip_state.1.c0), channel_id=1, source_target_pairs={{0,32},{8,40},{16,48},{24,56},{32,0},{40,8},{48,16},{56,24},{64,96... | collective-permute-start | bytes 98312 | tf_op jit(solution)/shard_map/ppermute | solution.py:648
  178.6 17.0 %collective-permute-start.32 = (f32[16,512]{1,0:T(8,128)S(1)}, f32[16,512]{1,0:T(8,128)S(1)}, u32[]{:S(2)}, u32[]{:S(2)}) collective-permute-start(f32[16,512]{1,0:T(8,128)S(1)} %get-tuple-element.148), channel_id=1, source_target_pairs={{0,64},{8,72},{16,80},{24,88},{32,96},{40,104},{48,112},{56,120},{... | collective-permute-start | bytes 98312 | tf_op jit(solution)/shard_map/ppermute | solution.py:661
  201.9 15.9 %collective-permute-start.37 = (bf16[256,512]{1,0:T(8,128)(2,1)S(1)}, bf16[256,512]{1,0:T(8,128)(2,1)S(1)}, u32[]{:S(2)}, u32[]{:S(2)}) collective-permute-start(bf16[256,512]{1,0:T(8,128)(2,1)S(1)} %get-tuple-element.152), channel_id=1, source_target_pairs={{0,4},{1,5},{2,6},{3,7},{4,0},{5,1},{6,2},{7,3},{8,12},{9,13},{10,... | collective-permute-start | bytes 786440 | tf_op jit(solution)/shard_map/ppermute | solution.py:578
  217.9 18.0 %collective-permute-start.38 = (bf16[256,512]{1,0:T(8,128)(2,1)S(1)}, bf16[256,512]{1,0:T(8,128)(2,1)S(1)}, u32[]{:S(2)}, u32[]{:S(2)}) collective-permute-start(bf16[256,512]{1,0:T(8,128)(2,1)S(1)} %add_convert_fusion.1), channel_id=1, source_target_pairs={{0,1},{1,0},{2,3},{3,2},{4,5},{5,4},{6,7},{7,6},{8,9},{9,8},{10,11... | collective-permute-start | bytes 786440 | tf_op jit(solution)/shard_map/ppermute | solution.py:588
  222.7 13.3 %collective-permute-start.39 = (bf16[256,512]{1,0:T(8,128)(2,1)S(1)}, bf16[256,512]{1,0:T(8,128)(2,1)S(1)}, u32[]{:S(2)}, u32[]{:S(2)}) collective-permute-start(bf16[256,512]{1,0:T(8,128)(2,1)S(1)} %get-tuple-element.160), channel_id=1, source_target_pairs={{0,2},{1,3},{2,4},{3,5},{4,6},{5,7},{6,0},{7,1},{8,10},{9,11},{10,... | collective-permute-start | bytes 786440 | tf_op jit(solution)/shard_map/ppermute | solution.py:589
  222.7 13.4 %collective-permute-start.40 = (bf16[256,512]{1,0:T(8,128)(2,1)S(1)}, bf16[256,512]{1,0:T(8,128)(2,1)S(1)}, u32[]{:S(2)}, u32[]{:S(2)}) collective-permute-start(bf16[256,512]{1,0:T(8,128)(2,1)S(1)} %get-tuple-element.161), channel_id=1, source_target_pairs={{0,6},{1,7},{2,0},{3,1},{4,2},{5,3},{6,4},{7,5},{8,14},{9,15},{10,... | collective-permute-start | bytes 786440 | tf_op jit(solution)/shard_map/ppermute | solution.py:589
  (46 other events, 528.3 us)
Sparse Core Ops, SparseCore 0:
  30.3 118.7 all-gather.2

commit v4 on v2

--- a/solution.py
+++ b/solution.py
@@ -16,7 +16,7 @@
 HALO = 144
 
 
-def params(mib=24):
+def params(mib=16):
     return pltpu.CompilerParams(vmem_limit_bytes=mib * 1024 * 1024)
 
 
@@ -242,7 +242,7 @@
         in_specs=[SMEM_SPEC] + vspecs(1) + hspecs(1),
         out_specs=vspecs(4),
         scratch_shapes=SHARE_SCRATCH,
-        compiler_params=params(48),
+        compiler_params=params(52),
         name="shares",
     )(where, y, weight)
 
@@ -284,76 +284,82 @@
             pltpu.VMEM((HALO + ROWS, LANES), F32),
             pltpu.VMEM((16 + ROWS, LANES), F32),
         ] + SHARE_SCRATCH,
-        compiler_params=params(48),
+        compiler_params=params(52),
         name="mr_op",
     )(where, q, k, v, halo, feat, toep, weight)
 
 
-def project_kernel(flips, slots, first, last, where_ref, *refs):
-    n = len(flips) * 4
+EXT = 16 + ROWS
+EXT_PIECE = jax.ShapeDtypeStruct((EXT, WIDTH), BF16)
+
+
+def pack_kernel(*refs):
+    for i in range(8):
+        refs[8][i] = refs[i][...]
+
+
+def packed(pieces):
+    return pl.pallas_call(
+        pack_kernel,
+        out_shape=jax.ShapeDtypeStruct((8, EXT, WIDTH), BF16),
+        in_specs=vspecs(8),
+        out_specs=pl.BlockSpec(memory_space=pltpu.VMEM),
+        compiler_params=params(),
+        name="packed",
+    )(*pieces)
+
+
+def project_kernel(slots, where_ref, hidden_ref, w_ref, *refs):
     count = len(slots)
-    hidden_refs = refs[:n]
-    w_ref = refs[n]
-    pos = n + 1
-    acc_refs = ()
-    if not first:
-        acc_refs = refs[pos : pos + count]
-        pos += count
-    out_refs = refs[pos : pos + count]
-    wbuf, wsem = refs[pos + count :]
+    out_refs = refs[:count]
+    wbuf, wsem = refs[count:]
     x = where_ref[0]
-    wcopies = []
-    for i in range(n):
-        e, d = flips[i // 4], (0, 1, 3, 2)[i % 4]
+    copies = []
+    for i in range(8):
+        e, d = i // 4, i % 4
         src_y = lax.rem(x + 4 - d, 4)
         for b in range(4):
             odd = 1 - b // 2
             high = odd if e == 1 else 1 - odd
-            member = gathered_at(src_y, high * 2 + odd, b % 2)
             copy = pltpu.make_async_copy(
-                w_ref.at[member, pl.ds(slots[0], count)],
+                w_ref.at[gathered_at(src_y, high * 2 + odd, b % 2), pl.ds(slots[0], count)],
                 wbuf.at[i, :, :, pl.ds(b * LANES, LANES)],
                 wsem.at[i, b],
             )
             copy.start()
-            wcopies.append(copy)
+            copies.append(copy)
     sums = [None] * count
-    for i in range(n):
+    for i in range(8):
         for b in range(4):
-            wcopies[i * 4 + b].wait()
+            copies[i * 4 + b].wait()
         for j in range(count):
-            prod = jnp.dot(hidden_refs[i][...], wbuf[i, j], preferred_element_type=F32)
-            if i == 0:
-                sums[j] = prod if first else prod + acc_refs[j][...]
-            else:
-                sums[j] = sums[j] + prod
+            prod = jnp.dot(hidden_ref[i], wbuf[i, j], preferred_element_type=F32)
+            sums[j] = prod if i == 0 else sums[j] + prod
     for j in range(count):
-        out_refs[j][...] = sums[j].astype(BF16) if last else sums[j]
-
-
-def project(where, pieces, weights, flips, slots, acc=(), last=True):
-    n, count = len(pieces), len(slots)
-    return pl.pallas_call(
-        functools.partial(project_kernel, flips, slots, not acc, last),
-        out_shape=[jax.ShapeDtypeStruct((ROWS, WIDTH), BF16 if last else F32)] * count,
-        in_specs=[SMEM_SPEC] + vspecs(n) + hspecs(1) + vspecs(len(acc)),
+        out_refs[j][...] = sums[j].astype(BF16)
+
+
+def project(where, pieces, weights, slots):
+    count = len(slots)
+    return pl.pallas_call(
+        functools.partial(project_kernel, slots),
+        out_shape=[EXT_PIECE] * count,
+        in_specs=[SMEM_SPEC] + vspecs(1) + hspecs(1),
         out_specs=vspecs(count),
         scratch_shapes=[
-            pltpu.VMEM((n, count, WIDTH, WIDTH), BF16),
-            pltpu.SemaphoreType.DMA((n, 4)),
+            pltpu.VMEM((8, count, WIDTH, WIDTH), BF16),
+            pltpu.SemaphoreType.DMA((8, 4)),
         ],
         compiler_params=params(48),
         name="project",
-    )(where, *pieces, weights, *acc)
-
-
-def li_gate_kernel(k_ref, v_ref, halo_ref, feat_ref, enter_ref, z_ref, load_ref, kx, vx):
+    )(where, pieces, weights)
+
+
+def li_gate_kernel(k_ref, v_ref, feat_ref, enter_ref, z_ref, load_ref, kx, vx):
     for block in range(WIDTH // LANES):
         cols = slice(block * LANES, (block + 1) * LANES)
-        kx[0:16, :] = halo_ref[0:16, cols].astype(F32)
-        kx[16:, :] = k_ref[:, cols].astype(F32)
-        vx[0:16, :] = halo_ref[16:32, cols].astype(F32)
-        vx[16:, :] = v_ref[:, cols].astype(F32)
+        kx[...] = k_ref[:, cols].astype(F32)
+        vx[...] = v_ref[:, cols].astype(F32)
         kf = feature(kx, 16, ROWS, feat_ref[1, :, cols])
         vf = feature(vx, 16, ROWS, feat_ref[2, :, cols])
         z = (kf * vf).astype(BF16)
@@ -369,16 +375,16 @@
         load_ref[:, cols] = load
 
 
-def li_gate(k, v, halo, feat, enter):
+def li_gate(k, v, feat, enter):
     return pl.pallas_call(
         li_gate_kernel,
         out_shape=[PIECE, STATE],
-        in_specs=vspecs(5),
+        in_specs=vspecs(4),
         out_specs=vspecs(2),
         scratch_shapes=[pltpu.VMEM((16 + ROWS, LANES), F32)] * 2,
         compiler_params=params(),
         name="li_gate",
-    )(k, v, halo, feat, enter)
+    )(k, v, feat, enter)
 
 
 STATE = jax.ShapeDtypeStruct((GS, WIDTH), F32)
@@ -452,7 +458,7 @@
 
 
 def li_outer_kernel(
-    where_ref, conv_ref, q_ref, halo_ref, feat_ref, leave_ref, rates_ref,
+    where_ref, conv_ref, q_ref, feat_ref, leave_ref, rates_ref,
     carry_ref, other_ref, y1_ref, y2_ref, y3_ref, w_ref,
     y_ref, o0, o1, o2, o3, qx, wbuf, sems,
 ):
@@ -466,8 +472,7 @@
     full = jnp.where(k == 0, chip, jnp.exp(-rates * (1.0 * ROWS)) * chip + other_ref[...])
     for block in range(WIDTH // LANES):
         cols = slice(block * LANES, (block + 1) * LANES)
-        qx[0:16, :] = halo_ref[:, cols].astype(F32)
-        qx[16:, :] = q_ref[:, cols].astype(F32)
+        qx[...] = q_ref[:, cols].astype(F32)
         qf = feature(qx, 16, ROWS, feat_ref[0, :, cols])
         state = full[:, cols]
         spread = jnp.concatenate(
@@ -480,16 +485,16 @@
     share_products(copies, y_ref, wbuf, (o0, o1, o2, o3))
 
 
-def li_outer(where, conv, q, halo, feat, leave, rates, carry, other, above, weight):
+def li_outer(where, conv, q, feat, leave, rates, carry, other, above, weight):
     return pl.pallas_call(
         li_outer_kernel,
         out_shape=[PIECE] * 5,
-        in_specs=[SMEM_SPEC] + vspecs(11) + hspecs(1),
+        in_specs=[SMEM_SPEC] + vspecs(10) + hspecs(1),
         out_specs=vspecs(5),
         scratch_shapes=[pltpu.VMEM((16 + ROWS, LANES), F32)] + SHARE_SCRATCH,
-        compiler_params=params(48),
+        compiler_params=params(52),
         name="li_outer",
-    )(where, conv, q, halo, feat, leave, rates, carry, other, *above, weight)
+    )(where, conv, q, feat, leave, rates, carry, other, *above, weight)
 
 
 def ctx_of(y, zl, k):
@@ -594,24 +599,22 @@
     hidden = sum_shares(where, gated_one, other_one, out_mr, residual)
     filters = prep(li_rates.T, li_residues.T)
 
-    crossed = lax.ppermute(hidden, "mp", H_SWAP)
-    own_pieces = [hidden] + [lax.ppermute(hidden, "mp", x_shift(d)) for d in (1, 3, 2)]
+    before_rows = lax.ppermute(hidden[ROWS - 16 :], "ctx", forward)
+    extended = jnp.concatenate([before_rows, hidden], axis=0)
+    crossed = lax.ppermute(extended, "mp", H_SWAP)
+    own_pieces = [extended] + [lax.ppermute(extended, "mp", x_shift(d)) for d in (1, 2, 3)]
     crossed, *filters = tied(crossed, *filters)
     toep_li, leave, enter, lane_rates = filters
-    far_pieces = [crossed] + [lax.ppermute(crossed, "mp", x_shift(d)) for d in (1, 3, 2)]
-    pieces = own_pieces + far_pieces
-    fresh_k, fresh_v = project(where, pieces, weights, (0, 1), (1, 2))
-    halo_kv = lax.ppermute(
-        jnp.concatenate([fresh_k[ROWS - 16 :], fresh_v[ROWS - 16 :]], axis=0), "ctx", forward
-    )
-    product, load = li_gate(fresh_k, fresh_v, halo_kv, featurizer_li, enter)
+    far_pieces = [crossed] + [lax.ppermute(crossed, "mp", x_shift(d)) for d in (1, 2, 3)]
+    pieces = packed(own_pieces + far_pieces)
+    fresh_k, fresh_v = project(where, pieces, weights, (1, 2))
+    product, load = li_gate(fresh_k, fresh_v, featurizer_li, enter)
     other_load = lax.ppermute(load, "ctx", CORE_SWAP)
     chip = chip_state(where, load, other_load, lane_rates)
     before = [lax.ppermute(chip, "ctx", z_shift(s)) for s in (1, 2, 3)]
-    (fresh_q,) = project(where, pieces, weights, (0, 1), (0,))
+    (fresh_q,) = project(where, pieces, weights, (0,))
     conv = li_inner(product, toep_li)
     *before, fresh_q, conv = tied(*before, fresh_q, conv)
-    halo_q = lax.ppermute(fresh_q[ROWS - 16 :], "ctx", forward)
     line_total, line_carry = line_state(where, [chip] + before, lane_rates)
     above = []
     for s in (1, 2, 3):
@@ -622,7 +625,7 @@
         above.append(lax.ppermute(line_total, "ctx", pairs))
 
     gated_two, *other_two = li_outer(
-        where, conv, fresh_q, halo_q, featurizer_li, leave, lane_rates,
+        where, conv, fresh_q, featurizer_li, leave, lane_rates,
         line_carry, other_load, above, out_li,
     )
     return sum_shares(where, gated_two, other_two, out_li, hidden)

time: 222 us -> 211 us (0.950)
  waiting for transfers between devices: 93.2 us -> 83.1 us
  Pallas kernels: 31 us -> 34.4 us
  starting transfers between devices: 70.2 us -> 66.9 us
    all_gather x1, waiting for transfers between devices: 24.1 us -> 17.9 us  [body(): weights = lax.all_gather(moved, 'ctx', axis_index_groups=[GATHER_ORDER])]
    ppermute x2, waiting for transfers between devices: 22.6 us -> 18.7 us  [sum_shares(): crossed = lax.ppermute(total_other, 'mp', H_SWAP)]
    ppermute x6, waiting for transfers between devices: 16.9 us -> 13 us  [sum_shares(): got = [lax.ppermute(other[d], 'mp', x_shift(d)) for d in (1, 3, 2)]]
    ppermute x6 -> x5, waiting for transfers between devices: 7.85 us -> 10 us  [the longest x1 9.17 us: body(): crossed = lax.ppermute(extended, 'mp', H_SWAP)]
    ppermute x6 -> x5, starting transfers between devices: 12.4 us -> 10.5 us  [the longest x3 4.97 us: body(): lax.ppermute(extended, 'mp', x_shift(d))]
    unnamed x41 -> x33, local copies, waits for them, and re-layouts: 11.1 us -> 10.1 us
    pallas_call x2 -> x3, Pallas kernels: 8.72 us -> 9.06 us  [the longest x2 8.91 us: project(): pl.pallas_call(functools.partial(project_kernel, slots), out_shape=[EXT_P...]
  transfers between devices with their start and end apart: 33 -> 32, of which waited for: 16 -> 18; matrix products, arithmetic and copies ran while one was open for 1% -> 1% of each run, Pallas kernels for 9% -> 11%
where the time goes in v4:
time: 211 us; the launch traced here: 210 us
  waiting for transfers between devices  83.1 us (39%)
  starting transfers between devices  66.9 us (32%)
  Pallas kernels  34.4 us (16%)
  between operations  13.8 us (7%)
  local copies, waits for them, and re-layouts  10.2 us (5%)
    ppermute x2, waiting for transfers between devices, sum_shares(): crossed = lax.ppermute(total_other, 'mp', H_SWAP)  18.7 us
    all_gather x1, waiting for transfers between devices, body(): weights = lax.all_gather(moved, 'ctx', axis_index_groups=[GATHER_ORDER])  17.9 us
    ppermute x6, starting transfers between devices, sum_shares(): got = [lax.ppermute(other[d], 'mp', x_shift(d)) for d in (1, 3, 2)]  15.5 us
    ppermute x6, waiting for transfers between devices, sum_shares(): got = [lax.ppermute(other[d], 'mp', x_shift(d)) for d in (1, 3, 2)]  13 us
    ppermute x3, waiting for transfers between devices, body(): lax.ppermute(crossed, 'mp', x_shift(d))  10.5 us
    unnamed x33, local copies, waits for them, and re-layouts  10.1 us
    ppermute x2, starting transfers between devices, sum_shares(): crossed = lax.ppermute(total_other, 'mp', H_SWAP)  9.71 us
    ppermute x1, waiting for transfers between devices, body(): crossed = lax.ppermute(extended, 'mp', H_SWAP)  9.17 us
  transfers between devices with their start and end apart: 32, of which 18 were waited for; matrix products, arithmetic and copies ran while one was open for 1% of the time, Pallas kernels for 11%

profile of v4, /device:TPU:2, one launch (start us, length us, event | category | flops | bytes accessed | tf_op | source)
XLA Modules:
  0.0 209.8 jit_solution(5253340394022437326)
XLA Ops:
  15.8 3.1 %toeplitz.1.toep_ref = bf16[4096,256]{1,0:T(8,128)(2,1)S(1)} custom-call(f32[128,32]{1,0:T(8,128)S(1)} %copy.14.taps_ref), custom_call_target="tpu_custom_call" | custom-call | tf_op jit(solution)/shard_map/toeplitz/pallas_call | solution.py:108
  20.2 9.0 %collective-permute-done.1 = bf16[3,512,128]{2,1,0:T(8,128)(2,1)S(1)} collective-permute-done((bf16[3,512,128]{2,1,0:T(8,128)(2,1)}, bf16[3,512,128]{2,1,0:T(8,128)(2,1)S(1)}, u32[]{:S(2)}, u32[]{:S(2)}) %collective-permute-start.1) | collective-permute-done | bytes 393248 | tf_op jit(solution)/shard_map/ppermute | solution.py:590
  30.9 5.3 %mr_op.1 = (bf16[256,512]{1,0:T(8,128)(2,1)S(1)}, bf16[256,512]{1,0:T(8,128)(2,1)S(1)}, bf16[256,512]{1,0:T(8,128)(2,1)S(1)}, bf16[256,512]{1,0:T(8,128)(2,1)S(1)}, bf16[256,512]{1,0:T(8,128)(2,1)S(1)}) custom-call(s32[5]{0:T(128)S(1)} %stack.23.where_ref, bf16[256,512]{1,0:T(8,128)(2,1)S(1)} %get-tuple-element.60.q_ref, ...), custom_call_target="tpu_custom_call" | custom-call | tf_op jit(solution)/shard_map/mr_op/pallas_call | solution.py:277
  36.2 9.8 %collective-permute-start.2 = (bf16[256,512]{1,0:T(8,128)(2,1)S(1)}, bf16[256,512]{1,0:T(8,128)(2,1)S(1)}, u32[]{:S(2)}, u32[]{:S(2)}) collective-permute-start(bf16[256,512]{1,0:T(8,128)(2,1)S(1)} %get-tuple-element.67), channel_id=1, source_target_pairs={{0,2},{1,3},{2,4},{3,5},{4,6},{5,7},{6,0},{7,1},{8,10},{9,11},{10,... | collective-permute-start | bytes 786440 | tf_op jit(solution)/shard_map/ppermute | solution.py:566
  47.5 3.0 %shares.2 = (bf16[256,512]{1,0:T(8,128)(2,1)S(1)}, bf16[256,512]{1,0:T(8,128)(2,1)S(1)}, bf16[256,512]{1,0:T(8,128)(2,1)S(1)}, bf16[256,512]{1,0:T(8,128)(2,1)S(1)}) custom-call(s32[5]{0:T(128)S(1)} %stack.23.where_ref, bf16[256,512]{1,0:T(8,128)(2,1)S(1)} %get-tuple-element.70.y_ref, bf16[512,4096]{1,0:T(8,128)(2,1)} %w_ref.5), custom_call_target="tpu_custom_call" | custom-call | tf_op jit(solution)/shard_map/shares/pallas_call | solution.py:239
  50.5 4.2 %collective-permute-done.2 = bf16[256,512]{1,0:T(8,128)(2,1)S(1)} collective-permute-done((bf16[256,512]{1,0:T(8,128)(2,1)S(1)}, bf16[256,512]{1,0:T(8,128)(2,1)S(1)}, u32[]{:S(2)}, u32[]{:S(2)}) %collective-permute-start.2) | collective-permute-done | bytes 262176 | tf_op jit(solution)/shard_map/ppermute | solution.py:566
  56.9 5.9 %collective-permute-start.5 = (bf16[256,512]{1,0:T(8,128)(2,1)S(1)}, bf16[256,512]{1,0:T(8,128)(2,1)S(1)}, u32[]{:S(2)}, u32[]{:S(2)}) collective-permute-start(bf16[256,512]{1,0:T(8,128)(2,1)S(1)} %add_convert_fusion.3), channel_id=1, source_target_pairs={{0,1},{1,0},{2,3},{3,2},{4,5},{5,4},{6,7},{7,6},{8,9},{9,8},{10,11... | collective-permute-start | bytes 786440 | tf_op jit(solution)/shard_map/ppermute | solution.py:571
  66.6 11.8 %collective-permute-done.5 = bf16[256,512]{1,0:T(8,128)(2,1)S(1)} collective-permute-done((bf16[256,512]{1,0:T(8,128)(2,1)S(1)}, bf16[256,512]{1,0:T(8,128)(2,1)S(1)}, u32[]{:S(2)}, u32[]{:S(2)}) %collective-permute-start.5) | collective-permute-done | bytes 262176 | tf_op jit(solution)/shard_map/ppermute | solution.py:571
  80.9 4.2 %collective-permute-start.13 = (bf16[272,512]{1,0:T(8,128)(2,1)S(1)}, bf16[272,512]{1,0:T(8,128)(2,1)S(1)}, u32[]{:S(2)}, u32[]{:S(2)}) collective-permute-start(bf16[272,512]{1,0:T(8,128)(2,1)S(1)} %pad_maximum_fusion.refs_0_), channel_id=1, source_target_pairs={{0,1},{1,0},{2,3},{3,2},{4,5},{5,4},{6,7},{7,6},{8,9},{9,8},{10,11... | collective-permute-start | bytes 835592 | tf_op jit(solution)/shard_map/ppermute | solution.py:604
  85.6 3.8 %prep.1 = (bf16[4096,256]{1,0:T(8,128)(2,1)S(1)}, f32[256,512]{1,0:T(8,128)S(1)}, f32[256,512]{1,0:T(8,128)S(1)}, f32[16,512]{1,0:T(8,128)S(1)}) custom-call(f32[16,32]{1,0:T(8,128)S(1)} %bitcast.8, f32[16,32]{1,0:T(8,128)S(1)} %bitcast.9), custom_call_target="tpu_custom_call" | custom-call | tf_op jit(solution)/shard_map/prep/pallas_call | solution.py:166
  96.0 9.2 %collective-permute-done.13.refs_4_ = bf16[272,512]{1,0:T(8,128)(2,1)S(1)} collective-permute-done((bf16[272,512]{1,0:T(8,128)(2,1)S(1)}, bf16[272,512]{1,0:T(8,128)(2,1)S(1)}, u32[]{:S(2)}, u32[]{:S(2)}) %collective-permute-start.13) | collective-permute-done | bytes 278560 | tf_op jit(solution)/shard_map/ppermute | solution.py:604
  105.2 3.1 %collective-permute-start.15 = (bf16[272,512]{1,0:T(8,128)(2,1)S(1)}, bf16[272,512]{1,0:T(8,128)(2,1)S(1)}, u32[]{:S(2)}, u32[]{:S(2)}) collective-permute-start(bf16[272,512]{1,0:T(8,128)(2,1)S(1)} %collective-permute-done.13.refs_4_), channel_id=1, source_target_pairs={{0,4},{1,5},{2,6},{3,7},{4,0},{5,1},{6,2},{7,3},{8,12},{9,13},{10,... | collective-permute-start | bytes 835592 | tf_op jit(solution)/shard_map/ppermute | solution.py:608
  110.0 4.8 %collective-permute-done.14.refs_5_ = bf16[272,512]{1,0:T(8,128)(2,1)S(1)} collective-permute-done((bf16[272,512]{1,0:T(8,128)(2,1)S(1)}, bf16[272,512]{1,0:T(8,128)(2,1)S(1)}, u32[]{:S(2)}, u32[]{:S(2)}) %collective-permute-start.14) | collective-permute-done | bytes 278560 | tf_op jit(solution)/shard_map/ppermute | solution.py:608
  116.4 4.1 %collective-permute-done.16.refs_7_ = bf16[272,512]{1,0:T(8,128)(2,1)S(1)} collective-permute-done((bf16[272,512]{1,0:T(8,128)(2,1)S(1)}, bf16[272,512]{1,0:T(8,128)(2,1)S(1)}, u32[]{:S(2)}, u32[]{:S(2)}) %collective-permute-start.16) | collective-permute-done | bytes 278560 | tf_op jit(solution)/shard_map/ppermute | solution.py:608
  120.6 17.9 %all-gather.3.cloned.1.call-done = bf16[96,512,128]{2,1,0:T(8,128)(2,1)} async-done(((bf16[3,512,128]{2,1,0:T(8,128)(2,1)}), bf16[96,512,128]{2,1,0:T(8,128)(2,1)}) %all-gather.3.cloned.1.call-update) | async-done | bytes 12582928 | tf_op jit(solution)/shard_map/all_gather | solution.py:595
  138.5 5.1 %project.2 = (bf16[272,512]{1,0:T(8,128)(2,1)S(1)}, bf16[272,512]{1,0:T(8,128)(2,1)S(1)}) custom-call(s32[5]{0:T(128)S(1)} %stack.23.where_ref, bf16[8,272,512]{2,1,0:T(8,128)(2,1)S(1)} %packed.1.hidden_ref, bf16[32,3,512,128]{3,2,1,0:T(8,128)(2,1)} %bitcast.10), custom_call_target="tpu_custom_call" | custom-call | tf_op jit(solution)/shard_map/project/pallas_call | solution.py:344
  151.3 3.8 %project.3.q_ref = bf16[272,512]{1,0:T(8,128)(2,1)S(1)} custom-call(s32[5]{0:T(128)S(1)} %stack.23.where_ref, bf16[8,272,512]{2,1,0:T(8,128)(2,1)S(1)} %packed.1.hidden_ref, bf16[32,3,512,128]{3,2,1,0:T(8,128)(2,1)} %bitcast.11), custom_call_target="tpu_custom_call" | custom-call | tf_op jit(solution)/shard_map/project/pallas_call | solution.py:344
  157.2 3.0 %collective-permute-start.21 = (f32[16,512]{1,0:T(8,128)S(1)}, f32[16,512]{1,0:T(8,128)S(1)}, u32[]{:S(2)}, u32[]{:S(2)}) collective-permute-start(f32[16,512]{1,0:T(8,128)S(1)} %get-tuple-element.100), channel_id=1, source_target_pairs={{0,64},{8,72},{16,80},{24,88},{32,96},{40,104},{48,112},{56,120},{... | collective-permute-start | bytes 98312 | tf_op jit(solution)/shard_map/ppermute | solution.py:625
  160.2 4.8 %collective-permute-start.22 = (f32[16,512]{1,0:T(8,128)S(1)}, f32[16,512]{1,0:T(8,128)S(1)}, u32[]{:S(2)}, u32[]{:S(2)}) collective-permute-start(f32[16,512]{1,0:T(8,128)S(1)} %get-tuple-element.100), channel_id=1, source_target_pairs={{0,128},{8,136},{16,144},{24,152},{32,160},{40,168},{48,176},{56,1... | collective-permute-start | bytes 98312 | tf_op jit(solution)/shard_map/ppermute | solution.py:625
  167.9 4.2 %li_outer.1 = (bf16[256,512]{1,0:T(8,128)(2,1)S(1)}, bf16[256,512]{1,0:T(8,128)(2,1)S(1)}, bf16[256,512]{1,0:T(8,128)(2,1)S(1)}, bf16[256,512]{1,0:T(8,128)(2,1)S(1)}, bf16[256,512]{1,0:T(8,128)(2,1)S(1)}) custom-call(s32[5]{0:T(128)S(1)} %stack.23.where_ref, f32[256,512]{1,0:T(8,128)} %copy-done.3, bf16[272,512]{1,0:T(8,128)(2,1)S(1)} %project.3.q_ref, ...), custom_call_target="tpu_custom_call" | custom-call | tf_op jit(solution)/shard_map/li_outer/pallas_call | solution.py:489
  176.3 3.0 %shares.3 = (bf16[256,512]{1,0:T(8,128)(2,1)S(1)}, bf16[256,512]{1,0:T(8,128)(2,1)S(1)}, bf16[256,512]{1,0:T(8,128)(2,1)S(1)}, bf16[256,512]{1,0:T(8,128)(2,1)S(1)}) custom-call(s32[5]{0:T(128)S(1)} %stack.23.where_ref, bf16[256,512]{1,0:T(8,128)(2,1)S(1)} %get-tuple-element.105.y_ref, bf16[512,4096]{1,0:T(8,128)(2,1)} %w_ref.7), custom_call_target="tpu_custom_call" | custom-call | tf_op jit(solution)/shard_map/shares/pallas_call | solution.py:239
  182.5 3.5 %collective-permute-done.26 = bf16[256,512]{1,0:T(8,128)(2,1)S(1)} collective-permute-done((bf16[256,512]{1,0:T(8,128)(2,1)S(1)}, bf16[256,512]{1,0:T(8,128)(2,1)S(1)}, u32[]{:S(2)}, u32[]{:S(2)}) %collective-permute-start.26) | collective-permute-done | bytes 262176 | tf_op jit(solution)/shard_map/ppermute | solution.py:566
  186.2 3.8 %collective-permute-start.27 = (bf16[256,512]{1,0:T(8,128)(2,1)S(1)}, bf16[256,512]{1,0:T(8,128)(2,1)S(1)}, u32[]{:S(2)}, u32[]{:S(2)}) collective-permute-start(bf16[256,512]{1,0:T(8,128)(2,1)S(1)} %add_convert_fusion.1), channel_id=1, source_target_pairs={{0,1},{1,0},{2,3},{3,2},{4,5},{5,4},{6,7},{7,6},{8,9},{9,8},{10,11... | collective-permute-start | bytes 786440 | tf_op jit(solution)/shard_map/ppermute | solution.py:571
  193.8 6.9 %collective-permute-done.27 = bf16[256,512]{1,0:T(8,128)(2,1)S(1)} collective-permute-done((bf16[256,512]{1,0:T(8,128)(2,1)S(1)}, bf16[256,512]{1,0:T(8,128)(2,1)S(1)}, u32[]{:S(2)}, u32[]{:S(2)}) %collective-permute-start.27) | collective-permute-done | bytes 262176 | tf_op jit(solution)/shard_map/ppermute | solution.py:571
  (97 shorter events, 58.7 us)
Async XLA Ops:
  6.5 132.0 %all-gather.3.cloned.1.call-start = ((), (), s32[]{:S(2)}) async-start(), calls=%async_computation | async-start | bytes 12976128 | tf_op jit(solution)/shard_map/all_gather | solution.py:595
  6.5 22.7 %collective-permute-start.1 = (bf16[3,512,128]{2,1,0:T(8,128)(2,1)}, bf16[3,512,128]{2,1,0:T(8,128)(2,1)S(1)}, u32[]{:S(2)}, u32[]{:S(2)}) collective-permute-start(bf16[3,512,128]{2,1,0:T(8,128)(2,1)} %param.19), channel_id=1, source_target_pairs={{0,16},{1,48},{2,80},{3,112},{4,144},{5,176},{6,208},{7,240},{8,24... | collective-permute-start | bytes 1179656 | tf_op jit(solution)/shard_map/ppermute | solution.py:590
  36.2 18.5 %collective-permute-start.2 = (bf16[256,512]{1,0:T(8,128)(2,1)S(1)}, bf16[256,512]{1,0:T(8,128)(2,1)S(1)}, u32[]{:S(2)}, u32[]{:S(2)}) collective-permute-start(bf16[256,512]{1,0:T(8,128)(2,1)S(1)} %get-tuple-element.67), channel_id=1, source_target_pairs={{0,2},{1,3},{2,4},{3,5},{4,6},{5,7},{6,0},{7,1},{8,10},{9,11},{10,... | collective-permute-start | bytes 786440 | tf_op jit(solution)/shard_map/ppermute | solution.py:566
  45.9 10.8 %collective-permute-start.3 = (bf16[256,512]{1,0:T(8,128)(2,1)S(1)}, bf16[256,512]{1,0:T(8,128)(2,1)S(1)}, u32[]{:S(2)}, u32[]{:S(2)}) collective-permute-start(bf16[256,512]{1,0:T(8,128)(2,1)S(1)} %get-tuple-element.68), channel_id=1, source_target_pairs={{0,6},{1,7},{2,0},{3,1},{4,2},{5,3},{6,4},{7,5},{8,14},{9,15},{10,... | collective-permute-start | bytes 786440 | tf_op jit(solution)/shard_map/ppermute | solution.py:566
  45.9 10.8 %collective-permute-start.4 = (bf16[256,512]{1,0:T(8,128)(2,1)S(1)}, bf16[256,512]{1,0:T(8,128)(2,1)S(1)}, u32[]{:S(2)}, u32[]{:S(2)}) collective-permute-start(bf16[256,512]{1,0:T(8,128)(2,1)S(1)} %get-tuple-element.69), channel_id=1, source_target_pairs={{0,4},{1,5},{2,6},{3,7},{4,0},{5,1},{6,2},{7,3},{8,12},{9,13},{10,... | collective-permute-start | bytes 786440 | tf_op jit(solution)/shard_map/ppermute | solution.py:566
  56.9 21.6 %collective-permute-start.5 = (bf16[256,512]{1,0:T(8,128)(2,1)S(1)}, bf16[256,512]{1,0:T(8,128)(2,1)S(1)}, u32[]{:S(2)}, u32[]{:S(2)}) collective-permute-start(bf16[256,512]{1,0:T(8,128)(2,1)S(1)} %add_convert_fusion.3), channel_id=1, source_target_pairs={{0,1},{1,0},{2,3},{3,2},{4,5},{5,4},{6,7},{7,6},{8,9},{9,8},{10,11... | collective-permute-start | bytes 786440 | tf_op jit(solution)/shard_map/ppermute | solution.py:571
  62.8 15.8 %collective-permute-start.6 = (bf16[256,512]{1,0:T(8,128)(2,1)S(1)}, bf16[256,512]{1,0:T(8,128)(2,1)S(1)}, u32[]{:S(2)}, u32[]{:S(2)}) collective-permute-start(bf16[256,512]{1,0:T(8,128)(2,1)S(1)} %get-tuple-element.77), channel_id=1, source_target_pairs={{0,2},{1,3},{2,4},{3,5},{4,6},{5,7},{6,0},{7,1},{8,10},{9,11},{10,... | collective-permute-start | bytes 786440 | tf_op jit(solution)/shard_map/ppermute | solution.py:572
  63.1 15.5 %collective-permute-start.7 = (bf16[256,512]{1,0:T(8,128)(2,1)S(1)}, bf16[256,512]{1,0:T(8,128)(2,1)S(1)}, u32[]{:S(2)}, u32[]{:S(2)}) collective-permute-start(bf16[256,512]{1,0:T(8,128)(2,1)S(1)} %get-tuple-element.78), channel_id=1, source_target_pairs={{0,6},{1,7},{2,0},{3,1},{4,2},{5,3},{6,4},{7,5},{8,14},{9,15},{10,... | collective-permute-start | bytes 786440 | tf_op jit(solution)/shard_map/ppermute | solution.py:572
  64.8 13.8 %collective-permute-start.8 = (bf16[256,512]{1,0:T(8,128)(2,1)S(1)}, bf16[256,512]{1,0:T(8,128)(2,1)S(1)}, u32[]{:S(2)}, u32[]{:S(2)}) collective-permute-start(bf16[256,512]{1,0:T(8,128)(2,1)S(1)} %get-tuple-element.79), channel_id=1, source_target_pairs={{0,4},{1,5},{2,6},{3,7},{4,0},{5,1},{6,2},{7,3},{8,12},{9,13},{10,... | collective-permute-start | bytes 786440 | tf_op jit(solution)/shard_map/ppermute | solution.py:572
  80.9 24.3 %collective-permute-start.13 = (bf16[272,512]{1,0:T(8,128)(2,1)S(1)}, bf16[272,512]{1,0:T(8,128)(2,1)S(1)}, u32[]{:S(2)}, u32[]{:S(2)}) collective-permute-start(bf16[272,512]{1,0:T(8,128)(2,1)S(1)} %pad_maximum_fusion.refs_0_), channel_id=1, source_target_pairs={{0,1},{1,0},{2,3},{3,2},{4,5},{5,4},{6,7},{7,6},{8,9},{9,8},{10,11... | collective-permute-start | bytes 835592 | tf_op jit(solution)/shard_map/ppermute | solution.py:604
  85.1 23.2 %collective-permute-start.10 = (bf16[272,512]{1,0:T(8,128)(2,1)S(1)}, bf16[272,512]{1,0:T(8,128)(2,1)S(1)}, u32[]{:S(2)}, u32[]{:S(2)}) collective-permute-start(bf16[272,512]{1,0:T(8,128)(2,1)S(1)} %pad_maximum_fusion.refs_0_), channel_id=1, source_target_pairs={{0,2},{1,3},{2,4},{3,5},{4,6},{5,7},{6,0},{7,1},{8,10},{9,11},{10,... | collective-permute-start | bytes 835592 | tf_op jit(solution)/shard_map/ppermute | solution.py:605
  91.5 18.4 %collective-permute-start.11 = (bf16[272,512]{1,0:T(8,128)(2,1)S(1)}, bf16[272,512]{1,0:T(8,128)(2,1)S(1)}, u32[]{:S(2)}, u32[]{:S(2)}) collective-permute-start(bf16[272,512]{1,0:T(8,128)(2,1)S(1)} %pad_maximum_fusion.refs_0_), channel_id=1, source_target_pairs={{0,4},{1,5},{2,6},{3,7},{4,0},{5,1},{6,2},{7,3},{8,12},{9,13},{10,... | collective-permute-start | bytes 835592 | tf_op jit(solution)/shard_map/ppermute | solution.py:605
  94.5 15.5 %collective-permute-start.12 = (bf16[272,512]{1,0:T(8,128)(2,1)S(1)}, bf16[272,512]{1,0:T(8,128)(2,1)S(1)}, u32[]{:S(2)}, u32[]{:S(2)}) collective-permute-start(bf16[272,512]{1,0:T(8,128)(2,1)S(1)} %pad_maximum_fusion.refs_0_), channel_id=1, source_target_pairs={{0,6},{1,7},{2,0},{3,1},{4,2},{5,3},{6,4},{7,5},{8,14},{9,15},{10,... | collective-permute-start | bytes 835592 | tf_op jit(solution)/shard_map/ppermute | solution.py:605
  105.2 9.6 %collective-permute-start.14 = (bf16[272,512]{1,0:T(8,128)(2,1)S(1)}, bf16[272,512]{1,0:T(8,128)(2,1)S(1)}, u32[]{:S(2)}, u32[]{:S(2)}) collective-permute-start(bf16[272,512]{1,0:T(8,128)(2,1)S(1)} %collective-permute-done.13.refs_4_), channel_id=1, source_target_pairs={{0,2},{1,3},{2,4},{3,5},{4,6},{5,7},{6,0},{7,1},{8,10},{9,11},{10,... | collective-permute-start | bytes 835592 | tf_op jit(solution)/shard_map/ppermute | solution.py:608
  105.2 11.1 %collective-permute-start.15 = (bf16[272,512]{1,0:T(8,128)(2,1)S(1)}, bf16[272,512]{1,0:T(8,128)(2,1)S(1)}, u32[]{:S(2)}, u32[]{:S(2)}) collective-permute-start(bf16[272,512]{1,0:T(8,128)(2,1)S(1)} %collective-permute-done.13.refs_4_), channel_id=1, source_target_pairs={{0,4},{1,5},{2,6},{3,7},{4,0},{5,1},{6,2},{7,3},{8,12},{9,13},{10,... | collective-permute-start | bytes 835592 | tf_op jit(solution)/shard_map/ppermute | solution.py:608
  108.3 12.1 %collective-permute-start.16 = (bf16[272,512]{1,0:T(8,128)(2,1)S(1)}, bf16[272,512]{1,0:T(8,128)(2,1)S(1)}, u32[]{:S(2)}, u32[]{:S(2)}) collective-permute-start(bf16[272,512]{1,0:T(8,128)(2,1)S(1)} %collective-permute-done.13.refs_4_), channel_id=1, source_target_pairs={{0,6},{1,7},{2,0},{3,1},{4,2},{5,3},{6,4},{7,5},{8,14},{9,15},{10,... | collective-permute-start | bytes 835592 | tf_op jit(solution)/shard_map/ppermute | solution.py:608
  146.1 10.4 %collective-permute-start.18 = (f32[16,512]{1,0:T(8,128)S(1)}, f32[16,512]{1,0:T(8,128)S(1)}, u32[]{:S(2)}, u32[]{:S(2)}) collective-permute-start(f32[16,512]{1,0:T(8,128)S(1)} %chip_state.1.c0), channel_id=1, source_target_pairs={{0,16},{8,24},{16,32},{24,40},{32,48},{40,56},{48,0},{56,8},{64,80... | collective-permute-start | bytes 98312 | tf_op jit(solution)/shard_map/ppermute | solution.py:614
  157.2 9.1 %collective-permute-start.21 = (f32[16,512]{1,0:T(8,128)S(1)}, f32[16,512]{1,0:T(8,128)S(1)}, u32[]{:S(2)}, u32[]{:S(2)}) collective-permute-start(f32[16,512]{1,0:T(8,128)S(1)} %get-tuple-element.100), channel_id=1, source_target_pairs={{0,64},{8,72},{16,80},{24,88},{32,96},{40,104},{48,112},{56,120},{... | collective-permute-start | bytes 98312 | tf_op jit(solution)/shard_map/ppermute | solution.py:625
  172.1 9.2 %collective-permute-start.24 = (bf16[256,512]{1,0:T(8,128)(2,1)S(1)}, bf16[256,512]{1,0:T(8,128)(2,1)S(1)}, u32[]{:S(2)}, u32[]{:S(2)}) collective-permute-start(bf16[256,512]{1,0:T(8,128)(2,1)S(1)} %get-tuple-element.102), channel_id=1, source_target_pairs={{0,2},{1,3},{2,4},{3,5},{4,6},{5,7},{6,0},{7,1},{8,10},{9,11},{10,... | collective-permute-start | bytes 786440 | tf_op jit(solution)/shard_map/ppermute | solution.py:566
  174.2 11.9 %collective-permute-start.26 = (bf16[256,512]{1,0:T(8,128)(2,1)S(1)}, bf16[256,512]{1,0:T(8,128)(2,1)S(1)}, u32[]{:S(2)}, u32[]{:S(2)}) collective-permute-start(bf16[256,512]{1,0:T(8,128)(2,1)S(1)} %get-tuple-element.104), channel_id=1, source_target_pairs={{0,4},{1,5},{2,6},{3,7},{4,0},{5,1},{6,2},{7,3},{8,12},{9,13},{10,... | collective-permute-start | bytes 786440 | tf_op jit(solution)/shard_map/ppermute | solution.py:566
  186.2 14.4 %collective-permute-start.27 = (bf16[256,512]{1,0:T(8,128)(2,1)S(1)}, bf16[256,512]{1,0:T(8,128)(2,1)S(1)}, u32[]{:S(2)}, u32[]{:S(2)}) collective-permute-start(bf16[256,512]{1,0:T(8,128)(2,1)S(1)} %add_convert_fusion.1), channel_id=1, source_target_pairs={{0,1},{1,0},{2,3},{3,2},{4,5},{5,4},{6,7},{7,6},{8,9},{9,8},{10,11... | collective-permute-start | bytes 786440 | tf_op jit(solution)/shard_map/ppermute | solution.py:571
  190.0 10.7 %collective-permute-start.28 = (bf16[256,512]{1,0:T(8,128)(2,1)S(1)}, bf16[256,512]{1,0:T(8,128)(2,1)S(1)}, u32[]{:S(2)}, u32[]{:S(2)}) collective-permute-start(bf16[256,512]{1,0:T(8,128)(2,1)S(1)} %get-tuple-element.112), channel_id=1, source_target_pairs={{0,2},{1,3},{2,4},{3,5},{4,6},{5,7},{6,0},{7,1},{8,10},{9,11},{10,... | collective-permute-start | bytes 786440 | tf_op jit(solution)/shard_map/ppermute | solution.py:572
  190.0 10.7 %collective-permute-start.29 = (bf16[256,512]{1,0:T(8,128)(2,1)S(1)}, bf16[256,512]{1,0:T(8,128)(2,1)S(1)}, u32[]{:S(2)}, u32[]{:S(2)}) collective-permute-start(bf16[256,512]{1,0:T(8,128)(2,1)S(1)} %get-tuple-element.113), channel_id=1, source_target_pairs={{0,6},{1,7},{2,0},{3,1},{4,2},{5,3},{6,4},{7,5},{8,14},{9,15},{10,... | collective-permute-start | bytes 786440 | tf_op jit(solution)/shard_map/ppermute | solution.py:572
  192.0 10.1 %collective-permute-start.30 = (bf16[256,512]{1,0:T(8,128)(2,1)S(1)}, bf16[256,512]{1,0:T(8,128)(2,1)S(1)}, u32[]{:S(2)}, u32[]{:S(2)}) collective-permute-start(bf16[256,512]{1,0:T(8,128)(2,1)S(1)} %get-tuple-element.114), channel_id=1, source_target_pairs={{0,4},{1,5},{2,6},{3,7},{4,0},{5,1},{6,2},{7,3},{8,12},{9,13},{10,... | collective-permute-start | bytes 786440 | tf_op jit(solution)/shard_map/ppermute | solution.py:572
  (24 other events, 196.8 us)
Sparse Core Ops, SparseCore 0:
  30.1 108.3 all-gather.2

commit v5 on v4

--- a/solution.py
+++ b/solution.py
@@ -242,7 +242,7 @@
         in_specs=[SMEM_SPEC] + vspecs(1) + hspecs(1),
         out_specs=vspecs(4),
         scratch_shapes=SHARE_SCRATCH,
-        compiler_params=params(52),
+        compiler_params=params(48),
         name="shares",
     )(where, y, weight)
 
@@ -284,7 +284,7 @@
             pltpu.VMEM((HALO + ROWS, LANES), F32),
             pltpu.VMEM((16 + ROWS, LANES), F32),
         ] + SHARE_SCRATCH,
-        compiler_params=params(52),
+        compiler_params=params(48),
         name="mr_op",
     )(where, q, k, v, halo, feat, toep, weight)
 
@@ -295,13 +295,13 @@
 
 def pack_kernel(*refs):
     for i in range(8):
-        refs[8][i] = refs[i][...]
+        refs[8][:, i * WIDTH : (i + 1) * WIDTH] = refs[i][...]
 
 
 def packed(pieces):
     return pl.pallas_call(
         pack_kernel,
-        out_shape=jax.ShapeDtypeStruct((8, EXT, WIDTH), BF16),
+        out_shape=jax.ShapeDtypeStruct((EXT, 8 * WIDTH), BF16),
         in_specs=vspecs(8),
         out_specs=pl.BlockSpec(memory_space=pltpu.VMEM),
         compiler_params=params(),
@@ -317,24 +317,25 @@
     copies = []
     for i in range(8):
         e, d = i // 4, i % 4
-        src_y = lax.rem(x + 4 - d, 4)
+        src_y = lax.bitwise_xor(lax.rem(x + 4 - d, 4), x)
         for b in range(4):
             odd = 1 - b // 2
             high = odd if e == 1 else 1 - odd
             copy = pltpu.make_async_copy(
                 w_ref.at[gathered_at(src_y, high * 2 + odd, b % 2), pl.ds(slots[0], count)],
-                wbuf.at[i, :, :, pl.ds(b * LANES, LANES)],
+                wbuf.at[:, pl.ds(i * WIDTH, WIDTH), pl.ds(b * LANES, LANES)],
                 wsem.at[i, b],
             )
             copy.start()
             copies.append(copy)
     sums = [None] * count
-    for i in range(8):
-        for b in range(4):
-            copies[i * 4 + b].wait()
+    for half in range(2):
+        for copy in copies[half * 16 : (half + 1) * 16]:
+            copy.wait()
+        deep = slice(half * 4 * WIDTH, (half + 1) * 4 * WIDTH)
         for j in range(count):
-            prod = jnp.dot(hidden_ref[i], wbuf[i, j], preferred_element_type=F32)
-            sums[j] = prod if i == 0 else sums[j] + prod
+            prod = jnp.dot(hidden_ref[:, deep], wbuf[j, deep, :], preferred_element_type=F32)
+            sums[j] = prod if half == 0 else sums[j] + prod
     for j in range(count):
         out_refs[j][...] = sums[j].astype(BF16)
 
@@ -347,7 +348,7 @@
         in_specs=[SMEM_SPEC] + vspecs(1) + hspecs(1),
         out_specs=vspecs(count),
         scratch_shapes=[
-            pltpu.VMEM((8, count, WIDTH, WIDTH), BF16),
+            pltpu.VMEM((count, 8 * WIDTH, WIDTH), BF16),
             pltpu.SemaphoreType.DMA((8, 4)),
         ],
         compiler_params=params(48),
@@ -463,11 +464,11 @@
     y_ref, o0, o1, o2, o3, qx, wbuf, sems,
 ):
     copies = share_loads(where_ref, w_ref, wbuf, sems, 1)
-    zl, k = where_ref[3], where_ref[4]
+    y, zl, k = where_ref[2], where_ref[3], where_ref[4]
     rates = rates_ref[...]
-    above = y1_ref[...]
-    above = above + jnp.exp(-rates * (2.0 * ROWS * NZ)) * y2_ref[...]
-    above = above + jnp.exp(-rates * (4.0 * ROWS * NZ)) * y3_ref[...]
+    above = jnp.where(y >= 1, y1_ref[...], 0.0)
+    above = above + jnp.where(y >= 2, jnp.exp(-rates * (2.0 * ROWS * NZ)) * y2_ref[...], 0.0)
+    above = above + jnp.where(y >= 3, jnp.exp(-rates * (4.0 * ROWS * NZ)) * y3_ref[...], 0.0)
     chip = carry_ref[...] + jnp.exp(-rates * (zl * (2 * ROWS)).astype(F32)) * above
     full = jnp.where(k == 0, chip, jnp.exp(-rates * (1.0 * ROWS)) * chip + other_ref[...])
     for block in range(WIDTH // LANES):
@@ -492,7 +493,7 @@
         in_specs=[SMEM_SPEC] + vspecs(10) + hspecs(1),
         out_specs=vspecs(5),
         scratch_shapes=[pltpu.VMEM((16 + ROWS, LANES), F32)] + SHARE_SCRATCH,
-        compiler_params=params(52),
+        compiler_params=params(48),
         name="li_outer",
     )(where, conv, q, feat, leave, rates, carry, other, *above, weight)
 
@@ -539,23 +540,24 @@
     return (z * NY + y) * NC + k
 
 
+def flat(y, zl, k, x, h):
+    return ctx_of(y, zl, k) * (NX * NH) + mp_of(x, h)
+
+
 def weight_moves():
-    moves = []
+    first, second = [], []
     for y in range(NY):
         for zl in range(NZ):
             for k in range(NC):
                 for x in range(NX):
                     for h in range(NH):
-                        x2, h2, y2 = y, zl // 2, x
-                        l0 = zl % 2
-                        odd = 1 - l0
-                        outer = h ^ h2
-                        high = odd if outer else 1 - odd
+                        h2, odd = zl // 2, 1 - zl % 2
+                        high = odd if h ^ h2 else 1 - odd
                         z2 = high * 2 + odd
-                        src = ctx_of(y, zl, k) * (NX * NH) + mp_of(x, h)
-                        dst = ctx_of(y2, z2, k) * (NX * NH) + mp_of(x2, h2)
-                        moves.append((src, dst))
-    return moves
+                        via = flat(x ^ y, z2, k, x, h2)
+                        first.append((flat(y, zl, k, x, h), via))
+                        second.append((via, flat(x ^ y, z2, k, y, h2)))
+    return first, second
 
 
 def tied(*values):
@@ -587,8 +589,11 @@
     where = jnp.stack([x, zh, y, zl, k]).astype(jnp.int32)
 
     forward = [(i, i + 1) for i in range(NY * NZ * NC - 1)]
-    moved = lax.ppermute(in_weight, ("ctx", "mp"), weight_moves())
+    first, second = weight_moves()
+    moved = lax.ppermute(in_weight, ("ctx", "mp"), first)
     rim, query_mr, key_mr, value_mr = rim_rows(query_mr, key_mr, value_mr)
+    moved, rim = tied(moved, rim)
+    moved = lax.ppermute(moved, ("ctx", "mp"), second)
     halo = lax.ppermute(rim, "ctx", forward)
     toep_mr = toeplitz(mr_taps)
     halo, moved, toep_mr = tied(halo, moved, toep_mr)
@@ -613,17 +618,10 @@
     chip = chip_state(where, load, other_load, lane_rates)
     before = [lax.ppermute(chip, "ctx", z_shift(s)) for s in (1, 2, 3)]
     (fresh_q,) = project(where, pieces, weights, (0,))
+    *before, fresh_q = tied(*before, fresh_q)
     conv = li_inner(product, toep_li)
-    *before, fresh_q, conv = tied(*before, fresh_q, conv)
     line_total, line_carry = line_state(where, [chip] + before, lane_rates)
-    above = []
-    for s in (1, 2, 3):
-        pairs = [
-            (ctx_of(a, b, c), ctx_of(a + s, b, c))
-            for a in range(NY - s) for b in range(NZ) for c in range(NC)
-        ]
-        above.append(lax.ppermute(line_total, "ctx", pairs))
-
+    above = [lax.ppermute(line_total, "ctx", y_shift(s)) for s in (1, 2, 3)]
     gated_two, *other_two = li_outer(
         where, conv, fresh_q, featurizer_li, leave, lane_rates,
         line_carry, other_load, above, out_li,

time: 211 us -> 211 us (level)
  waiting for transfers between devices: 83.1 us -> 95.1 us
  starting transfers between devices: 66.9 us -> 59.5 us
  local copies, waits for them, and re-layouts: 10.2 us -> 5.98 us
    ppermute x6, starting transfers between devices: 15.5 us -> 9.85 us  [sum_shares(): got = [lax.ppermute(other[d], 'mp', x_shift(d)) for d in (1, 3, 2)]]
    all_gather x1, waiting for transfers between devices: 17.9 us -> 22.1 us  [body(): weights = lax.all_gather(moved, 'ctx', axis_index_groups=[GATHER_ORDER])]
    unnamed x33 -> x29, local copies, waits for them, and re-layouts: 10.1 us -> 5.89 us
    ppermute x6, waiting for transfers between devices: 13 us -> 17.1 us  [sum_shares(): got = [lax.ppermute(other[d], 'mp', x_shift(d)) for d in (1, 3, 2)]]
    ppermute x1, waiting for transfers between devices: 9.17 us -> 6.63 us  [body(): crossed = lax.ppermute(extended, 'mp', H_SWAP)]
    pallas_call x2, Pallas kernels: 8.91 us -> 11 us  [project(): pl.pallas_call(functools.partial(project_kernel, slots), out_shape=[EXT_P...]
    ppermute x2, starting transfers between devices: 9.71 us -> 7.59 us  [sum_shares(): crossed = lax.ppermute(total_other, 'mp', H_SWAP)]
    ppermute x4 -> x5, waiting for transfers between devices: 10.6 us -> 12.3 us  [the longest x1 10.2 us: body(): moved = lax.ppermute(in_weight, ('ctx', 'mp'), first)]
  transfers between devices with their start and end apart: 32 -> 33, of which waited for: 18 -> 19; matrix products, arithmetic and copies ran while one was open for 1% -> 1% of each run, Pallas kernels for 11% -> 10%
where the time goes in v5:
time: 211 us; the launch traced here: 209 us
  waiting for transfers between devices  95.1 us (45%)
  starting transfers between devices  59.5 us (28%)
  Pallas kernels  33.5 us (16%)
  between operations  13.8 us (7%)
  local copies, waits for them, and re-layouts  5.98 us (3%)
    all_gather x1, waiting for transfers between devices, body(): weights = lax.all_gather(moved, 'ctx', axis_index_groups=[GATHER_ORDER])  22.1 us
    ppermute x2, waiting for transfers between devices, sum_shares(): crossed = lax.ppermute(total_other, 'mp', H_SWAP)  20.4 us
    ppermute x6, waiting for transfers between devices, sum_shares(): got = [lax.ppermute(other[d], 'mp', x_shift(d)) for d in (1, 3, 2)]  17.1 us
    ppermute x3, waiting for transfers between devices, body(): lax.ppermute(crossed, 'mp', x_shift(d))  11.9 us
    pallas_call x2, Pallas kernels, project(): pl.pallas_call(functools.partial(project_kernel, slots), out_shape=[EXT_P...  11 us
    ppermute x1, waiting for transfers between devices, body(): moved = lax.ppermute(in_weight, ('ctx', 'mp'), first)  10.2 us
    ppermute x6, starting transfers between devices, sum_shares(): got = [lax.ppermute(other[d], 'mp', x_shift(d)) for d in (1, 3, 2)]  9.85 us
    ppermute x2, starting transfers between devices, sum_shares(): crossed = lax.ppermute(total_other, 'mp', H_SWAP)  7.59 us
  transfers between devices with their start and end apart: 33, of which 19 were waited for; matrix products, arithmetic and copies ran while one was open for 1% of the time, Pallas kernels for 10%

profile of v5, /device:TPU:2, one launch (start us, length us, event | category | flops | bytes accessed | tf_op | source)
XLA Modules:
  0.0 209.2 jit_solution(11011011189813753188)
XLA Ops:
  6.5 2.9 %collective-permute-start = (bf16[3,512,128]{2,1,0:T(8,128)(2,1)}, bf16[3,512,128]{2,1,0:T(8,128)(2,1)}, u32[]{:S(2)}, u32[]{:S(2)}) collective-permute-start(bf16[3,512,128]{2,1,0:T(8,128)(2,1)} %param.19), channel_id=1, source_target_pairs={{0,16},{1,48},{2,82},{3,114},{4,148},{5,180},{6,214},{7,246},{8,24... | collective-permute-start | bytes 1179656 | tf_op jit(solution)/shard_map/ppermute | solution.py:593
  13.6 10.2 %collective-permute-done = bf16[3,512,128]{2,1,0:T(8,128)(2,1)} collective-permute-done((bf16[3,512,128]{2,1,0:T(8,128)(2,1)}, bf16[3,512,128]{2,1,0:T(8,128)(2,1)}, u32[]{:S(2)}, u32[]{:S(2)}) %collective-permute-start) | collective-permute-done | bytes 393248 | tf_op jit(solution)/shard_map/ppermute | solution.py:593
  23.7 4.5 %collective-permute-start.2 = (bf16[3,512,128]{2,1,0:T(8,128)(2,1)}, bf16[3,512,128]{2,1,0:T(8,128)(2,1)}, u32[]{:S(2)}, u32[]{:S(2)}) collective-permute-start(bf16[3,512,128]{2,1,0:T(8,128)(2,1)} %collective-permute-done), channel_id=1, source_target_pairs={{16,16},{48,48},{82,80},{114,112},{148,144},{180,176},{214,208},{2... | collective-permute-start | bytes 1179656 | tf_op jit(solution)/shard_map/ppermute | solution.py:596
  30.3 3.1 %toeplitz.1.toep_ref = bf16[4096,256]{1,0:T(8,128)(2,1)S(1)} custom-call(f32[128,32]{1,0:T(8,128)S(1)} %copy.14.taps_ref), custom_call_target="tpu_custom_call" | custom-call | tf_op jit(solution)/shard_map/toeplitz/pallas_call | solution.py:108
  34.5 4.0 %mr_op.1 = (bf16[256,512]{1,0:T(8,128)(2,1)S(1)}, bf16[256,512]{1,0:T(8,128)(2,1)S(1)}, bf16[256,512]{1,0:T(8,128)(2,1)S(1)}, bf16[256,512]{1,0:T(8,128)(2,1)S(1)}, bf16[256,512]{1,0:T(8,128)(2,1)S(1)}) custom-call(s32[5]{0:T(128)S(1)} %stack.23.where_ref, bf16[256,512]{1,0:T(8,128)(2,1)S(1)} %get-tuple-element.61.q_ref, ...), custom_call_target="tpu_custom_call" | custom-call | tf_op jit(solution)/shard_map/mr_op/pallas_call | solution.py:277
  38.5 3.2 %collective-permute-start.3 = (bf16[256,512]{1,0:T(8,128)(2,1)S(1)}, bf16[256,512]{1,0:T(8,128)(2,1)S(1)}, u32[]{:S(2)}, u32[]{:S(2)}) collective-permute-start(bf16[256,512]{1,0:T(8,128)(2,1)S(1)} %get-tuple-element.70), channel_id=1, source_target_pairs={{0,2},{1,3},{2,4},{3,5},{4,6},{5,7},{6,0},{7,1},{8,10},{9,11},{10,... | collective-permute-start | bytes 786440 | tf_op jit(solution)/shard_map/ppermute | solution.py:568
  46.3 6.9 %collective-permute-done.3 = bf16[256,512]{1,0:T(8,128)(2,1)S(1)} collective-permute-done((bf16[256,512]{1,0:T(8,128)(2,1)S(1)}, bf16[256,512]{1,0:T(8,128)(2,1)S(1)}, u32[]{:S(2)}, u32[]{:S(2)}) %collective-permute-start.3) | collective-permute-done | bytes 262176 | tf_op jit(solution)/shard_map/ppermute | solution.py:568
  55.9 3.8 %collective-permute-start.6 = (bf16[256,512]{1,0:T(8,128)(2,1)S(1)}, bf16[256,512]{1,0:T(8,128)(2,1)S(1)}, u32[]{:S(2)}, u32[]{:S(2)}) collective-permute-start(bf16[256,512]{1,0:T(8,128)(2,1)S(1)} %add_convert_fusion.3), channel_id=1, source_target_pairs={{0,1},{1,0},{2,3},{3,2},{4,5},{5,4},{6,7},{7,6},{8,9},{9,8},{10,11... | collective-permute-start | bytes 786440 | tf_op jit(solution)/shard_map/ppermute | solution.py:573
  63.3 13.8 %collective-permute-done.6 = bf16[256,512]{1,0:T(8,128)(2,1)S(1)} collective-permute-done((bf16[256,512]{1,0:T(8,128)(2,1)S(1)}, bf16[256,512]{1,0:T(8,128)(2,1)S(1)}, u32[]{:S(2)}, u32[]{:S(2)}) %collective-permute-start.6) | collective-permute-done | bytes 262176 | tf_op jit(solution)/shard_map/ppermute | solution.py:573
  79.6 5.8 %collective-permute-start.14 = (bf16[272,512]{1,0:T(8,128)(2,1)S(1)}, bf16[272,512]{1,0:T(8,128)(2,1)S(1)}, u32[]{:S(2)}, u32[]{:S(2)}) collective-permute-start(bf16[272,512]{1,0:T(8,128)(2,1)S(1)} %pad_maximum_fusion.refs_0_), channel_id=1, source_target_pairs={{0,1},{1,0},{2,3},{3,2},{4,5},{5,4},{6,7},{7,6},{8,9},{9,8},{10,11... | collective-permute-start | bytes 835592 | tf_op jit(solution)/shard_map/ppermute | solution.py:609
  85.4 3.8 %prep.1 = (bf16[4096,256]{1,0:T(8,128)(2,1)S(1)}, f32[256,512]{1,0:T(8,128)S(1)}, f32[256,512]{1,0:T(8,128)S(1)}, f32[16,512]{1,0:T(8,128)S(1)}) custom-call(f32[16,32]{1,0:T(8,128)S(1)} %bitcast.8, f32[16,32]{1,0:T(8,128)S(1)} %bitcast.9), custom_call_target="tpu_custom_call" | custom-call | tf_op jit(solution)/shard_map/prep/pallas_call | solution.py:166
  90.6 3.1 %collective-permute-start.12 = (bf16[272,512]{1,0:T(8,128)(2,1)S(1)}, bf16[272,512]{1,0:T(8,128)(2,1)S(1)}, u32[]{:S(2)}, u32[]{:S(2)}) collective-permute-start(bf16[272,512]{1,0:T(8,128)(2,1)S(1)} %pad_maximum_fusion.refs_0_), channel_id=1, source_target_pairs={{0,4},{1,5},{2,6},{3,7},{4,0},{5,1},{6,2},{7,3},{8,12},{9,13},{10,... | collective-permute-start | bytes 835592 | tf_op jit(solution)/shard_map/ppermute | solution.py:610
  94.6 6.6 %collective-permute-done.14.refs_4_ = bf16[272,512]{1,0:T(8,128)(2,1)S(1)} collective-permute-done((bf16[272,512]{1,0:T(8,128)(2,1)S(1)}, bf16[272,512]{1,0:T(8,128)(2,1)S(1)}, u32[]{:S(2)}, u32[]{:S(2)}) %collective-permute-start.14) | collective-permute-done | bytes 278560 | tf_op jit(solution)/shard_map/ppermute | solution.py:609
  101.2 3.2 %collective-permute-start.16 = (bf16[272,512]{1,0:T(8,128)(2,1)S(1)}, bf16[272,512]{1,0:T(8,128)(2,1)S(1)}, u32[]{:S(2)}, u32[]{:S(2)}) collective-permute-start(bf16[272,512]{1,0:T(8,128)(2,1)S(1)} %collective-permute-done.14.refs_4_), channel_id=1, source_target_pairs={{0,4},{1,5},{2,6},{3,7},{4,0},{5,1},{6,2},{7,3},{8,12},{9,13},{10,... | collective-permute-start | bytes 835592 | tf_op jit(solution)/shard_map/ppermute | solution.py:613
  110.9 7.9 %collective-permute-done.17.refs_7_ = bf16[272,512]{1,0:T(8,128)(2,1)S(1)} collective-permute-done((bf16[272,512]{1,0:T(8,128)(2,1)S(1)}, bf16[272,512]{1,0:T(8,128)(2,1)S(1)}, u32[]{:S(2)}, u32[]{:S(2)}) %collective-permute-start.17) | collective-permute-done | bytes 278560 | tf_op jit(solution)/shard_map/ppermute | solution.py:613
  118.9 22.1 %all-gather.3.cloned.1.call-done = bf16[96,512,128]{2,1,0:T(8,128)(2,1)} async-done(((bf16[3,512,128]{2,1,0:T(8,128)(2,1)}), bf16[96,512,128]{2,1,0:T(8,128)(2,1)}) %all-gather.3.cloned.1.call-update) | async-done | bytes 12582928 | tf_op jit(solution)/shard_map/all_gather | solution.py:600
  141.0 6.7 %project.2 = (bf16[272,512]{1,0:T(8,128)(2,1)S(1)}, bf16[272,512]{1,0:T(8,128)(2,1)S(1)}) custom-call(s32[5]{0:T(128)S(1)} %stack.23.where_ref, bf16[272,4096]{1,0:T(8,128)(2,1)S(1)} %packed.1.hidden_ref, bf16[32,3,512,128]{3,2,1,0:T(8,128)(2,1)} %bitcast.10), custom_call_target="tpu_custom_call" | custom-call | tf_op jit(solution)/shard_map/project/pallas_call | solution.py:345
  155.3 4.4 %project.3.q_ref = bf16[272,512]{1,0:T(8,128)(2,1)S(1)} custom-call(s32[5]{0:T(128)S(1)} %stack.23.where_ref, bf16[272,4096]{1,0:T(8,128)(2,1)S(1)} %packed.1.hidden_ref, bf16[32,3,512,128]{3,2,1,0:T(8,128)(2,1)} %bitcast.11), custom_call_target="tpu_custom_call" | custom-call | tf_op jit(solution)/shard_map/project/pallas_call | solution.py:345
  161.5 2.9 %collective-permute-start.23 = (f32[16,512]{1,0:T(8,128)S(1)}, f32[16,512]{1,0:T(8,128)S(1)}, u32[]{:S(2)}, u32[]{:S(2)}) collective-permute-start(f32[16,512]{1,0:T(8,128)S(1)} %get-tuple-element.102), channel_id=1, source_target_pairs={{0,128},{8,136},{16,144},{24,152},{32,160},{40,168},{48,176},{56,1... | collective-permute-start | bytes 98312 | tf_op jit(solution)/shard_map/ppermute | solution.py:624
  168.3 3.5 %li_outer.1 = (bf16[256,512]{1,0:T(8,128)(2,1)S(1)}, bf16[256,512]{1,0:T(8,128)(2,1)S(1)}, bf16[256,512]{1,0:T(8,128)(2,1)S(1)}, bf16[256,512]{1,0:T(8,128)(2,1)S(1)}, bf16[256,512]{1,0:T(8,128)(2,1)S(1)}) custom-call(s32[5]{0:T(128)S(1)} %stack.23.where_ref, f32[256,512]{1,0:T(8,128)S(1)} %li_inner.1.conv_ref, bf16[272,512]{1,0:T(8,128)(2,1)S(1)} %project.3.q_ref, ...), custom_call_target="tpu_custom_call" | custom-call | tf_op jit(solution)/shard_map/li_outer/pallas_call | solution.py:490
  178.1 2.9 %collective-permute-done.25 = bf16[256,512]{1,0:T(8,128)(2,1)S(1)} collective-permute-done((bf16[256,512]{1,0:T(8,128)(2,1)S(1)}, bf16[256,512]{1,0:T(8,128)(2,1)S(1)}, u32[]{:S(2)}, u32[]{:S(2)}) %collective-permute-start.25) | collective-permute-done | bytes 262176 | tf_op jit(solution)/shard_map/ppermute | solution.py:568
  182.5 3.1 %collective-permute-done.27 = bf16[256,512]{1,0:T(8,128)(2,1)S(1)} collective-permute-done((bf16[256,512]{1,0:T(8,128)(2,1)S(1)}, bf16[256,512]{1,0:T(8,128)(2,1)S(1)}, u32[]{:S(2)}, u32[]{:S(2)}) %collective-permute-start.27) | collective-permute-done | bytes 262176 | tf_op jit(solution)/shard_map/ppermute | solution.py:568
  185.8 3.8 %collective-permute-start.28 = (bf16[256,512]{1,0:T(8,128)(2,1)S(1)}, bf16[256,512]{1,0:T(8,128)(2,1)S(1)}, u32[]{:S(2)}, u32[]{:S(2)}) collective-permute-start(bf16[256,512]{1,0:T(8,128)(2,1)S(1)} %add_convert_fusion.1), channel_id=1, source_target_pairs={{0,1},{1,0},{2,3},{3,2},{4,5},{5,4},{6,7},{7,6},{8,9},{9,8},{10,11... | collective-permute-start | bytes 786440 | tf_op jit(solution)/shard_map/ppermute | solution.py:573
  193.4 6.6 %collective-permute-done.28 = bf16[256,512]{1,0:T(8,128)(2,1)S(1)} collective-permute-done((bf16[256,512]{1,0:T(8,128)(2,1)S(1)}, bf16[256,512]{1,0:T(8,128)(2,1)S(1)}, u32[]{:S(2)}, u32[]{:S(2)}) %collective-permute-start.28) | collective-permute-done | bytes 262176 | tf_op jit(solution)/shard_map/ppermute | solution.py:573
  (95 shorter events, 56.8 us)
Async XLA Ops:
  6.5 134.5 %all-gather.3.cloned.1.call-start = ((), (), s32[]{:S(2)}) async-start(), calls=%async_computation | async-start | bytes 12976128 | tf_op jit(solution)/shard_map/all_gather | solution.py:600
  6.5 17.2 %collective-permute-start = (bf16[3,512,128]{2,1,0:T(8,128)(2,1)}, bf16[3,512,128]{2,1,0:T(8,128)(2,1)}, u32[]{:S(2)}, u32[]{:S(2)}) collective-permute-start(bf16[3,512,128]{2,1,0:T(8,128)(2,1)} %param.19), channel_id=1, source_target_pairs={{0,16},{1,48},{2,82},{3,114},{4,148},{5,180},{6,214},{7,246},{8,24... | collective-permute-start | bytes 1179656 | tf_op jit(solution)/shard_map/ppermute | solution.py:593
  23.7 9.7 %collective-permute-start.2 = (bf16[3,512,128]{2,1,0:T(8,128)(2,1)}, bf16[3,512,128]{2,1,0:T(8,128)(2,1)}, u32[]{:S(2)}, u32[]{:S(2)}) collective-permute-start(bf16[3,512,128]{2,1,0:T(8,128)(2,1)} %collective-permute-done), channel_id=1, source_target_pairs={{16,16},{48,48},{82,80},{114,112},{148,144},{180,176},{214,208},{2... | collective-permute-start | bytes 1179656 | tf_op jit(solution)/shard_map/ppermute | solution.py:596
  38.5 14.7 %collective-permute-start.3 = (bf16[256,512]{1,0:T(8,128)(2,1)S(1)}, bf16[256,512]{1,0:T(8,128)(2,1)S(1)}, u32[]{:S(2)}, u32[]{:S(2)}) collective-permute-start(bf16[256,512]{1,0:T(8,128)(2,1)S(1)} %get-tuple-element.70), channel_id=1, source_target_pairs={{0,2},{1,3},{2,4},{3,5},{4,6},{5,7},{6,0},{7,1},{8,10},{9,11},{10,... | collective-permute-start | bytes 786440 | tf_op jit(solution)/shard_map/ppermute | solution.py:568
  41.7 11.5 %collective-permute-start.4 = (bf16[256,512]{1,0:T(8,128)(2,1)S(1)}, bf16[256,512]{1,0:T(8,128)(2,1)S(1)}, u32[]{:S(2)}, u32[]{:S(2)}) collective-permute-start(bf16[256,512]{1,0:T(8,128)(2,1)S(1)} %get-tuple-element.71), channel_id=1, source_target_pairs={{0,6},{1,7},{2,0},{3,1},{4,2},{5,3},{6,4},{7,5},{8,14},{9,15},{10,... | collective-permute-start | bytes 786440 | tf_op jit(solution)/shard_map/ppermute | solution.py:568
  41.7 14.1 %collective-permute-start.5 = (bf16[256,512]{1,0:T(8,128)(2,1)S(1)}, bf16[256,512]{1,0:T(8,128)(2,1)S(1)}, u32[]{:S(2)}, u32[]{:S(2)}) collective-permute-start(bf16[256,512]{1,0:T(8,128)(2,1)S(1)} %get-tuple-element.72), channel_id=1, source_target_pairs={{0,4},{1,5},{2,6},{3,7},{4,0},{5,1},{6,2},{7,3},{8,12},{9,13},{10,... | collective-permute-start | bytes 786440 | tf_op jit(solution)/shard_map/ppermute | solution.py:568
  55.9 21.1 %collective-permute-start.6 = (bf16[256,512]{1,0:T(8,128)(2,1)S(1)}, bf16[256,512]{1,0:T(8,128)(2,1)S(1)}, u32[]{:S(2)}, u32[]{:S(2)}) collective-permute-start(bf16[256,512]{1,0:T(8,128)(2,1)S(1)} %add_convert_fusion.3), channel_id=1, source_target_pairs={{0,1},{1,0},{2,3},{3,2},{4,5},{5,4},{6,7},{7,6},{8,9},{9,8},{10,11... | collective-permute-start | bytes 786440 | tf_op jit(solution)/shard_map/ppermute | solution.py:573
  59.7 17.5 %collective-permute-start.7 = (bf16[256,512]{1,0:T(8,128)(2,1)S(1)}, bf16[256,512]{1,0:T(8,128)(2,1)S(1)}, u32[]{:S(2)}, u32[]{:S(2)}) collective-permute-start(bf16[256,512]{1,0:T(8,128)(2,1)S(1)} %get-tuple-element.80), channel_id=1, source_target_pairs={{0,2},{1,3},{2,4},{3,5},{4,6},{5,7},{6,0},{7,1},{8,10},{9,11},{10,... | collective-permute-start | bytes 786440 | tf_op jit(solution)/shard_map/ppermute | solution.py:574
  59.7 17.5 %collective-permute-start.8 = (bf16[256,512]{1,0:T(8,128)(2,1)S(1)}, bf16[256,512]{1,0:T(8,128)(2,1)S(1)}, u32[]{:S(2)}, u32[]{:S(2)}) collective-permute-start(bf16[256,512]{1,0:T(8,128)(2,1)S(1)} %get-tuple-element.81), channel_id=1, source_target_pairs={{0,6},{1,7},{2,0},{3,1},{4,2},{5,3},{6,4},{7,5},{8,14},{9,15},{10,... | collective-permute-start | bytes 786440 | tf_op jit(solution)/shard_map/ppermute | solution.py:574
  61.7 15.5 %collective-permute-start.9 = (bf16[256,512]{1,0:T(8,128)(2,1)S(1)}, bf16[256,512]{1,0:T(8,128)(2,1)S(1)}, u32[]{:S(2)}, u32[]{:S(2)}) collective-permute-start(bf16[256,512]{1,0:T(8,128)(2,1)S(1)} %get-tuple-element.82), channel_id=1, source_target_pairs={{0,4},{1,5},{2,6},{3,7},{4,0},{5,1},{6,2},{7,3},{8,12},{9,13},{10,... | collective-permute-start | bytes 786440 | tf_op jit(solution)/shard_map/ppermute | solution.py:574
  79.6 21.7 %collective-permute-start.14 = (bf16[272,512]{1,0:T(8,128)(2,1)S(1)}, bf16[272,512]{1,0:T(8,128)(2,1)S(1)}, u32[]{:S(2)}, u32[]{:S(2)}) collective-permute-start(bf16[272,512]{1,0:T(8,128)(2,1)S(1)} %pad_maximum_fusion.refs_0_), channel_id=1, source_target_pairs={{0,1},{1,0},{2,3},{3,2},{4,5},{5,4},{6,7},{7,6},{8,9},{9,8},{10,11... | collective-permute-start | bytes 835592 | tf_op jit(solution)/shard_map/ppermute | solution.py:609
  85.4 19.1 %collective-permute-start.11 = (bf16[272,512]{1,0:T(8,128)(2,1)S(1)}, bf16[272,512]{1,0:T(8,128)(2,1)S(1)}, u32[]{:S(2)}, u32[]{:S(2)}) collective-permute-start(bf16[272,512]{1,0:T(8,128)(2,1)S(1)} %pad_maximum_fusion.refs_0_), channel_id=1, source_target_pairs={{0,2},{1,3},{2,4},{3,5},{4,6},{5,7},{6,0},{7,1},{8,10},{9,11},{10,... | collective-permute-start | bytes 835592 | tf_op jit(solution)/shard_map/ppermute | solution.py:610
  90.6 14.9 %collective-permute-start.12 = (bf16[272,512]{1,0:T(8,128)(2,1)S(1)}, bf16[272,512]{1,0:T(8,128)(2,1)S(1)}, u32[]{:S(2)}, u32[]{:S(2)}) collective-permute-start(bf16[272,512]{1,0:T(8,128)(2,1)S(1)} %pad_maximum_fusion.refs_0_), channel_id=1, source_target_pairs={{0,4},{1,5},{2,6},{3,7},{4,0},{5,1},{6,2},{7,3},{8,12},{9,13},{10,... | collective-permute-start | bytes 835592 | tf_op jit(solution)/shard_map/ppermute | solution.py:610
  93.7 13.1 %collective-permute-start.13 = (bf16[272,512]{1,0:T(8,128)(2,1)S(1)}, bf16[272,512]{1,0:T(8,128)(2,1)S(1)}, u32[]{:S(2)}, u32[]{:S(2)}) collective-permute-start(bf16[272,512]{1,0:T(8,128)(2,1)S(1)} %pad_maximum_fusion.refs_0_), channel_id=1, source_target_pairs={{0,6},{1,7},{2,0},{3,1},{4,2},{5,3},{6,4},{7,5},{8,14},{9,15},{10,... | collective-permute-start | bytes 835592 | tf_op jit(solution)/shard_map/ppermute | solution.py:610
  101.2 9.6 %collective-permute-start.16 = (bf16[272,512]{1,0:T(8,128)(2,1)S(1)}, bf16[272,512]{1,0:T(8,128)(2,1)S(1)}, u32[]{:S(2)}, u32[]{:S(2)}) collective-permute-start(bf16[272,512]{1,0:T(8,128)(2,1)S(1)} %collective-permute-done.14.refs_4_), channel_id=1, source_target_pairs={{0,4},{1,5},{2,6},{3,7},{4,0},{5,1},{6,2},{7,3},{8,12},{9,13},{10,... | collective-permute-start | bytes 835592 | tf_op jit(solution)/shard_map/ppermute | solution.py:613
  104.5 14.2 %collective-permute-start.17 = (bf16[272,512]{1,0:T(8,128)(2,1)S(1)}, bf16[272,512]{1,0:T(8,128)(2,1)S(1)}, u32[]{:S(2)}, u32[]{:S(2)}) collective-permute-start(bf16[272,512]{1,0:T(8,128)(2,1)S(1)} %collective-permute-done.14.refs_4_), channel_id=1, source_target_pairs={{0,6},{1,7},{2,0},{3,1},{4,2},{5,3},{6,4},{7,5},{8,14},{9,15},{10,... | collective-permute-start | bytes 835592 | tf_op jit(solution)/shard_map/ppermute | solution.py:613
  150.2 9.5 %collective-permute-start.19 = (f32[16,512]{1,0:T(8,128)S(1)}, f32[16,512]{1,0:T(8,128)S(1)}, u32[]{:S(2)}, u32[]{:S(2)}) collective-permute-start(f32[16,512]{1,0:T(8,128)S(1)} %chip_state.1.c0), channel_id=1, source_target_pairs={{0,16},{8,24},{16,32},{24,40},{32,48},{40,56},{48,0},{56,8},{64,80... | collective-permute-start | bytes 98312 | tf_op jit(solution)/shard_map/ppermute | solution.py:619
  171.8 9.2 %collective-permute-start.25 = (bf16[256,512]{1,0:T(8,128)(2,1)S(1)}, bf16[256,512]{1,0:T(8,128)(2,1)S(1)}, u32[]{:S(2)}, u32[]{:S(2)}) collective-permute-start(bf16[256,512]{1,0:T(8,128)(2,1)S(1)} %get-tuple-element.104), channel_id=1, source_target_pairs={{0,2},{1,3},{2,4},{3,5},{4,6},{5,7},{6,0},{7,1},{8,10},{9,11},{10,... | collective-permute-start | bytes 786440 | tf_op jit(solution)/shard_map/ppermute | solution.py:568
  173.4 9.2 %collective-permute-start.26 = (bf16[256,512]{1,0:T(8,128)(2,1)S(1)}, bf16[256,512]{1,0:T(8,128)(2,1)S(1)}, u32[]{:S(2)}, u32[]{:S(2)}) collective-permute-start(bf16[256,512]{1,0:T(8,128)(2,1)S(1)} %get-tuple-element.105), channel_id=1, source_target_pairs={{0,6},{1,7},{2,0},{3,1},{4,2},{5,3},{6,4},{7,5},{8,14},{9,15},{10,... | collective-permute-start | bytes 786440 | tf_op jit(solution)/shard_map/ppermute | solution.py:568
  173.9 11.7 %collective-permute-start.27 = (bf16[256,512]{1,0:T(8,128)(2,1)S(1)}, bf16[256,512]{1,0:T(8,128)(2,1)S(1)}, u32[]{:S(2)}, u32[]{:S(2)}) collective-permute-start(bf16[256,512]{1,0:T(8,128)(2,1)S(1)} %get-tuple-element.106), channel_id=1, source_target_pairs={{0,4},{1,5},{2,6},{3,7},{4,0},{5,1},{6,2},{7,3},{8,12},{9,13},{10,... | collective-permute-start | bytes 786440 | tf_op jit(solution)/shard_map/ppermute | solution.py:568
  185.8 14.2 %collective-permute-start.28 = (bf16[256,512]{1,0:T(8,128)(2,1)S(1)}, bf16[256,512]{1,0:T(8,128)(2,1)S(1)}, u32[]{:S(2)}, u32[]{:S(2)}) collective-permute-start(bf16[256,512]{1,0:T(8,128)(2,1)S(1)} %add_convert_fusion.1), channel_id=1, source_target_pairs={{0,1},{1,0},{2,3},{3,2},{4,5},{5,4},{6,7},{7,6},{8,9},{9,8},{10,11... | collective-permute-start | bytes 786440 | tf_op jit(solution)/shard_map/ppermute | solution.py:573
  189.6 10.5 %collective-permute-start.29 = (bf16[256,512]{1,0:T(8,128)(2,1)S(1)}, bf16[256,512]{1,0:T(8,128)(2,1)S(1)}, u32[]{:S(2)}, u32[]{:S(2)}) collective-permute-start(bf16[256,512]{1,0:T(8,128)(2,1)S(1)} %get-tuple-element.114), channel_id=1, source_target_pairs={{0,2},{1,3},{2,4},{3,5},{4,6},{5,7},{6,0},{7,1},{8,10},{9,11},{10,... | collective-permute-start | bytes 786440 | tf_op jit(solution)/shard_map/ppermute | solution.py:574
  189.6 10.5 %collective-permute-start.30 = (bf16[256,512]{1,0:T(8,128)(2,1)S(1)}, bf16[256,512]{1,0:T(8,128)(2,1)S(1)}, u32[]{:S(2)}, u32[]{:S(2)}) collective-permute-start(bf16[256,512]{1,0:T(8,128)(2,1)S(1)} %get-tuple-element.115), channel_id=1, source_target_pairs={{0,6},{1,7},{2,0},{3,1},{4,2},{5,3},{6,4},{7,5},{8,14},{9,15},{10,... | collective-permute-start | bytes 786440 | tf_op jit(solution)/shard_map/ppermute | solution.py:574
  191.6 9.9 %collective-permute-start.31 = (bf16[256,512]{1,0:T(8,128)(2,1)S(1)}, bf16[256,512]{1,0:T(8,128)(2,1)S(1)}, u32[]{:S(2)}, u32[]{:S(2)}) collective-permute-start(bf16[256,512]{1,0:T(8,128)(2,1)S(1)} %get-tuple-element.116), channel_id=1, source_target_pairs={{0,4},{1,5},{2,6},{3,7},{4,0},{5,1},{6,2},{7,3},{8,12},{9,13},{10,... | collective-permute-start | bytes 786440 | tf_op jit(solution)/shard_map/ppermute | solution.py:574
  (23 other events, 251.3 us)
Sparse Core Ops, SparseCore 0:
  33.5 107.4 all-gather.2

commit v6 on v4

--- a/solution.py
+++ b/solution.py
@@ -242,7 +242,7 @@
         in_specs=[SMEM_SPEC] + vspecs(1) + hspecs(1),
         out_specs=vspecs(4),
         scratch_shapes=SHARE_SCRATCH,
-        compiler_params=params(52),
+        compiler_params=params(48),
         name="shares",
     )(where, y, weight)
 
@@ -284,7 +284,7 @@
             pltpu.VMEM((HALO + ROWS, LANES), F32),
             pltpu.VMEM((16 + ROWS, LANES), F32),
         ] + SHARE_SCRATCH,
-        compiler_params=params(52),
+        compiler_params=params(48),
         name="mr_op",
     )(where, q, k, v, halo, feat, toep, weight)
 
@@ -463,11 +463,11 @@
     y_ref, o0, o1, o2, o3, qx, wbuf, sems,
 ):
     copies = share_loads(where_ref, w_ref, wbuf, sems, 1)
-    zl, k = where_ref[3], where_ref[4]
+    y, zl, k = where_ref[2], where_ref[3], where_ref[4]
     rates = rates_ref[...]
-    above = y1_ref[...]
-    above = above + jnp.exp(-rates * (2.0 * ROWS * NZ)) * y2_ref[...]
-    above = above + jnp.exp(-rates * (4.0 * ROWS * NZ)) * y3_ref[...]
+    above = jnp.where(y >= 1, y1_ref[...], 0.0)
+    above = above + jnp.where(y >= 2, jnp.exp(-rates * (2.0 * ROWS * NZ)) * y2_ref[...], 0.0)
+    above = above + jnp.where(y >= 3, jnp.exp(-rates * (4.0 * ROWS * NZ)) * y3_ref[...], 0.0)
     chip = carry_ref[...] + jnp.exp(-rates * (zl * (2 * ROWS)).astype(F32)) * above
     full = jnp.where(k == 0, chip, jnp.exp(-rates * (1.0 * ROWS)) * chip + other_ref[...])
     for block in range(WIDTH // LANES):
@@ -492,7 +492,7 @@
         in_specs=[SMEM_SPEC] + vspecs(10) + hspecs(1),
         out_specs=vspecs(5),
         scratch_shapes=[pltpu.VMEM((16 + ROWS, LANES), F32)] + SHARE_SCRATCH,
-        compiler_params=params(52),
+        compiler_params=params(48),
         name="li_outer",
     )(where, conv, q, feat, leave, rates, carry, other, *above, weight)
 
@@ -527,16 +527,15 @@
     ]
 
 
-GATHER_ORDER = [
-    ctx_of(y if z % 2 == 0 else NY - 1 - y, z, k)
-    for z in range(NZ) for y in range(NY) for k in range(NC)
-]
+GATHER_RING = [
+    (y, z) for z in range(NZ) for y in (range(1, NY) if z % 2 == 0 else range(NY - 1, 0, -1))
+] + [(0, z) for z in range(NZ - 1, -1, -1)]
+GATHER_ORDER = [ctx_of(y, z, k) for y, z in GATHER_RING for k in range(NC)]
 
 
 def gathered_at(y, z, k):
-    if z % 2 == 1:
-        y = NY - 1 - y
-    return (z * NY + y) * NC + k
+    along = y - 1 if z % 2 == 0 else NY - 1 - y
+    return jnp.where(y == 0, NZ * (NY - 1) + NZ - 1 - z, z * (NY - 1) + along) * NC + k
 
 
 def weight_moves():
@@ -613,17 +612,10 @@
     chip = chip_state(where, load, other_load, lane_rates)
     before = [lax.ppermute(chip, "ctx", z_shift(s)) for s in (1, 2, 3)]
     (fresh_q,) = project(where, pieces, weights, (0,))
+    *before, fresh_q = tied(*before, fresh_q)
     conv = li_inner(product, toep_li)
-    *before, fresh_q, conv = tied(*before, fresh_q, conv)
     line_total, line_carry = line_state(where, [chip] + before, lane_rates)
-    above = []
-    for s in (1, 2, 3):
-        pairs = [
-            (ctx_of(a, b, c), ctx_of(a + s, b, c))
-            for a in range(NY - s) for b in range(NZ) for c in range(NC)
-        ]
-        above.append(lax.ppermute(line_total, "ctx", pairs))
-
+    above = [lax.ppermute(line_total, "ctx", y_shift(s)) for s in (1, 2, 3)]
     gated_two, *other_two = li_outer(
         where, conv, fresh_q, featurizer_li, leave, lane_rates,
         line_carry, other_load, above, out_li,

time: 211 us -> 205 us (0.972)
  waiting for transfers between devices: 83.1 us -> 88.8 us
  local copies, waits for them, and re-layouts: 10.2 us -> 5.97 us
  starting transfers between devices: 66.9 us -> 62.9 us
  Pallas kernels: 34.4 us -> 31.3 us
    unnamed x33 -> x29, local copies, waits for them, and re-layouts: 10.1 us -> 5.88 us
    ppermute x3, starting transfers between devices: 9.09 us -> 5.11 us  [body(): above = [lax.ppermute(line_total, 'ctx', y_shift(s)) for s in (1, 2, 3)]]
  transfers between devices with their start and end apart: 32 -> 32, of which waited for: 18 -> 18; matrix products, arithmetic and copies ran while one was open for 1% -> 1% of each run, Pallas kernels for 11% -> 10%
where the time goes in v6:
time: 205 us; the launch traced here: 204 us
  waiting for transfers between devices  88.8 us (43%)
  starting transfers between devices  62.9 us (31%)
  Pallas kernels  31.3 us (15%)
  between operations  13.8 us (7%)
  local copies, waits for them, and re-layouts  5.97 us (3%)
    all_gather x1, waiting for transfers between devices, body(): weights = lax.all_gather(moved, 'ctx', axis_index_groups=[GATHER_ORDER])  18.8 us
    ppermute x2, waiting for transfers between devices, sum_shares(): crossed = lax.ppermute(total_other, 'mp', H_SWAP)  18.8 us
    ppermute x6, starting transfers between devices, sum_shares(): got = [lax.ppermute(other[d], 'mp', x_shift(d)) for d in (1, 3, 2)]  15.7 us
    ppermute x6, waiting for transfers between devices, sum_shares(): got = [lax.ppermute(other[d], 'mp', x_shift(d)) for d in (1, 3, 2)]  14.7 us
    ppermute x3, waiting for transfers between devices, body(): lax.ppermute(crossed, 'mp', x_shift(d))  10.7 us
    ppermute x1, waiting for transfers between devices, body(): moved = lax.ppermute(in_weight, ('ctx', 'mp'), weight_moves())  10.4 us
    ppermute x1, waiting for transfers between devices, body(): crossed = lax.ppermute(extended, 'mp', H_SWAP)  10.2 us
    ppermute x2, starting transfers between devices, sum_shares(): crossed = lax.ppermute(total_other, 'mp', H_SWAP)  9.77 us
  transfers between devices with their start and end apart: 32, of which 18 were waited for; matrix products, arithmetic and copies ran while one was open for 1% of the time, Pallas kernels for 10%

profile of v6, /device:TPU:2, one launch (start us, length us, event | category | flops | bytes accessed | tf_op | source)
XLA Modules:
  0.0 204.1 jit_solution(633747872911454765)
XLA Ops:
  6.5 2.9 %collective-permute-start.1 = (bf16[3,512,128]{2,1,0:T(8,128)(2,1)}, bf16[3,512,128]{2,1,0:T(8,128)(2,1)}, u32[]{:S(2)}, u32[]{:S(2)}) collective-permute-start(bf16[3,512,128]{2,1,0:T(8,128)(2,1)} %param.19), channel_id=1, source_target_pairs={{0,16},{1,48},{2,80},{3,112},{4,144},{5,176},{6,208},{7,240},{8,24... | collective-permute-start | bytes 1179656 | tf_op jit(solution)/shard_map/ppermute | solution.py:589
  15.8 3.1 %toeplitz.1.toep_ref = bf16[4096,256]{1,0:T(8,128)(2,1)S(1)} custom-call(f32[128,32]{1,0:T(8,128)S(1)} %copy.14.taps_ref), custom_call_target="tpu_custom_call" | custom-call | tf_op jit(solution)/shard_map/toeplitz/pallas_call | solution.py:108
  18.9 10.4 %collective-permute-done.1 = bf16[3,512,128]{2,1,0:T(8,128)(2,1)} collective-permute-done((bf16[3,512,128]{2,1,0:T(8,128)(2,1)}, bf16[3,512,128]{2,1,0:T(8,128)(2,1)}, u32[]{:S(2)}, u32[]{:S(2)}) %collective-permute-start.1) | collective-permute-done | bytes 393248 | tf_op jit(solution)/shard_map/ppermute | solution.py:589
  30.4 4.0 %mr_op.1 = (bf16[256,512]{1,0:T(8,128)(2,1)S(1)}, bf16[256,512]{1,0:T(8,128)(2,1)S(1)}, bf16[256,512]{1,0:T(8,128)(2,1)S(1)}, bf16[256,512]{1,0:T(8,128)(2,1)S(1)}, bf16[256,512]{1,0:T(8,128)(2,1)S(1)}) custom-call(s32[5]{0:T(128)S(1)} %stack.23.where_ref, bf16[256,512]{1,0:T(8,128)(2,1)S(1)} %get-tuple-element.59.q_ref, ...), custom_call_target="tpu_custom_call" | custom-call | tf_op jit(solution)/shard_map/mr_op/pallas_call | solution.py:277
  34.4 9.8 %collective-permute-start.2 = (bf16[256,512]{1,0:T(8,128)(2,1)S(1)}, bf16[256,512]{1,0:T(8,128)(2,1)S(1)}, u32[]{:S(2)}, u32[]{:S(2)}) collective-permute-start(bf16[256,512]{1,0:T(8,128)(2,1)S(1)} %get-tuple-element.66), channel_id=1, source_target_pairs={{0,2},{1,3},{2,4},{3,5},{4,6},{5,7},{6,0},{7,1},{8,10},{9,11},{10,... | collective-permute-start | bytes 786440 | tf_op jit(solution)/shard_map/ppermute | solution.py:565
  47.8 5.1 %collective-permute-done.2 = bf16[256,512]{1,0:T(8,128)(2,1)S(1)} collective-permute-done((bf16[256,512]{1,0:T(8,128)(2,1)S(1)}, bf16[256,512]{1,0:T(8,128)(2,1)S(1)}, u32[]{:S(2)}, u32[]{:S(2)}) %collective-permute-start.2) | collective-permute-done | bytes 262176 | tf_op jit(solution)/shard_map/ppermute | solution.py:565
  55.1 5.9 %collective-permute-start.5 = (bf16[256,512]{1,0:T(8,128)(2,1)S(1)}, bf16[256,512]{1,0:T(8,128)(2,1)S(1)}, u32[]{:S(2)}, u32[]{:S(2)}) collective-permute-start(bf16[256,512]{1,0:T(8,128)(2,1)S(1)} %add_convert_fusion.3), channel_id=1, source_target_pairs={{0,1},{1,0},{2,3},{3,2},{4,5},{5,4},{6,7},{7,6},{8,9},{9,8},{10,11... | collective-permute-start | bytes 786440 | tf_op jit(solution)/shard_map/ppermute | solution.py:570
  64.9 11.9 %collective-permute-done.5 = bf16[256,512]{1,0:T(8,128)(2,1)S(1)} collective-permute-done((bf16[256,512]{1,0:T(8,128)(2,1)S(1)}, bf16[256,512]{1,0:T(8,128)(2,1)S(1)}, u32[]{:S(2)}, u32[]{:S(2)}) %collective-permute-start.5) | collective-permute-done | bytes 262176 | tf_op jit(solution)/shard_map/ppermute | solution.py:570
  79.3 4.1 %collective-permute-start.13 = (bf16[272,512]{1,0:T(8,128)(2,1)S(1)}, bf16[272,512]{1,0:T(8,128)(2,1)S(1)}, u32[]{:S(2)}, u32[]{:S(2)}) collective-permute-start(bf16[272,512]{1,0:T(8,128)(2,1)S(1)} %pad_maximum_fusion.refs_0_), channel_id=1, source_target_pairs={{0,1},{1,0},{2,3},{3,2},{4,5},{5,4},{6,7},{7,6},{8,9},{9,8},{10,11... | collective-permute-start | bytes 835592 | tf_op jit(solution)/shard_map/ppermute | solution.py:603
  83.8 3.8 %prep.1 = (bf16[4096,256]{1,0:T(8,128)(2,1)S(1)}, f32[256,512]{1,0:T(8,128)S(1)}, f32[256,512]{1,0:T(8,128)S(1)}, f32[16,512]{1,0:T(8,128)S(1)}) custom-call(f32[16,32]{1,0:T(8,128)S(1)} %bitcast.8, f32[16,32]{1,0:T(8,128)S(1)} %bitcast.9), custom_call_target="tpu_custom_call" | custom-call | tf_op jit(solution)/shard_map/prep/pallas_call | solution.py:166
  88.9 3.0 %collective-permute-start.11 = (bf16[272,512]{1,0:T(8,128)(2,1)S(1)}, bf16[272,512]{1,0:T(8,128)(2,1)S(1)}, u32[]{:S(2)}, u32[]{:S(2)}) collective-permute-start(bf16[272,512]{1,0:T(8,128)(2,1)S(1)} %pad_maximum_fusion.refs_0_), channel_id=1, source_target_pairs={{0,4},{1,5},{2,6},{3,7},{4,0},{5,1},{6,2},{7,3},{8,12},{9,13},{10,... | collective-permute-start | bytes 835592 | tf_op jit(solution)/shard_map/ppermute | solution.py:604
  93.5 10.2 %collective-permute-done.13.refs_4_ = bf16[272,512]{1,0:T(8,128)(2,1)S(1)} collective-permute-done((bf16[272,512]{1,0:T(8,128)(2,1)S(1)}, bf16[272,512]{1,0:T(8,128)(2,1)S(1)}, u32[]{:S(2)}, u32[]{:S(2)}) %collective-permute-start.13) | collective-permute-done | bytes 278560 | tf_op jit(solution)/shard_map/ppermute | solution.py:603
  103.7 3.0 %collective-permute-start.15 = (bf16[272,512]{1,0:T(8,128)(2,1)S(1)}, bf16[272,512]{1,0:T(8,128)(2,1)S(1)}, u32[]{:S(2)}, u32[]{:S(2)}) collective-permute-start(bf16[272,512]{1,0:T(8,128)(2,1)S(1)} %collective-permute-done.13.refs_4_), channel_id=1, source_target_pairs={{0,4},{1,5},{2,6},{3,7},{4,0},{5,1},{6,2},{7,3},{8,12},{9,13},{10,... | collective-permute-start | bytes 835592 | tf_op jit(solution)/shard_map/ppermute | solution.py:607
  108.3 5.0 %collective-permute-done.14.refs_5_ = bf16[272,512]{1,0:T(8,128)(2,1)S(1)} collective-permute-done((bf16[272,512]{1,0:T(8,128)(2,1)S(1)}, bf16[272,512]{1,0:T(8,128)(2,1)S(1)}, u32[]{:S(2)}, u32[]{:S(2)}) %collective-permute-start.14) | collective-permute-done | bytes 278560 | tf_op jit(solution)/shard_map/ppermute | solution.py:607
  114.9 4.1 %collective-permute-done.16.refs_7_ = bf16[272,512]{1,0:T(8,128)(2,1)S(1)} collective-permute-done((bf16[272,512]{1,0:T(8,128)(2,1)S(1)}, bf16[272,512]{1,0:T(8,128)(2,1)S(1)}, u32[]{:S(2)}, u32[]{:S(2)}) %collective-permute-start.16) | collective-permute-done | bytes 278560 | tf_op jit(solution)/shard_map/ppermute | solution.py:607
  119.2 18.8 %all-gather.3.cloned.1.call-done = bf16[96,512,128]{2,1,0:T(8,128)(2,1)} async-done(((bf16[3,512,128]{2,1,0:T(8,128)(2,1)}), bf16[96,512,128]{2,1,0:T(8,128)(2,1)}) %all-gather.3.cloned.1.call-update) | async-done | bytes 12582928 | tf_op jit(solution)/shard_map/all_gather | solution.py:594
  138.0 5.1 %project.2 = (bf16[272,512]{1,0:T(8,128)(2,1)S(1)}, bf16[272,512]{1,0:T(8,128)(2,1)S(1)}) custom-call(s32[5]{0:T(128)S(1)} %stack.23.where_ref, bf16[8,272,512]{2,1,0:T(8,128)(2,1)S(1)} %packed.1.hidden_ref, bf16[32,3,512,128]{3,2,1,0:T(8,128)(2,1)} %bitcast.10), custom_call_target="tpu_custom_call" | custom-call | tf_op jit(solution)/shard_map/project/pallas_call | solution.py:344
  150.6 3.8 %project.3.q_ref = bf16[272,512]{1,0:T(8,128)(2,1)S(1)} custom-call(s32[5]{0:T(128)S(1)} %stack.23.where_ref, bf16[8,272,512]{2,1,0:T(8,128)(2,1)S(1)} %packed.1.hidden_ref, bf16[32,3,512,128]{3,2,1,0:T(8,128)(2,1)} %bitcast.11), custom_call_target="tpu_custom_call" | custom-call | tf_op jit(solution)/shard_map/project/pallas_call | solution.py:344
  156.2 2.9 %collective-permute-start.22 = (f32[16,512]{1,0:T(8,128)S(1)}, f32[16,512]{1,0:T(8,128)S(1)}, u32[]{:S(2)}, u32[]{:S(2)}) collective-permute-start(f32[16,512]{1,0:T(8,128)S(1)} %get-tuple-element.98), channel_id=1, source_target_pairs={{0,128},{8,136},{16,144},{24,152},{32,160},{40,168},{48,176},{56,1... | collective-permute-start | bytes 98312 | tf_op jit(solution)/shard_map/ppermute | solution.py:618
  163.0 3.5 %li_outer.1 = (bf16[256,512]{1,0:T(8,128)(2,1)S(1)}, bf16[256,512]{1,0:T(8,128)(2,1)S(1)}, bf16[256,512]{1,0:T(8,128)(2,1)S(1)}, bf16[256,512]{1,0:T(8,128)(2,1)S(1)}, bf16[256,512]{1,0:T(8,128)(2,1)S(1)}) custom-call(s32[5]{0:T(128)S(1)} %stack.23.where_ref, f32[256,512]{1,0:T(8,128)S(1)} %li_inner.1.conv_ref, bf16[272,512]{1,0:T(8,128)(2,1)S(1)} %project.3.q_ref, ...), custom_call_target="tpu_custom_call" | custom-call | tf_op jit(solution)/shard_map/li_outer/pallas_call | solution.py:489
  173.0 2.9 %collective-permute-done.24 = bf16[256,512]{1,0:T(8,128)(2,1)S(1)} collective-permute-done((bf16[256,512]{1,0:T(8,128)(2,1)S(1)}, bf16[256,512]{1,0:T(8,128)(2,1)S(1)}, u32[]{:S(2)}, u32[]{:S(2)}) %collective-permute-start.24) | collective-permute-done | bytes 262176 | tf_op jit(solution)/shard_map/ppermute | solution.py:565
  177.4 3.1 %collective-permute-done.26 = bf16[256,512]{1,0:T(8,128)(2,1)S(1)} collective-permute-done((bf16[256,512]{1,0:T(8,128)(2,1)S(1)}, bf16[256,512]{1,0:T(8,128)(2,1)S(1)}, u32[]{:S(2)}, u32[]{:S(2)}) %collective-permute-start.26) | collective-permute-done | bytes 262176 | tf_op jit(solution)/shard_map/ppermute | solution.py:565
  180.7 3.8 %collective-permute-start.27 = (bf16[256,512]{1,0:T(8,128)(2,1)S(1)}, bf16[256,512]{1,0:T(8,128)(2,1)S(1)}, u32[]{:S(2)}, u32[]{:S(2)}) collective-permute-start(bf16[256,512]{1,0:T(8,128)(2,1)S(1)} %add_convert_fusion.1), channel_id=1, source_target_pairs={{0,1},{1,0},{2,3},{3,2},{4,5},{5,4},{6,7},{7,6},{8,9},{9,8},{10,11... | collective-permute-start | bytes 786440 | tf_op jit(solution)/shard_map/ppermute | solution.py:570
  188.3 6.9 %collective-permute-done.27 = bf16[256,512]{1,0:T(8,128)(2,1)S(1)} collective-permute-done((bf16[256,512]{1,0:T(8,128)(2,1)S(1)}, bf16[256,512]{1,0:T(8,128)(2,1)S(1)}, u32[]{:S(2)}, u32[]{:S(2)}) %collective-permute-start.27) | collective-permute-done | bytes 262176 | tf_op jit(solution)/shard_map/ppermute | solution.py:570
  (93 shorter events, 53.2 us)
Async XLA Ops:
  6.5 131.4 %all-gather.3.cloned.1.call-start = ((), (), s32[]{:S(2)}) async-start(), calls=%async_computation | async-start | bytes 12976128 | tf_op jit(solution)/shard_map/all_gather | solution.py:594
  6.5 22.8 %collective-permute-start.1 = (bf16[3,512,128]{2,1,0:T(8,128)(2,1)}, bf16[3,512,128]{2,1,0:T(8,128)(2,1)}, u32[]{:S(2)}, u32[]{:S(2)}) collective-permute-start(bf16[3,512,128]{2,1,0:T(8,128)(2,1)} %param.19), channel_id=1, source_target_pairs={{0,16},{1,48},{2,80},{3,112},{4,144},{5,176},{6,208},{7,240},{8,24... | collective-permute-start | bytes 1179656 | tf_op jit(solution)/shard_map/ppermute | solution.py:589
  34.4 18.5 %collective-permute-start.2 = (bf16[256,512]{1,0:T(8,128)(2,1)S(1)}, bf16[256,512]{1,0:T(8,128)(2,1)S(1)}, u32[]{:S(2)}, u32[]{:S(2)}) collective-permute-start(bf16[256,512]{1,0:T(8,128)(2,1)S(1)} %get-tuple-element.66), channel_id=1, source_target_pairs={{0,2},{1,3},{2,4},{3,5},{4,6},{5,7},{6,0},{7,1},{8,10},{9,11},{10,... | collective-permute-start | bytes 786440 | tf_op jit(solution)/shard_map/ppermute | solution.py:565
  44.2 10.8 %collective-permute-start.3 = (bf16[256,512]{1,0:T(8,128)(2,1)S(1)}, bf16[256,512]{1,0:T(8,128)(2,1)S(1)}, u32[]{:S(2)}, u32[]{:S(2)}) collective-permute-start(bf16[256,512]{1,0:T(8,128)(2,1)S(1)} %get-tuple-element.67), channel_id=1, source_target_pairs={{0,6},{1,7},{2,0},{3,1},{4,2},{5,3},{6,4},{7,5},{8,14},{9,15},{10,... | collective-permute-start | bytes 786440 | tf_op jit(solution)/shard_map/ppermute | solution.py:565
  44.2 10.8 %collective-permute-start.4 = (bf16[256,512]{1,0:T(8,128)(2,1)S(1)}, bf16[256,512]{1,0:T(8,128)(2,1)S(1)}, u32[]{:S(2)}, u32[]{:S(2)}) collective-permute-start(bf16[256,512]{1,0:T(8,128)(2,1)S(1)} %get-tuple-element.68), channel_id=1, source_target_pairs={{0,4},{1,5},{2,6},{3,7},{4,0},{5,1},{6,2},{7,3},{8,12},{9,13},{10,... | collective-permute-start | bytes 786440 | tf_op jit(solution)/shard_map/ppermute | solution.py:565
  55.1 21.7 %collective-permute-start.5 = (bf16[256,512]{1,0:T(8,128)(2,1)S(1)}, bf16[256,512]{1,0:T(8,128)(2,1)S(1)}, u32[]{:S(2)}, u32[]{:S(2)}) collective-permute-start(bf16[256,512]{1,0:T(8,128)(2,1)S(1)} %add_convert_fusion.3), channel_id=1, source_target_pairs={{0,1},{1,0},{2,3},{3,2},{4,5},{5,4},{6,7},{7,6},{8,9},{9,8},{10,11... | collective-permute-start | bytes 786440 | tf_op jit(solution)/shard_map/ppermute | solution.py:570
  61.1 15.8 %collective-permute-start.6 = (bf16[256,512]{1,0:T(8,128)(2,1)S(1)}, bf16[256,512]{1,0:T(8,128)(2,1)S(1)}, u32[]{:S(2)}, u32[]{:S(2)}) collective-permute-start(bf16[256,512]{1,0:T(8,128)(2,1)S(1)} %get-tuple-element.76), channel_id=1, source_target_pairs={{0,2},{1,3},{2,4},{3,5},{4,6},{5,7},{6,0},{7,1},{8,10},{9,11},{10,... | collective-permute-start | bytes 786440 | tf_op jit(solution)/shard_map/ppermute | solution.py:571
  61.4 15.6 %collective-permute-start.7 = (bf16[256,512]{1,0:T(8,128)(2,1)S(1)}, bf16[256,512]{1,0:T(8,128)(2,1)S(1)}, u32[]{:S(2)}, u32[]{:S(2)}) collective-permute-start(bf16[256,512]{1,0:T(8,128)(2,1)S(1)} %get-tuple-element.77), channel_id=1, source_target_pairs={{0,6},{1,7},{2,0},{3,1},{4,2},{5,3},{6,4},{7,5},{8,14},{9,15},{10,... | collective-permute-start | bytes 786440 | tf_op jit(solution)/shard_map/ppermute | solution.py:571
  63.1 13.8 %collective-permute-start.8 = (bf16[256,512]{1,0:T(8,128)(2,1)S(1)}, bf16[256,512]{1,0:T(8,128)(2,1)S(1)}, u32[]{:S(2)}, u32[]{:S(2)}) collective-permute-start(bf16[256,512]{1,0:T(8,128)(2,1)S(1)} %get-tuple-element.78), channel_id=1, source_target_pairs={{0,4},{1,5},{2,6},{3,7},{4,0},{5,1},{6,2},{7,3},{8,12},{9,13},{10,... | collective-permute-start | bytes 786440 | tf_op jit(solution)/shard_map/ppermute | solution.py:571
  79.3 24.4 %collective-permute-start.13 = (bf16[272,512]{1,0:T(8,128)(2,1)S(1)}, bf16[272,512]{1,0:T(8,128)(2,1)S(1)}, u32[]{:S(2)}, u32[]{:S(2)}) collective-permute-start(bf16[272,512]{1,0:T(8,128)(2,1)S(1)} %pad_maximum_fusion.refs_0_), channel_id=1, source_target_pairs={{0,1},{1,0},{2,3},{3,2},{4,5},{5,4},{6,7},{7,6},{8,9},{9,8},{10,11... | collective-permute-start | bytes 835592 | tf_op jit(solution)/shard_map/ppermute | solution.py:603
  83.4 23.3 %collective-permute-start.10 = (bf16[272,512]{1,0:T(8,128)(2,1)S(1)}, bf16[272,512]{1,0:T(8,128)(2,1)S(1)}, u32[]{:S(2)}, u32[]{:S(2)}) collective-permute-start(bf16[272,512]{1,0:T(8,128)(2,1)S(1)} %pad_maximum_fusion.refs_0_), channel_id=1, source_target_pairs={{0,2},{1,3},{2,4},{3,5},{4,6},{5,7},{6,0},{7,1},{8,10},{9,11},{10,... | collective-permute-start | bytes 835592 | tf_op jit(solution)/shard_map/ppermute | solution.py:604
  88.9 19.4 %collective-permute-start.11 = (bf16[272,512]{1,0:T(8,128)(2,1)S(1)}, bf16[272,512]{1,0:T(8,128)(2,1)S(1)}, u32[]{:S(2)}, u32[]{:S(2)}) collective-permute-start(bf16[272,512]{1,0:T(8,128)(2,1)S(1)} %pad_maximum_fusion.refs_0_), channel_id=1, source_target_pairs={{0,4},{1,5},{2,6},{3,7},{4,0},{5,1},{6,2},{7,3},{8,12},{9,13},{10,... | collective-permute-start | bytes 835592 | tf_op jit(solution)/shard_map/ppermute | solution.py:604
  91.9 16.4 %collective-permute-start.12 = (bf16[272,512]{1,0:T(8,128)(2,1)S(1)}, bf16[272,512]{1,0:T(8,128)(2,1)S(1)}, u32[]{:S(2)}, u32[]{:S(2)}) collective-permute-start(bf16[272,512]{1,0:T(8,128)(2,1)S(1)} %pad_maximum_fusion.refs_0_), channel_id=1, source_target_pairs={{0,6},{1,7},{2,0},{3,1},{4,2},{5,3},{6,4},{7,5},{8,14},{9,15},{10,... | collective-permute-start | bytes 835592 | tf_op jit(solution)/shard_map/ppermute | solution.py:604
  103.7 9.6 %collective-permute-start.14 = (bf16[272,512]{1,0:T(8,128)(2,1)S(1)}, bf16[272,512]{1,0:T(8,128)(2,1)S(1)}, u32[]{:S(2)}, u32[]{:S(2)}) collective-permute-start(bf16[272,512]{1,0:T(8,128)(2,1)S(1)} %collective-permute-done.13.refs_4_), channel_id=1, source_target_pairs={{0,2},{1,3},{2,4},{3,5},{4,6},{5,7},{6,0},{7,1},{8,10},{9,11},{10,... | collective-permute-start | bytes 835592 | tf_op jit(solution)/shard_map/ppermute | solution.py:607
  103.7 11.1 %collective-permute-start.15 = (bf16[272,512]{1,0:T(8,128)(2,1)S(1)}, bf16[272,512]{1,0:T(8,128)(2,1)S(1)}, u32[]{:S(2)}, u32[]{:S(2)}) collective-permute-start(bf16[272,512]{1,0:T(8,128)(2,1)S(1)} %collective-permute-done.13.refs_4_), channel_id=1, source_target_pairs={{0,4},{1,5},{2,6},{3,7},{4,0},{5,1},{6,2},{7,3},{8,12},{9,13},{10,... | collective-permute-start | bytes 835592 | tf_op jit(solution)/shard_map/ppermute | solution.py:607
  106.7 12.3 %collective-permute-start.16 = (bf16[272,512]{1,0:T(8,128)(2,1)S(1)}, bf16[272,512]{1,0:T(8,128)(2,1)S(1)}, u32[]{:S(2)}, u32[]{:S(2)}) collective-permute-start(bf16[272,512]{1,0:T(8,128)(2,1)S(1)} %collective-permute-done.13.refs_4_), channel_id=1, source_target_pairs={{0,6},{1,7},{2,0},{3,1},{4,2},{5,3},{6,4},{7,5},{8,14},{9,15},{10,... | collective-permute-start | bytes 835592 | tf_op jit(solution)/shard_map/ppermute | solution.py:607
  145.6 8.8 %collective-permute-start.18 = (f32[16,512]{1,0:T(8,128)S(1)}, f32[16,512]{1,0:T(8,128)S(1)}, u32[]{:S(2)}, u32[]{:S(2)}) collective-permute-start(f32[16,512]{1,0:T(8,128)S(1)} %chip_state.1.c0), channel_id=1, source_target_pairs={{0,16},{8,24},{16,32},{24,40},{32,48},{40,56},{48,0},{56,8},{64,80... | collective-permute-start | bytes 98312 | tf_op jit(solution)/shard_map/ppermute | solution.py:613
  166.5 9.4 %collective-permute-start.24 = (bf16[256,512]{1,0:T(8,128)(2,1)S(1)}, bf16[256,512]{1,0:T(8,128)(2,1)S(1)}, u32[]{:S(2)}, u32[]{:S(2)}) collective-permute-start(bf16[256,512]{1,0:T(8,128)(2,1)S(1)} %get-tuple-element.100), channel_id=1, source_target_pairs={{0,2},{1,3},{2,4},{3,5},{4,6},{5,7},{6,0},{7,1},{8,10},{9,11},{10,... | collective-permute-start | bytes 786440 | tf_op jit(solution)/shard_map/ppermute | solution.py:565
  168.3 9.2 %collective-permute-start.25 = (bf16[256,512]{1,0:T(8,128)(2,1)S(1)}, bf16[256,512]{1,0:T(8,128)(2,1)S(1)}, u32[]{:S(2)}, u32[]{:S(2)}) collective-permute-start(bf16[256,512]{1,0:T(8,128)(2,1)S(1)} %get-tuple-element.101), channel_id=1, source_target_pairs={{0,6},{1,7},{2,0},{3,1},{4,2},{5,3},{6,4},{7,5},{8,14},{9,15},{10,... | collective-permute-start | bytes 786440 | tf_op jit(solution)/shard_map/ppermute | solution.py:565
  168.8 11.7 %collective-permute-start.26 = (bf16[256,512]{1,0:T(8,128)(2,1)S(1)}, bf16[256,512]{1,0:T(8,128)(2,1)S(1)}, u32[]{:S(2)}, u32[]{:S(2)}) collective-permute-start(bf16[256,512]{1,0:T(8,128)(2,1)S(1)} %get-tuple-element.102), channel_id=1, source_target_pairs={{0,4},{1,5},{2,6},{3,7},{4,0},{5,1},{6,2},{7,3},{8,12},{9,13},{10,... | collective-permute-start | bytes 786440 | tf_op jit(solution)/shard_map/ppermute | solution.py:565
  180.7 14.5 %collective-permute-start.27 = (bf16[256,512]{1,0:T(8,128)(2,1)S(1)}, bf16[256,512]{1,0:T(8,128)(2,1)S(1)}, u32[]{:S(2)}, u32[]{:S(2)}) collective-permute-start(bf16[256,512]{1,0:T(8,128)(2,1)S(1)} %add_convert_fusion.1), channel_id=1, source_target_pairs={{0,1},{1,0},{2,3},{3,2},{4,5},{5,4},{6,7},{7,6},{8,9},{9,8},{10,11... | collective-permute-start | bytes 786440 | tf_op jit(solution)/shard_map/ppermute | solution.py:570
  184.5 10.8 %collective-permute-start.28 = (bf16[256,512]{1,0:T(8,128)(2,1)S(1)}, bf16[256,512]{1,0:T(8,128)(2,1)S(1)}, u32[]{:S(2)}, u32[]{:S(2)}) collective-permute-start(bf16[256,512]{1,0:T(8,128)(2,1)S(1)} %get-tuple-element.110), channel_id=1, source_target_pairs={{0,2},{1,3},{2,4},{3,5},{4,6},{5,7},{6,0},{7,1},{8,10},{9,11},{10,... | collective-permute-start | bytes 786440 | tf_op jit(solution)/shard_map/ppermute | solution.py:571
  184.5 10.8 %collective-permute-start.29 = (bf16[256,512]{1,0:T(8,128)(2,1)S(1)}, bf16[256,512]{1,0:T(8,128)(2,1)S(1)}, u32[]{:S(2)}, u32[]{:S(2)}) collective-permute-start(bf16[256,512]{1,0:T(8,128)(2,1)S(1)} %get-tuple-element.111), channel_id=1, source_target_pairs={{0,6},{1,7},{2,0},{3,1},{4,2},{5,3},{6,4},{7,5},{8,14},{9,15},{10,... | collective-permute-start | bytes 786440 | tf_op jit(solution)/shard_map/ppermute | solution.py:571
  186.5 9.9 %collective-permute-start.30 = (bf16[256,512]{1,0:T(8,128)(2,1)S(1)}, bf16[256,512]{1,0:T(8,128)(2,1)S(1)}, u32[]{:S(2)}, u32[]{:S(2)}) collective-permute-start(bf16[256,512]{1,0:T(8,128)(2,1)S(1)} %get-tuple-element.112), channel_id=1, source_target_pairs={{0,4},{1,5},{2,6},{3,7},{4,0},{5,1},{6,2},{7,3},{8,12},{9,13},{10,... | collective-permute-start | bytes 786440 | tf_op jit(solution)/shard_map/ppermute | solution.py:571
  (22 other events, 243.3 us)
Sparse Core Ops, SparseCore 0:
  29.5 108.4 all-gather.2

commit v7 on v6

--- a/solution.py
+++ b/solution.py
@@ -317,7 +317,7 @@
     copies = []
     for i in range(8):
         e, d = i // 4, i % 4
-        src_y = lax.rem(x + 4 - d, 4)
+        src_y = lax.rem(x + 6 - d, 4)
         for b in range(4):
             odd = 1 - b // 2
             high = odd if e == 1 else 1 - odd
@@ -545,7 +545,7 @@
             for k in range(NC):
                 for x in range(NX):
                     for h in range(NH):
-                        x2, h2, y2 = y, zl // 2, x
+                        x2, h2, y2 = y, zl // 2, (x + 2) % NY
                         l0 = zl % 2
                         odd = 1 - l0
                         outer = h ^ h2
@@ -606,14 +606,13 @@
     toep_li, leave, enter, lane_rates = filters
     far_pieces = [crossed] + [lax.ppermute(crossed, "mp", x_shift(d)) for d in (1, 2, 3)]
     pieces = packed(own_pieces + far_pieces)
-    fresh_k, fresh_v = project(where, pieces, weights, (1, 2))
+    fresh_q, fresh_k, fresh_v = project(where, pieces, weights, (0, 1, 2))
     product, load = li_gate(fresh_k, fresh_v, featurizer_li, enter)
     other_load = lax.ppermute(load, "ctx", CORE_SWAP)
     chip = chip_state(where, load, other_load, lane_rates)
     before = [lax.ppermute(chip, "ctx", z_shift(s)) for s in (1, 2, 3)]
-    (fresh_q,) = project(where, pieces, weights, (0,))
-    *before, fresh_q = tied(*before, fresh_q)
     conv = li_inner(product, toep_li)
+    *before, conv = tied(*before, conv)
     line_total, line_carry = line_state(where, [chip] + before, lane_rates)
     above = [lax.ppermute(line_total, "ctx", y_shift(s)) for s in (1, 2, 3)]
     gated_two, *other_two = li_outer(

time: 205 us -> 205 us (level)
  waiting for transfers between devices: 88.8 us -> 101 us
  starting transfers between devices: 62.9 us -> 51.9 us
  Pallas kernels: 31.3 us -> 29.1 us
    ppermute x6, starting transfers between devices: 15.7 us -> 10.3 us  [sum_shares(): got = [lax.ppermute(other[d], 'mp', x_shift(d)) for d in (1, 3, 2)]]
    ppermute x1, starting transfers between devices: 4.1 us -> 0.09 us  [body(): crossed = lax.ppermute(extended, 'mp', H_SWAP)]
    ppermute x2, starting transfers between devices: 9.77 us -> 6.24 us  [sum_shares(): crossed = lax.ppermute(total_other, 'mp', H_SWAP)]
    ppermute x1, waiting for transfers between devices: 10.2 us -> 13.8 us  [body(): crossed = lax.ppermute(extended, 'mp', H_SWAP)]
    ppermute x2, waiting for transfers between devices: 18.8 us -> 21.4 us  [sum_shares(): crossed = lax.ppermute(total_other, 'mp', H_SWAP)]
    ppermute x6, waiting for transfers between devices: 1.18 us -> 3.43 us  [sum_shares(): got_mine = [lax.ppermute(mine[d], 'mp', x_shift(d)) for d in (1, 3, 2)]]
    pallas_call x2 -> x1, Pallas kernels: 8.91 us -> 6.71 us  [project(): pl.pallas_call(functools.partial(project_kernel, slots), out_shape=[EXT_P...]
  transfers between devices with their start and end apart: 32 -> 32, of which waited for: 18 -> 22; matrix products, arithmetic and copies ran while one was open for 1% -> 1% of each run, Pallas kernels for 10% -> 8%
where the time goes in v7:
time: 205 us; the launch traced here: 203 us
  waiting for transfers between devices  101 us (49%)
  starting transfers between devices  51.9 us (25%)
  Pallas kernels  29.1 us (14%)
  between operations  13.7 us (7%)
  local copies, waits for them, and re-layouts  5.97 us (3%)
    ppermute x2, waiting for transfers between devices, sum_shares(): crossed = lax.ppermute(total_other, 'mp', H_SWAP)  21.4 us
    all_gather x1, waiting for transfers between devices, body(): weights = lax.all_gather(moved, 'ctx', axis_index_groups=[GATHER_ORDER])  19.3 us
    ppermute x6, waiting for transfers between devices, sum_shares(): got = [lax.ppermute(other[d], 'mp', x_shift(d)) for d in (1, 3, 2)]  14.1 us
    ppermute x1, waiting for transfers between devices, body(): crossed = lax.ppermute(extended, 'mp', H_SWAP)  13.8 us
    ppermute x1, waiting for transfers between devices, body(): moved = lax.ppermute(in_weight, ('ctx', 'mp'), weight_moves())  12.3 us
    ppermute x3, waiting for transfers between devices, body(): lax.ppermute(crossed, 'mp', x_shift(d))  11.2 us
    ppermute x6, starting transfers between devices, sum_shares(): got = [lax.ppermute(other[d], 'mp', x_shift(d)) for d in (1, 3, 2)]  10.3 us
    ppermute x6, starting transfers between devices, sum_shares(): got_mine = [lax.ppermute(mine[d], 'mp', x_shift(d)) for d in (1, 3, 2)]  8.82 us
  transfers between devices with their start and end apart: 32, of which 22 were waited for; matrix products, arithmetic and copies ran while one was open for 1% of the time, Pallas kernels for 8%

profile of v7, /device:TPU:2, one launch (start us, length us, event | category | flops | bytes accessed | tf_op | source)
XLA Modules:
  0.0 203.4 jit_solution(17437726954467572294)
XLA Ops:
  6.5 4.3 %collective-permute-start.1 = (bf16[3,512,128]{2,1,0:T(8,128)(2,1)}, bf16[3,512,128]{2,1,0:T(8,128)(2,1)}, u32[]{:S(2)}, u32[]{:S(2)}) collective-permute-start(bf16[3,512,128]{2,1,0:T(8,128)(2,1)} %param.19), channel_id=1, source_target_pairs={{0,144},{1,176},{2,208},{3,240},{4,16},{5,48},{6,80},{7,112},{8,15... | collective-permute-start | bytes 1179656 | tf_op jit(solution)/shard_map/ppermute | solution.py:589
  17.2 3.1 %toeplitz.1.toep_ref = bf16[4096,256]{1,0:T(8,128)(2,1)S(1)} custom-call(f32[128,32]{1,0:T(8,128)S(1)} %copy.14.taps_ref), custom_call_target="tpu_custom_call" | custom-call | tf_op jit(solution)/shard_map/toeplitz/pallas_call | solution.py:108
  20.3 12.3 %collective-permute-done.1 = bf16[3,512,128]{2,1,0:T(8,128)(2,1)} collective-permute-done((bf16[3,512,128]{2,1,0:T(8,128)(2,1)}, bf16[3,512,128]{2,1,0:T(8,128)(2,1)}, u32[]{:S(2)}, u32[]{:S(2)}) %collective-permute-start.1) | collective-permute-done | bytes 393248 | tf_op jit(solution)/shard_map/ppermute | solution.py:589
  33.7 4.0 %mr_op.1 = (bf16[256,512]{1,0:T(8,128)(2,1)S(1)}, bf16[256,512]{1,0:T(8,128)(2,1)S(1)}, bf16[256,512]{1,0:T(8,128)(2,1)S(1)}, bf16[256,512]{1,0:T(8,128)(2,1)S(1)}, bf16[256,512]{1,0:T(8,128)(2,1)S(1)}) custom-call(s32[5]{0:T(128)S(1)} %stack.23.where_ref, bf16[256,512]{1,0:T(8,128)(2,1)S(1)} %get-tuple-element.60.q_ref, ...), custom_call_target="tpu_custom_call" | custom-call | tf_op jit(solution)/shard_map/mr_op/pallas_call | solution.py:277
  37.7 4.6 %collective-permute-start.2 = (bf16[256,512]{1,0:T(8,128)(2,1)S(1)}, bf16[256,512]{1,0:T(8,128)(2,1)S(1)}, u32[]{:S(2)}, u32[]{:S(2)}) collective-permute-start(bf16[256,512]{1,0:T(8,128)(2,1)S(1)} %get-tuple-element.67), channel_id=1, source_target_pairs={{0,2},{1,3},{2,4},{3,5},{4,6},{5,7},{6,0},{7,1},{8,10},{9,11},{10,... | collective-permute-start | bytes 786440 | tf_op jit(solution)/shard_map/ppermute | solution.py:565
  43.8 2.1 %shares.2 = (bf16[256,512]{1,0:T(8,128)(2,1)S(1)}, bf16[256,512]{1,0:T(8,128)(2,1)S(1)}, bf16[256,512]{1,0:T(8,128)(2,1)S(1)}, bf16[256,512]{1,0:T(8,128)(2,1)S(1)}) custom-call(s32[5]{0:T(128)S(1)} %stack.23.where_ref, bf16[256,512]{1,0:T(8,128)(2,1)S(1)} %get-tuple-element.70.y_ref, bf16[512,4096]{1,0:T(8,128)(2,1)S(1)} %copy-done), custom_call_target="tpu_custom_call" | custom-call | tf_op jit(solution)/shard_map/shares/pallas_call | solution.py:239
  45.9 6.7 %collective-permute-done.2 = bf16[256,512]{1,0:T(8,128)(2,1)S(1)} collective-permute-done((bf16[256,512]{1,0:T(8,128)(2,1)S(1)}, bf16[256,512]{1,0:T(8,128)(2,1)S(1)}, u32[]{:S(2)}, u32[]{:S(2)}) %collective-permute-start.2) | collective-permute-done | bytes 262176 | tf_op jit(solution)/shard_map/ppermute | solution.py:565
  55.9 3.0 %collective-permute-start.8 = (bf16[256,512]{1,0:T(8,128)(2,1)S(1)}, bf16[256,512]{1,0:T(8,128)(2,1)S(1)}, u32[]{:S(2)}, u32[]{:S(2)}) collective-permute-start(bf16[256,512]{1,0:T(8,128)(2,1)S(1)} %get-tuple-element.79), channel_id=1, source_target_pairs={{0,4},{1,5},{2,6},{3,7},{4,0},{5,1},{6,2},{7,3},{8,12},{9,13},{10,... | collective-permute-start | bytes 786440 | tf_op jit(solution)/shard_map/ppermute | solution.py:571
  58.8 16.7 %collective-permute-done.5 = bf16[256,512]{1,0:T(8,128)(2,1)S(1)} collective-permute-done((bf16[256,512]{1,0:T(8,128)(2,1)S(1)}, bf16[256,512]{1,0:T(8,128)(2,1)S(1)}, u32[]{:S(2)}, u32[]{:S(2)}) %collective-permute-start.5) | collective-permute-done | bytes 262176 | tf_op jit(solution)/shard_map/ppermute | solution.py:570
  79.1 3.8 %prep.1 = (bf16[4096,256]{1,0:T(8,128)(2,1)S(1)}, f32[256,512]{1,0:T(8,128)S(1)}, f32[256,512]{1,0:T(8,128)S(1)}, f32[16,512]{1,0:T(8,128)S(1)}) custom-call(f32[16,32]{1,0:T(8,128)S(1)} %bitcast.8, f32[16,32]{1,0:T(8,128)S(1)} %bitcast.9), custom_call_target="tpu_custom_call" | custom-call | tf_op jit(solution)/shard_map/prep/pallas_call | solution.py:166
  87.7 13.8 %collective-permute-done.13.refs_4_ = bf16[272,512]{1,0:T(8,128)(2,1)S(1)} collective-permute-done((bf16[272,512]{1,0:T(8,128)(2,1)S(1)}, bf16[272,512]{1,0:T(8,128)(2,1)S(1)}, u32[]{:S(2)}, u32[]{:S(2)}) %collective-permute-start.13) | collective-permute-done | bytes 278560 | tf_op jit(solution)/shard_map/ppermute | solution.py:603
  105.7 8.5 %collective-permute-done.14.refs_5_ = bf16[272,512]{1,0:T(8,128)(2,1)S(1)} collective-permute-done((bf16[272,512]{1,0:T(8,128)(2,1)S(1)}, bf16[272,512]{1,0:T(8,128)(2,1)S(1)}, u32[]{:S(2)}, u32[]{:S(2)}) %collective-permute-start.14) | collective-permute-done | bytes 278560 | tf_op jit(solution)/shard_map/ppermute | solution.py:607
  114.4 2.6 %collective-permute-done.16.refs_7_ = bf16[272,512]{1,0:T(8,128)(2,1)S(1)} collective-permute-done((bf16[272,512]{1,0:T(8,128)(2,1)S(1)}, bf16[272,512]{1,0:T(8,128)(2,1)S(1)}, u32[]{:S(2)}, u32[]{:S(2)}) %collective-permute-start.16) | collective-permute-done | bytes 278560 | tf_op jit(solution)/shard_map/ppermute | solution.py:607
  117.1 19.3 %all-gather.3.cloned.1.call-done = bf16[96,512,128]{2,1,0:T(8,128)(2,1)} async-done(((bf16[3,512,128]{2,1,0:T(8,128)(2,1)}), bf16[96,512,128]{2,1,0:T(8,128)(2,1)}) %all-gather.3.cloned.1.call-update) | async-done | bytes 12582928 | tf_op jit(solution)/shard_map/all_gather | solution.py:594
  136.4 6.7 %project.1 = (bf16[272,512]{1,0:T(8,128)(2,1)S(1)}, bf16[272,512]{1,0:T(8,128)(2,1)S(1)}, bf16[272,512]{1,0:T(8,128)(2,1)S(1)}) custom-call(s32[5]{0:T(128)S(1)} %stack.23.where_ref, bf16[8,272,512]{2,1,0:T(8,128)(2,1)S(1)} %packed.1.hidden_ref, bf16[32,3,512,128]{3,2,1,0:T(8,128)(2,1)} %bitcast.10), custom_call_target="tpu_custom_call" | custom-call | tf_op jit(solution)/shard_map/project/pallas_call | solution.py:344
  148.5 2.3 %collective-permute-start.20 = (f32[16,512]{1,0:T(8,128)S(1)}, f32[16,512]{1,0:T(8,128)S(1)}, u32[]{:S(2)}, u32[]{:S(2)}) collective-permute-start(f32[16,512]{1,0:T(8,128)S(1)} %chip_state.1.c0), channel_id=1, source_target_pairs={{0,48},{8,56},{16,0},{24,8},{32,16},{40,24},{48,32},{56,40},{64,11... | collective-permute-start | bytes 98312 | tf_op jit(solution)/shard_map/ppermute | solution.py:613
  154.7 2.4 %collective-permute-start.22 = (f32[16,512]{1,0:T(8,128)S(1)}, f32[16,512]{1,0:T(8,128)S(1)}, u32[]{:S(2)}, u32[]{:S(2)}) collective-permute-start(f32[16,512]{1,0:T(8,128)S(1)} %get-tuple-element.100), channel_id=1, source_target_pairs={{0,128},{8,136},{16,144},{24,152},{32,160},{40,168},{48,176},{56,1... | collective-permute-start | bytes 98312 | tf_op jit(solution)/shard_map/ppermute | solution.py:617
  161.1 3.5 %li_outer.1 = (bf16[256,512]{1,0:T(8,128)(2,1)S(1)}, bf16[256,512]{1,0:T(8,128)(2,1)S(1)}, bf16[256,512]{1,0:T(8,128)(2,1)S(1)}, bf16[256,512]{1,0:T(8,128)(2,1)S(1)}, bf16[256,512]{1,0:T(8,128)(2,1)S(1)}) custom-call(s32[5]{0:T(128)S(1)} %stack.23.where_ref, f32[256,512]{1,0:T(8,128)S(1)} %li_inner.1.conv_ref, ...), custom_call_target="tpu_custom_call" | custom-call | tf_op jit(solution)/shard_map/li_outer/pallas_call | solution.py:489
  168.8 2.1 %shares.3 = (bf16[256,512]{1,0:T(8,128)(2,1)S(1)}, bf16[256,512]{1,0:T(8,128)(2,1)S(1)}, bf16[256,512]{1,0:T(8,128)(2,1)S(1)}, bf16[256,512]{1,0:T(8,128)(2,1)S(1)}) custom-call(s32[5]{0:T(128)S(1)} %stack.23.where_ref, bf16[256,512]{1,0:T(8,128)(2,1)S(1)} %get-tuple-element.105.y_ref, bf16[512,4096]{1,0:T(8,128)(2,1)S(1)} %copy-done.1), custom_call_target="tpu_custom_call" | custom-call | tf_op jit(solution)/shard_map/shares/pallas_call | solution.py:239
  170.9 2.3 %collective-permute-done.24 = bf16[256,512]{1,0:T(8,128)(2,1)S(1)} collective-permute-done((bf16[256,512]{1,0:T(8,128)(2,1)S(1)}, bf16[256,512]{1,0:T(8,128)(2,1)S(1)}, u32[]{:S(2)}, u32[]{:S(2)}) %collective-permute-start.24) | collective-permute-done | bytes 262176 | tf_op jit(solution)/shard_map/ppermute | solution.py:565
  175.0 2.8 %collective-permute-done.26 = bf16[256,512]{1,0:T(8,128)(2,1)S(1)} collective-permute-done((bf16[256,512]{1,0:T(8,128)(2,1)S(1)}, bf16[256,512]{1,0:T(8,128)(2,1)S(1)}, u32[]{:S(2)}, u32[]{:S(2)}) %collective-permute-start.26) | collective-permute-done | bytes 262176 | tf_op jit(solution)/shard_map/ppermute | solution.py:565
  177.9 5.7 %collective-permute-start.27 = (bf16[256,512]{1,0:T(8,128)(2,1)S(1)}, bf16[256,512]{1,0:T(8,128)(2,1)S(1)}, u32[]{:S(2)}, u32[]{:S(2)}) collective-permute-start(bf16[256,512]{1,0:T(8,128)(2,1)S(1)} %add_convert_fusion.1), channel_id=1, source_target_pairs={{0,1},{1,0},{2,3},{3,2},{4,5},{5,4},{6,7},{7,6},{8,9},{9,8},{10,11... | collective-permute-start | bytes 786440 | tf_op jit(solution)/shard_map/ppermute | solution.py:570
  187.5 4.7 %collective-permute-done.27 = bf16[256,512]{1,0:T(8,128)(2,1)S(1)} collective-permute-done((bf16[256,512]{1,0:T(8,128)(2,1)S(1)}, bf16[256,512]{1,0:T(8,128)(2,1)S(1)}, u32[]{:S(2)}, u32[]{:S(2)}) %collective-permute-start.27) | collective-permute-done | bytes 262176 | tf_op jit(solution)/shard_map/ppermute | solution.py:570
  192.9 2.8 %collective-permute-done.30 = bf16[256,512]{1,0:T(8,128)(2,1)S(1)} collective-permute-done((bf16[256,512]{1,0:T(8,128)(2,1)S(1)}, bf16[256,512]{1,0:T(8,128)(2,1)S(1)}, u32[]{:S(2)}, u32[]{:S(2)}) %collective-permute-start.30) | collective-permute-done | bytes 262176 | tf_op jit(solution)/shard_map/ppermute | solution.py:571
  (92 shorter events, 49.6 us)
Async XLA Ops:
  6.5 129.8 %all-gather.3.cloned.1.call-start = ((), (), s32[]{:S(2)}) async-start(), calls=%async_computation | async-start | bytes 12976128 | tf_op jit(solution)/shard_map/all_gather | solution.py:594
  6.5 26.1 %collective-permute-start.1 = (bf16[3,512,128]{2,1,0:T(8,128)(2,1)}, bf16[3,512,128]{2,1,0:T(8,128)(2,1)}, u32[]{:S(2)}, u32[]{:S(2)}) collective-permute-start(bf16[3,512,128]{2,1,0:T(8,128)(2,1)} %param.19), channel_id=1, source_target_pairs={{0,144},{1,176},{2,208},{3,240},{4,16},{5,48},{6,80},{7,112},{8,15... | collective-permute-start | bytes 1179656 | tf_op jit(solution)/shard_map/ppermute | solution.py:589
  37.7 15.0 %collective-permute-start.2 = (bf16[256,512]{1,0:T(8,128)(2,1)S(1)}, bf16[256,512]{1,0:T(8,128)(2,1)S(1)}, u32[]{:S(2)}, u32[]{:S(2)}) collective-permute-start(bf16[256,512]{1,0:T(8,128)(2,1)S(1)} %get-tuple-element.67), channel_id=1, source_target_pairs={{0,2},{1,3},{2,4},{3,5},{4,6},{5,7},{6,0},{7,1},{8,10},{9,11},{10,... | collective-permute-start | bytes 786440 | tf_op jit(solution)/shard_map/ppermute | solution.py:565
  42.3 10.9 %collective-permute-start.3 = (bf16[256,512]{1,0:T(8,128)(2,1)S(1)}, bf16[256,512]{1,0:T(8,128)(2,1)S(1)}, u32[]{:S(2)}, u32[]{:S(2)}) collective-permute-start(bf16[256,512]{1,0:T(8,128)(2,1)S(1)} %get-tuple-element.68), channel_id=1, source_target_pairs={{0,6},{1,7},{2,0},{3,1},{4,2},{5,3},{6,4},{7,5},{8,14},{9,15},{10,... | collective-permute-start | bytes 786440 | tf_op jit(solution)/shard_map/ppermute | solution.py:565
  42.3 10.9 %collective-permute-start.4 = (bf16[256,512]{1,0:T(8,128)(2,1)S(1)}, bf16[256,512]{1,0:T(8,128)(2,1)S(1)}, u32[]{:S(2)}, u32[]{:S(2)}) collective-permute-start(bf16[256,512]{1,0:T(8,128)(2,1)S(1)} %get-tuple-element.69), channel_id=1, source_target_pairs={{0,4},{1,5},{2,6},{3,7},{4,0},{5,1},{6,2},{7,3},{8,12},{9,13},{10,... | collective-permute-start | bytes 786440 | tf_op jit(solution)/shard_map/ppermute | solution.py:565
  53.3 22.2 %collective-permute-start.5 = (bf16[256,512]{1,0:T(8,128)(2,1)S(1)}, bf16[256,512]{1,0:T(8,128)(2,1)S(1)}, u32[]{:S(2)}, u32[]{:S(2)}) collective-permute-start(bf16[256,512]{1,0:T(8,128)(2,1)S(1)} %add_convert_fusion.3), channel_id=1, source_target_pairs={{0,1},{1,0},{2,3},{3,2},{4,5},{5,4},{6,7},{7,6},{8,9},{9,8},{10,11... | collective-permute-start | bytes 786440 | tf_op jit(solution)/shard_map/ppermute | solution.py:570
  53.9 21.8 %collective-permute-start.6 = (bf16[256,512]{1,0:T(8,128)(2,1)S(1)}, bf16[256,512]{1,0:T(8,128)(2,1)S(1)}, u32[]{:S(2)}, u32[]{:S(2)}) collective-permute-start(bf16[256,512]{1,0:T(8,128)(2,1)S(1)} %get-tuple-element.77), channel_id=1, source_target_pairs={{0,2},{1,3},{2,4},{3,5},{4,6},{5,7},{6,0},{7,1},{8,10},{9,11},{10,... | collective-permute-start | bytes 786440 | tf_op jit(solution)/shard_map/ppermute | solution.py:571
  55.5 20.2 %collective-permute-start.7 = (bf16[256,512]{1,0:T(8,128)(2,1)S(1)}, bf16[256,512]{1,0:T(8,128)(2,1)S(1)}, u32[]{:S(2)}, u32[]{:S(2)}) collective-permute-start(bf16[256,512]{1,0:T(8,128)(2,1)S(1)} %get-tuple-element.78), channel_id=1, source_target_pairs={{0,6},{1,7},{2,0},{3,1},{4,2},{5,3},{6,4},{7,5},{8,14},{9,15},{10,... | collective-permute-start | bytes 786440 | tf_op jit(solution)/shard_map/ppermute | solution.py:571
  55.9 19.8 %collective-permute-start.8 = (bf16[256,512]{1,0:T(8,128)(2,1)S(1)}, bf16[256,512]{1,0:T(8,128)(2,1)S(1)}, u32[]{:S(2)}, u32[]{:S(2)}) collective-permute-start(bf16[256,512]{1,0:T(8,128)(2,1)S(1)} %get-tuple-element.79), channel_id=1, source_target_pairs={{0,4},{1,5},{2,6},{3,7},{4,0},{5,1},{6,2},{7,3},{8,12},{9,13},{10,... | collective-permute-start | bytes 786440 | tf_op jit(solution)/shard_map/ppermute | solution.py:571
  78.0 23.5 %collective-permute-start.13 = (bf16[272,512]{1,0:T(8,128)(2,1)S(1)}, bf16[272,512]{1,0:T(8,128)(2,1)S(1)}, u32[]{:S(2)}, u32[]{:S(2)}) collective-permute-start(bf16[272,512]{1,0:T(8,128)(2,1)S(1)} %pad_maximum_fusion.refs_0_), channel_id=1, source_target_pairs={{0,1},{1,0},{2,3},{3,2},{4,5},{5,4},{6,7},{7,6},{8,9},{9,8},{10,11... | collective-permute-start | bytes 835592 | tf_op jit(solution)/shard_map/ppermute | solution.py:603
  78.1 26.0 %collective-permute-start.10 = (bf16[272,512]{1,0:T(8,128)(2,1)S(1)}, bf16[272,512]{1,0:T(8,128)(2,1)S(1)}, u32[]{:S(2)}, u32[]{:S(2)}) collective-permute-start(bf16[272,512]{1,0:T(8,128)(2,1)S(1)} %pad_maximum_fusion.refs_0_), channel_id=1, source_target_pairs={{0,2},{1,3},{2,4},{3,5},{4,6},{5,7},{6,0},{7,1},{8,10},{9,11},{10,... | collective-permute-start | bytes 835592 | tf_op jit(solution)/shard_map/ppermute | solution.py:604
  84.2 21.5 %collective-permute-start.11 = (bf16[272,512]{1,0:T(8,128)(2,1)S(1)}, bf16[272,512]{1,0:T(8,128)(2,1)S(1)}, u32[]{:S(2)}, u32[]{:S(2)}) collective-permute-start(bf16[272,512]{1,0:T(8,128)(2,1)S(1)} %pad_maximum_fusion.refs_0_), channel_id=1, source_target_pairs={{0,4},{1,5},{2,6},{3,7},{4,0},{5,1},{6,2},{7,3},{8,12},{9,13},{10,... | collective-permute-start | bytes 835592 | tf_op jit(solution)/shard_map/ppermute | solution.py:604
  86.1 19.6 %collective-permute-start.12 = (bf16[272,512]{1,0:T(8,128)(2,1)S(1)}, bf16[272,512]{1,0:T(8,128)(2,1)S(1)}, u32[]{:S(2)}, u32[]{:S(2)}) collective-permute-start(bf16[272,512]{1,0:T(8,128)(2,1)S(1)} %pad_maximum_fusion.refs_0_), channel_id=1, source_target_pairs={{0,6},{1,7},{2,0},{3,1},{4,2},{5,3},{6,4},{7,5},{8,14},{9,15},{10,... | collective-permute-start | bytes 835592 | tf_op jit(solution)/shard_map/ppermute | solution.py:604
  101.5 12.8 %collective-permute-start.14 = (bf16[272,512]{1,0:T(8,128)(2,1)S(1)}, bf16[272,512]{1,0:T(8,128)(2,1)S(1)}, u32[]{:S(2)}, u32[]{:S(2)}) collective-permute-start(bf16[272,512]{1,0:T(8,128)(2,1)S(1)} %collective-permute-done.13.refs_4_), channel_id=1, source_target_pairs={{0,2},{1,3},{2,4},{3,5},{4,6},{5,7},{6,0},{7,1},{8,10},{9,11},{10,... | collective-permute-start | bytes 835592 | tf_op jit(solution)/shard_map/ppermute | solution.py:607
  103.3 11.1 %collective-permute-start.15 = (bf16[272,512]{1,0:T(8,128)(2,1)S(1)}, bf16[272,512]{1,0:T(8,128)(2,1)S(1)}, u32[]{:S(2)}, u32[]{:S(2)}) collective-permute-start(bf16[272,512]{1,0:T(8,128)(2,1)S(1)} %collective-permute-done.13.refs_4_), channel_id=1, source_target_pairs={{0,4},{1,5},{2,6},{3,7},{4,0},{5,1},{6,2},{7,3},{8,12},{9,13},{10,... | collective-permute-start | bytes 835592 | tf_op jit(solution)/shard_map/ppermute | solution.py:607
  104.1 12.8 %collective-permute-start.16 = (bf16[272,512]{1,0:T(8,128)(2,1)S(1)}, bf16[272,512]{1,0:T(8,128)(2,1)S(1)}, u32[]{:S(2)}, u32[]{:S(2)}) collective-permute-start(bf16[272,512]{1,0:T(8,128)(2,1)S(1)} %collective-permute-done.13.refs_4_), channel_id=1, source_target_pairs={{0,6},{1,7},{2,0},{3,1},{4,2},{5,3},{6,4},{7,5},{8,14},{9,15},{10,... | collective-permute-start | bytes 835592 | tf_op jit(solution)/shard_map/ppermute | solution.py:607
  145.6 6.0 %collective-permute-start.18 = (f32[16,512]{1,0:T(8,128)S(1)}, f32[16,512]{1,0:T(8,128)S(1)}, u32[]{:S(2)}, u32[]{:S(2)}) collective-permute-start(f32[16,512]{1,0:T(8,128)S(1)} %chip_state.1.c0), channel_id=1, source_target_pairs={{0,16},{8,24},{16,32},{24,40},{32,48},{40,56},{48,0},{56,8},{64,80... | collective-permute-start | bytes 98312 | tf_op jit(solution)/shard_map/ppermute | solution.py:613
  164.6 8.6 %collective-permute-start.24 = (bf16[256,512]{1,0:T(8,128)(2,1)S(1)}, bf16[256,512]{1,0:T(8,128)(2,1)S(1)}, u32[]{:S(2)}, u32[]{:S(2)}) collective-permute-start(bf16[256,512]{1,0:T(8,128)(2,1)S(1)} %get-tuple-element.102), channel_id=1, source_target_pairs={{0,2},{1,3},{2,4},{3,5},{4,6},{5,7},{6,0},{7,1},{8,10},{9,11},{10,... | collective-permute-start | bytes 786440 | tf_op jit(solution)/shard_map/ppermute | solution.py:565
  166.2 8.8 %collective-permute-start.25 = (bf16[256,512]{1,0:T(8,128)(2,1)S(1)}, bf16[256,512]{1,0:T(8,128)(2,1)S(1)}, u32[]{:S(2)}, u32[]{:S(2)}) collective-permute-start(bf16[256,512]{1,0:T(8,128)(2,1)S(1)} %get-tuple-element.103), channel_id=1, source_target_pairs={{0,6},{1,7},{2,0},{3,1},{4,2},{5,3},{6,4},{7,5},{8,14},{9,15},{10,... | collective-permute-start | bytes 786440 | tf_op jit(solution)/shard_map/ppermute | solution.py:565
  166.7 11.1 %collective-permute-start.26 = (bf16[256,512]{1,0:T(8,128)(2,1)S(1)}, bf16[256,512]{1,0:T(8,128)(2,1)S(1)}, u32[]{:S(2)}, u32[]{:S(2)}) collective-permute-start(bf16[256,512]{1,0:T(8,128)(2,1)S(1)} %get-tuple-element.104), channel_id=1, source_target_pairs={{0,4},{1,5},{2,6},{3,7},{4,0},{5,1},{6,2},{7,3},{8,12},{9,13},{10,... | collective-permute-start | bytes 786440 | tf_op jit(solution)/shard_map/ppermute | solution.py:565
  177.9 14.3 %collective-permute-start.27 = (bf16[256,512]{1,0:T(8,128)(2,1)S(1)}, bf16[256,512]{1,0:T(8,128)(2,1)S(1)}, u32[]{:S(2)}, u32[]{:S(2)}) collective-permute-start(bf16[256,512]{1,0:T(8,128)(2,1)S(1)} %add_convert_fusion.1), channel_id=1, source_target_pairs={{0,1},{1,0},{2,3},{3,2},{4,5},{5,4},{6,7},{7,6},{8,9},{9,8},{10,11... | collective-permute-start | bytes 786440 | tf_op jit(solution)/shard_map/ppermute | solution.py:570
  183.6 8.6 %collective-permute-start.28 = (bf16[256,512]{1,0:T(8,128)(2,1)S(1)}, bf16[256,512]{1,0:T(8,128)(2,1)S(1)}, u32[]{:S(2)}, u32[]{:S(2)}) collective-permute-start(bf16[256,512]{1,0:T(8,128)(2,1)S(1)} %get-tuple-element.112), channel_id=1, source_target_pairs={{0,2},{1,3},{2,4},{3,5},{4,6},{5,7},{6,0},{7,1},{8,10},{9,11},{10,... | collective-permute-start | bytes 786440 | tf_op jit(solution)/shard_map/ppermute | solution.py:571
  183.6 9.3 %collective-permute-start.29 = (bf16[256,512]{1,0:T(8,128)(2,1)S(1)}, bf16[256,512]{1,0:T(8,128)(2,1)S(1)}, u32[]{:S(2)}, u32[]{:S(2)}) collective-permute-start(bf16[256,512]{1,0:T(8,128)(2,1)S(1)} %get-tuple-element.113), channel_id=1, source_target_pairs={{0,6},{1,7},{2,0},{3,1},{4,2},{5,3},{6,4},{7,5},{8,14},{9,15},{10,... | collective-permute-start | bytes 786440 | tf_op jit(solution)/shard_map/ppermute | solution.py:571
  185.7 10.0 %collective-permute-start.30 = (bf16[256,512]{1,0:T(8,128)(2,1)S(1)}, bf16[256,512]{1,0:T(8,128)(2,1)S(1)}, u32[]{:S(2)}, u32[]{:S(2)}) collective-permute-start(bf16[256,512]{1,0:T(8,128)(2,1)S(1)} %get-tuple-element.114), channel_id=1, source_target_pairs={{0,4},{1,5},{2,6},{3,7},{4,0},{5,1},{6,2},{7,3},{8,12},{9,13},{10,... | collective-permute-start | bytes 786440 | tf_op jit(solution)/shard_map/ppermute | solution.py:571
  (22 other events, 227.2 us)
Sparse Core Ops, SparseCore 0:
  32.7 103.5 all-gather.2

commit v8 on v7

--- a/solution.py
+++ b/solution.py
@@ -309,57 +309,46 @@
     )(*pieces)
 
 
-def project_kernel(slots, where_ref, hidden_ref, w_ref, *refs):
-    count = len(slots)
-    out_refs = refs[:count]
-    wbuf, wsem = refs[count:]
+STATE = jax.ShapeDtypeStruct((GS, WIDTH), F32)
+AHEAD = 3
+
+
+def project_kernel(
+    where_ref, hidden_ref, w_ref, feat_ref, enter_ref, q_ref, z_ref, load_ref, wbuf, kx, vx, wsem
+):
     x = where_ref[0]
-    copies = []
-    for i in range(8):
+
+    def piece_copies(i):
         e, d = i // 4, i % 4
         src_y = lax.rem(x + 6 - d, 4)
+        copies = []
         for b in range(4):
             odd = 1 - b // 2
             high = odd if e == 1 else 1 - odd
             copy = pltpu.make_async_copy(
-                w_ref.at[gathered_at(src_y, high * 2 + odd, b % 2), pl.ds(slots[0], count)],
+                w_ref.at[gathered_at(src_y, high * 2 + odd, b % 2)],
                 wbuf.at[i, :, :, pl.ds(b * LANES, LANES)],
                 wsem.at[i, b],
             )
             copy.start()
             copies.append(copy)
-    sums = [None] * count
+        return copies
+
+    pending = [piece_copies(i) for i in range(AHEAD)]
+    sums = [None] * 3
     for i in range(8):
-        for b in range(4):
-            copies[i * 4 + b].wait()
-        for j in range(count):
+        for copy in pending[i]:
+            copy.wait()
+        if i + AHEAD < 8:
+            pending.append(piece_copies(i + AHEAD))
+        for j in range(3):
             prod = jnp.dot(hidden_ref[i], wbuf[i, j], preferred_element_type=F32)
             sums[j] = prod if i == 0 else sums[j] + prod
-    for j in range(count):
-        out_refs[j][...] = sums[j].astype(BF16)
-
-
-def project(where, pieces, weights, slots):
-    count = len(slots)
-    return pl.pallas_call(
-        functools.partial(project_kernel, slots),
-        out_shape=[EXT_PIECE] * count,
-        in_specs=[SMEM_SPEC] + vspecs(1) + hspecs(1),
-        out_specs=vspecs(count),
-        scratch_shapes=[
-            pltpu.VMEM((8, count, WIDTH, WIDTH), BF16),
-            pltpu.SemaphoreType.DMA((8, 4)),
-        ],
-        compiler_params=params(48),
-        name="project",
-    )(where, pieces, weights)
-
-
-def li_gate_kernel(k_ref, v_ref, feat_ref, enter_ref, z_ref, load_ref, kx, vx):
+    q_ref[...] = sums[0].astype(BF16)
     for block in range(WIDTH // LANES):
         cols = slice(block * LANES, (block + 1) * LANES)
-        kx[...] = k_ref[:, cols].astype(F32)
-        vx[...] = v_ref[:, cols].astype(F32)
+        kx[...] = sums[1][:, cols].astype(BF16).astype(F32)
+        vx[...] = sums[2][:, cols].astype(BF16).astype(F32)
         kf = feature(kx, 16, ROWS, feat_ref[1, :, cols])
         vf = feature(vx, 16, ROWS, feat_ref[2, :, cols])
         z = (kf * vf).astype(BF16)
@@ -375,19 +364,21 @@
         load_ref[:, cols] = load
 
 
-def li_gate(k, v, feat, enter):
-    return pl.pallas_call(
-        li_gate_kernel,
-        out_shape=[PIECE, STATE],
-        in_specs=vspecs(4),
-        out_specs=vspecs(2),
-        scratch_shapes=[pltpu.VMEM((16 + ROWS, LANES), F32)] * 2,
-        compiler_params=params(),
-        name="li_gate",
-    )(k, v, feat, enter)
-
-
-STATE = jax.ShapeDtypeStruct((GS, WIDTH), F32)
+def project(where, pieces, weights, feat, enter):
+    return pl.pallas_call(
+        project_kernel,
+        out_shape=[EXT_PIECE, PIECE, STATE],
+        in_specs=[SMEM_SPEC] + vspecs(1) + hspecs(1) + vspecs(2),
+        out_specs=vspecs(3),
+        scratch_shapes=[
+            pltpu.VMEM((8, 3, WIDTH, WIDTH), BF16),
+            pltpu.VMEM((EXT, LANES), F32),
+            pltpu.VMEM((EXT, LANES), F32),
+            pltpu.SemaphoreType.DMA((8, 4)),
+        ],
+        compiler_params=params(48),
+        name="project",
+    )(where, pieces, weights, feat, enter)
 
 
 def chip_kernel(where_ref, load_ref, other_ref, rates_ref, chip_ref):
@@ -606,8 +597,7 @@
     toep_li, leave, enter, lane_rates = filters
     far_pieces = [crossed] + [lax.ppermute(crossed, "mp", x_shift(d)) for d in (1, 2, 3)]
     pieces = packed(own_pieces + far_pieces)
-    fresh_q, fresh_k, fresh_v = project(where, pieces, weights, (0, 1, 2))
-    product, load = li_gate(fresh_k, fresh_v, featurizer_li, enter)
+    fresh_q, product, load = project(where, pieces, weights, featurizer_li, enter)
     other_load = lax.ppermute(load, "ctx", CORE_SWAP)
     chip = chip_state(where, load, other_load, lane_rates)
     before = [lax.ppermute(chip, "ctx", z_shift(s)) for s in (1, 2, 3)]

time: 205 us -> 205 us (level)
    pallas_call x2 -> x1, Pallas kernels: 7.3 us -> 7.26 us  [project(): pl.pallas_call(project_kernel, out_shape=[EXT_PIECE, PIECE, STATE], in_sp...]
where the time goes in v8:
time: 205 us; the launch traced here: 203 us
  waiting for transfers between devices  101 us (49%)
  starting transfers between devices  51.9 us (25%)
  Pallas kernels  29.1 us (14%)
  between operations  13.7 us (7%)
  local copies, waits for them, and re-layouts  5.97 us (3%)
    ppermute x2, waiting for transfers between devices, sum_shares(): crossed = lax.ppermute(total_other, 'mp', H_SWAP)  21.4 us
    all_gather x1, waiting for transfers between devices, body(): weights = lax.all_gather(moved, 'ctx', axis_index_groups=[GATHER_ORDER])  19.2 us
    ppermute x6, waiting for transfers between devices, sum_shares(): got = [lax.ppermute(other[d], 'mp', x_shift(d)) for d in (1, 3, 2)]  14.2 us
    ppermute x1, waiting for transfers between devices, body(): crossed = lax.ppermute(extended, 'mp', H_SWAP)  13.8 us
    ppermute x1, waiting for transfers between devices, body(): moved = lax.ppermute(in_weight, ('ctx', 'mp'), weight_moves())  12.3 us
    ppermute x3, waiting for transfers between devices, body(): lax.ppermute(crossed, 'mp', x_shift(d))  11.3 us
    ppermute x6, starting transfers between devices, sum_shares(): got = [lax.ppermute(other[d], 'mp', x_shift(d)) for d in (1, 3, 2)]  10.3 us
    ppermute x6, starting transfers between devices, sum_shares(): got_mine = [lax.ppermute(mine[d], 'mp', x_shift(d)) for d in (1, 3, 2)]  8.82 us
  transfers between devices with their start and end apart: 32, of which 22 were waited for; matrix products, arithmetic and copies ran while one was open for 1% of the time, Pallas kernels for 8%

profile of v8, /device:TPU:2, one launch (start us, length us, event | category | flops | bytes accessed | tf_op | source)
XLA Modules:
  0.0 203.4 jit_solution(3585725664834240954)
XLA Ops:
  6.5 4.3 %collective-permute-start.1 = (bf16[3,512,128]{2,1,0:T(8,128)(2,1)}, bf16[3,512,128]{2,1,0:T(8,128)(2,1)}, u32[]{:S(2)}, u32[]{:S(2)}) collective-permute-start(bf16[3,512,128]{2,1,0:T(8,128)(2,1)} %param.19), channel_id=1, source_target_pairs={{0,144},{1,176},{2,208},{3,240},{4,16},{5,48},{6,80},{7,112},{8,15... | collective-permute-start | bytes 1179656 | tf_op jit(solution)/shard_map/ppermute | solution.py:580
  17.2 3.1 %toeplitz.1.toep_ref = bf16[4096,256]{1,0:T(8,128)(2,1)S(1)} custom-call(f32[128,32]{1,0:T(8,128)S(1)} %copy.14.taps_ref), custom_call_target="tpu_custom_call" | custom-call | tf_op jit(solution)/shard_map/toeplitz/pallas_call | solution.py:108
  20.3 12.3 %collective-permute-done.1 = bf16[3,512,128]{2,1,0:T(8,128)(2,1)} collective-permute-done((bf16[3,512,128]{2,1,0:T(8,128)(2,1)}, bf16[3,512,128]{2,1,0:T(8,128)(2,1)}, u32[]{:S(2)}, u32[]{:S(2)}) %collective-permute-start.1) | collective-permute-done | bytes 393248 | tf_op jit(solution)/shard_map/ppermute | solution.py:580
  33.7 4.0 %mr_op.1 = (bf16[256,512]{1,0:T(8,128)(2,1)S(1)}, bf16[256,512]{1,0:T(8,128)(2,1)S(1)}, bf16[256,512]{1,0:T(8,128)(2,1)S(1)}, bf16[256,512]{1,0:T(8,128)(2,1)S(1)}, bf16[256,512]{1,0:T(8,128)(2,1)S(1)}) custom-call(s32[5]{0:T(128)S(1)} %stack.23.where_ref, bf16[256,512]{1,0:T(8,128)(2,1)S(1)} %get-tuple-element.58.q_ref, ...), custom_call_target="tpu_custom_call" | custom-call | tf_op jit(solution)/shard_map/mr_op/pallas_call | solution.py:277
  37.7 4.6 %collective-permute-start.2 = (bf16[256,512]{1,0:T(8,128)(2,1)S(1)}, bf16[256,512]{1,0:T(8,128)(2,1)S(1)}, u32[]{:S(2)}, u32[]{:S(2)}) collective-permute-start(bf16[256,512]{1,0:T(8,128)(2,1)S(1)} %get-tuple-element.65), channel_id=1, source_target_pairs={{0,2},{1,3},{2,4},{3,5},{4,6},{5,7},{6,0},{7,1},{8,10},{9,11},{10,... | collective-permute-start | bytes 786440 | tf_op jit(solution)/shard_map/ppermute | solution.py:556
  43.8 2.1 %shares.2 = (bf16[256,512]{1,0:T(8,128)(2,1)S(1)}, bf16[256,512]{1,0:T(8,128)(2,1)S(1)}, bf16[256,512]{1,0:T(8,128)(2,1)S(1)}, bf16[256,512]{1,0:T(8,128)(2,1)S(1)}) custom-call(s32[5]{0:T(128)S(1)} %stack.23.where_ref, bf16[256,512]{1,0:T(8,128)(2,1)S(1)} %get-tuple-element.68.y_ref, bf16[512,4096]{1,0:T(8,128)(2,1)S(1)} %copy-done), custom_call_target="tpu_custom_call" | custom-call | tf_op jit(solution)/shard_map/shares/pallas_call | solution.py:239
  45.9 6.7 %collective-permute-done.2 = bf16[256,512]{1,0:T(8,128)(2,1)S(1)} collective-permute-done((bf16[256,512]{1,0:T(8,128)(2,1)S(1)}, bf16[256,512]{1,0:T(8,128)(2,1)S(1)}, u32[]{:S(2)}, u32[]{:S(2)}) %collective-permute-start.2) | collective-permute-done | bytes 262176 | tf_op jit(solution)/shard_map/ppermute | solution.py:556
  55.9 3.0 %collective-permute-start.8 = (bf16[256,512]{1,0:T(8,128)(2,1)S(1)}, bf16[256,512]{1,0:T(8,128)(2,1)S(1)}, u32[]{:S(2)}, u32[]{:S(2)}) collective-permute-start(bf16[256,512]{1,0:T(8,128)(2,1)S(1)} %get-tuple-element.77), channel_id=1, source_target_pairs={{0,4},{1,5},{2,6},{3,7},{4,0},{5,1},{6,2},{7,3},{8,12},{9,13},{10,... | collective-permute-start | bytes 786440 | tf_op jit(solution)/shard_map/ppermute | solution.py:562
  58.9 16.7 %collective-permute-done.5 = bf16[256,512]{1,0:T(8,128)(2,1)S(1)} collective-permute-done((bf16[256,512]{1,0:T(8,128)(2,1)S(1)}, bf16[256,512]{1,0:T(8,128)(2,1)S(1)}, u32[]{:S(2)}, u32[]{:S(2)}) %collective-permute-start.5) | collective-permute-done | bytes 262176 | tf_op jit(solution)/shard_map/ppermute | solution.py:561
  79.1 3.8 %prep.1 = (bf16[4096,256]{1,0:T(8,128)(2,1)S(1)}, f32[256,512]{1,0:T(8,128)S(1)}, f32[256,512]{1,0:T(8,128)S(1)}, f32[16,512]{1,0:T(8,128)S(1)}) custom-call(f32[16,32]{1,0:T(8,128)S(1)} %bitcast.8, f32[16,32]{1,0:T(8,128)S(1)} %bitcast.9), custom_call_target="tpu_custom_call" | custom-call | tf_op jit(solution)/shard_map/prep/pallas_call | solution.py:166
  87.8 13.8 %collective-permute-done.13.refs_4_ = bf16[272,512]{1,0:T(8,128)(2,1)S(1)} collective-permute-done((bf16[272,512]{1,0:T(8,128)(2,1)S(1)}, bf16[272,512]{1,0:T(8,128)(2,1)S(1)}, u32[]{:S(2)}, u32[]{:S(2)}) %collective-permute-start.13) | collective-permute-done | bytes 278560 | tf_op jit(solution)/shard_map/ppermute | solution.py:594
  105.7 8.5 %collective-permute-done.14.refs_5_ = bf16[272,512]{1,0:T(8,128)(2,1)S(1)} collective-permute-done((bf16[272,512]{1,0:T(8,128)(2,1)S(1)}, bf16[272,512]{1,0:T(8,128)(2,1)S(1)}, u32[]{:S(2)}, u32[]{:S(2)}) %collective-permute-start.14) | collective-permute-done | bytes 278560 | tf_op jit(solution)/shard_map/ppermute | solution.py:598
  114.4 2.6 %collective-permute-done.16.refs_7_ = bf16[272,512]{1,0:T(8,128)(2,1)S(1)} collective-permute-done((bf16[272,512]{1,0:T(8,128)(2,1)S(1)}, bf16[272,512]{1,0:T(8,128)(2,1)S(1)}, u32[]{:S(2)}, u32[]{:S(2)}) %collective-permute-start.16) | collective-permute-done | bytes 278560 | tf_op jit(solution)/shard_map/ppermute | solution.py:598
  117.1 19.2 %all-gather.3.cloned.1.call-done = bf16[96,512,128]{2,1,0:T(8,128)(2,1)} async-done(((bf16[3,512,128]{2,1,0:T(8,128)(2,1)}), bf16[96,512,128]{2,1,0:T(8,128)(2,1)}) %all-gather.3.cloned.1.call-update) | async-done | bytes 12582928 | tf_op jit(solution)/shard_map/all_gather | solution.py:585
  136.4 7.3 %project.1 = (bf16[272,512]{1,0:T(8,128)(2,1)S(1)}, bf16[256,512]{1,0:T(8,128)(2,1)S(1)}, f32[16,512]{1,0:T(8,128)S(1)}) custom-call(s32[5]{0:T(128)S(1)} %stack.23.where_ref, bf16[8,272,512]{2,1,0:T(8,128)(2,1)S(1)} %packed.1.hidden_ref, bf16[32,3,512,128]{3,2,1,0:T(8,128)(2,1)} %bitcast.10, f32[3,3,512]{2,1,0:T(4,128)S(1)} %copy-done.7, ...), custom_call_target="tpu_custom_call" | custom-call | tf_op jit(solution)/shard_map/project/pallas_call | solution.py:368
  148.5 2.3 %collective-permute-start.20 = (f32[16,512]{1,0:T(8,128)S(1)}, f32[16,512]{1,0:T(8,128)S(1)}, u32[]{:S(2)}, u32[]{:S(2)}) collective-permute-start(f32[16,512]{1,0:T(8,128)S(1)} %chip_state.1.c0), channel_id=1, source_target_pairs={{0,48},{8,56},{16,0},{24,8},{32,16},{40,24},{48,32},{56,40},{64,11... | collective-permute-start | bytes 98312 | tf_op jit(solution)/shard_map/ppermute | solution.py:603
  154.7 2.5 %collective-permute-start.22 = (f32[16,512]{1,0:T(8,128)S(1)}, f32[16,512]{1,0:T(8,128)S(1)}, u32[]{:S(2)}, u32[]{:S(2)}) collective-permute-start(f32[16,512]{1,0:T(8,128)S(1)} %get-tuple-element.96), channel_id=1, source_target_pairs={{0,128},{8,136},{16,144},{24,152},{32,160},{40,168},{48,176},{56,1... | collective-permute-start | bytes 98312 | tf_op jit(solution)/shard_map/ppermute | solution.py:607
  161.0 3.5 %li_outer.1 = (bf16[256,512]{1,0:T(8,128)(2,1)S(1)}, bf16[256,512]{1,0:T(8,128)(2,1)S(1)}, bf16[256,512]{1,0:T(8,128)(2,1)S(1)}, bf16[256,512]{1,0:T(8,128)(2,1)S(1)}, bf16[256,512]{1,0:T(8,128)(2,1)S(1)}) custom-call(s32[5]{0:T(128)S(1)} %stack.23.where_ref, f32[256,512]{1,0:T(8,128)S(1)} %li_inner.1.conv_ref, ...), custom_call_target="tpu_custom_call" | custom-call | tf_op jit(solution)/shard_map/li_outer/pallas_call | solution.py:480
  168.7 2.1 %shares.3 = (bf16[256,512]{1,0:T(8,128)(2,1)S(1)}, bf16[256,512]{1,0:T(8,128)(2,1)S(1)}, bf16[256,512]{1,0:T(8,128)(2,1)S(1)}, bf16[256,512]{1,0:T(8,128)(2,1)S(1)}) custom-call(s32[5]{0:T(128)S(1)} %stack.23.where_ref, bf16[256,512]{1,0:T(8,128)(2,1)S(1)} %get-tuple-element.101.y_ref, bf16[512,4096]{1,0:T(8,128)(2,1)S(1)} %copy-done.1), custom_call_target="tpu_custom_call" | custom-call | tf_op jit(solution)/shard_map/shares/pallas_call | solution.py:239
  170.8 2.3 %collective-permute-done.24 = bf16[256,512]{1,0:T(8,128)(2,1)S(1)} collective-permute-done((bf16[256,512]{1,0:T(8,128)(2,1)S(1)}, bf16[256,512]{1,0:T(8,128)(2,1)S(1)}, u32[]{:S(2)}, u32[]{:S(2)}) %collective-permute-start.24) | collective-permute-done | bytes 262176 | tf_op jit(solution)/shard_map/ppermute | solution.py:556
  174.9 2.8 %collective-permute-done.26 = bf16[256,512]{1,0:T(8,128)(2,1)S(1)} collective-permute-done((bf16[256,512]{1,0:T(8,128)(2,1)S(1)}, bf16[256,512]{1,0:T(8,128)(2,1)S(1)}, u32[]{:S(2)}, u32[]{:S(2)}) %collective-permute-start.26) | collective-permute-done | bytes 262176 | tf_op jit(solution)/shard_map/ppermute | solution.py:556
  177.9 5.8 %collective-permute-start.27 = (bf16[256,512]{1,0:T(8,128)(2,1)S(1)}, bf16[256,512]{1,0:T(8,128)(2,1)S(1)}, u32[]{:S(2)}, u32[]{:S(2)}) collective-permute-start(bf16[256,512]{1,0:T(8,128)(2,1)S(1)} %add_convert_fusion.1), channel_id=1, source_target_pairs={{0,1},{1,0},{2,3},{3,2},{4,5},{5,4},{6,7},{7,6},{8,9},{9,8},{10,11... | collective-permute-start | bytes 786440 | tf_op jit(solution)/shard_map/ppermute | solution.py:561
  187.4 4.7 %collective-permute-done.27 = bf16[256,512]{1,0:T(8,128)(2,1)S(1)} collective-permute-done((bf16[256,512]{1,0:T(8,128)(2,1)S(1)}, bf16[256,512]{1,0:T(8,128)(2,1)S(1)}, u32[]{:S(2)}, u32[]{:S(2)}) %collective-permute-start.27) | collective-permute-done | bytes 262176 | tf_op jit(solution)/shard_map/ppermute | solution.py:561
  192.9 2.8 %collective-permute-done.30 = bf16[256,512]{1,0:T(8,128)(2,1)S(1)} collective-permute-done((bf16[256,512]{1,0:T(8,128)(2,1)S(1)}, bf16[256,512]{1,0:T(8,128)(2,1)S(1)}, u32[]{:S(2)}, u32[]{:S(2)}) %collective-permute-start.30) | collective-permute-done | bytes 262176 | tf_op jit(solution)/shard_map/ppermute | solution.py:562
  (91 shorter events, 49.1 us)
Async XLA Ops:
  6.5 129.8 %all-gather.3.cloned.1.call-start = ((), (), s32[]{:S(2)}) async-start(), calls=%async_computation | async-start | bytes 12976128 | tf_op jit(solution)/shard_map/all_gather | solution.py:585
  6.5 26.1 %collective-permute-start.1 = (bf16[3,512,128]{2,1,0:T(8,128)(2,1)}, bf16[3,512,128]{2,1,0:T(8,128)(2,1)}, u32[]{:S(2)}, u32[]{:S(2)}) collective-permute-start(bf16[3,512,128]{2,1,0:T(8,128)(2,1)} %param.19), channel_id=1, source_target_pairs={{0,144},{1,176},{2,208},{3,240},{4,16},{5,48},{6,80},{7,112},{8,15... | collective-permute-start | bytes 1179656 | tf_op jit(solution)/shard_map/ppermute | solution.py:580
  37.7 15.0 %collective-permute-start.2 = (bf16[256,512]{1,0:T(8,128)(2,1)S(1)}, bf16[256,512]{1,0:T(8,128)(2,1)S(1)}, u32[]{:S(2)}, u32[]{:S(2)}) collective-permute-start(bf16[256,512]{1,0:T(8,128)(2,1)S(1)} %get-tuple-element.65), channel_id=1, source_target_pairs={{0,2},{1,3},{2,4},{3,5},{4,6},{5,7},{6,0},{7,1},{8,10},{9,11},{10,... | collective-permute-start | bytes 786440 | tf_op jit(solution)/shard_map/ppermute | solution.py:556
  42.3 10.9 %collective-permute-start.3 = (bf16[256,512]{1,0:T(8,128)(2,1)S(1)}, bf16[256,512]{1,0:T(8,128)(2,1)S(1)}, u32[]{:S(2)}, u32[]{:S(2)}) collective-permute-start(bf16[256,512]{1,0:T(8,128)(2,1)S(1)} %get-tuple-element.66), channel_id=1, source_target_pairs={{0,6},{1,7},{2,0},{3,1},{4,2},{5,3},{6,4},{7,5},{8,14},{9,15},{10,... | collective-permute-start | bytes 786440 | tf_op jit(solution)/shard_map/ppermute | solution.py:556
  42.3 10.9 %collective-permute-start.4 = (bf16[256,512]{1,0:T(8,128)(2,1)S(1)}, bf16[256,512]{1,0:T(8,128)(2,1)S(1)}, u32[]{:S(2)}, u32[]{:S(2)}) collective-permute-start(bf16[256,512]{1,0:T(8,128)(2,1)S(1)} %get-tuple-element.67), channel_id=1, source_target_pairs={{0,4},{1,5},{2,6},{3,7},{4,0},{5,1},{6,2},{7,3},{8,12},{9,13},{10,... | collective-permute-start | bytes 786440 | tf_op jit(solution)/shard_map/ppermute | solution.py:556
  53.4 22.2 %collective-permute-start.5 = (bf16[256,512]{1,0:T(8,128)(2,1)S(1)}, bf16[256,512]{1,0:T(8,128)(2,1)S(1)}, u32[]{:S(2)}, u32[]{:S(2)}) collective-permute-start(bf16[256,512]{1,0:T(8,128)(2,1)S(1)} %add_convert_fusion.3), channel_id=1, source_target_pairs={{0,1},{1,0},{2,3},{3,2},{4,5},{5,4},{6,7},{7,6},{8,9},{9,8},{10,11... | collective-permute-start | bytes 786440 | tf_op jit(solution)/shard_map/ppermute | solution.py:561
  53.9 21.8 %collective-permute-start.6 = (bf16[256,512]{1,0:T(8,128)(2,1)S(1)}, bf16[256,512]{1,0:T(8,128)(2,1)S(1)}, u32[]{:S(2)}, u32[]{:S(2)}) collective-permute-start(bf16[256,512]{1,0:T(8,128)(2,1)S(1)} %get-tuple-element.75), channel_id=1, source_target_pairs={{0,2},{1,3},{2,4},{3,5},{4,6},{5,7},{6,0},{7,1},{8,10},{9,11},{10,... | collective-permute-start | bytes 786440 | tf_op jit(solution)/shard_map/ppermute | solution.py:562
  55.5 20.2 %collective-permute-start.7 = (bf16[256,512]{1,0:T(8,128)(2,1)S(1)}, bf16[256,512]{1,0:T(8,128)(2,1)S(1)}, u32[]{:S(2)}, u32[]{:S(2)}) collective-permute-start(bf16[256,512]{1,0:T(8,128)(2,1)S(1)} %get-tuple-element.76), channel_id=1, source_target_pairs={{0,6},{1,7},{2,0},{3,1},{4,2},{5,3},{6,4},{7,5},{8,14},{9,15},{10,... | collective-permute-start | bytes 786440 | tf_op jit(solution)/shard_map/ppermute | solution.py:562
  55.9 19.8 %collective-permute-start.8 = (bf16[256,512]{1,0:T(8,128)(2,1)S(1)}, bf16[256,512]{1,0:T(8,128)(2,1)S(1)}, u32[]{:S(2)}, u32[]{:S(2)}) collective-permute-start(bf16[256,512]{1,0:T(8,128)(2,1)S(1)} %get-tuple-element.77), channel_id=1, source_target_pairs={{0,4},{1,5},{2,6},{3,7},{4,0},{5,1},{6,2},{7,3},{8,12},{9,13},{10,... | collective-permute-start | bytes 786440 | tf_op jit(solution)/shard_map/ppermute | solution.py:562
  78.0 23.5 %collective-permute-start.13 = (bf16[272,512]{1,0:T(8,128)(2,1)S(1)}, bf16[272,512]{1,0:T(8,128)(2,1)S(1)}, u32[]{:S(2)}, u32[]{:S(2)}) collective-permute-start(bf16[272,512]{1,0:T(8,128)(2,1)S(1)} %pad_maximum_fusion.refs_0_), channel_id=1, source_target_pairs={{0,1},{1,0},{2,3},{3,2},{4,5},{5,4},{6,7},{7,6},{8,9},{9,8},{10,11... | collective-permute-start | bytes 835592 | tf_op jit(solution)/shard_map/ppermute | solution.py:594
  78.1 26.0 %collective-permute-start.10 = (bf16[272,512]{1,0:T(8,128)(2,1)S(1)}, bf16[272,512]{1,0:T(8,128)(2,1)S(1)}, u32[]{:S(2)}, u32[]{:S(2)}) collective-permute-start(bf16[272,512]{1,0:T(8,128)(2,1)S(1)} %pad_maximum_fusion.refs_0_), channel_id=1, source_target_pairs={{0,2},{1,3},{2,4},{3,5},{4,6},{5,7},{6,0},{7,1},{8,10},{9,11},{10,... | collective-permute-start | bytes 835592 | tf_op jit(solution)/shard_map/ppermute | solution.py:595
  84.2 21.5 %collective-permute-start.11 = (bf16[272,512]{1,0:T(8,128)(2,1)S(1)}, bf16[272,512]{1,0:T(8,128)(2,1)S(1)}, u32[]{:S(2)}, u32[]{:S(2)}) collective-permute-start(bf16[272,512]{1,0:T(8,128)(2,1)S(1)} %pad_maximum_fusion.refs_0_), channel_id=1, source_target_pairs={{0,4},{1,5},{2,6},{3,7},{4,0},{5,1},{6,2},{7,3},{8,12},{9,13},{10,... | collective-permute-start | bytes 835592 | tf_op jit(solution)/shard_map/ppermute | solution.py:595
  86.1 19.6 %collective-permute-start.12 = (bf16[272,512]{1,0:T(8,128)(2,1)S(1)}, bf16[272,512]{1,0:T(8,128)(2,1)S(1)}, u32[]{:S(2)}, u32[]{:S(2)}) collective-permute-start(bf16[272,512]{1,0:T(8,128)(2,1)S(1)} %pad_maximum_fusion.refs_0_), channel_id=1, source_target_pairs={{0,6},{1,7},{2,0},{3,1},{4,2},{5,3},{6,4},{7,5},{8,14},{9,15},{10,... | collective-permute-start | bytes 835592 | tf_op jit(solution)/shard_map/ppermute | solution.py:595
  101.5 12.7 %collective-permute-start.14 = (bf16[272,512]{1,0:T(8,128)(2,1)S(1)}, bf16[272,512]{1,0:T(8,128)(2,1)S(1)}, u32[]{:S(2)}, u32[]{:S(2)}) collective-permute-start(bf16[272,512]{1,0:T(8,128)(2,1)S(1)} %collective-permute-done.13.refs_4_), channel_id=1, source_target_pairs={{0,2},{1,3},{2,4},{3,5},{4,6},{5,7},{6,0},{7,1},{8,10},{9,11},{10,... | collective-permute-start | bytes 835592 | tf_op jit(solution)/shard_map/ppermute | solution.py:598
  103.3 11.1 %collective-permute-start.15 = (bf16[272,512]{1,0:T(8,128)(2,1)S(1)}, bf16[272,512]{1,0:T(8,128)(2,1)S(1)}, u32[]{:S(2)}, u32[]{:S(2)}) collective-permute-start(bf16[272,512]{1,0:T(8,128)(2,1)S(1)} %collective-permute-done.13.refs_4_), channel_id=1, source_target_pairs={{0,4},{1,5},{2,6},{3,7},{4,0},{5,1},{6,2},{7,3},{8,12},{9,13},{10,... | collective-permute-start | bytes 835592 | tf_op jit(solution)/shard_map/ppermute | solution.py:598
  104.1 12.8 %collective-permute-start.16 = (bf16[272,512]{1,0:T(8,128)(2,1)S(1)}, bf16[272,512]{1,0:T(8,128)(2,1)S(1)}, u32[]{:S(2)}, u32[]{:S(2)}) collective-permute-start(bf16[272,512]{1,0:T(8,128)(2,1)S(1)} %collective-permute-done.13.refs_4_), channel_id=1, source_target_pairs={{0,6},{1,7},{2,0},{3,1},{4,2},{5,3},{6,4},{7,5},{8,14},{9,15},{10,... | collective-permute-start | bytes 835592 | tf_op jit(solution)/shard_map/ppermute | solution.py:598
  145.5 6.0 %collective-permute-start.18 = (f32[16,512]{1,0:T(8,128)S(1)}, f32[16,512]{1,0:T(8,128)S(1)}, u32[]{:S(2)}, u32[]{:S(2)}) collective-permute-start(f32[16,512]{1,0:T(8,128)S(1)} %chip_state.1.c0), channel_id=1, source_target_pairs={{0,16},{8,24},{16,32},{24,40},{32,48},{40,56},{48,0},{56,8},{64,80... | collective-permute-start | bytes 98312 | tf_op jit(solution)/shard_map/ppermute | solution.py:603
  164.6 8.6 %collective-permute-start.24 = (bf16[256,512]{1,0:T(8,128)(2,1)S(1)}, bf16[256,512]{1,0:T(8,128)(2,1)S(1)}, u32[]{:S(2)}, u32[]{:S(2)}) collective-permute-start(bf16[256,512]{1,0:T(8,128)(2,1)S(1)} %get-tuple-element.98), channel_id=1, source_target_pairs={{0,2},{1,3},{2,4},{3,5},{4,6},{5,7},{6,0},{7,1},{8,10},{9,11},{10,... | collective-permute-start | bytes 786440 | tf_op jit(solution)/shard_map/ppermute | solution.py:556
  166.1 8.8 %collective-permute-start.25 = (bf16[256,512]{1,0:T(8,128)(2,1)S(1)}, bf16[256,512]{1,0:T(8,128)(2,1)S(1)}, u32[]{:S(2)}, u32[]{:S(2)}) collective-permute-start(bf16[256,512]{1,0:T(8,128)(2,1)S(1)} %get-tuple-element.99), channel_id=1, source_target_pairs={{0,6},{1,7},{2,0},{3,1},{4,2},{5,3},{6,4},{7,5},{8,14},{9,15},{10,... | collective-permute-start | bytes 786440 | tf_op jit(solution)/shard_map/ppermute | solution.py:556
  166.7 11.1 %collective-permute-start.26 = (bf16[256,512]{1,0:T(8,128)(2,1)S(1)}, bf16[256,512]{1,0:T(8,128)(2,1)S(1)}, u32[]{:S(2)}, u32[]{:S(2)}) collective-permute-start(bf16[256,512]{1,0:T(8,128)(2,1)S(1)} %get-tuple-element.100), channel_id=1, source_target_pairs={{0,4},{1,5},{2,6},{3,7},{4,0},{5,1},{6,2},{7,3},{8,12},{9,13},{10,... | collective-permute-start | bytes 786440 | tf_op jit(solution)/shard_map/ppermute | solution.py:556
  177.9 14.2 %collective-permute-start.27 = (bf16[256,512]{1,0:T(8,128)(2,1)S(1)}, bf16[256,512]{1,0:T(8,128)(2,1)S(1)}, u32[]{:S(2)}, u32[]{:S(2)}) collective-permute-start(bf16[256,512]{1,0:T(8,128)(2,1)S(1)} %add_convert_fusion.1), channel_id=1, source_target_pairs={{0,1},{1,0},{2,3},{3,2},{4,5},{5,4},{6,7},{7,6},{8,9},{9,8},{10,11... | collective-permute-start | bytes 786440 | tf_op jit(solution)/shard_map/ppermute | solution.py:561
  183.6 8.6 %collective-permute-start.28 = (bf16[256,512]{1,0:T(8,128)(2,1)S(1)}, bf16[256,512]{1,0:T(8,128)(2,1)S(1)}, u32[]{:S(2)}, u32[]{:S(2)}) collective-permute-start(bf16[256,512]{1,0:T(8,128)(2,1)S(1)} %get-tuple-element.108), channel_id=1, source_target_pairs={{0,2},{1,3},{2,4},{3,5},{4,6},{5,7},{6,0},{7,1},{8,10},{9,11},{10,... | collective-permute-start | bytes 786440 | tf_op jit(solution)/shard_map/ppermute | solution.py:562
  183.6 9.3 %collective-permute-start.29 = (bf16[256,512]{1,0:T(8,128)(2,1)S(1)}, bf16[256,512]{1,0:T(8,128)(2,1)S(1)}, u32[]{:S(2)}, u32[]{:S(2)}) collective-permute-start(bf16[256,512]{1,0:T(8,128)(2,1)S(1)} %get-tuple-element.109), channel_id=1, source_target_pairs={{0,6},{1,7},{2,0},{3,1},{4,2},{5,3},{6,4},{7,5},{8,14},{9,15},{10,... | collective-permute-start | bytes 786440 | tf_op jit(solution)/shard_map/ppermute | solution.py:562
  185.6 10.1 %collective-permute-start.30 = (bf16[256,512]{1,0:T(8,128)(2,1)S(1)}, bf16[256,512]{1,0:T(8,128)(2,1)S(1)}, u32[]{:S(2)}, u32[]{:S(2)}) collective-permute-start(bf16[256,512]{1,0:T(8,128)(2,1)S(1)} %get-tuple-element.110), channel_id=1, source_target_pairs={{0,4},{1,5},{2,6},{3,7},{4,0},{5,1},{6,2},{7,3},{8,12},{9,13},{10,... | collective-permute-start | bytes 786440 | tf_op jit(solution)/shard_map/ppermute | solution.py:562
  (22 other events, 303.5 us)
Sparse Core Ops, SparseCore 0:
  32.7 103.5 all-gather.2

commit v9 on v8

--- a/solution.py
+++ b/solution.py
@@ -295,13 +295,13 @@
 
 def pack_kernel(*refs):
     for i in range(8):
-        refs[8][i] = refs[i][...]
+        refs[8][i // 2, :, (i % 2) * WIDTH : (i % 2 + 1) * WIDTH] = refs[i][...]
 
 
 def packed(pieces):
     return pl.pallas_call(
         pack_kernel,
-        out_shape=jax.ShapeDtypeStruct((8, EXT, WIDTH), BF16),
+        out_shape=jax.ShapeDtypeStruct((4, EXT, 2 * WIDTH), BF16),
         in_specs=vspecs(8),
         out_specs=pl.BlockSpec(memory_space=pltpu.VMEM),
         compiler_params=params(),
@@ -310,7 +310,7 @@
 
 
 STATE = jax.ShapeDtypeStruct((GS, WIDTH), F32)
-AHEAD = 3
+AHEAD = 4
 
 
 def project_kernel(
@@ -327,7 +327,7 @@
             high = odd if e == 1 else 1 - odd
             copy = pltpu.make_async_copy(
                 w_ref.at[gathered_at(src_y, high * 2 + odd, b % 2)],
-                wbuf.at[i, :, :, pl.ds(b * LANES, LANES)],
+                wbuf.at[i // 2, :, pl.ds((i % 2) * WIDTH, WIDTH), pl.ds(b * LANES, LANES)],
                 wsem.at[i, b],
             )
             copy.start()
@@ -336,14 +336,14 @@
 
     pending = [piece_copies(i) for i in range(AHEAD)]
     sums = [None] * 3
-    for i in range(8):
-        for copy in pending[i]:
+    for pair in range(4):
+        for copy in pending[2 * pair] + pending[2 * pair + 1]:
             copy.wait()
-        if i + AHEAD < 8:
-            pending.append(piece_copies(i + AHEAD))
+        for i in range(2 * pair + AHEAD, min(8, 2 * pair + 2 + AHEAD)):
+            pending.append(piece_copies(i))
         for j in range(3):
-            prod = jnp.dot(hidden_ref[i], wbuf[i, j], preferred_element_type=F32)
-            sums[j] = prod if i == 0 else sums[j] + prod
+            prod = jnp.dot(hidden_ref[pair], wbuf[pair, j], preferred_element_type=F32)
+            sums[j] = prod if pair == 0 else sums[j] + prod
     q_ref[...] = sums[0].astype(BF16)
     for block in range(WIDTH // LANES):
         cols = slice(block * LANES, (block + 1) * LANES)
@@ -371,7 +371,7 @@
         in_specs=[SMEM_SPEC] + vspecs(1) + hspecs(1) + vspecs(2),
         out_specs=vspecs(3),
         scratch_shapes=[
-            pltpu.VMEM((8, 3, WIDTH, WIDTH), BF16),
+            pltpu.VMEM((4, 3, 2 * WIDTH, WIDTH), BF16),
             pltpu.VMEM((EXT, LANES), F32),
             pltpu.VMEM((EXT, LANES), F32),
             pltpu.SemaphoreType.DMA((8, 4)),

time: 205 us -> 205 us (level)
  no operation moved by 1% of the time
where the time goes in v9:
time: 205 us; the launch traced here: 204 us
  waiting for transfers between devices  101 us (49%)
  starting transfers between devices  52 us (25%)
  Pallas kernels  29.7 us (14%)
  between operations  13.7 us (7%)
  local copies, waits for them, and re-layouts  5.97 us (3%)
    ppermute x2, waiting for transfers between devices, sum_shares(): crossed = lax.ppermute(total_other, 'mp', H_SWAP)  21.5 us
    all_gather x1, waiting for transfers between devices, body(): weights = lax.all_gather(moved, 'ctx', axis_index_groups=[GATHER_ORDER])  19.2 us
    ppermute x6, waiting for transfers between devices, sum_shares(): got = [lax.ppermute(other[d], 'mp', x_shift(d)) for d in (1, 3, 2)]  14.2 us
    ppermute x1, waiting for transfers between devices, body(): crossed = lax.ppermute(extended, 'mp', H_SWAP)  13.8 us
    ppermute x1, waiting for transfers between devices, body(): moved = lax.ppermute(in_weight, ('ctx', 'mp'), weight_moves())  12.3 us
    ppermute x3, waiting for transfers between devices, body(): lax.ppermute(crossed, 'mp', x_shift(d))  11.3 us
    ppermute x6, starting transfers between devices, sum_shares(): got = [lax.ppermute(other[d], 'mp', x_shift(d)) for d in (1, 3, 2)]  10.5 us
    ppermute x6, starting transfers between devices, sum_shares(): got_mine = [lax.ppermute(mine[d], 'mp', x_shift(d)) for d in (1, 3, 2)]  8.73 us
  transfers between devices with their start and end apart: 32, of which 22 were waited for; matrix products, arithmetic and copies ran while one was open for 1% of the time, Pallas kernels for 8%

profile of v9, /device:TPU:2, one launch (start us, length us, event | category | flops | bytes accessed | tf_op | source)
XLA Modules:
  0.0 204.3 jit_solution(2867739772625961838)
XLA Ops:
  6.5 4.3 %collective-permute-start.1 = (bf16[3,512,128]{2,1,0:T(8,128)(2,1)}, bf16[3,512,128]{2,1,0:T(8,128)(2,1)}, u32[]{:S(2)}, u32[]{:S(2)}) collective-permute-start(bf16[3,512,128]{2,1,0:T(8,128)(2,1)} %param.19), channel_id=1, source_target_pairs={{0,144},{1,176},{2,208},{3,240},{4,16},{5,48},{6,80},{7,112},{8,15... | collective-permute-start | bytes 1179656 | tf_op jit(solution)/shard_map/ppermute | solution.py:580
  17.2 3.1 %toeplitz.1.toep_ref = bf16[4096,256]{1,0:T(8,128)(2,1)S(1)} custom-call(f32[128,32]{1,0:T(8,128)S(1)} %copy.14.taps_ref), custom_call_target="tpu_custom_call" | custom-call | tf_op jit(solution)/shard_map/toeplitz/pallas_call | solution.py:108
  20.3 12.3 %collective-permute-done.1 = bf16[3,512,128]{2,1,0:T(8,128)(2,1)} collective-permute-done((bf16[3,512,128]{2,1,0:T(8,128)(2,1)}, bf16[3,512,128]{2,1,0:T(8,128)(2,1)}, u32[]{:S(2)}, u32[]{:S(2)}) %collective-permute-start.1) | collective-permute-done | bytes 393248 | tf_op jit(solution)/shard_map/ppermute | solution.py:580
  33.7 4.0 %mr_op.1 = (bf16[256,512]{1,0:T(8,128)(2,1)S(1)}, bf16[256,512]{1,0:T(8,128)(2,1)S(1)}, bf16[256,512]{1,0:T(8,128)(2,1)S(1)}, bf16[256,512]{1,0:T(8,128)(2,1)S(1)}, bf16[256,512]{1,0:T(8,128)(2,1)S(1)}) custom-call(s32[5]{0:T(128)S(1)} %stack.23.where_ref, bf16[256,512]{1,0:T(8,128)(2,1)S(1)} %get-tuple-element.58.q_ref, ...), custom_call_target="tpu_custom_call" | custom-call | tf_op jit(solution)/shard_map/mr_op/pallas_call | solution.py:277
  37.7 4.6 %collective-permute-start.2 = (bf16[256,512]{1,0:T(8,128)(2,1)S(1)}, bf16[256,512]{1,0:T(8,128)(2,1)S(1)}, u32[]{:S(2)}, u32[]{:S(2)}) collective-permute-start(bf16[256,512]{1,0:T(8,128)(2,1)S(1)} %get-tuple-element.65), channel_id=1, source_target_pairs={{0,2},{1,3},{2,4},{3,5},{4,6},{5,7},{6,0},{7,1},{8,10},{9,11},{10,... | collective-permute-start | bytes 786440 | tf_op jit(solution)/shard_map/ppermute | solution.py:556
  43.8 2.1 %shares.2 = (bf16[256,512]{1,0:T(8,128)(2,1)S(1)}, bf16[256,512]{1,0:T(8,128)(2,1)S(1)}, bf16[256,512]{1,0:T(8,128)(2,1)S(1)}, bf16[256,512]{1,0:T(8,128)(2,1)S(1)}) custom-call(s32[5]{0:T(128)S(1)} %stack.23.where_ref, bf16[256,512]{1,0:T(8,128)(2,1)S(1)} %get-tuple-element.68.y_ref, bf16[512,4096]{1,0:T(8,128)(2,1)S(1)} %copy-done), custom_call_target="tpu_custom_call" | custom-call | tf_op jit(solution)/shard_map/shares/pallas_call | solution.py:239
  45.9 6.7 %collective-permute-done.2 = bf16[256,512]{1,0:T(8,128)(2,1)S(1)} collective-permute-done((bf16[256,512]{1,0:T(8,128)(2,1)S(1)}, bf16[256,512]{1,0:T(8,128)(2,1)S(1)}, u32[]{:S(2)}, u32[]{:S(2)}) %collective-permute-start.2) | collective-permute-done | bytes 262176 | tf_op jit(solution)/shard_map/ppermute | solution.py:556
  55.9 3.0 %collective-permute-start.8 = (bf16[256,512]{1,0:T(8,128)(2,1)S(1)}, bf16[256,512]{1,0:T(8,128)(2,1)S(1)}, u32[]{:S(2)}, u32[]{:S(2)}) collective-permute-start(bf16[256,512]{1,0:T(8,128)(2,1)S(1)} %get-tuple-element.77), channel_id=1, source_target_pairs={{0,4},{1,5},{2,6},{3,7},{4,0},{5,1},{6,2},{7,3},{8,12},{9,13},{10,... | collective-permute-start | bytes 786440 | tf_op jit(solution)/shard_map/ppermute | solution.py:562
  58.9 16.7 %collective-permute-done.5 = bf16[256,512]{1,0:T(8,128)(2,1)S(1)} collective-permute-done((bf16[256,512]{1,0:T(8,128)(2,1)S(1)}, bf16[256,512]{1,0:T(8,128)(2,1)S(1)}, u32[]{:S(2)}, u32[]{:S(2)}) %collective-permute-start.5) | collective-permute-done | bytes 262176 | tf_op jit(solution)/shard_map/ppermute | solution.py:561
  79.1 3.8 %prep.1 = (bf16[4096,256]{1,0:T(8,128)(2,1)S(1)}, f32[256,512]{1,0:T(8,128)S(1)}, f32[256,512]{1,0:T(8,128)S(1)}, f32[16,512]{1,0:T(8,128)S(1)}) custom-call(f32[16,32]{1,0:T(8,128)S(1)} %bitcast.8, f32[16,32]{1,0:T(8,128)S(1)} %bitcast.9), custom_call_target="tpu_custom_call" | custom-call | tf_op jit(solution)/shard_map/prep/pallas_call | solution.py:166
  87.8 13.8 %collective-permute-done.13.refs_4_ = bf16[272,512]{1,0:T(8,128)(2,1)S(1)} collective-permute-done((bf16[272,512]{1,0:T(8,128)(2,1)S(1)}, bf16[272,512]{1,0:T(8,128)(2,1)S(1)}, u32[]{:S(2)}, u32[]{:S(2)}) %collective-permute-start.13) | collective-permute-done | bytes 278560 | tf_op jit(solution)/shard_map/ppermute | solution.py:594
  105.7 8.5 %collective-permute-done.14.refs_5_ = bf16[272,512]{1,0:T(8,128)(2,1)S(1)} collective-permute-done((bf16[272,512]{1,0:T(8,128)(2,1)S(1)}, bf16[272,512]{1,0:T(8,128)(2,1)S(1)}, u32[]{:S(2)}, u32[]{:S(2)}) %collective-permute-start.14) | collective-permute-done | bytes 278560 | tf_op jit(solution)/shard_map/ppermute | solution.py:598
  114.4 2.6 %collective-permute-done.16.refs_7_ = bf16[272,512]{1,0:T(8,128)(2,1)S(1)} collective-permute-done((bf16[272,512]{1,0:T(8,128)(2,1)S(1)}, bf16[272,512]{1,0:T(8,128)(2,1)S(1)}, u32[]{:S(2)}, u32[]{:S(2)}) %collective-permute-start.16) | collective-permute-done | bytes 278560 | tf_op jit(solution)/shard_map/ppermute | solution.py:598
  117.2 19.2 %all-gather.3.cloned.1.call-done = bf16[96,512,128]{2,1,0:T(8,128)(2,1)} async-done(((bf16[3,512,128]{2,1,0:T(8,128)(2,1)}), bf16[96,512,128]{2,1,0:T(8,128)(2,1)}) %all-gather.3.cloned.1.call-update) | async-done | bytes 12582928 | tf_op jit(solution)/shard_map/all_gather | solution.py:585
  136.4 7.9 %project.1 = (bf16[272,512]{1,0:T(8,128)(2,1)S(1)}, bf16[256,512]{1,0:T(8,128)(2,1)S(1)}, f32[16,512]{1,0:T(8,128)S(1)}) custom-call(s32[5]{0:T(128)S(1)} %stack.23.where_ref, bf16[4,272,1024]{2,1,0:T(8,128)(2,1)S(1)} %packed.1.hidden_ref, bf16[32,3,512,128]{3,2,1,0:T(8,128)(2,1)} %bitcast.10, f32[3,3,512]{2,1,0:T(4,128)S(1)} %copy-done.7, ...), custom_call_target="tpu_custom_call" | custom-call | tf_op jit(solution)/shard_map/project/pallas_call | solution.py:368
  149.1 2.3 %collective-permute-start.20 = (f32[16,512]{1,0:T(8,128)S(1)}, f32[16,512]{1,0:T(8,128)S(1)}, u32[]{:S(2)}, u32[]{:S(2)}) collective-permute-start(f32[16,512]{1,0:T(8,128)S(1)} %chip_state.1.c0), channel_id=1, source_target_pairs={{0,48},{8,56},{16,0},{24,8},{32,16},{40,24},{48,32},{56,40},{64,11... | collective-permute-start | bytes 98312 | tf_op jit(solution)/shard_map/ppermute | solution.py:603
  155.3 2.5 %collective-permute-start.22 = (f32[16,512]{1,0:T(8,128)S(1)}, f32[16,512]{1,0:T(8,128)S(1)}, u32[]{:S(2)}, u32[]{:S(2)}) collective-permute-start(f32[16,512]{1,0:T(8,128)S(1)} %get-tuple-element.96), channel_id=1, source_target_pairs={{0,128},{8,136},{16,144},{24,152},{32,160},{40,168},{48,176},{56,1... | collective-permute-start | bytes 98312 | tf_op jit(solution)/shard_map/ppermute | solution.py:607
  161.6 3.5 %li_outer.1 = (bf16[256,512]{1,0:T(8,128)(2,1)S(1)}, bf16[256,512]{1,0:T(8,128)(2,1)S(1)}, bf16[256,512]{1,0:T(8,128)(2,1)S(1)}, bf16[256,512]{1,0:T(8,128)(2,1)S(1)}, bf16[256,512]{1,0:T(8,128)(2,1)S(1)}) custom-call(s32[5]{0:T(128)S(1)} %stack.23.where_ref, f32[256,512]{1,0:T(8,128)S(1)} %li_inner.1.conv_ref, ...), custom_call_target="tpu_custom_call" | custom-call | tf_op jit(solution)/shard_map/li_outer/pallas_call | solution.py:480
  169.6 2.1 %shares.3 = (bf16[256,512]{1,0:T(8,128)(2,1)S(1)}, bf16[256,512]{1,0:T(8,128)(2,1)S(1)}, bf16[256,512]{1,0:T(8,128)(2,1)S(1)}, bf16[256,512]{1,0:T(8,128)(2,1)S(1)}) custom-call(s32[5]{0:T(128)S(1)} %stack.23.where_ref, bf16[256,512]{1,0:T(8,128)(2,1)S(1)} %get-tuple-element.101.y_ref, bf16[512,4096]{1,0:T(8,128)(2,1)S(1)} %copy-done.1), custom_call_target="tpu_custom_call" | custom-call | tf_op jit(solution)/shard_map/shares/pallas_call | solution.py:239
  171.7 2.3 %collective-permute-done.24 = bf16[256,512]{1,0:T(8,128)(2,1)S(1)} collective-permute-done((bf16[256,512]{1,0:T(8,128)(2,1)S(1)}, bf16[256,512]{1,0:T(8,128)(2,1)S(1)}, u32[]{:S(2)}, u32[]{:S(2)}) %collective-permute-start.24) | collective-permute-done | bytes 262176 | tf_op jit(solution)/shard_map/ppermute | solution.py:556
  175.7 2.8 %collective-permute-done.26 = bf16[256,512]{1,0:T(8,128)(2,1)S(1)} collective-permute-done((bf16[256,512]{1,0:T(8,128)(2,1)S(1)}, bf16[256,512]{1,0:T(8,128)(2,1)S(1)}, u32[]{:S(2)}, u32[]{:S(2)}) %collective-permute-start.26) | collective-permute-done | bytes 262176 | tf_op jit(solution)/shard_map/ppermute | solution.py:556
  178.7 5.7 %collective-permute-start.27 = (bf16[256,512]{1,0:T(8,128)(2,1)S(1)}, bf16[256,512]{1,0:T(8,128)(2,1)S(1)}, u32[]{:S(2)}, u32[]{:S(2)}) collective-permute-start(bf16[256,512]{1,0:T(8,128)(2,1)S(1)} %add_convert_fusion.1), channel_id=1, source_target_pairs={{0,1},{1,0},{2,3},{3,2},{4,5},{5,4},{6,7},{7,6},{8,9},{9,8},{10,11... | collective-permute-start | bytes 786440 | tf_op jit(solution)/shard_map/ppermute | solution.py:561
  188.2 4.8 %collective-permute-done.27 = bf16[256,512]{1,0:T(8,128)(2,1)S(1)} collective-permute-done((bf16[256,512]{1,0:T(8,128)(2,1)S(1)}, bf16[256,512]{1,0:T(8,128)(2,1)S(1)}, u32[]{:S(2)}, u32[]{:S(2)}) %collective-permute-start.27) | collective-permute-done | bytes 262176 | tf_op jit(solution)/shard_map/ppermute | solution.py:561
  193.7 2.8 %collective-permute-done.30 = bf16[256,512]{1,0:T(8,128)(2,1)S(1)} collective-permute-done((bf16[256,512]{1,0:T(8,128)(2,1)S(1)}, bf16[256,512]{1,0:T(8,128)(2,1)S(1)}, u32[]{:S(2)}, u32[]{:S(2)}) %collective-permute-start.30) | collective-permute-done | bytes 262176 | tf_op jit(solution)/shard_map/ppermute | solution.py:562
  (91 shorter events, 49.2 us)
Async XLA Ops:
  6.5 129.8 %all-gather.3.cloned.1.call-start = ((), (), s32[]{:S(2)}) async-start(), calls=%async_computation | async-start | bytes 12976128 | tf_op jit(solution)/shard_map/all_gather | solution.py:585
  6.5 26.1 %collective-permute-start.1 = (bf16[3,512,128]{2,1,0:T(8,128)(2,1)}, bf16[3,512,128]{2,1,0:T(8,128)(2,1)}, u32[]{:S(2)}, u32[]{:S(2)}) collective-permute-start(bf16[3,512,128]{2,1,0:T(8,128)(2,1)} %param.19), channel_id=1, source_target_pairs={{0,144},{1,176},{2,208},{3,240},{4,16},{5,48},{6,80},{7,112},{8,15... | collective-permute-start | bytes 1179656 | tf_op jit(solution)/shard_map/ppermute | solution.py:580
  37.7 15.0 %collective-permute-start.2 = (bf16[256,512]{1,0:T(8,128)(2,1)S(1)}, bf16[256,512]{1,0:T(8,128)(2,1)S(1)}, u32[]{:S(2)}, u32[]{:S(2)}) collective-permute-start(bf16[256,512]{1,0:T(8,128)(2,1)S(1)} %get-tuple-element.65), channel_id=1, source_target_pairs={{0,2},{1,3},{2,4},{3,5},{4,6},{5,7},{6,0},{7,1},{8,10},{9,11},{10,... | collective-permute-start | bytes 786440 | tf_op jit(solution)/shard_map/ppermute | solution.py:556
  42.3 10.9 %collective-permute-start.3 = (bf16[256,512]{1,0:T(8,128)(2,1)S(1)}, bf16[256,512]{1,0:T(8,128)(2,1)S(1)}, u32[]{:S(2)}, u32[]{:S(2)}) collective-permute-start(bf16[256,512]{1,0:T(8,128)(2,1)S(1)} %get-tuple-element.66), channel_id=1, source_target_pairs={{0,6},{1,7},{2,0},{3,1},{4,2},{5,3},{6,4},{7,5},{8,14},{9,15},{10,... | collective-permute-start | bytes 786440 | tf_op jit(solution)/shard_map/ppermute | solution.py:556
  42.3 10.9 %collective-permute-start.4 = (bf16[256,512]{1,0:T(8,128)(2,1)S(1)}, bf16[256,512]{1,0:T(8,128)(2,1)S(1)}, u32[]{:S(2)}, u32[]{:S(2)}) collective-permute-start(bf16[256,512]{1,0:T(8,128)(2,1)S(1)} %get-tuple-element.67), channel_id=1, source_target_pairs={{0,4},{1,5},{2,6},{3,7},{4,0},{5,1},{6,2},{7,3},{8,12},{9,13},{10,... | collective-permute-start | bytes 786440 | tf_op jit(solution)/shard_map/ppermute | solution.py:556
  53.4 22.2 %collective-permute-start.5 = (bf16[256,512]{1,0:T(8,128)(2,1)S(1)}, bf16[256,512]{1,0:T(8,128)(2,1)S(1)}, u32[]{:S(2)}, u32[]{:S(2)}) collective-permute-start(bf16[256,512]{1,0:T(8,128)(2,1)S(1)} %add_convert_fusion.3), channel_id=1, source_target_pairs={{0,1},{1,0},{2,3},{3,2},{4,5},{5,4},{6,7},{7,6},{8,9},{9,8},{10,11... | collective-permute-start | bytes 786440 | tf_op jit(solution)/shard_map/ppermute | solution.py:561
  53.9 21.8 %collective-permute-start.6 = (bf16[256,512]{1,0:T(8,128)(2,1)S(1)}, bf16[256,512]{1,0:T(8,128)(2,1)S(1)}, u32[]{:S(2)}, u32[]{:S(2)}) collective-permute-start(bf16[256,512]{1,0:T(8,128)(2,1)S(1)} %get-tuple-element.75), channel_id=1, source_target_pairs={{0,2},{1,3},{2,4},{3,5},{4,6},{5,7},{6,0},{7,1},{8,10},{9,11},{10,... | collective-permute-start | bytes 786440 | tf_op jit(solution)/shard_map/ppermute | solution.py:562
  55.5 20.2 %collective-permute-start.7 = (bf16[256,512]{1,0:T(8,128)(2,1)S(1)}, bf16[256,512]{1,0:T(8,128)(2,1)S(1)}, u32[]{:S(2)}, u32[]{:S(2)}) collective-permute-start(bf16[256,512]{1,0:T(8,128)(2,1)S(1)} %get-tuple-element.76), channel_id=1, source_target_pairs={{0,6},{1,7},{2,0},{3,1},{4,2},{5,3},{6,4},{7,5},{8,14},{9,15},{10,... | collective-permute-start | bytes 786440 | tf_op jit(solution)/shard_map/ppermute | solution.py:562
  55.9 19.8 %collective-permute-start.8 = (bf16[256,512]{1,0:T(8,128)(2,1)S(1)}, bf16[256,512]{1,0:T(8,128)(2,1)S(1)}, u32[]{:S(2)}, u32[]{:S(2)}) collective-permute-start(bf16[256,512]{1,0:T(8,128)(2,1)S(1)} %get-tuple-element.77), channel_id=1, source_target_pairs={{0,4},{1,5},{2,6},{3,7},{4,0},{5,1},{6,2},{7,3},{8,12},{9,13},{10,... | collective-permute-start | bytes 786440 | tf_op jit(solution)/shard_map/ppermute | solution.py:562
  78.0 23.5 %collective-permute-start.13 = (bf16[272,512]{1,0:T(8,128)(2,1)S(1)}, bf16[272,512]{1,0:T(8,128)(2,1)S(1)}, u32[]{:S(2)}, u32[]{:S(2)}) collective-permute-start(bf16[272,512]{1,0:T(8,128)(2,1)S(1)} %pad_maximum_fusion.refs_0_), channel_id=1, source_target_pairs={{0,1},{1,0},{2,3},{3,2},{4,5},{5,4},{6,7},{7,6},{8,9},{9,8},{10,11... | collective-permute-start | bytes 835592 | tf_op jit(solution)/shard_map/ppermute | solution.py:594
  78.1 26.0 %collective-permute-start.10 = (bf16[272,512]{1,0:T(8,128)(2,1)S(1)}, bf16[272,512]{1,0:T(8,128)(2,1)S(1)}, u32[]{:S(2)}, u32[]{:S(2)}) collective-permute-start(bf16[272,512]{1,0:T(8,128)(2,1)S(1)} %pad_maximum_fusion.refs_0_), channel_id=1, source_target_pairs={{0,2},{1,3},{2,4},{3,5},{4,6},{5,7},{6,0},{7,1},{8,10},{9,11},{10,... | collective-permute-start | bytes 835592 | tf_op jit(solution)/shard_map/ppermute | solution.py:595
  84.2 21.5 %collective-permute-start.11 = (bf16[272,512]{1,0:T(8,128)(2,1)S(1)}, bf16[272,512]{1,0:T(8,128)(2,1)S(1)}, u32[]{:S(2)}, u32[]{:S(2)}) collective-permute-start(bf16[272,512]{1,0:T(8,128)(2,1)S(1)} %pad_maximum_fusion.refs_0_), channel_id=1, source_target_pairs={{0,4},{1,5},{2,6},{3,7},{4,0},{5,1},{6,2},{7,3},{8,12},{9,13},{10,... | collective-permute-start | bytes 835592 | tf_op jit(solution)/shard_map/ppermute | solution.py:595
  86.1 19.6 %collective-permute-start.12 = (bf16[272,512]{1,0:T(8,128)(2,1)S(1)}, bf16[272,512]{1,0:T(8,128)(2,1)S(1)}, u32[]{:S(2)}, u32[]{:S(2)}) collective-permute-start(bf16[272,512]{1,0:T(8,128)(2,1)S(1)} %pad_maximum_fusion.refs_0_), channel_id=1, source_target_pairs={{0,6},{1,7},{2,0},{3,1},{4,2},{5,3},{6,4},{7,5},{8,14},{9,15},{10,... | collective-permute-start | bytes 835592 | tf_op jit(solution)/shard_map/ppermute | solution.py:595
  101.5 12.7 %collective-permute-start.14 = (bf16[272,512]{1,0:T(8,128)(2,1)S(1)}, bf16[272,512]{1,0:T(8,128)(2,1)S(1)}, u32[]{:S(2)}, u32[]{:S(2)}) collective-permute-start(bf16[272,512]{1,0:T(8,128)(2,1)S(1)} %collective-permute-done.13.refs_4_), channel_id=1, source_target_pairs={{0,2},{1,3},{2,4},{3,5},{4,6},{5,7},{6,0},{7,1},{8,10},{9,11},{10,... | collective-permute-start | bytes 835592 | tf_op jit(solution)/shard_map/ppermute | solution.py:598
  103.3 11.1 %collective-permute-start.15 = (bf16[272,512]{1,0:T(8,128)(2,1)S(1)}, bf16[272,512]{1,0:T(8,128)(2,1)S(1)}, u32[]{:S(2)}, u32[]{:S(2)}) collective-permute-start(bf16[272,512]{1,0:T(8,128)(2,1)S(1)} %collective-permute-done.13.refs_4_), channel_id=1, source_target_pairs={{0,4},{1,5},{2,6},{3,7},{4,0},{5,1},{6,2},{7,3},{8,12},{9,13},{10,... | collective-permute-start | bytes 835592 | tf_op jit(solution)/shard_map/ppermute | solution.py:598
  104.1 12.8 %collective-permute-start.16 = (bf16[272,512]{1,0:T(8,128)(2,1)S(1)}, bf16[272,512]{1,0:T(8,128)(2,1)S(1)}, u32[]{:S(2)}, u32[]{:S(2)}) collective-permute-start(bf16[272,512]{1,0:T(8,128)(2,1)S(1)} %collective-permute-done.13.refs_4_), channel_id=1, source_target_pairs={{0,6},{1,7},{2,0},{3,1},{4,2},{5,3},{6,4},{7,5},{8,14},{9,15},{10,... | collective-permute-start | bytes 835592 | tf_op jit(solution)/shard_map/ppermute | solution.py:598
  146.1 6.0 %collective-permute-start.18 = (f32[16,512]{1,0:T(8,128)S(1)}, f32[16,512]{1,0:T(8,128)S(1)}, u32[]{:S(2)}, u32[]{:S(2)}) collective-permute-start(f32[16,512]{1,0:T(8,128)S(1)} %chip_state.1.c0), channel_id=1, source_target_pairs={{0,16},{8,24},{16,32},{24,40},{32,48},{40,56},{48,0},{56,8},{64,80... | collective-permute-start | bytes 98312 | tf_op jit(solution)/shard_map/ppermute | solution.py:603
  165.2 8.8 %collective-permute-start.24 = (bf16[256,512]{1,0:T(8,128)(2,1)S(1)}, bf16[256,512]{1,0:T(8,128)(2,1)S(1)}, u32[]{:S(2)}, u32[]{:S(2)}) collective-permute-start(bf16[256,512]{1,0:T(8,128)(2,1)S(1)} %get-tuple-element.98), channel_id=1, source_target_pairs={{0,2},{1,3},{2,4},{3,5},{4,6},{5,7},{6,0},{7,1},{8,10},{9,11},{10,... | collective-permute-start | bytes 786440 | tf_op jit(solution)/shard_map/ppermute | solution.py:556
  166.9 8.8 %collective-permute-start.25 = (bf16[256,512]{1,0:T(8,128)(2,1)S(1)}, bf16[256,512]{1,0:T(8,128)(2,1)S(1)}, u32[]{:S(2)}, u32[]{:S(2)}) collective-permute-start(bf16[256,512]{1,0:T(8,128)(2,1)S(1)} %get-tuple-element.99), channel_id=1, source_target_pairs={{0,6},{1,7},{2,0},{3,1},{4,2},{5,3},{6,4},{7,5},{8,14},{9,15},{10,... | collective-permute-start | bytes 786440 | tf_op jit(solution)/shard_map/ppermute | solution.py:556
  167.5 11.1 %collective-permute-start.26 = (bf16[256,512]{1,0:T(8,128)(2,1)S(1)}, bf16[256,512]{1,0:T(8,128)(2,1)S(1)}, u32[]{:S(2)}, u32[]{:S(2)}) collective-permute-start(bf16[256,512]{1,0:T(8,128)(2,1)S(1)} %get-tuple-element.100), channel_id=1, source_target_pairs={{0,4},{1,5},{2,6},{3,7},{4,0},{5,1},{6,2},{7,3},{8,12},{9,13},{10,... | collective-permute-start | bytes 786440 | tf_op jit(solution)/shard_map/ppermute | solution.py:556
  178.7 14.3 %collective-permute-start.27 = (bf16[256,512]{1,0:T(8,128)(2,1)S(1)}, bf16[256,512]{1,0:T(8,128)(2,1)S(1)}, u32[]{:S(2)}, u32[]{:S(2)}) collective-permute-start(bf16[256,512]{1,0:T(8,128)(2,1)S(1)} %add_convert_fusion.1), channel_id=1, source_target_pairs={{0,1},{1,0},{2,3},{3,2},{4,5},{5,4},{6,7},{7,6},{8,9},{9,8},{10,11... | collective-permute-start | bytes 786440 | tf_op jit(solution)/shard_map/ppermute | solution.py:561
  184.4 8.6 %collective-permute-start.28 = (bf16[256,512]{1,0:T(8,128)(2,1)S(1)}, bf16[256,512]{1,0:T(8,128)(2,1)S(1)}, u32[]{:S(2)}, u32[]{:S(2)}) collective-permute-start(bf16[256,512]{1,0:T(8,128)(2,1)S(1)} %get-tuple-element.108), channel_id=1, source_target_pairs={{0,2},{1,3},{2,4},{3,5},{4,6},{5,7},{6,0},{7,1},{8,10},{9,11},{10,... | collective-permute-start | bytes 786440 | tf_op jit(solution)/shard_map/ppermute | solution.py:562
  184.4 9.3 %collective-permute-start.29 = (bf16[256,512]{1,0:T(8,128)(2,1)S(1)}, bf16[256,512]{1,0:T(8,128)(2,1)S(1)}, u32[]{:S(2)}, u32[]{:S(2)}) collective-permute-start(bf16[256,512]{1,0:T(8,128)(2,1)S(1)} %get-tuple-element.109), channel_id=1, source_target_pairs={{0,6},{1,7},{2,0},{3,1},{4,2},{5,3},{6,4},{7,5},{8,14},{9,15},{10,... | collective-permute-start | bytes 786440 | tf_op jit(solution)/shard_map/ppermute | solution.py:562
  186.5 10.1 %collective-permute-start.30 = (bf16[256,512]{1,0:T(8,128)(2,1)S(1)}, bf16[256,512]{1,0:T(8,128)(2,1)S(1)}, u32[]{:S(2)}, u32[]{:S(2)}) collective-permute-start(bf16[256,512]{1,0:T(8,128)(2,1)S(1)} %get-tuple-element.110), channel_id=1, source_target_pairs={{0,4},{1,5},{2,6},{3,7},{4,0},{5,1},{6,2},{7,3},{8,12},{9,13},{10,... | collective-permute-start | bytes 786440 | tf_op jit(solution)/shard_map/ppermute | solution.py:562
  (22 other events, 304.5 us)
Sparse Core Ops, SparseCore 0:
  32.7 103.5 all-gather.2
